TPU v7x, 256 devices: a whole 4x4x8 slice. The times are simulated.
256 devices in a mesh: dp: 64 (over x, z, core), tensor: 4 (over y).
Axes of the slice: x: 4, y: 4, z: 8, core: 2. Of those that a mesh axis runs over, the one named last changes fastest.
Arguments:
- features: bfloat16 [1, 16384, 4096], P(None, 'dp', 'tensor'), may hold values from -6 to 6
- cotangent: bfloat16 [1, 16384, 11008], P(None, 'dp', 'tensor'), may hold values from -16 to 16
- basis: bfloat16 [1, 4096, 512], P(None, 'tensor'), may hold values from -0.25 to 0.25
- first_moment: float32 [1, 11008, 512], P(None, ('tensor', 'dp')), may hold values from -0.06 to 0.06
- second_moment: float32 [1, 11008, 512], P(None, ('tensor', 'dp')), may hold values from 1e-07 to 1e-05
Outputs:
- new_first: float32 [1, 11008, 512], P(None, ('tensor', 'dp'))
- new_second: float32 [1, 11008, 512], P(None, ('tensor', 'dp'))
- weight_change: bfloat16 [1, 4096, 4, 2752], P(None, 'tensor', None, 'dp')
All inputs are finite; a program needn't handle non-finite values.
Results may differ from a plain program's by a relative error of at most 0.0059.
Values may be sent and summed in bfloat16 or wider, within the bound.
No kernel may reach another device: no remote copies, remote signals or barrier semaphores. Data moves between devices by JAX's collectives and lax.ppermute only.
A program may use at most 64 MiB of HBM per device.

v0:
```python
import jax
import jax.numpy as jnp
from jax import lax
from jax.sharding import PartitionSpec as P


def make_term(cotangent, projected, layer):
    columns = cotangent[layer]
    return lax.dot_general(
        columns, projected[layer], (((0,), (0,)), ((), ())), preferred_element_type=jnp.float32
    )


def local(features, cotangent, basis, first_moment, second_moment):
    layer_count = features.shape[0]
    owned = first_moment.shape[1]
    scale = 1.0 / (features.shape[1] * lax.axis_size("dp"))
    partial_proj = jnp.einsum("ltd,ldr->ltr", features, basis, preferred_element_type=jnp.float32)
    projected = lax.psum(partial_proj, "tensor").astype(jnp.bfloat16)
    grads = jnp.stack(
        [
            lax.psum_scatter(
                make_term(cotangent, projected, 0), "dp", scatter_dimension=0, tiled=True
            )
        ]
    )
    grads = grads * scale
    new_first = 0.9 * first_moment + 0.1 * grads
    new_second = 0.999 * second_moment + 0.001 * grads * grads
    update = (
        new_first / (1.0 - 0.9**10) / (jnp.sqrt(new_second / (1.0 - 0.999**10)) + 1e-08)
    ).astype(jnp.bfloat16)
    change = jnp.einsum(
        "ldr,lcr->ldc",
        basis,
        lax.all_gather(update, "tensor", axis=1, tiled=True),
        preferred_element_type=jnp.float32,
    )
    rows_here = basis.shape[1]
    weight_change = change.astype(jnp.bfloat16).reshape(
        layer_count, rows_here, lax.axis_size("tensor"), owned
    )
    return (new_first, new_second, weight_change)


def solution(mesh):
    return jax.shard_map(
        local,
        mesh=mesh,
        in_specs=(
            P(None, "dp", "tensor"),
            P(None, "dp", "tensor"),
            P(None, "tensor", None),
            P(None, ("tensor", "dp"), None),
            P(None, ("tensor", "dp"), None),
        ),
        out_specs=(
            P(None, ("tensor", "dp"), None),
            P(None, ("tensor", "dp"), None),
            P(None, "tensor", None, "dp"),
        ),
        check_vma=False,
    )
```

profile of v0, /device:TPU:38, one launch (start us, length us, event | category | flops | bytes accessed | tf_op | source)
XLA Modules:
  0.0 234.8 jit_solution(6105404311601979917)
XLA Ops:
  0.6 1.9 convolution_bitcast_fusion.1
  2.6 23.1 %all-reduce.3 = bf16[1,256,512]{2,1,0:T(8,128)(2,1)S(1)} all-reduce(f32[1,256,512]{2,1,0:T(8,128)S(1)} %convolution_bitcast_fusion.1), channel_id=1, replica_groups=mesh['dp'=64,'tensor'=4] {'tensor'}, use_global_device_ids=true, to_apply=%region_0.0 | all-reduce | flops 131072 | bytes 786432 | tf_op jit(solution)/shard_map/psum | solution.py:19
  25.7 3.3 %convolution_bitcast_fusion = f32[2752,512]{1,0:T(8,128)} fusion(bf16[1,256,2752]{1,2,0:T(8,128)(2,1)S(1)} %copy-done, bf16[1,256,512]{2,1,0:T(8,128)(2,1)S(1)} %all-reduce.3), kind=kOutput, calls=%fused_computation | convolution fusion | flops 721420288 | bytes 7307264 | tf_op jit(solution)/shard_map/dot_general | solution.py:9
  29.0 127.7 %fusion = f32[48,512]{1,0:T(8,128)S(1)} fusion(f32[2752,512]{1,0:T(8,128)} %convolution_bitcast_fusion), kind=kCustom, calls=%all-reduce-scatter | all-reduce-scatter fusion | flops 1572865 | bytes 5735424
  156.7 1.9 collective-permute-start
  158.6 13.1 %collective-permute-start.6 = (f32[27,512]{1,0:T(8,128)S(1)}, f32[27,512]{1,0:T(8,128)S(1)}, u32[]{:S(2)}, u32[]{:S(2)}) collective-permute-start(f32[27,512]{1,0:T(8,128)S(1)} %slice), channel_id=1, source_target_pairs={{0,28},{4,32},{8,36},{12,40},{16,44},{20,48},{24,52},{28,56},{32,6... | collective-permute-start | bytes 165896
  171.7 7.8 %collective-permute-start.1 = (f32[48,512]{1,0:T(8,128)S(1)}, f32[48,512]{1,0:T(8,128)S(1)}, u32[]{:S(2)}, u32[]{:S(2)}) collective-permute-start(f32[48,512]{1,0:T(8,128)S(1)} %fusion), channel_id=1, source_target_pairs={{0,8},{4,12},{8,16},{12,20},{16,24},{20,28},{24,32},{28,36},{32,40... | collective-permute-start | bytes 294920
  179.5 10.8 %collective-permute-start.2 = (f32[48,512]{1,0:T(8,128)S(1)}, f32[48,512]{1,0:T(8,128)S(1)}, u32[]{:S(2)}, u32[]{:S(2)}) collective-permute-start(f32[48,512]{1,0:T(8,128)S(1)} %fusion), channel_id=1, source_target_pairs={{0,12},{4,16},{8,20},{12,24},{16,28},{20,32},{24,36},{28,40},{32,4... | collective-permute-start | bytes 294920
  190.3 1.9 collective-permute-start.3
  192.2 1.9 collective-permute-start.4
  194.2 1.9 collective-permute-start.5
  196.1 0.6 dynamic-slice.4
  197.4 4.3 %collective-permute-done.3 = f32[48,512]{1,0:T(8,128)S(1)} collective-permute-done((f32[48,512]{1,0:T(8,128)S(1)}, f32[48,512]{1,0:T(8,128)S(1)}, u32[]{:S(2)}, u32[]{:S(2)}) %collective-permute-start.3) | collective-permute-done | bytes 98336
  201.7 6.6 %collective-permute-done.4 = f32[48,512]{1,0:T(8,128)S(1)} collective-permute-done((f32[48,512]{1,0:T(8,128)S(1)}, f32[48,512]{1,0:T(8,128)S(1)}, u32[]{:S(2)}, u32[]{:S(2)}) %collective-permute-start.4) | collective-permute-done | bytes 98336
  208.2 0.6 copy-done.4
  208.9 3.8 %collective-permute-done.5 = f32[48,512]{1,0:T(8,128)} collective-permute-done((f32[48,512]{1,0:T(8,128)S(1)}, f32[48,512]{1,0:T(8,128)}, u32[]{:S(2)}, u32[]{:S(2)}) %collective-permute-start.5) | collective-permute-done | bytes 98336
  212.7 5.0 %concatenate = f32[363,512]{1,0:T(8,128)S(1)} concatenate(f32[27,512]{1,0:T(8,128)} %copy-done.5, f32[48,512]{1,0:T(8,128)} %collective-permute-done.5, f32[48,512]{1,0:T(8,128)} %copy-done.4, f32[48,512]{1,0:T(8,128)} %copy-done.3, f32[48,512]{1,0:T(8,128)} %copy-done.2, f32[48,512]{1,0:T(8,128)S(1)} %collective-permute-done.1, f32[48,512]{1,0:T(8,128)S(1)} %collective-permute-done, ...), dimensions={0} | concatenate | bytes 1486848
  217.8 1.0 divide_convert_fusion
  218.9 12.9 %all_gather.3 = bf16[1,172,512]{2,0,1:T(2,128)(2,1)S(1)} all-gather(bf16[1,43,512]{2,0,1:T(2,128)(2,1)S(1)} %copy.26), channel_id=1, replica_groups=mesh['dp'=64,'tensor'=4] {'tensor'}, dimensions={1}, use_global_device_ids=true | all-gather | bytes 220160 | tf_op jit(solution)/shard_map/all_gather | solution.py:36
  231.7 0.5 fusion.2
  232.2 0.1 reshape.30
  232.4 1.0 copy.29
  233.4 0.7 copy.27
  234.1 0.7 copy.28
  (19 shorter events, 0.1 us)
Async XLA Ops:
  0.6 25.0 %copy-start = (bf16[1,256,2752]{1,2,0:T(8,128)(2,1)S(1)}, bf16[1,256,2752]{1,2,0:T(8,128)(2,1)}, u32[]{:S(2)}) copy-start(bf16[1,256,2752]{1,2,0:T(8,128)(2,1)} %param.6) | copy-start | bytes 4227076
  25.6 170.4 %copy-start.6 = (u32[256]{0:T(256)S(1)}, u32[256]{0:T(256)}, u32[]{:S(2)}) copy-start(u32[256]{0:T(256)} %constant.24) | copy-start | bytes 3076
  29.0 202.7 %copy-start.1 = (bf16[1,1024,512]{2,1,0:T(8,128)(2,1)S(1)}, bf16[1,1024,512]{2,1,0:T(8,128)(2,1)}, u32[]{:S(2)}) copy-start(bf16[1,1024,512]{2,1,0:T(8,128)(2,1)} %param.7) | copy-start | bytes 3145732
  156.7 37.5 %collective-permute-start = (f32[48,512]{1,0:T(8,128)S(1)}, f32[48,512]{1,0:T(8,128)S(1)}, u32[]{:S(2)}, u32[]{:S(2)}) collective-permute-start(f32[48,512]{1,0:T(8,128)S(1)} %fusion), channel_id=1, source_target_pairs={{0,4},{4,8},{8,12},{12,16},{16,20},{20,24},{24,28},{28,32},{32,36}... | collective-permute-start | bytes 294920
  158.6 33.6 %collective-permute-start.6 = (f32[27,512]{1,0:T(8,128)S(1)}, f32[27,512]{1,0:T(8,128)S(1)}, u32[]{:S(2)}, u32[]{:S(2)}) collective-permute-start(f32[27,512]{1,0:T(8,128)S(1)} %slice), channel_id=1, source_target_pairs={{0,28},{4,32},{8,36},{12,40},{16,44},{20,48},{24,52},{28,56},{32,6... | collective-permute-start | bytes 165896
  171.7 25.6 %collective-permute-start.1 = (f32[48,512]{1,0:T(8,128)S(1)}, f32[48,512]{1,0:T(8,128)S(1)}, u32[]{:S(2)}, u32[]{:S(2)}) collective-permute-start(f32[48,512]{1,0:T(8,128)S(1)} %fusion), channel_id=1, source_target_pairs={{0,8},{4,12},{8,16},{12,20},{16,24},{20,28},{24,32},{28,36},{32,40... | collective-permute-start | bytes 294920
  179.5 17.9 %collective-permute-start.2 = (f32[48,512]{1,0:T(8,128)S(1)}, f32[48,512]{1,0:T(8,128)S(1)}, u32[]{:S(2)}, u32[]{:S(2)}) collective-permute-start(f32[48,512]{1,0:T(8,128)S(1)} %fusion), channel_id=1, source_target_pairs={{0,12},{4,16},{8,20},{12,24},{16,28},{20,32},{24,36},{28,40},{32,4... | collective-permute-start | bytes 294920
  190.3 11.4 %collective-permute-start.3 = (f32[48,512]{1,0:T(8,128)S(1)}, f32[48,512]{1,0:T(8,128)S(1)}, u32[]{:S(2)}, u32[]{:S(2)}) collective-permute-start(f32[48,512]{1,0:T(8,128)S(1)} %fusion), channel_id=1, source_target_pairs={{0,16},{4,20},{8,24},{12,28},{16,32},{20,36},{24,40},{28,44},{32,4... | collective-permute-start | bytes 294920
  192.2 2.0 copy-start.5
  192.2 16.0 %collective-permute-start.4 = (f32[48,512]{1,0:T(8,128)S(1)}, f32[48,512]{1,0:T(8,128)S(1)}, u32[]{:S(2)}, u32[]{:S(2)}) collective-permute-start(f32[48,512]{1,0:T(8,128)S(1)} %fusion), channel_id=1, source_target_pairs={{0,20},{4,24},{8,28},{12,32},{16,36},{20,40},{24,44},{28,48},{32,5... | collective-permute-start | bytes 294920
  194.2 18.6 %collective-permute-start.5 = (f32[48,512]{1,0:T(8,128)S(1)}, f32[48,512]{1,0:T(8,128)}, u32[]{:S(2)}, u32[]{:S(2)}) collective-permute-start(f32[48,512]{1,0:T(8,128)S(1)} %fusion), channel_id=1, source_target_pairs={{0,24},{4,28},{8,32},{12,36},{16,40},{20,44},{24,48},{28,52},{32,5... | collective-permute-start | bytes 294920
  197.4 10.9 %copy-start.2 = (f32[48,512]{1,0:T(8,128)}, f32[48,512]{1,0:T(8,128)S(1)}, u32[]{:S(2)}) copy-start(f32[48,512]{1,0:T(8,128)S(1)} %collective-permute-done.2) | copy-start | bytes 294916
  201.7 6.6 %copy-start.3 = (f32[48,512]{1,0:T(8,128)}, f32[48,512]{1,0:T(8,128)S(1)}, u32[]{:S(2)}) copy-start(f32[48,512]{1,0:T(8,128)S(1)} %collective-permute-done.3) | copy-start | bytes 294916
  208.2 0.6 copy-start.4
where the time goes:
time: 236 us; the launch traced here: 235 us
  blocking collectives  164 us (69%)
  starting transfers between devices  39.3 us (17%)
  waiting for transfers between devices  14.7 us (6%)
  local copies, waits for them, and re-layouts  8.94 us (4%)
  matrix products  5.76 us (2%)
    unnamed x1, blocking collectives  128 us
    unnamed x7, starting transfers between devices  39.3 us
    psum x1, blocking collectives, local(): projected = lax.psum(partial_proj, 'tensor').astype(jnp.bfloat16)  23.1 us
    unnamed x7, waiting for transfers between devices  14.7 us
    all_gather x1, blocking collectives, local(): lax.all_gather(update, 'tensor', axis=1, tiled=True)  12.9 us
    unnamed x20, local copies, waits for them, and re-layouts  8.77 us
  transfers between devices with their start and end apart: 7, of which 3 were waited for; matrix products, arithmetic and copies ran while one was open for 0% of the time, Pallas kernels for 0%

commit v1 on v0

v1 whole, which is shorter than its diff:
```python
import functools

import jax
import jax.numpy as jnp
from jax import lax
from jax.experimental import pallas as pl
from jax.experimental.pallas import tpu as pltpu
from jax.sharding import PartitionSpec as P

NX, NZ, NCORE, NY = 4, 8, 2, 4
OWNED, PADDED = 43, 48
BF, F32 = jnp.bfloat16, jnp.float32

Z_ORDER = (7, 3, 5, 1, 6, 2, 4, 0)
X_ORDER = {0: (2, 1, 3, 0), 1: (2, 3, 1, 0)}
X_STEPS = {0: (1, 3), 1: (3, 1)}


def send_dp(value, move):
    pairs = []
    for d in range(NX * NZ * NCORE):
        x, z, c = d // (NZ * NCORE), (d // NCORE) % NZ, d % NCORE
        x, z, c = move(x, z, c)
        pairs.append((d, (x * NZ + z) * NCORE + c))
    return lax.ppermute(value, "dp", pairs)


def swap_core(value):
    return send_dp(value, lambda x, z, c: (x, z, 1 - c))


def swap_x(value, m):
    return send_dp(value, lambda x, z, c: (x ^ m, z, c))


def swap_z(value, m, shift):
    return send_dp(value, lambda x, z, c: (x, (((z + shift) % NZ) ^ m) - shift & (NZ - 1), c))


def swap_y(value, m):
    return lax.ppermute(value, "tensor", [(y, y ^ m) for y in range(NY)])


def arrange_kernel(order_ref, core_ref, source, a_send, a_keep, b_send, b_keep, blocks):
    rows = source.shape[0]

    def unpack(core):
        for n in range(NX * NZ):
            first = (2 * n + core) * OWNED
            low = first // 16 * 16
            high = min(rows, -(-(first + PADDED) // 16) * 16)
            piece = source[low:high, :].astype(F32)
            piece = piece[first - low : min(first - low + PADDED, high - low), :]
            if piece.shape[0] < PADDED:
                fill = jnp.zeros((PADDED - piece.shape[0], piece.shape[1]), F32)
                piece = jnp.concatenate([piece, fill], axis=0)
            blocks[n] = piece.astype(BF)

    for core in range(NCORE):
        pl.when(core_ref[0] == core)(functools.partial(unpack, core))
    half = NX * NZ // 2
    for k, out in enumerate((a_send, a_keep, b_send, b_keep)):
        for i in range(half):
            out[i * PADDED : (i + 1) * PADDED, :] = blocks[order_ref[k * half + i]]


def arrange(order, core, source):
    half = NX * NZ // 2 * PADDED
    shape = jax.ShapeDtypeStruct((half, source.shape[1]), BF)
    vmem = pl.BlockSpec(memory_space=pltpu.VMEM)
    smem = pl.BlockSpec(memory_space=pltpu.SMEM)
    return pl.pallas_call(
        arrange_kernel,
        out_shape=[shape] * 4,
        in_specs=[smem, smem, vmem],
        out_specs=[vmem] * 4,
        scratch_shapes=[pltpu.VMEM((NX * NZ, PADDED, source.shape[1]), BF)],
        compiler_params=pltpu.CompilerParams(vmem_limit_bytes=16 * 1024 * 1024),
        cost_estimate=pl.CostEstimate(flops=0, bytes_accessed=8 * 1024 * 1024, transcendentals=0),
    )(order, core, source)


def dot(a, b):
    return lax.dot_general(a, b, (((1,), (0,)), ((), ())), preferred_element_type=F32)


def local(features, cotangent, basis, first_moment, second_moment):
    rank = basis.shape[2]
    half = rank // 2
    scale = 1.0 / (features.shape[1] * lax.axis_size("dp"))
    dp = lax.axis_index("dp")
    core, z, x = dp % NCORE, (dp // NCORE) % NZ, dp // (NCORE * NZ)
    y = lax.axis_index("tensor")

    columns = cotangent[0].T
    other_columns = swap_core(columns)
    order = []
    for part in range(2):
        zz = jnp.array(Z_ORDER, jnp.int32) ^ ((z + part) % NZ)
        zz = (zz + NZ - part) % NZ
        xx = jnp.array(X_ORDER[part], jnp.int32) ^ x
        order.append((xx[:, None] * NZ + zz[None, :]).reshape(-1))
    order = jnp.concatenate(order)
    core1 = core.reshape(1)
    mine = arrange(order, core1, columns)
    theirs = arrange(order, core1, other_columns)

    partial = dot(features[0], basis[0])
    halves = [partial[:, :half], partial[:, half:]]
    for step in range(2):
        came = [swap_y(halves[p].astype(BF), X_STEPS[p][step]) for p in range(2)]
        halves = [h + c.astype(F32) for h, c in zip(halves, came)]
    projected = jnp.concatenate([h.astype(BF) for h in halves], axis=1)
    other_projected = swap_core(projected)

    def term(k, p):
        lanes = slice(p * half, (p + 1) * half)
        return dot(mine[k], projected[:, lanes]) + dot(theirs[k], other_projected[:, lanes])

    sends = [term(2 * p, p).astype(BF) for p in range(2)]
    came = [swap_x(sends[p], X_STEPS[p][0]) for p in range(2)]
    kept = [term(2 * p + 1, p) for p in range(2)]
    kept = [k + c.astype(F32) for k, c in zip(kept, came)]
    n = NZ * PADDED
    came = [swap_x(kept[p][:n].astype(BF), X_STEPS[p][1]) for p in range(2)]
    kept = [k[n:] + c.astype(F32) for k, c in zip(kept, came)]
    for m in (1, 2, 4):
        n //= 2
        came = [swap_z(kept[p][:n].astype(BF), m, p) for p in range(2)]
        kept = [k[n:] + c.astype(F32) for k, c in zip(kept, came)]

    grads = (jnp.concatenate([k[:OWNED] for k in kept], axis=1) * scale)[None]
    new_first = 0.9 * first_moment + 0.1 * grads
    new_second = 0.999 * second_moment + 0.001 * grads * grads
    update = (
        new_first / (1.0 - 0.9**10) / (jnp.sqrt(new_second / (1.0 - 0.999**10)) + 1e-08)
    ).astype(BF)[0]

    around = [update] + [swap_y(update, m) for m in (1, 2, 3)]
    ordered = jnp.stack([lax.select_n(y ^ a, *around) for a in range(NY)])
    change = jnp.einsum("dr,acr->dac", basis[0], ordered, preferred_element_type=F32)
    return (new_first, new_second, change.astype(BF)[None])


def solution(mesh):
    return jax.shard_map(
        local,
        mesh=mesh,
        in_specs=(
            P(None, "dp", "tensor"),
            P(None, "dp", "tensor"),
            P(None, "tensor", None),
            P(None, ("tensor", "dp"), None),
            P(None, ("tensor", "dp"), None),
        ),
        out_specs=(
            P(None, ("tensor", "dp"), None),
            P(None, ("tensor", "dp"), None),
            P(None, "tensor", None, "dp"),
        ),
        check_vma=False,
    )
```

time: 236 us -> 77.4 us (0.33)
  the two profiles are of different devices: /device:TPU:38 before, /device:TPU:32 now
where the time goes in v1:
time: 77.4 us; the launch traced here: 76.1 us
  starting transfers between devices  35.9 us (46%)
  waiting for transfers between devices  28.3 us (37%)
  matrix products  4.06 us (5%)
  local copies, waits for them, and re-layouts  3.89 us (5%)
  Pallas kernels  2.31 us (3%)
  between operations  1.01 us (1%)
    ppermute x12, starting transfers between devices, send_dp(): return lax.ppermute(value, 'dp', pairs)  25 us
    ppermute x12, waiting for transfers between devices, send_dp(): return lax.ppermute(value, 'dp', pairs)  17.6 us
    ppermute x7, starting transfers between devices, swap_y(): return lax.ppermute(value, 'tensor', [(y, y ^ m) for y in range(NY)])  10.9 us
    ppermute x7, waiting for transfers between devices, swap_y(): return lax.ppermute(value, 'tensor', [(y, y ^ m) for y in range(NY)])  10.7 us
    unnamed x17, local copies, waits for them, and re-layouts  3.59 us
    dot_general x9, matrix products, dot(): lax.dot_general(a, b, (((1,), (0,)), ((), ())), preferred_element_type=F32)  3.56 us
    pallas_call x2, Pallas kernels, arrange(): pl.pallas_call(arrange_kernel, out_shape=[shape] * 4, in_specs=[smem, sme...  2.31 us
  transfers between devices with their start and end apart: 19, of which 11 were waited for; matrix products, arithmetic and copies ran while one was open for 7% of the time, Pallas kernels for 3%

profile of v1, /device:TPU:32, one launch (start us, length us, event | category | flops | bytes accessed | tf_op | source)
XLA Modules:
  0.0 76.1 jit_solution(14708910940511839299)
XLA Ops:
  0.8 1.1 %copy-done = bf16[1,1024,512]{2,1,0:T(8,128)(2,1)S(1)} copy-done((bf16[1,1024,512]{2,1,0:T(8,128)(2,1)S(1)}, bf16[1,1024,512]{2,1,0:T(8,128)(2,1)}, u32[]{:S(2)}) %copy-start) | copy-done | bytes 1048600
  1.9 1.5 %fusion.6 = f32[256,512]{1,0:T(8,128)S(1)} fusion(bf16[1,1024,512]{2,1,0:T(8,128)(2,1)S(1)} %copy-done, bf16[1,256,1024]{2,1,0:T(8,128)(2,1)} %param.9), kind=kOutput, calls=%fused_computation.11 | convolution fusion | flops 268435456 | bytes 2097152 | tf_op jit(solution)/shard_map/dot_general | solution.py:84
  3.4 1.7 %collective-permute-start = (bf16[256,256]{1,0:T(8,128)(2,1)S(1)}, bf16[256,256]{1,0:T(8,128)(2,1)S(1)}, u32[]{:S(2)}, u32[]{:S(2)}) collective-permute-start(bf16[256,256]{1,0:T(8,128)(2,1)S(1)} %get-tuple-element.29), channel_id=1, source_target_pairs={{0,1},{1,0},{2,3},{3,2},{4,5},{5,4},{6,7},{7,6},{8,9},{9,8},{10,11... | collective-permute-start | bytes 393224 | tf_op jit(solution)/shard_map/ppermute | solution.py:41
  5.0 2.2 %collective-permute-start.3 = (bf16[256,256]{1,0:T(8,128)(2,1)S(1)}, bf16[256,256]{1,0:T(8,128)(2,1)S(1)}, u32[]{:S(2)}, u32[]{:S(2)}) collective-permute-start(bf16[256,256]{1,0:T(8,128)(2,1)S(1)} %get-tuple-element.30), channel_id=1, source_target_pairs={{0,3},{1,2},{2,1},{3,0},{4,7},{5,6},{6,5},{7,4},{8,11},{9,10},{10,... | collective-permute-start | bytes 393224 | tf_op jit(solution)/shard_map/ppermute | solution.py:41
  7.3 1.4 %collective-permute-done = bf16[256,256]{1,0:T(8,128)(2,1)S(1)} collective-permute-done((bf16[256,256]{1,0:T(8,128)(2,1)S(1)}, bf16[256,256]{1,0:T(8,128)(2,1)S(1)}, u32[]{:S(2)}, u32[]{:S(2)}) %collective-permute-start) | collective-permute-done | bytes 131104 | tf_op jit(solution)/shard_map/ppermute | solution.py:41
  8.7 2.5 %collective-permute-done.3 = bf16[256,256]{1,0:T(8,128)(2,1)S(1)} collective-permute-done((bf16[256,256]{1,0:T(8,128)(2,1)S(1)}, bf16[256,256]{1,0:T(8,128)(2,1)S(1)}, u32[]{:S(2)}, u32[]{:S(2)}) %collective-permute-start.3) | collective-permute-done | bytes 131104 | tf_op jit(solution)/shard_map/ppermute | solution.py:41
  11.3 2.3 %collective-permute-start.1 = (bf16[256,256]{1,0:T(8,128)(2,1)S(1)}, bf16[256,256]{1,0:T(8,128)(2,1)S(1)}, u32[]{:S(2)}, u32[]{:S(2)}) collective-permute-start(bf16[256,256]{1,0:T(8,128)(2,1)S(1)} %get-tuple-element.27), channel_id=1, source_target_pairs={{0,3},{1,2},{2,1},{3,0},{4,7},{5,6},{6,5},{7,4},{8,11},{9,10},{10,... | collective-permute-start | bytes 393224 | tf_op jit(solution)/shard_map/ppermute | solution.py:41
  13.6 4.0 %collective-permute-done.1 = bf16[256,256]{1,0:T(8,128)(2,1)S(1)} collective-permute-done((bf16[256,256]{1,0:T(8,128)(2,1)S(1)}, bf16[256,256]{1,0:T(8,128)(2,1)S(1)}, u32[]{:S(2)}, u32[]{:S(2)}) %collective-permute-start.1) | collective-permute-done | bytes 131104 | tf_op jit(solution)/shard_map/ppermute | solution.py:41
  19.8 1.6 %shard_map.113 = (bf16[768,256]{1,0:T(8,128)(2,1)S(1)}, bf16[768,256]{1,0:T(8,128)(2,1)S(1)}, bf16[768,256]{1,0:T(8,128)(2,1)S(1)}, bf16[768,256]{1,0:T(8,128)(2,1)S(1)}) custom-call(s32[64]{0:T(128)S(1)} %pad_add_fusion.order_ref, s32[1]{0:T(128)} %bitcast.core_ref, bf16[2752,256]{1,0:T(8,128)(2,1)} %collective-permute-done.2.source), custom_call_target="tpu_custom_call" | custom-call | bytes 8388608 | tf_op jit(solution)/shard_map/pallas_call | solution.py:72
  21.9 1.6 %collective-permute-start.6 = (bf16[768,256]{1,0:T(8,128)(2,1)S(1)}, bf16[768,256]{1,0:T(8,128)(2,1)S(1)}, u32[]{:S(2)}, u32[]{:S(2)}) collective-permute-start(bf16[768,256]{1,0:T(8,128)(2,1)S(1)} %fusion.2), channel_id=1, source_target_pairs={{0,64},{4,68},{8,72},{12,76},{16,80},{20,84},{24,88},{28,92},{32,9... | collective-permute-start | bytes 1179656 | tf_op jit(solution)/shard_map/ppermute | solution.py:25
  24.0 2.2 %collective-permute-start.11 = (bf16[768,256]{1,0:T(8,128)(2,1)S(1)}, bf16[768,256]{1,0:T(8,128)(2,1)S(1)}, u32[]{:S(2)}, u32[]{:S(2)}) collective-permute-start(bf16[768,256]{1,0:T(8,128)(2,1)S(1)} %fusion.3), channel_id=1, source_target_pairs={{0,192},{4,196},{8,200},{12,204},{16,208},{20,212},{24,216},{28,22... | collective-permute-start | bytes 1179656 | tf_op jit(solution)/shard_map/ppermute | solution.py:25
  26.8 7.1 %collective-permute-done.6 = bf16[768,256]{1,0:T(8,128)(2,1)S(1)} collective-permute-done((bf16[768,256]{1,0:T(8,128)(2,1)S(1)}, bf16[768,256]{1,0:T(8,128)(2,1)S(1)}, u32[]{:S(2)}, u32[]{:S(2)}) %collective-permute-start.6) | collective-permute-done | bytes 393248 | tf_op jit(solution)/shard_map/ppermute | solution.py:25
  34.1 2.8 %collective-permute-start.7 = (bf16[384,256]{1,0:T(8,128)(2,1)S(1)}, bf16[384,256]{1,0:T(8,128)(2,1)S(1)}, u32[]{:S(2)}, u32[]{:S(2)}) collective-permute-start(bf16[384,256]{1,0:T(8,128)(2,1)S(1)} %slice.165), channel_id=1, source_target_pairs={{0,192},{4,196},{8,200},{12,204},{16,208},{20,212},{24,216},{28,22... | collective-permute-start | bytes 589832 | tf_op jit(solution)/shard_map/ppermute | solution.py:25
  37.6 4.5 %collective-permute-done.7 = bf16[384,256]{1,0:T(8,128)(2,1)S(1)} collective-permute-done((bf16[384,256]{1,0:T(8,128)(2,1)S(1)}, bf16[384,256]{1,0:T(8,128)(2,1)S(1)}, u32[]{:S(2)}, u32[]{:S(2)}) %collective-permute-start.7) | collective-permute-done | bytes 196640 | tf_op jit(solution)/shard_map/ppermute | solution.py:25
  42.4 1.4 %collective-permute-done.12 = bf16[384,256]{1,0:T(8,128)(2,1)S(1)} collective-permute-done((bf16[384,256]{1,0:T(8,128)(2,1)S(1)}, bf16[384,256]{1,0:T(8,128)(2,1)S(1)}, u32[]{:S(2)}, u32[]{:S(2)}) %collective-permute-start.12) | collective-permute-done | bytes 196640 | tf_op jit(solution)/shard_map/ppermute | solution.py:25
  43.9 2.4 %collective-permute-start.13 = (bf16[192,256]{1,0:T(8,128)(2,1)S(1)}, bf16[192,256]{1,0:T(8,128)(2,1)S(1)}, u32[]{:S(2)}, u32[]{:S(2)}) collective-permute-start(bf16[192,256]{1,0:T(8,128)(2,1)S(1)} %slice.168), channel_id=1, source_target_pairs={{0,56},{4,60},{8,16},{12,20},{16,8},{20,12},{24,32},{28,36},{32,24... | collective-permute-start | bytes 294920 | tf_op jit(solution)/shard_map/ppermute | solution.py:25
  46.9 3.6 %collective-permute-start.9 = (bf16[96,256]{1,0:T(8,128)(2,1)S(1)}, bf16[96,256]{1,0:T(8,128)(2,1)S(1)}, u32[]{:S(2)}, u32[]{:S(2)}) collective-permute-start(bf16[96,256]{1,0:T(8,128)(2,1)S(1)} %slice.171), channel_id=1, source_target_pairs={{0,16},{4,20},{8,24},{12,28},{16,0},{20,4},{24,8},{28,12},{32,48},... | collective-permute-start | bytes 147464 | tf_op jit(solution)/shard_map/ppermute | solution.py:25
  50.5 4.8 %collective-permute-start.14 = (bf16[96,256]{1,0:T(8,128)(2,1)S(1)}, bf16[96,256]{1,0:T(8,128)(2,1)S(1)}, u32[]{:S(2)}, u32[]{:S(2)}) collective-permute-start(bf16[96,256]{1,0:T(8,128)(2,1)S(1)} %slice.170), channel_id=1, source_target_pairs={{0,16},{4,20},{8,56},{12,60},{16,0},{20,4},{24,40},{28,44},{32,48}... | collective-permute-start | bytes 147464 | tf_op jit(solution)/shard_map/ppermute | solution.py:25
  55.3 3.1 %collective-permute-start.10 = (bf16[48,256]{1,0:T(8,128)(2,1)S(1)}, bf16[48,256]{1,0:T(8,128)(2,1)S(1)}, u32[]{:S(2)}, u32[]{:S(2)}) collective-permute-start(bf16[48,256]{1,0:T(8,128)(2,1)S(1)} %slice.173), channel_id=1, source_target_pairs={{0,32},{4,36},{8,40},{12,44},{16,48},{20,52},{24,56},{28,60},{32,0... | collective-permute-start | bytes 73736 | tf_op jit(solution)/shard_map/ppermute | solution.py:25
  58.5 3.8 %collective-permute-start.15 = (bf16[48,256]{1,0:T(8,128)(2,1)S(1)}, bf16[48,256]{1,0:T(8,128)(2,1)S(1)}, u32[]{:S(2)}, u32[]{:S(2)}) collective-permute-start(bf16[48,256]{1,0:T(8,128)(2,1)S(1)} %slice.172), channel_id=1, source_target_pairs={{0,32},{4,36},{8,40},{12,44},{16,48},{20,52},{24,56},{28,60},{32,0... | collective-permute-start | bytes 73736 | tf_op jit(solution)/shard_map/ppermute | solution.py:25
  63.2 3.2 %collective-permute-done.15 = bf16[48,256]{1,0:T(8,128)(2,1)S(1)} collective-permute-done((bf16[48,256]{1,0:T(8,128)(2,1)S(1)}, bf16[48,256]{1,0:T(8,128)(2,1)S(1)}, u32[]{:S(2)}, u32[]{:S(2)}) %collective-permute-start.15) | collective-permute-done | bytes 24608 | tf_op jit(solution)/shard_map/ppermute | solution.py:25
  66.6 2.7 %collective-permute-start.17 = (bf16[43,512]{1,0:T(8,128)(2,1)S(1)}, bf16[43,512]{1,0:T(8,128)(2,1)S(1)}, u32[]{:S(2)}, u32[]{:S(2)}) collective-permute-start(bf16[43,512]{1,0:T(8,128)(2,1)S(1)} %get-tuple-element.22), channel_id=1, source_target_pairs={{0,2},{1,3},{2,0},{3,1},{4,6},{5,7},{6,4},{7,5},{8,10},{9,11},{10,... | collective-permute-start | bytes 132104 | tf_op jit(solution)/shard_map/ppermute | solution.py:41
  69.2 2.0 %collective-permute-start.18 = (bf16[43,512]{1,0:T(8,128)(2,1)S(1)}, bf16[43,512]{1,0:T(8,128)(2,1)S(1)}, u32[]{:S(2)}, u32[]{:S(2)}) collective-permute-start(bf16[43,512]{1,0:T(8,128)(2,1)S(1)} %get-tuple-element.22), channel_id=1, source_target_pairs={{0,3},{1,2},{2,1},{3,0},{4,7},{5,6},{6,5},{7,4},{8,11},{9,10},{10,... | collective-permute-start | bytes 132104 | tf_op jit(solution)/shard_map/ppermute | solution.py:41
  72.7 1.8 %collective-permute-done.18 = bf16[43,512]{1,0:T(8,128)(2,1)S(1)} collective-permute-done((bf16[43,512]{1,0:T(8,128)(2,1)S(1)}, bf16[43,512]{1,0:T(8,128)(2,1)S(1)}, u32[]{:S(2)}, u32[]{:S(2)}) %collective-permute-start.18) | collective-permute-done | bytes 44064 | tf_op jit(solution)/shard_map/ppermute | solution.py:41
  (74 shorter events, 9.9 us)
Async XLA Ops:
  0.7 6.6 %copy-start.6 = (s32[4]{0:T(128)S(1)}, s32[4]{0:T(128)}, u32[]{:S(2)}) copy-start(s32[4]{0:T(128)} %constant.111.clone) | copy-start | bytes 52
  0.7 12.9 %copy-start.5 = (s32[4]{0:T(128)S(1)}, s32[4]{0:T(128)}, u32[]{:S(2)}) copy-start(s32[4]{0:T(128)} %constant.110.clone) | copy-start | bytes 52
  0.7 19.1 %collective-permute-start.2 = (bf16[2752,256]{1,0:T(8,128)(2,1)}, bf16[2752,256]{1,0:T(8,128)(2,1)}, u32[]{:S(2)}, u32[]{:S(2)}) collective-permute-start(bf16[2752,256]{1,0:T(8,128)(2,1)} %bitcast.43), channel_id=1, source_target_pairs={{0,4},{4,0},{8,12},{12,8},{16,20},{20,16},{24,28},{28,24},{32,36},... | collective-permute-start | bytes 4227080 | tf_op jit(solution)/shard_map/ppermute | solution.py:25
  3.4 5.3 %collective-permute-start = (bf16[256,256]{1,0:T(8,128)(2,1)S(1)}, bf16[256,256]{1,0:T(8,128)(2,1)S(1)}, u32[]{:S(2)}, u32[]{:S(2)}) collective-permute-start(bf16[256,256]{1,0:T(8,128)(2,1)S(1)} %get-tuple-element.29), channel_id=1, source_target_pairs={{0,1},{1,0},{2,3},{3,2},{4,5},{5,4},{6,7},{7,6},{8,9},{9,8},{10,11... | collective-permute-start | bytes 393224 | tf_op jit(solution)/shard_map/ppermute | solution.py:41
  5.0 6.2 %collective-permute-start.3 = (bf16[256,256]{1,0:T(8,128)(2,1)S(1)}, bf16[256,256]{1,0:T(8,128)(2,1)S(1)}, u32[]{:S(2)}, u32[]{:S(2)}) collective-permute-start(bf16[256,256]{1,0:T(8,128)(2,1)S(1)} %get-tuple-element.30), channel_id=1, source_target_pairs={{0,3},{1,2},{2,1},{3,0},{4,7},{5,6},{6,5},{7,4},{8,11},{9,10},{10,... | collective-permute-start | bytes 393224 | tf_op jit(solution)/shard_map/ppermute | solution.py:41
  7.3 11.8 %copy-start.1 = (bf16[1,256,2752]{1,2,0:T(8,128)(2,1)S(1)}, bf16[1,256,2752]{1,2,0:T(8,128)(2,1)}, u32[]{:S(2)}) copy-start(bf16[1,256,2752]{1,2,0:T(8,128)(2,1)} %param.10) | copy-start | bytes 4227076
  11.3 6.3 %collective-permute-start.1 = (bf16[256,256]{1,0:T(8,128)(2,1)S(1)}, bf16[256,256]{1,0:T(8,128)(2,1)S(1)}, u32[]{:S(2)}, u32[]{:S(2)}) collective-permute-start(bf16[256,256]{1,0:T(8,128)(2,1)S(1)} %get-tuple-element.27), channel_id=1, source_target_pairs={{0,3},{1,2},{2,1},{3,0},{4,7},{5,6},{6,5},{7,4},{8,11},{9,10},{10,... | collective-permute-start | bytes 393224 | tf_op jit(solution)/shard_map/ppermute | solution.py:41
  13.5 5.0 %collective-permute-start.4 = (bf16[256,256]{1,0:T(8,128)(2,1)S(1)}, bf16[256,256]{1,0:T(8,128)(2,1)S(1)}, u32[]{:S(2)}, u32[]{:S(2)}) collective-permute-start(bf16[256,256]{1,0:T(8,128)(2,1)S(1)} %get-tuple-element.28), channel_id=1, source_target_pairs={{0,1},{1,0},{2,3},{3,2},{4,5},{5,4},{6,7},{7,6},{8,9},{9,8},{10,11... | collective-permute-start | bytes 393224 | tf_op jit(solution)/shard_map/ppermute | solution.py:41
  18.6 2.8 %collective-permute-start.5 = (bf16[256,512]{1,0:T(8,128)(2,1)S(1)}, bf16[256,512]{1,0:T(8,128)(2,1)S(1)}, u32[]{:S(2)}, u32[]{:S(2)}) collective-permute-start(bf16[256,512]{1,0:T(8,128)(2,1)S(1)} %pad_maximum_fusion), channel_id=1, source_target_pairs={{0,4},{4,0},{8,12},{12,8},{16,20},{20,16},{24,28},{28,24},{32,36},... | collective-permute-start | bytes 786440 | tf_op jit(solution)/shard_map/ppermute | solution.py:25
  21.9 11.9 %collective-permute-start.6 = (bf16[768,256]{1,0:T(8,128)(2,1)S(1)}, bf16[768,256]{1,0:T(8,128)(2,1)S(1)}, u32[]{:S(2)}, u32[]{:S(2)}) collective-permute-start(bf16[768,256]{1,0:T(8,128)(2,1)S(1)} %fusion.2), channel_id=1, source_target_pairs={{0,64},{4,68},{8,72},{12,76},{16,80},{20,84},{24,88},{28,92},{32,9... | collective-permute-start | bytes 1179656 | tf_op jit(solution)/shard_map/ppermute | solution.py:25
  24.0 12.9 %collective-permute-start.11 = (bf16[768,256]{1,0:T(8,128)(2,1)S(1)}, bf16[768,256]{1,0:T(8,128)(2,1)S(1)}, u32[]{:S(2)}, u32[]{:S(2)}) collective-permute-start(bf16[768,256]{1,0:T(8,128)(2,1)S(1)} %fusion.3), channel_id=1, source_target_pairs={{0,192},{4,196},{8,200},{12,204},{16,208},{20,212},{24,216},{28,22... | collective-permute-start | bytes 1179656 | tf_op jit(solution)/shard_map/ppermute | solution.py:25
  34.1 8.0 %collective-permute-start.7 = (bf16[384,256]{1,0:T(8,128)(2,1)S(1)}, bf16[384,256]{1,0:T(8,128)(2,1)S(1)}, u32[]{:S(2)}, u32[]{:S(2)}) collective-permute-start(bf16[384,256]{1,0:T(8,128)(2,1)S(1)} %slice.165), channel_id=1, source_target_pairs={{0,192},{4,196},{8,200},{12,204},{16,208},{20,212},{24,216},{28,22... | collective-permute-start | bytes 589832 | tf_op jit(solution)/shard_map/ppermute | solution.py:25
  37.3 6.5 %collective-permute-start.12 = (bf16[384,256]{1,0:T(8,128)(2,1)S(1)}, bf16[384,256]{1,0:T(8,128)(2,1)S(1)}, u32[]{:S(2)}, u32[]{:S(2)}) collective-permute-start(bf16[384,256]{1,0:T(8,128)(2,1)S(1)} %slice.164), channel_id=1, source_target_pairs={{0,64},{4,68},{8,72},{12,76},{16,80},{20,84},{24,88},{28,92},{32,9... | collective-permute-start | bytes 589832 | tf_op jit(solution)/shard_map/ppermute | solution.py:25
  42.2 4.7 %collective-permute-start.8 = (bf16[192,256]{1,0:T(8,128)(2,1)S(1)}, bf16[192,256]{1,0:T(8,128)(2,1)S(1)}, u32[]{:S(2)}, u32[]{:S(2)}) collective-permute-start(bf16[192,256]{1,0:T(8,128)(2,1)S(1)} %slice.169), channel_id=1, source_target_pairs={{0,8},{4,12},{8,0},{12,4},{16,24},{20,28},{24,16},{28,20},{32,40},... | collective-permute-start | bytes 294920 | tf_op jit(solution)/shard_map/ppermute | solution.py:25
  43.8 22.6 %copy-start.2 = (f32[1,43,512]{2,0,1:T(1,128)S(1)}, f32[1,43,512]{2,0,1:T(1,128)}, u32[]{:S(2)}) copy-start(f32[1,43,512]{2,0,1:T(1,128)} %param.13) | copy-start | bytes 264196
  43.8 22.6 %copy-start.3 = (f32[1,43,512]{2,0,1:T(1,128)S(1)}, f32[1,43,512]{2,0,1:T(1,128)}, u32[]{:S(2)}) copy-start(f32[1,43,512]{2,0,1:T(1,128)} %param.12) | copy-start | bytes 264196
  43.9 6.6 %collective-permute-start.13 = (bf16[192,256]{1,0:T(8,128)(2,1)S(1)}, bf16[192,256]{1,0:T(8,128)(2,1)S(1)}, u32[]{:S(2)}, u32[]{:S(2)}) collective-permute-start(bf16[192,256]{1,0:T(8,128)(2,1)S(1)} %slice.168), channel_id=1, source_target_pairs={{0,56},{4,60},{8,16},{12,20},{16,8},{20,12},{24,32},{28,36},{32,24... | collective-permute-start | bytes 294920 | tf_op jit(solution)/shard_map/ppermute | solution.py:25
  46.9 8.4 %collective-permute-start.9 = (bf16[96,256]{1,0:T(8,128)(2,1)S(1)}, bf16[96,256]{1,0:T(8,128)(2,1)S(1)}, u32[]{:S(2)}, u32[]{:S(2)}) collective-permute-start(bf16[96,256]{1,0:T(8,128)(2,1)S(1)} %slice.171), channel_id=1, source_target_pairs={{0,16},{4,20},{8,24},{12,28},{16,0},{20,4},{24,8},{28,12},{32,48},... | collective-permute-start | bytes 147464 | tf_op jit(solution)/shard_map/ppermute | solution.py:25
  50.5 8.0 %collective-permute-start.14 = (bf16[96,256]{1,0:T(8,128)(2,1)S(1)}, bf16[96,256]{1,0:T(8,128)(2,1)S(1)}, u32[]{:S(2)}, u32[]{:S(2)}) collective-permute-start(bf16[96,256]{1,0:T(8,128)(2,1)S(1)} %slice.170), channel_id=1, source_target_pairs={{0,16},{4,20},{8,56},{12,60},{16,0},{20,4},{24,40},{28,44},{32,48}... | collective-permute-start | bytes 147464 | tf_op jit(solution)/shard_map/ppermute | solution.py:25
  55.3 7.8 %collective-permute-start.10 = (bf16[48,256]{1,0:T(8,128)(2,1)S(1)}, bf16[48,256]{1,0:T(8,128)(2,1)S(1)}, u32[]{:S(2)}, u32[]{:S(2)}) collective-permute-start(bf16[48,256]{1,0:T(8,128)(2,1)S(1)} %slice.173), channel_id=1, source_target_pairs={{0,32},{4,36},{8,40},{12,44},{16,48},{20,52},{24,56},{28,60},{32,0... | collective-permute-start | bytes 73736 | tf_op jit(solution)/shard_map/ppermute | solution.py:25
  58.5 7.8 %collective-permute-start.15 = (bf16[48,256]{1,0:T(8,128)(2,1)S(1)}, bf16[48,256]{1,0:T(8,128)(2,1)S(1)}, u32[]{:S(2)}, u32[]{:S(2)}) collective-permute-start(bf16[48,256]{1,0:T(8,128)(2,1)S(1)} %slice.172), channel_id=1, source_target_pairs={{0,32},{4,36},{8,40},{12,44},{16,48},{20,52},{24,56},{28,60},{32,0... | collective-permute-start | bytes 73736 | tf_op jit(solution)/shard_map/ppermute | solution.py:25
  66.5 6.2 %collective-permute-start.16 = (bf16[43,512]{1,0:T(8,128)(2,1)S(1)}, bf16[43,512]{1,0:T(8,128)(2,1)S(1)}, u32[]{:S(2)}, u32[]{:S(2)}) collective-permute-start(bf16[43,512]{1,0:T(8,128)(2,1)S(1)} %get-tuple-element.22), channel_id=1, source_target_pairs={{0,1},{1,0},{2,3},{3,2},{4,5},{5,4},{6,7},{7,6},{8,9},{9,8},{10,11... | collective-permute-start | bytes 132104 | tf_op jit(solution)/shard_map/ppermute | solution.py:41
  66.6 6.1 %collective-permute-start.17 = (bf16[43,512]{1,0:T(8,128)(2,1)S(1)}, bf16[43,512]{1,0:T(8,128)(2,1)S(1)}, u32[]{:S(2)}, u32[]{:S(2)}) collective-permute-start(bf16[43,512]{1,0:T(8,128)(2,1)S(1)} %get-tuple-element.22), channel_id=1, source_target_pairs={{0,2},{1,3},{2,0},{3,1},{4,6},{5,7},{6,4},{7,5},{8,10},{9,11},{10,... | collective-permute-start | bytes 132104 | tf_op jit(solution)/shard_map/ppermute | solution.py:41
  69.2 5.3 %collective-permute-start.18 = (bf16[43,512]{1,0:T(8,128)(2,1)S(1)}, bf16[43,512]{1,0:T(8,128)(2,1)S(1)}, u32[]{:S(2)}, u32[]{:S(2)}) collective-permute-start(bf16[43,512]{1,0:T(8,128)(2,1)S(1)} %get-tuple-element.22), channel_id=1, source_target_pairs={{0,3},{1,2},{2,1},{3,0},{4,7},{5,6},{6,5},{7,4},{8,11},{9,10},{10,... | collective-permute-start | bytes 132104 | tf_op jit(solution)/shard_map/ppermute | solution.py:41
  (2 other events, 7.8 us)

commit v2 on v1

v2 whole, which is shorter than its diff:
```python
import functools

import jax
import jax.numpy as jnp
from jax import lax
from jax.experimental import pallas as pl
from jax.experimental.pallas import tpu as pltpu
from jax.sharding import PartitionSpec as P

NX, NZ, NCORE, NY = 4, 8, 2, 4
OWNED, PADDED = 43, 48
BF, F32 = jnp.bfloat16, jnp.float32

Z_ORDER = (6, 1, 4, 7, 2, 5, 0, 3)
UP, DOWN = 2 * PADDED, 5 * PADDED


def send_dp(value, move):
    pairs = []
    for d in range(NX * NZ * NCORE):
        x, z, c = d // (NZ * NCORE), (d // NCORE) % NZ, d % NCORE
        x, z, c = move(x, z, c)
        pairs.append((d, (x * NZ + z) * NCORE + c))
    return lax.ppermute(value, "dp", pairs)


def swap_core(value):
    return send_dp(value, lambda x, z, c: (x, z, 1 - c))


def swap_x(value, m):
    return send_dp(value, lambda x, z, c: (x ^ m, z, c))


def shift_z(value, k):
    return send_dp(value, lambda x, z, c: (x, (z + k) % NZ, c))


def swap_y(value, m):
    return lax.ppermute(value, "tensor", [(y, y ^ m) for y in range(NY)])


def arrange_kernel(order_ref, core_ref, *refs):
    sources, (other, mine, blocks) = refs[:NX], refs[NX:]
    rows, tokens = sources[0].shape
    for s, source in enumerate(sources):
        for n in range(NZ * NCORE):
            first = n * OWNED
            low = first // 16 * 16
            high = min(rows, -(-(first + PADDED) // 16) * 16)
            piece = source[low:high, :].astype(F32)
            piece = piece[first - low : min(first - low + PADDED, high - low), :]
            if piece.shape[0] < PADDED:
                fill = jnp.zeros((PADDED - piece.shape[0], tokens), F32)
                piece = jnp.concatenate([piece, fill], axis=0)
            blocks[n, :, s * tokens : (s + 1) * tokens] = piece.astype(BF)
    core = core_ref[0]
    for i in range(NZ):
        place = pl.ds(i * PADDED, PADDED)
        other[place, :] = blocks[order_ref[i] * NCORE + 1 - core]
        mine[place, :] = blocks[order_ref[i] * NCORE + core]


def arrange(order, core, sources):
    rows, tokens = sources[0].shape
    shape = jax.ShapeDtypeStruct((NZ * PADDED, NX * tokens), BF)
    vmem = pl.BlockSpec(memory_space=pltpu.VMEM)
    smem = pl.BlockSpec(memory_space=pltpu.SMEM)
    return pl.pallas_call(
        arrange_kernel,
        out_shape=[shape] * 2,
        in_specs=[smem, smem] + [vmem] * NX,
        out_specs=[vmem] * 2,
        scratch_shapes=[pltpu.VMEM((NZ * NCORE, PADDED, NX * tokens), BF)],
        compiler_params=pltpu.CompilerParams(vmem_limit_bytes=16 * 1024 * 1024),
        cost_estimate=pl.CostEstimate(flops=0, bytes_accessed=8 * 1024 * 1024, transcendentals=0),
    )(order, core, *sources)


def dot(a, b):
    return lax.dot_general(a, b, (((1,), (0,)), ((), ())), preferred_element_type=F32)


def local(features, cotangent, basis, first_moment, second_moment):
    scale = 1.0 / (features.shape[1] * lax.axis_size("dp"))
    dp = lax.axis_index("dp")
    core, z, x = dp % NCORE, (dp // NCORE) % NZ, dp // (NCORE * NZ)
    y = lax.axis_index("tensor")

    columns = cotangent[0].T.reshape(NX, -1, cotangent.shape[1])
    pieces = [lax.dynamic_index_in_dim(columns, x ^ m, 0, keepdims=False) for m in range(NX)]
    pieces = pieces[:1] + [swap_x(pieces[m], m) for m in range(1, NX)]

    partial = dot(features[0], basis[0])
    sent = partial.astype(BF)
    came = [swap_y(sent, m).astype(F32) for m in range(1, NY)]
    projected = (partial + came[0] + came[1] + came[2]).astype(BF)
    projected = jnp.concatenate([projected] + [swap_x(projected, m) for m in range(1, NX)], axis=0)

    order = (jnp.array(Z_ORDER, jnp.int32) + z) % NZ
    other, mine = arrange(order, core.reshape(1), pieces)
    came = swap_core(dot(other, projected).astype(BF))
    term = dot(mine, projected) + came.astype(F32)
    lower = shift_z(term[:UP].astype(BF), 1).astype(F32)
    upper = shift_z(term[UP:DOWN].astype(BF), -1).astype(F32)
    keep = term[DOWN:] + upper
    keep = [
        keep[:PADDED] + lower[:PADDED],
        keep[PADDED:UP] + lower[PADDED:],
        keep[UP:],
    ]
    lower = shift_z(keep[0].astype(BF), -3).astype(F32)
    upper = shift_z(keep[2].astype(BF), 3).astype(F32)
    total = keep[1] + lower + upper

    grads = (total[:OWNED] * scale)[None]
    new_first = 0.9 * first_moment + 0.1 * grads
    new_second = 0.999 * second_moment + 0.001 * grads * grads
    update = (
        new_first / (1.0 - 0.9**10) / (jnp.sqrt(new_second / (1.0 - 0.999**10)) + 1e-08)
    ).astype(BF)[0]

    around = [update] + [swap_y(update, m) for m in (1, 2, 3)]
    ordered = jnp.stack([lax.select_n(y ^ a, *around) for a in range(NY)])
    change = jnp.einsum("dr,acr->dac", basis[0], ordered, preferred_element_type=F32)
    return (new_first, new_second, change.astype(BF)[None])


def solution(mesh):
    return jax.shard_map(
        local,
        mesh=mesh,
        in_specs=(
            P(None, "dp", "tensor"),
            P(None, "dp", "tensor"),
            P(None, "tensor", None),
            P(None, ("tensor", "dp"), None),
            P(None, ("tensor", "dp"), None),
        ),
        out_specs=(
            P(None, ("tensor", "dp"), None),
            P(None, ("tensor", "dp"), None),
            P(None, "tensor", None, "dp"),
        ),
        check_vma=False,
    )
```

time: 77.4 us -> 77.3 us (level)
  waiting for transfers between devices: 28.3 us -> 36.6 us
  starting transfers between devices: 35.9 us -> 28.3 us
  Pallas kernels: 2.31 us -> 0.94 us
  other arithmetic: 0.61 us -> 1.46 us
  local copies, waits for them, and re-layouts: 3.89 us -> 4.7 us
    ppermute x12 -> x11, waiting for transfers between devices: 17.6 us -> 26.2 us  [send_dp(): return lax.ppermute(value, 'dp', pairs)]
    ppermute x12 -> x11, starting transfers between devices: 25 us -> 18.8 us  [send_dp(): return lax.ppermute(value, 'dp', pairs)]
    ppermute x7 -> x6, starting transfers between devices: 10.9 us -> 9.48 us  [swap_y(): return lax.ppermute(value, 'tensor', [(y, y ^ m) for y in range(NY)])]
    pallas_call x2 -> x1, Pallas kernels: 2.31 us -> 0.94 us  [arrange(): pl.pallas_call(arrange_kernel, out_shape=[shape] * 2, in_specs=[smem, sme...]
    convert_element_type x2, other arithmetic: 0.15 us -> 1.26 us  [the longest x1 1.25 us: local(): projected = (partial + came[0] + came[1] + came[2]).astype(BF)]
    squeeze x0 -> x1, local copies, waits for them, and re-layouts: none -> 0.96 us  [local(): lax.dynamic_index_in_dim(columns, x ^ m, 0, keepdims=False)]
    ppermute x7 -> x6, waiting for transfers between devices: 10.7 us -> 10.4 us  [swap_y(): return lax.ppermute(value, 'tensor', [(y, y ^ m) for y in range(NY)])]
    dot_general x9 -> x3, matrix products: 3.56 us -> 3.31 us  [dot(): lax.dot_general(a, b, (((1,), (0,)), ((), ())), preferred_element_type=F32)]
  transfers between devices with their start and end apart: 19 -> 17, of which waited for: 11 -> 12; matrix products, arithmetic and copies ran while one was open for 7% -> 5% of each run, Pallas kernels for 3% -> 1%
where the time goes in v2:
time: 77.3 us; the launch traced here: 76.5 us
  waiting for transfers between devices  36.6 us (47%)
  starting transfers between devices  28.3 us (37%)
  local copies, waits for them, and re-layouts  4.7 us (6%)
  matrix products  3.82 us (5%)
  other arithmetic  1.46 us (2%)
  Pallas kernels  0.94 us (1%)
  between operations  0.78 us (1%)
    ppermute x11, waiting for transfers between devices, send_dp(): return lax.ppermute(value, 'dp', pairs)  26.2 us
    ppermute x11, starting transfers between devices, send_dp(): return lax.ppermute(value, 'dp', pairs)  18.8 us
    ppermute x6, waiting for transfers between devices, swap_y(): return lax.ppermute(value, 'tensor', [(y, y ^ m) for y in range(NY)])  10.4 us
    ppermute x6, starting transfers between devices, swap_y(): return lax.ppermute(value, 'tensor', [(y, y ^ m) for y in range(NY)])  9.48 us
    unnamed x13, local copies, waits for them, and re-layouts  3.7 us
    dot_general x3, matrix products, dot(): lax.dot_general(a, b, (((1,), (0,)), ((), ())), preferred_element_type=F32)  3.31 us
  transfers between devices with their start and end apart: 17, of which 12 were waited for; matrix products, arithmetic and copies ran while one was open for 5% of the time, Pallas kernels for 1%

profile of v2, /device:TPU:32, one launch (start us, length us, event | category | flops | bytes accessed | tf_op | source)
XLA Modules:
  0.0 76.5 jit_solution(16770541914631973342)
XLA Ops:
  0.7 1.2 %copy-done = bf16[1,1024,512]{2,1,0:T(8,128)(2,1)S(1)} copy-done((bf16[1,1024,512]{2,1,0:T(8,128)(2,1)S(1)}, bf16[1,1024,512]{2,1,0:T(8,128)(2,1)}, u32[]{:S(2)}) %copy-start) | copy-done | bytes 1048600
  1.9 2.2 %fusion.21 = (bf16[256,512]{1,0:T(8,128)(2,1)}, f32[256,512]{1,0:T(8,128)S(1)}) fusion(bf16[1,1024,512]{2,1,0:T(8,128)(2,1)S(1)} %copy-done, bf16[1,256,1024]{2,1,0:T(8,128)(2,1)} %param.6), kind=kOutput, calls=%fused_computation.46 | convolution fusion | flops 268566528 | bytes 2359296 | tf_op jit(solution)/shard_map/dot_general | solution.py:81
  4.0 1.6 %collective-permute-start.3 = (bf16[256,512]{1,0:T(8,128)(2,1)}, bf16[256,512]{1,0:T(8,128)(2,1)}, u32[]{:S(2)}, u32[]{:S(2)}) collective-permute-start(bf16[256,512]{1,0:T(8,128)(2,1)} %get-tuple-element.23), channel_id=1, source_target_pairs={{0,1},{1,0},{2,3},{3,2},{4,5},{5,4},{6,7},{7,6},{8,9},{9,8},{10,11... | collective-permute-start | bytes 786440 | tf_op jit(solution)/shard_map/ppermute | solution.py:40
  5.6 2.9 %collective-permute-start.4 = (bf16[256,512]{1,0:T(8,128)(2,1)}, bf16[256,512]{1,0:T(8,128)(2,1)}, u32[]{:S(2)}, u32[]{:S(2)}) collective-permute-start(bf16[256,512]{1,0:T(8,128)(2,1)} %get-tuple-element.23), channel_id=1, source_target_pairs={{0,2},{1,3},{2,0},{3,1},{4,6},{5,7},{6,4},{7,5},{8,10},{9,11},{10,... | collective-permute-start | bytes 786440 | tf_op jit(solution)/shard_map/ppermute | solution.py:40
  9.7 1.5 %collective-permute-start = (bf16[688,256]{1,0:T(8,128)(2,1)S(1)}, bf16[688,256]{1,0:T(8,128)(2,1)S(1)}, u32[]{:S(2)}, u32[]{:S(2)}) collective-permute-start(bf16[688,256]{1,0:T(8,128)(2,1)S(1)} %get-tuple-element.15), channel_id=1, source_target_pairs={{0,64},{4,68},{8,72},{12,76},{16,80},{20,84},{24,88},{28,92},{32,9... | collective-permute-start | bytes 1056776 | tf_op jit(solution)/shard_map/ppermute | solution.py:24
  11.2 2.7 %collective-permute-start.1 = (bf16[688,256]{1,0:T(8,128)(2,1)}, bf16[688,256]{1,0:T(8,128)(2,1)S(1)}, u32[]{:S(2)}, u32[]{:S(2)}) collective-permute-start(bf16[688,256]{1,0:T(8,128)(2,1)} %get-tuple-element.14), channel_id=1, source_target_pairs={{0,128},{4,132},{8,136},{12,140},{16,144},{20,148},{24,152},{28,15... | collective-permute-start | bytes 1056776 | tf_op jit(solution)/shard_map/ppermute | solution.py:24
  13.9 2.4 %collective-permute-start.2 = (bf16[688,256]{1,0:T(8,128)(2,1)}, bf16[688,256]{1,0:T(8,128)(2,1)S(1)}, u32[]{:S(2)}, u32[]{:S(2)}) collective-permute-start(bf16[688,256]{1,0:T(8,128)(2,1)} %get-tuple-element.13), channel_id=1, source_target_pairs={{0,192},{4,196},{8,200},{12,204},{16,208},{20,212},{24,216},{28,22... | collective-permute-start | bytes 1056776 | tf_op jit(solution)/shard_map/ppermute | solution.py:24
  16.3 4.3 %collective-permute-done.4 = bf16[256,512]{1,0:T(8,128)(2,1)} collective-permute-done((bf16[256,512]{1,0:T(8,128)(2,1)}, bf16[256,512]{1,0:T(8,128)(2,1)}, u32[]{:S(2)}, u32[]{:S(2)}) %collective-permute-start.4) | collective-permute-done | bytes 262176 | tf_op jit(solution)/shard_map/ppermute | solution.py:40
  20.6 2.6 %collective-permute-done.5 = bf16[256,512]{1,0:T(8,128)(2,1)} collective-permute-done((bf16[256,512]{1,0:T(8,128)(2,1)}, bf16[256,512]{1,0:T(8,128)(2,1)}, u32[]{:S(2)}, u32[]{:S(2)}) %collective-permute-start.5) | collective-permute-done | bytes 262176 | tf_op jit(solution)/shard_map/ppermute | solution.py:40
  23.1 1.2 %add_convert_fusion = bf16[256,512]{1,0:T(8,128)(2,1)S(1)} fusion(bf16[256,512]{1,0:T(8,128)(2,1)} %collective-permute-done.5, bf16[256,512]{1,0:T(8,128)(2,1)} %collective-permute-done.4, f32[256,512]{1,0:T(8,128)S(1)} %get-tuple-element.24, bf16[256,512]{1,0:T(8,128)(2,1)} %collective-permute-done.3), kind=kLoop, calls=%fused_computation.9 | loop fusion | flops 917504 | bytes 1572864 | tf_op jit(solution)/shard_map/convert_element_type | solution.py:97
  24.4 1.6 %collective-permute-start.6 = (bf16[256,512]{1,0:T(8,128)(2,1)S(1)}, bf16[256,512]{1,0:T(8,128)(2,1)S(1)}, u32[]{:S(2)}, u32[]{:S(2)}) collective-permute-start(bf16[256,512]{1,0:T(8,128)(2,1)S(1)} %add_convert_fusion), channel_id=1, source_target_pairs={{0,64},{4,68},{8,72},{12,76},{16,80},{20,84},{24,88},{28,92},{32,9... | collective-permute-start | bytes 786440 | tf_op jit(solution)/shard_map/ppermute | solution.py:24
  26.0 2.7 %collective-permute-start.7 = (bf16[256,512]{1,0:T(8,128)(2,1)S(1)}, bf16[256,512]{1,0:T(8,128)(2,1)S(1)}, u32[]{:S(2)}, u32[]{:S(2)}) collective-permute-start(bf16[256,512]{1,0:T(8,128)(2,1)S(1)} %add_convert_fusion), channel_id=1, source_target_pairs={{0,128},{4,132},{8,136},{12,140},{16,144},{20,148},{24,152},{28,15... | collective-permute-start | bytes 786440 | tf_op jit(solution)/shard_map/ppermute | solution.py:24
  29.7 7.8 %collective-permute-done.2.refs_3_ = bf16[688,256]{1,0:T(8,128)(2,1)S(1)} collective-permute-done((bf16[688,256]{1,0:T(8,128)(2,1)}, bf16[688,256]{1,0:T(8,128)(2,1)S(1)}, u32[]{:S(2)}, u32[]{:S(2)}) %collective-permute-start.2) | collective-permute-done | bytes 352288 | tf_op jit(solution)/shard_map/ppermute | solution.py:24
  38.5 1.6 %collective-permute-done.7 = bf16[256,512]{1,0:T(8,128)(2,1)S(1)} collective-permute-done((bf16[256,512]{1,0:T(8,128)(2,1)S(1)}, bf16[256,512]{1,0:T(8,128)(2,1)S(1)}, u32[]{:S(2)}, u32[]{:S(2)}) %collective-permute-start.7) | collective-permute-done | bytes 262176 | tf_op jit(solution)/shard_map/ppermute | solution.py:24
  40.0 2.7 %collective-permute-done.8 = bf16[256,512]{1,0:T(8,128)(2,1)S(1)} collective-permute-done((bf16[256,512]{1,0:T(8,128)(2,1)S(1)}, bf16[256,512]{1,0:T(8,128)(2,1)S(1)}, u32[]{:S(2)}, u32[]{:S(2)}) %collective-permute-start.8) | collective-permute-done | bytes 262176 | tf_op jit(solution)/shard_map/ppermute | solution.py:24
  43.4 1.7 %collective-permute-done.9 = bf16[384,512]{1,0:T(8,128)(2,1)S(1)} collective-permute-done((bf16[384,512]{1,0:T(8,128)(2,1)S(1)}, bf16[384,512]{1,0:T(8,128)(2,1)S(1)}, u32[]{:S(2)}, u32[]{:S(2)}) %collective-permute-start.9) | collective-permute-done | bytes 393248 | tf_op jit(solution)/shard_map/ppermute | solution.py:24
  46.0 2.0 %collective-permute-start.11 = (bf16[96,512]{1,0:T(8,128)(2,1)S(1)}, bf16[96,512]{1,0:T(8,128)(2,1)S(1)}, u32[]{:S(2)}, u32[]{:S(2)}) collective-permute-start(bf16[96,512]{1,0:T(8,128)(2,1)S(1)} %slice.42), channel_id=1, source_target_pairs={{0,8},{4,12},{8,16},{12,20},{16,24},{20,28},{24,32},{28,36},{32,40... | collective-permute-start | bytes 294920 | tf_op jit(solution)/shard_map/ppermute | solution.py:24
  48.0 6.8 %collective-permute-done.11 = bf16[96,512]{1,0:T(8,128)(2,1)S(1)} collective-permute-done((bf16[96,512]{1,0:T(8,128)(2,1)S(1)}, bf16[96,512]{1,0:T(8,128)(2,1)S(1)}, u32[]{:S(2)}, u32[]{:S(2)}) %collective-permute-start.11) | collective-permute-done | bytes 98336 | tf_op jit(solution)/shard_map/ppermute | solution.py:24
  54.8 2.9 %collective-permute-start.12 = (bf16[48,512]{1,0:T(8,128)(2,1)S(1)}, bf16[48,512]{1,0:T(8,128)(2,1)S(1)}, u32[]{:S(2)}, u32[]{:S(2)}) collective-permute-start(bf16[48,512]{1,0:T(8,128)(2,1)S(1)} %get-tuple-element.18), channel_id=1, source_target_pairs={{0,40},{4,44},{8,48},{12,52},{16,56},{20,60},{24,0},{28,4},{32,8},... | collective-permute-start | bytes 147464 | tf_op jit(solution)/shard_map/ppermute | solution.py:24
  57.8 2.2 %collective-permute-start.13 = (bf16[48,512]{1,0:T(8,128)(2,1)S(1)}, bf16[48,512]{1,0:T(8,128)(2,1)S(1)}, u32[]{:S(2)}, u32[]{:S(2)}) collective-permute-start(bf16[48,512]{1,0:T(8,128)(2,1)S(1)} %slice.81), channel_id=1, source_target_pairs={{0,24},{4,28},{8,32},{12,36},{16,40},{20,44},{24,48},{28,52},{32,5... | collective-permute-start | bytes 147464 | tf_op jit(solution)/shard_map/ppermute | solution.py:24
  60.0 2.6 %collective-permute-done.12 = bf16[48,512]{1,0:T(8,128)(2,1)S(1)} collective-permute-done((bf16[48,512]{1,0:T(8,128)(2,1)S(1)}, bf16[48,512]{1,0:T(8,128)(2,1)S(1)}, u32[]{:S(2)}, u32[]{:S(2)}) %collective-permute-start.12) | collective-permute-done | bytes 49184 | tf_op jit(solution)/shard_map/ppermute | solution.py:24
  62.6 2.5 %collective-permute-done.13 = bf16[48,512]{1,0:T(8,128)(2,1)S(1)} collective-permute-done((bf16[48,512]{1,0:T(8,128)(2,1)S(1)}, bf16[48,512]{1,0:T(8,128)(2,1)S(1)}, u32[]{:S(2)}, u32[]{:S(2)}) %collective-permute-start.13) | collective-permute-done | bytes 49184 | tf_op jit(solution)/shard_map/ppermute | solution.py:24
  65.8 3.9 %collective-permute-start.15 = (bf16[43,512]{1,0:T(8,128)(2,1)S(1)}, bf16[43,512]{1,0:T(8,128)(2,1)S(1)}, u32[]{:S(2)}, u32[]{:S(2)}) collective-permute-start(bf16[43,512]{1,0:T(8,128)(2,1)S(1)} %get-tuple-element.10), channel_id=1, source_target_pairs={{0,2},{1,3},{2,0},{3,1},{4,6},{5,7},{6,4},{7,5},{8,10},{9,11},{10,... | collective-permute-start | bytes 132104 | tf_op jit(solution)/shard_map/ppermute | solution.py:40
  72.4 2.6 %collective-permute-done.16 = bf16[43,512]{1,0:T(8,128)(2,1)S(1)} collective-permute-done((bf16[43,512]{1,0:T(8,128)(2,1)S(1)}, bf16[43,512]{1,0:T(8,128)(2,1)S(1)}, u32[]{:S(2)}, u32[]{:S(2)}) %collective-permute-start.16) | collective-permute-done | bytes 44064 | tf_op jit(solution)/shard_map/ppermute | solution.py:40
  (40 shorter events, 9.6 us)
Async XLA Ops:
  0.6 1.2 %copy-start = (bf16[1,1024,512]{2,1,0:T(8,128)(2,1)S(1)}, bf16[1,1024,512]{2,1,0:T(8,128)(2,1)}, u32[]{:S(2)}) copy-start(bf16[1,1024,512]{2,1,0:T(8,128)(2,1)} %param.8) | copy-start | bytes 3145732
  0.6 8.1 %copy-start.1 = (bf16[1,256,2752]{1,2,0:T(8,128)(2,1)S(1)}, bf16[1,256,2752]{1,2,0:T(8,128)(2,1)}, u32[]{:S(2)}) copy-start(bf16[1,256,2752]{1,2,0:T(8,128)(2,1)} %param.7) | copy-start | bytes 4227076
  4.0 9.9 %collective-permute-start.3 = (bf16[256,512]{1,0:T(8,128)(2,1)}, bf16[256,512]{1,0:T(8,128)(2,1)}, u32[]{:S(2)}, u32[]{:S(2)}) collective-permute-start(bf16[256,512]{1,0:T(8,128)(2,1)} %get-tuple-element.23), channel_id=1, source_target_pairs={{0,1},{1,0},{2,3},{3,2},{4,5},{5,4},{6,7},{7,6},{8,9},{9,8},{10,11... | collective-permute-start | bytes 786440 | tf_op jit(solution)/shard_map/ppermute | solution.py:40
  5.6 15.0 %collective-permute-start.4 = (bf16[256,512]{1,0:T(8,128)(2,1)}, bf16[256,512]{1,0:T(8,128)(2,1)}, u32[]{:S(2)}, u32[]{:S(2)}) collective-permute-start(bf16[256,512]{1,0:T(8,128)(2,1)} %get-tuple-element.23), channel_id=1, source_target_pairs={{0,2},{1,3},{2,0},{3,1},{4,6},{5,7},{6,4},{7,5},{8,10},{9,11},{10,... | collective-permute-start | bytes 786440 | tf_op jit(solution)/shard_map/ppermute | solution.py:40
  8.5 14.6 %collective-permute-start.5 = (bf16[256,512]{1,0:T(8,128)(2,1)}, bf16[256,512]{1,0:T(8,128)(2,1)}, u32[]{:S(2)}, u32[]{:S(2)}) collective-permute-start(bf16[256,512]{1,0:T(8,128)(2,1)} %get-tuple-element.23), channel_id=1, source_target_pairs={{0,3},{1,2},{2,1},{3,0},{4,7},{5,6},{6,5},{7,4},{8,11},{9,10},{10,... | collective-permute-start | bytes 786440 | tf_op jit(solution)/shard_map/ppermute | solution.py:40
  9.7 19.5 %copy-start.4 = (s32[8]{0:T(128)S(1)}, s32[8]{0:T(128)}, u32[]{:S(2)}) copy-start(s32[8]{0:T(128)} %constant.97.clone) | copy-start | bytes 100
  9.7 19.0 %collective-permute-start = (bf16[688,256]{1,0:T(8,128)(2,1)S(1)}, bf16[688,256]{1,0:T(8,128)(2,1)S(1)}, u32[]{:S(2)}, u32[]{:S(2)}) collective-permute-start(bf16[688,256]{1,0:T(8,128)(2,1)S(1)} %get-tuple-element.15), channel_id=1, source_target_pairs={{0,64},{4,68},{8,72},{12,76},{16,80},{20,84},{24,88},{28,92},{32,9... | collective-permute-start | bytes 1056776 | tf_op jit(solution)/shard_map/ppermute | solution.py:24
  11.2 18.5 %collective-permute-start.1 = (bf16[688,256]{1,0:T(8,128)(2,1)}, bf16[688,256]{1,0:T(8,128)(2,1)S(1)}, u32[]{:S(2)}, u32[]{:S(2)}) collective-permute-start(bf16[688,256]{1,0:T(8,128)(2,1)} %get-tuple-element.14), channel_id=1, source_target_pairs={{0,128},{4,132},{8,136},{12,140},{16,144},{20,148},{24,152},{28,15... | collective-permute-start | bytes 1056776 | tf_op jit(solution)/shard_map/ppermute | solution.py:24
  13.9 23.6 %collective-permute-start.2 = (bf16[688,256]{1,0:T(8,128)(2,1)}, bf16[688,256]{1,0:T(8,128)(2,1)S(1)}, u32[]{:S(2)}, u32[]{:S(2)}) collective-permute-start(bf16[688,256]{1,0:T(8,128)(2,1)} %get-tuple-element.13), channel_id=1, source_target_pairs={{0,192},{4,196},{8,200},{12,204},{16,208},{20,212},{24,216},{28,22... | collective-permute-start | bytes 1056776 | tf_op jit(solution)/shard_map/ppermute | solution.py:24
  24.4 14.1 %collective-permute-start.6 = (bf16[256,512]{1,0:T(8,128)(2,1)S(1)}, bf16[256,512]{1,0:T(8,128)(2,1)S(1)}, u32[]{:S(2)}, u32[]{:S(2)}) collective-permute-start(bf16[256,512]{1,0:T(8,128)(2,1)S(1)} %add_convert_fusion), channel_id=1, source_target_pairs={{0,64},{4,68},{8,72},{12,76},{16,80},{20,84},{24,88},{28,92},{32,9... | collective-permute-start | bytes 786440 | tf_op jit(solution)/shard_map/ppermute | solution.py:24
  26.0 14.1 %collective-permute-start.7 = (bf16[256,512]{1,0:T(8,128)(2,1)S(1)}, bf16[256,512]{1,0:T(8,128)(2,1)S(1)}, u32[]{:S(2)}, u32[]{:S(2)}) collective-permute-start(bf16[256,512]{1,0:T(8,128)(2,1)S(1)} %add_convert_fusion), channel_id=1, source_target_pairs={{0,128},{4,132},{8,136},{12,140},{16,144},{20,148},{24,152},{28,15... | collective-permute-start | bytes 786440 | tf_op jit(solution)/shard_map/ppermute | solution.py:24
  28.7 14.1 %collective-permute-start.8 = (bf16[256,512]{1,0:T(8,128)(2,1)S(1)}, bf16[256,512]{1,0:T(8,128)(2,1)S(1)}, u32[]{:S(2)}, u32[]{:S(2)}) collective-permute-start(bf16[256,512]{1,0:T(8,128)(2,1)S(1)} %add_convert_fusion), channel_id=1, source_target_pairs={{0,192},{4,196},{8,200},{12,204},{16,208},{20,212},{24,216},{28,22... | collective-permute-start | bytes 786440 | tf_op jit(solution)/shard_map/ppermute | solution.py:24
  43.3 1.8 %collective-permute-start.9 = (bf16[384,512]{1,0:T(8,128)(2,1)S(1)}, bf16[384,512]{1,0:T(8,128)(2,1)S(1)}, u32[]{:S(2)}, u32[]{:S(2)}) collective-permute-start(bf16[384,512]{1,0:T(8,128)(2,1)S(1)} %convolution_convert_fusion.1), channel_id=1, source_target_pairs={{0,4},{4,0},{8,12},{12,8},{16,20},{20,16},{24,28},{28,24},{32,36},... | collective-permute-start | bytes 1179656 | tf_op jit(solution)/shard_map/ppermute | solution.py:24
  45.7 19.3 %copy-start.2 = (f32[1,43,512]{2,0,1:T(1,128)S(1)}, f32[1,43,512]{2,0,1:T(1,128)}, u32[]{:S(2)}) copy-start(f32[1,43,512]{2,0,1:T(1,128)} %param.10) | copy-start | bytes 264196
  45.7 19.3 %copy-start.3 = (f32[1,43,512]{2,0,1:T(1,128)S(1)}, f32[1,43,512]{2,0,1:T(1,128)}, u32[]{:S(2)}) copy-start(f32[1,43,512]{2,0,1:T(1,128)} %param.9) | copy-start | bytes 264196
  45.8 9.0 %collective-permute-start.10 = (bf16[144,512]{1,0:T(8,128)(2,1)S(1)}, bf16[144,512]{1,0:T(8,128)(2,1)S(1)}, u32[]{:S(2)}, u32[]{:S(2)}) collective-permute-start(bf16[144,512]{1,0:T(8,128)(2,1)S(1)} %slice.40), channel_id=1, source_target_pairs={{0,56},{4,60},{8,0},{12,4},{16,8},{20,12},{24,16},{28,20},{32,24},... | collective-permute-start | bytes 442376 | tf_op jit(solution)/shard_map/ppermute | solution.py:24
  46.0 8.7 %collective-permute-start.11 = (bf16[96,512]{1,0:T(8,128)(2,1)S(1)}, bf16[96,512]{1,0:T(8,128)(2,1)S(1)}, u32[]{:S(2)}, u32[]{:S(2)}) collective-permute-start(bf16[96,512]{1,0:T(8,128)(2,1)S(1)} %slice.42), channel_id=1, source_target_pairs={{0,8},{4,12},{8,16},{12,20},{16,24},{20,28},{24,32},{28,36},{32,40... | collective-permute-start | bytes 294920 | tf_op jit(solution)/shard_map/ppermute | solution.py:24
  54.8 7.8 %collective-permute-start.12 = (bf16[48,512]{1,0:T(8,128)(2,1)S(1)}, bf16[48,512]{1,0:T(8,128)(2,1)S(1)}, u32[]{:S(2)}, u32[]{:S(2)}) collective-permute-start(bf16[48,512]{1,0:T(8,128)(2,1)S(1)} %get-tuple-element.18), channel_id=1, source_target_pairs={{0,40},{4,44},{8,48},{12,52},{16,56},{20,60},{24,0},{28,4},{32,8},... | collective-permute-start | bytes 147464 | tf_op jit(solution)/shard_map/ppermute | solution.py:24
  57.8 7.3 %collective-permute-start.13 = (bf16[48,512]{1,0:T(8,128)(2,1)S(1)}, bf16[48,512]{1,0:T(8,128)(2,1)S(1)}, u32[]{:S(2)}, u32[]{:S(2)}) collective-permute-start(bf16[48,512]{1,0:T(8,128)(2,1)S(1)} %slice.81), channel_id=1, source_target_pairs={{0,24},{4,28},{8,32},{12,36},{16,40},{20,44},{24,48},{28,52},{32,5... | collective-permute-start | bytes 147464 | tf_op jit(solution)/shard_map/ppermute | solution.py:24
  65.2 6.2 %collective-permute-start.14 = (bf16[43,512]{1,0:T(8,128)(2,1)S(1)}, bf16[43,512]{1,0:T(8,128)(2,1)S(1)}, u32[]{:S(2)}, u32[]{:S(2)}) collective-permute-start(bf16[43,512]{1,0:T(8,128)(2,1)S(1)} %get-tuple-element.10), channel_id=1, source_target_pairs={{0,1},{1,0},{2,3},{3,2},{4,5},{5,4},{6,7},{7,6},{8,9},{9,8},{10,11... | collective-permute-start | bytes 132104 | tf_op jit(solution)/shard_map/ppermute | solution.py:40
  65.8 6.6 %collective-permute-start.15 = (bf16[43,512]{1,0:T(8,128)(2,1)S(1)}, bf16[43,512]{1,0:T(8,128)(2,1)S(1)}, u32[]{:S(2)}, u32[]{:S(2)}) collective-permute-start(bf16[43,512]{1,0:T(8,128)(2,1)S(1)} %get-tuple-element.10), channel_id=1, source_target_pairs={{0,2},{1,3},{2,0},{3,1},{4,6},{5,7},{6,4},{7,5},{8,10},{9,11},{10,... | collective-permute-start | bytes 132104 | tf_op jit(solution)/shard_map/ppermute | solution.py:40
  69.7 5.3 %collective-permute-start.16 = (bf16[43,512]{1,0:T(8,128)(2,1)S(1)}, bf16[43,512]{1,0:T(8,128)(2,1)S(1)}, u32[]{:S(2)}, u32[]{:S(2)}) collective-permute-start(bf16[43,512]{1,0:T(8,128)(2,1)S(1)} %get-tuple-element.10), channel_id=1, source_target_pairs={{0,3},{1,2},{2,1},{3,0},{4,7},{5,6},{6,5},{7,4},{8,11},{9,10},{10,... | collective-permute-start | bytes 132104 | tf_op jit(solution)/shard_map/ppermute | solution.py:40

commit v3 on v2

--- a/solution.py
+++ b/solution.py
@@ -9,6 +9,7 @@
 
 NX, NZ, NCORE, NY = 4, 8, 2, 4
 OWNED, PADDED = 43, 48
+CHUNKS = 2
 BF, F32 = jnp.bfloat16, jnp.float32
 
 Z_ORDER = (6, 1, 4, 7, 2, 5, 0, 3)
@@ -40,41 +41,44 @@
     return lax.ppermute(value, "tensor", [(y, y ^ m) for y in range(NY)])
 
 
-def arrange_kernel(order_ref, core_ref, *refs):
-    sources, (other, mine, blocks) = refs[:NX], refs[NX:]
-    rows, tokens = sources[0].shape
-    for s, source in enumerate(sources):
-        for n in range(NZ * NCORE):
-            first = n * OWNED
-            low = first // 16 * 16
-            high = min(rows, -(-(first + PADDED) // 16) * 16)
-            piece = source[low:high, :].astype(F32)
-            piece = piece[first - low : min(first - low + PADDED, high - low), :]
-            if piece.shape[0] < PADDED:
-                fill = jnp.zeros((PADDED - piece.shape[0], tokens), F32)
-                piece = jnp.concatenate([piece, fill], axis=0)
-            blocks[n, :, s * tokens : (s + 1) * tokens] = piece.astype(BF)
-    core = core_ref[0]
-    for i in range(NZ):
-        place = pl.ds(i * PADDED, PADDED)
-        other[place, :] = blocks[order_ref[i] * NCORE + 1 - core]
-        mine[place, :] = blocks[order_ref[i] * NCORE + core]
+def arrange_kernel(order_ref, core_ref, own, came, *refs):
+    outs, blocks = refs[:NX], refs[NX]
+    rows, tokens = own.shape
+
+    def unpack(core):
+        for s, source in enumerate((own, came)):
+            for n in range(NX * NZ):
+                first = (NCORE * n + core) * OWNED
+                low = first // 16 * 16
+                high = min(rows, -(-(first + PADDED) // 16) * 16)
+                piece = source[low:high, :].astype(F32)
+                piece = piece[first - low : min(first - low + PADDED, high - low), :]
+                if piece.shape[0] < PADDED:
+                    fill = jnp.zeros((PADDED - piece.shape[0], tokens), F32)
+                    piece = jnp.concatenate([piece, fill], axis=0)
+                blocks[n, :, s * tokens : (s + 1) * tokens] = piece.astype(BF)
+
+    for core in range(NCORE):
+        pl.when(core_ref[0] == core)(functools.partial(unpack, core))
+    for m, out in enumerate(outs):
+        for i in range(NZ):
+            out[pl.ds(i * PADDED, PADDED), :] = blocks[order_ref[m * NZ + i]]
 
 
-def arrange(order, core, sources):
-    rows, tokens = sources[0].shape
-    shape = jax.ShapeDtypeStruct((NZ * PADDED, NX * tokens), BF)
+def arrange(order, core, own, came):
+    tokens = own.shape[1]
+    shape = jax.ShapeDtypeStruct((NZ * PADDED, NCORE * tokens), BF)
     vmem = pl.BlockSpec(memory_space=pltpu.VMEM)
     smem = pl.BlockSpec(memory_space=pltpu.SMEM)
     return pl.pallas_call(
         arrange_kernel,
-        out_shape=[shape] * 2,
-        in_specs=[smem, smem] + [vmem] * NX,
-        out_specs=[vmem] * 2,
-        scratch_shapes=[pltpu.VMEM((NZ * NCORE, PADDED, NX * tokens), BF)],
+        out_shape=[shape] * NX,
+        in_specs=[smem, smem, vmem, vmem],
+        out_specs=[vmem] * NX,
+        scratch_shapes=[pltpu.VMEM((NX * NZ, PADDED, NCORE * tokens), BF)],
         compiler_params=pltpu.CompilerParams(vmem_limit_bytes=16 * 1024 * 1024),
         cost_estimate=pl.CostEstimate(flops=0, bytes_accessed=8 * 1024 * 1024, transcendentals=0),
-    )(order, core, *sources)
+    )(order, core, own, came)
 
 
 def dot(a, b):
@@ -87,20 +91,32 @@
     core, z, x = dp % NCORE, (dp // NCORE) % NZ, dp // (NCORE * NZ)
     y = lax.axis_index("tensor")
 
-    columns = cotangent[0].T.reshape(NX, -1, cotangent.shape[1])
-    pieces = [lax.dynamic_index_in_dim(columns, x ^ m, 0, keepdims=False) for m in range(NX)]
-    pieces = pieces[:1] + [swap_x(pieces[m], m) for m in range(1, NX)]
+    columns = cotangent[0].T
+    other_columns = swap_core(columns)
+    blocks_x = jnp.arange(NX, dtype=jnp.int32) ^ x
+    blocks_z = (jnp.array(Z_ORDER, jnp.int32) + z) % NZ
+    order = (blocks_x[:, None] * NZ + blocks_z[None, :]).reshape(-1)
+    parts = arrange(order, core.reshape(1), columns, other_columns)
 
-    partial = dot(features[0], basis[0])
-    sent = partial.astype(BF)
-    came = [swap_y(sent, m).astype(F32) for m in range(1, NY)]
-    projected = (partial + came[0] + came[1] + came[2]).astype(BF)
-    projected = jnp.concatenate([projected] + [swap_x(projected, m) for m in range(1, NX)], axis=0)
+    lanes = basis.shape[2] // CHUNKS
+    projected = []
+    for c in range(CHUNKS):
+        partial = dot(features[0], basis[0, :, c * lanes : (c + 1) * lanes])
+        sent = partial.astype(BF)
+        came = [swap_y(sent, m).astype(F32) for m in range(1, NY)]
+        projected.append((partial + came[0] + came[1] + came[2]).astype(BF))
+    projected[0], parts = lax.optimization_barrier((projected[0], parts))
 
-    order = (jnp.array(Z_ORDER, jnp.int32) + z) % NZ
-    other, mine = arrange(order, core.reshape(1), pieces)
-    came = swap_core(dot(other, projected).astype(BF))
-    term = dot(mine, projected) + came.astype(F32)
+    terms = []
+    for c in range(CHUNKS):
+        both = jnp.concatenate([projected[c], swap_core(projected[c])], axis=0)
+        came = [swap_x(dot(parts[m], both).astype(BF), m) for m in range(1, NX)]
+        term = dot(parts[0], both)
+        for value in came:
+            term = term + value.astype(F32)
+        terms.append(term)
+    term = jnp.concatenate(terms, axis=1)
+
     lower = shift_z(term[:UP].astype(BF), 1).astype(F32)
     upper = shift_z(term[UP:DOWN].astype(BF), -1).astype(F32)
     keep = term[DOWN:] + upper

time: 77.3 us -> 89.6 us (1.16)
  waiting for transfers between devices: 36.6 us -> 42 us
  starting transfers between devices: 28.3 us -> 31.2 us
  matrix products: 3.82 us -> 6.69 us
  other arithmetic: 1.46 us -> 2.98 us
    ppermute x11 -> x13, waiting for transfers between devices: 26.2 us -> 31.7 us  [send_dp(): return lax.ppermute(value, 'dp', pairs)]
    ppermute x6 -> x9, starting transfers between devices: 9.48 us -> 13.7 us  [swap_y(): return lax.ppermute(value, 'tensor', [(y, y ^ m) for y in range(NY)])]
    dot_general x3 -> x10, matrix products: 3.31 us -> 5.97 us  [dot(): lax.dot_general(a, b, (((1,), (0,)), ((), ())), preferred_element_type=F32)]
    ppermute x11 -> x13, starting transfers between devices: 18.8 us -> 17.5 us  [send_dp(): return lax.ppermute(value, 'dp', pairs)]
    squeeze x1 -> x0, local copies, waits for them, and re-layouts: 0.96 us -> none  [local(): lax.dynamic_index_in_dim(columns, x ^ m, 0, keepdims=False)]
    convert_element_type x1 -> x2, other arithmetic: 1.25 us -> 2.19 us  [local(): projected.append((partial + came[0] + came[1] + came[2]).astype(BF))]
    unnamed x13 -> x20, local copies, waits for them, and re-layouts: 3.7 us -> 3.77 us
    ppermute x6 -> x9, waiting for transfers between devices: 10.4 us -> 10.3 us  [swap_y(): return lax.ppermute(value, 'tensor', [(y, y ^ m) for y in range(NY)])]
  transfers between devices with their start and end apart: 17 -> 22, of which waited for: 12 -> 16; matrix products, arithmetic and copies ran while one was open for 5% -> 11% of each run, Pallas kernels for 1% -> 1%
where the time goes in v3:
time: 89.6 us; the launch traced here: 88.8 us
  waiting for transfers between devices  42 us (47%)
  starting transfers between devices  31.2 us (35%)
  matrix products  6.69 us (7%)
  local copies, waits for them, and re-layouts  4.22 us (5%)
  other arithmetic  2.98 us (3%)
  between operations  0.93 us (1%)
    ppermute x13, waiting for transfers between devices, send_dp(): return lax.ppermute(value, 'dp', pairs)  31.7 us
    ppermute x13, starting transfers between devices, send_dp(): return lax.ppermute(value, 'dp', pairs)  17.5 us
    ppermute x9, starting transfers between devices, swap_y(): return lax.ppermute(value, 'tensor', [(y, y ^ m) for y in range(NY)])  13.7 us
    ppermute x9, waiting for transfers between devices, swap_y(): return lax.ppermute(value, 'tensor', [(y, y ^ m) for y in range(NY)])  10.3 us
    dot_general x10, matrix products, dot(): lax.dot_general(a, b, (((1,), (0,)), ((), ())), preferred_element_type=F32)  5.97 us
    unnamed x20, local copies, waits for them, and re-layouts  3.77 us
    convert_element_type x2, other arithmetic, local(): projected.append((partial + came[0] + came[1] + came[2]).astype(BF))  2.19 us
  transfers between devices with their start and end apart: 22, of which 16 were waited for; matrix products, arithmetic and copies ran while one was open for 11% of the time, Pallas kernels for 1%

profile of v3, /device:TPU:32, one launch (start us, length us, event | category | flops | bytes accessed | tf_op | source)
XLA Modules:
  0.0 88.8 jit_solution(6068862627196508804)
XLA Ops:
  1.7 2.1 %fusion.32 = (bf16[256,256]{1,0:T(8,128)(2,1)}, f32[256,256]{1,0:T(8,128)}) fusion(bf16[1,1024,512]{2,1,0:T(8,128)(2,1)} %param.8, bf16[1,256,1024]{2,1,0:T(8,128)(2,1)S(1)} %copy-done), kind=kOutput, calls=%fused_computation.64 | convolution fusion | flops 134283264 | bytes 1441792 | tf_op jit(solution)/shard_map/dot_general | solution.py:85
  3.8 3.0 %collective-permute-start.10 = (bf16[256,256]{1,0:T(8,128)(2,1)}, bf16[256,256]{1,0:T(8,128)(2,1)}, u32[]{:S(2)}, u32[]{:S(2)}) collective-permute-start(bf16[256,256]{1,0:T(8,128)(2,1)} %get-tuple-element.41), channel_id=1, source_target_pairs={{0,3},{1,2},{2,1},{3,0},{4,7},{5,6},{6,5},{7,4},{8,11},{9,10},{10,... | collective-permute-start | bytes 393224 | tf_op jit(solution)/shard_map/ppermute | solution.py:41
  6.9 1.5 %collective-permute-start.9 = (bf16[256,256]{1,0:T(8,128)(2,1)}, bf16[256,256]{1,0:T(8,128)(2,1)}, u32[]{:S(2)}, u32[]{:S(2)}) collective-permute-start(bf16[256,256]{1,0:T(8,128)(2,1)} %get-tuple-element.41), channel_id=1, source_target_pairs={{0,2},{1,3},{2,0},{3,1},{4,6},{5,7},{6,4},{7,5},{8,10},{9,11},{10,... | collective-permute-start | bytes 393224 | tf_op jit(solution)/shard_map/ppermute | solution.py:41
  8.5 1.0 %fusion.31 = (bf16[256,256]{1,0:T(8,128)(2,1)}, f32[256,256]{1,0:T(8,128)}) fusion(bf16[1,1024,512]{2,1,0:T(8,128)(2,1)S(1)} %copy-done.2, bf16[1,256,1024]{2,1,0:T(8,128)(2,1)S(1)} %copy-done), kind=kOutput, calls=%fused_computation.63 | convolution fusion | flops 134283264 | bytes 1441792 | tf_op jit(solution)/shard_map/dot_general | solution.py:85
  10.6 3.6 %collective-permute-start.1 = (bf16[256,256]{1,0:T(8,128)(2,1)}, bf16[256,256]{1,0:T(8,128)(2,1)S(1)}, u32[]{:S(2)}, u32[]{:S(2)}) collective-permute-start(bf16[256,256]{1,0:T(8,128)(2,1)} %get-tuple-element.39), channel_id=1, source_target_pairs={{0,2},{1,3},{2,0},{3,1},{4,6},{5,7},{6,4},{7,5},{8,10},{9,11},{10,... | collective-permute-start | bytes 393224 | tf_op jit(solution)/shard_map/ppermute | solution.py:41
  15.2 1.2 %add_convert_fusion = bf16[256,256]{1,0:T(8,128)(2,1)S(1)} fusion(bf16[256,256]{1,0:T(8,128)(2,1)} %collective-permute-done.10, bf16[256,256]{1,0:T(8,128)(2,1)} %collective-permute-done.9, f32[256,256]{1,0:T(8,128)} %get-tuple-element.42, bf16[256,256]{1,0:T(8,128)(2,1)} %collective-permute-done.8), kind=kLoop, calls=%fused_computation.46 | loop fusion | flops 458752 | bytes 786432 | tf_op jit(solution)/shard_map/convert_element_type | solution.py:107
  16.5 2.5 %collective-permute-done = bf16[256,256]{1,0:T(8,128)(2,1)S(1)} collective-permute-done((bf16[256,256]{1,0:T(8,128)(2,1)}, bf16[256,256]{1,0:T(8,128)(2,1)S(1)}, u32[]{:S(2)}, u32[]{:S(2)}) %collective-permute-start) | collective-permute-done | bytes 131104 | tf_op jit(solution)/shard_map/ppermute | solution.py:41
  19.0 1.2 %collective-permute-done.1 = bf16[256,256]{1,0:T(8,128)(2,1)S(1)} collective-permute-done((bf16[256,256]{1,0:T(8,128)(2,1)}, bf16[256,256]{1,0:T(8,128)(2,1)S(1)}, u32[]{:S(2)}, u32[]{:S(2)}) %collective-permute-start.1) | collective-permute-done | bytes 131104 | tf_op jit(solution)/shard_map/ppermute | solution.py:41
  20.2 1.7 %collective-permute-done.2 = bf16[256,256]{1,0:T(8,128)(2,1)S(1)} collective-permute-done((bf16[256,256]{1,0:T(8,128)(2,1)}, bf16[256,256]{1,0:T(8,128)(2,1)S(1)}, u32[]{:S(2)}, u32[]{:S(2)}) %collective-permute-start.2) | collective-permute-done | bytes 131104 | tf_op jit(solution)/shard_map/ppermute | solution.py:41
  24.2 1.6 %collective-permute-start.12 = (bf16[384,256]{0,1:T(8,128)(2,1)S(1)}, bf16[384,256]{0,1:T(8,128)(2,1)S(1)}, u32[]{:S(2)}, u32[]{:S(2)}) collective-permute-start(bf16[384,256]{0,1:T(8,128)(2,1)S(1)} %convolution_convert_fusion.3), channel_id=1, source_target_pairs={{0,64},{4,68},{8,72},{12,76},{16,80},{20,84},{24,88},{28,92},{32,9... | collective-permute-start | bytes 589832 | tf_op jit(solution)/shard_map/ppermute | solution.py:25
  26.1 2.8 %collective-permute-start.13 = (bf16[384,256]{0,1:T(8,128)(2,1)S(1)}, bf16[384,256]{0,1:T(8,128)(2,1)S(1)}, u32[]{:S(2)}, u32[]{:S(2)}) collective-permute-start(bf16[384,256]{0,1:T(8,128)(2,1)S(1)} %convolution_convert_fusion.2), channel_id=1, source_target_pairs={{0,128},{4,132},{8,136},{12,140},{16,144},{20,148},{24,152},{28,15... | collective-permute-start | bytes 589832 | tf_op jit(solution)/shard_map/ppermute | solution.py:25
  31.3 3.6 %collective-permute-start.6 = (bf16[384,256]{0,1:T(8,128)(2,1)S(1)}, bf16[384,256]{0,1:T(8,128)(2,1)S(1)}, u32[]{:S(2)}, u32[]{:S(2)}) collective-permute-start(bf16[384,256]{0,1:T(8,128)(2,1)S(1)} %convolution_convert_fusion.5), channel_id=1, source_target_pairs={{0,128},{4,132},{8,136},{12,140},{16,144},{20,148},{24,152},{28,15... | collective-permute-start | bytes 589832 | tf_op jit(solution)/shard_map/ppermute | solution.py:25
  36.2 1.5 %collective-permute-done.13 = bf16[384,256]{0,1:T(8,128)(2,1)S(1)} collective-permute-done((bf16[384,256]{0,1:T(8,128)(2,1)S(1)}, bf16[384,256]{0,1:T(8,128)(2,1)S(1)}, u32[]{:S(2)}, u32[]{:S(2)}) %collective-permute-start.13) | collective-permute-done | bytes 196640 | tf_op jit(solution)/shard_map/ppermute | solution.py:25
  37.7 4.0 %collective-permute-done.14 = bf16[384,256]{0,1:T(8,128)(2,1)S(1)} collective-permute-done((bf16[384,256]{0,1:T(8,128)(2,1)S(1)}, bf16[384,256]{0,1:T(8,128)(2,1)S(1)}, u32[]{:S(2)}, u32[]{:S(2)}) %collective-permute-start.14) | collective-permute-done | bytes 196640 | tf_op jit(solution)/shard_map/ppermute | solution.py:25
  42.0 3.2 %collective-permute-done.6 = bf16[384,256]{0,1:T(8,128)(2,1)S(1)} collective-permute-done((bf16[384,256]{0,1:T(8,128)(2,1)S(1)}, bf16[384,256]{0,1:T(8,128)(2,1)S(1)}, u32[]{:S(2)}, u32[]{:S(2)}) %collective-permute-start.6) | collective-permute-done | bytes 196640 | tf_op jit(solution)/shard_map/ppermute | solution.py:25
  45.3 3.8 %collective-permute-done.7 = bf16[384,256]{0,1:T(8,128)(2,1)S(1)} collective-permute-done((bf16[384,256]{0,1:T(8,128)(2,1)S(1)}, bf16[384,256]{0,1:T(8,128)(2,1)S(1)}, u32[]{:S(2)}, u32[]{:S(2)}) %collective-permute-start.7) | collective-permute-done | bytes 196640 | tf_op jit(solution)/shard_map/ppermute | solution.py:25
  50.0 2.0 %collective-permute-start.16 = (bf16[96,512]{0,1:T(8,128)(2,1)S(1)}, bf16[96,512]{0,1:T(8,128)(2,1)S(1)}, u32[]{:S(2)}, u32[]{:S(2)}) collective-permute-start(bf16[96,512]{0,1:T(8,128)(2,1)S(1)} %slice.51), channel_id=1, source_target_pairs={{0,8},{4,12},{8,16},{12,20},{16,24},{20,28},{24,32},{28,36},{32,40... | collective-permute-start | bytes 294920 | tf_op jit(solution)/shard_map/ppermute | solution.py:25
  52.0 7.2 %collective-permute-done.16 = bf16[96,512]{0,1:T(8,128)(2,1)S(1)} collective-permute-done((bf16[96,512]{0,1:T(8,128)(2,1)S(1)}, bf16[96,512]{0,1:T(8,128)(2,1)S(1)}, u32[]{:S(2)}, u32[]{:S(2)}) %collective-permute-start.16) | collective-permute-done | bytes 98336 | tf_op jit(solution)/shard_map/ppermute | solution.py:25
  59.7 4.6 %collective-permute-start.17 = (bf16[48,512]{0,1:T(8,128)(2,1)S(1)}, bf16[48,512]{0,1:T(8,128)(2,1)S(1)}, u32[]{:S(2)}, u32[]{:S(2)}) collective-permute-start(bf16[48,512]{0,1:T(8,128)(2,1)S(1)} %get-tuple-element.38), channel_id=1, source_target_pairs={{0,40},{4,44},{8,48},{12,52},{16,56},{20,60},{24,0},{28,4},{32,8},... | collective-permute-start | bytes 147464 | tf_op jit(solution)/shard_map/ppermute | solution.py:25
  65.2 6.6 %collective-permute-done.17 = bf16[48,512]{0,1:T(8,128)(2,1)S(1)} collective-permute-done((bf16[48,512]{0,1:T(8,128)(2,1)S(1)}, bf16[48,512]{0,1:T(8,128)(2,1)S(1)}, u32[]{:S(2)}, u32[]{:S(2)}) %collective-permute-start.17) | collective-permute-done | bytes 49184 | tf_op jit(solution)/shard_map/ppermute | solution.py:25
  71.8 5.1 %collective-permute-done.18 = bf16[48,512]{0,1:T(8,128)(2,1)S(1)} collective-permute-done((bf16[48,512]{0,1:T(8,128)(2,1)S(1)}, bf16[48,512]{0,1:T(8,128)(2,1)S(1)}, u32[]{:S(2)}, u32[]{:S(2)}) %collective-permute-start.18) | collective-permute-done | bytes 49184 | tf_op jit(solution)/shard_map/ppermute | solution.py:25
  77.6 4.3 %collective-permute-start.21 = (bf16[43,512]{0,1:T(8,128)(2,1)S(1)}, bf16[43,512]{0,1:T(8,128)(2,1)S(1)}, u32[]{:S(2)}, u32[]{:S(2)}) collective-permute-start(bf16[43,512]{0,1:T(8,128)(2,1)S(1)} %get-tuple-element.30), channel_id=1, source_target_pairs={{0,3},{1,2},{2,1},{3,0},{4,7},{5,6},{6,5},{7,4},{8,11},{9,10},{10,... | collective-permute-start | bytes 132104 | tf_op jit(solution)/shard_map/ppermute | solution.py:41
  84.3 2.7 %collective-permute-done.21 = bf16[43,512]{0,1:T(8,128)(2,1)S(1)} collective-permute-done((bf16[43,512]{0,1:T(8,128)(2,1)S(1)}, bf16[43,512]{0,1:T(8,128)(2,1)S(1)}, u32[]{:S(2)}, u32[]{:S(2)}) %collective-permute-start.21) | collective-permute-done | bytes 44064 | tf_op jit(solution)/shard_map/ppermute | solution.py:41
  87.8 1.0 %copy.48 = bf16[1,1024,4,43]{1,2,3,0:T(4,128)(2,1)} copy(bf16[1,1024,4,43]{1,3,2,0:T(8,128)(2,1)S(1)} %fusion) | data formatting | bytes 704512
  (69 shorter events, 16.1 us)
Async XLA Ops:
  0.7 22.3 %collective-permute-start.3 = (bf16[2752,256]{1,0:T(8,128)(2,1)}, bf16[2752,256]{1,0:T(8,128)(2,1)S(1)}, u32[]{:S(2)}, u32[]{:S(2)}) collective-permute-start(bf16[2752,256]{1,0:T(8,128)(2,1)} %bitcast.59), channel_id=1, source_target_pairs={{0,4},{4,0},{8,12},{12,8},{16,20},{20,16},{24,28},{28,24},{32,36},... | collective-permute-start | bytes 4227080 | tf_op jit(solution)/shard_map/ppermute | solution.py:25
  3.8 19.2 %copy-start.1 = (bf16[1,256,2752]{1,2,0:T(8,128)(2,1)S(1)}, bf16[1,256,2752]{1,2,0:T(8,128)(2,1)}, u32[]{:S(2)}) copy-start(bf16[1,256,2752]{1,2,0:T(8,128)(2,1)} %param.7) | copy-start | bytes 4227076
  3.8 6.8 %collective-permute-start.10 = (bf16[256,256]{1,0:T(8,128)(2,1)}, bf16[256,256]{1,0:T(8,128)(2,1)}, u32[]{:S(2)}, u32[]{:S(2)}) collective-permute-start(bf16[256,256]{1,0:T(8,128)(2,1)} %get-tuple-element.41), channel_id=1, source_target_pairs={{0,3},{1,2},{2,1},{3,0},{4,7},{5,6},{6,5},{7,4},{8,11},{9,10},{10,... | collective-permute-start | bytes 393224 | tf_op jit(solution)/shard_map/ppermute | solution.py:41
  6.8 7.4 %collective-permute-start.8 = (bf16[256,256]{1,0:T(8,128)(2,1)}, bf16[256,256]{1,0:T(8,128)(2,1)}, u32[]{:S(2)}, u32[]{:S(2)}) collective-permute-start(bf16[256,256]{1,0:T(8,128)(2,1)} %get-tuple-element.41), channel_id=1, source_target_pairs={{0,1},{1,0},{2,3},{3,2},{4,5},{5,4},{6,7},{7,6},{8,9},{9,8},{10,11... | collective-permute-start | bytes 393224 | tf_op jit(solution)/shard_map/ppermute | solution.py:41
  6.9 8.3 %collective-permute-start.9 = (bf16[256,256]{1,0:T(8,128)(2,1)}, bf16[256,256]{1,0:T(8,128)(2,1)}, u32[]{:S(2)}, u32[]{:S(2)}) collective-permute-start(bf16[256,256]{1,0:T(8,128)(2,1)} %get-tuple-element.41), channel_id=1, source_target_pairs={{0,2},{1,3},{2,0},{3,1},{4,6},{5,7},{6,4},{7,5},{8,10},{9,11},{10,... | collective-permute-start | bytes 393224 | tf_op jit(solution)/shard_map/ppermute | solution.py:41
  9.5 9.5 %collective-permute-start = (bf16[256,256]{1,0:T(8,128)(2,1)}, bf16[256,256]{1,0:T(8,128)(2,1)S(1)}, u32[]{:S(2)}, u32[]{:S(2)}) collective-permute-start(bf16[256,256]{1,0:T(8,128)(2,1)} %get-tuple-element.39), channel_id=1, source_target_pairs={{0,1},{1,0},{2,3},{3,2},{4,5},{5,4},{6,7},{7,6},{8,9},{9,8},{10,11... | collective-permute-start | bytes 393224 | tf_op jit(solution)/shard_map/ppermute | solution.py:41
  10.6 9.6 %collective-permute-start.1 = (bf16[256,256]{1,0:T(8,128)(2,1)}, bf16[256,256]{1,0:T(8,128)(2,1)S(1)}, u32[]{:S(2)}, u32[]{:S(2)}) collective-permute-start(bf16[256,256]{1,0:T(8,128)(2,1)} %get-tuple-element.39), channel_id=1, source_target_pairs={{0,2},{1,3},{2,0},{3,1},{4,6},{5,7},{6,4},{7,5},{8,10},{9,11},{10,... | collective-permute-start | bytes 393224 | tf_op jit(solution)/shard_map/ppermute | solution.py:41
  14.2 7.7 %collective-permute-start.2 = (bf16[256,256]{1,0:T(8,128)(2,1)}, bf16[256,256]{1,0:T(8,128)(2,1)S(1)}, u32[]{:S(2)}, u32[]{:S(2)}) collective-permute-start(bf16[256,256]{1,0:T(8,128)(2,1)} %get-tuple-element.39), channel_id=1, source_target_pairs={{0,3},{1,2},{2,1},{3,0},{4,7},{5,6},{6,5},{7,4},{8,11},{9,10},{10,... | collective-permute-start | bytes 393224 | tf_op jit(solution)/shard_map/ppermute | solution.py:41
  16.4 7.4 %collective-permute-start.11 = (bf16[256,256]{1,0:T(8,128)(2,1)S(1)}, bf16[256,256]{1,0:T(8,128)(2,1)S(1)}, u32[]{:S(2)}, u32[]{:S(2)}) collective-permute-start(bf16[256,256]{1,0:T(8,128)(2,1)S(1)} %add_convert_fusion), channel_id=1, source_target_pairs={{0,4},{4,0},{8,12},{12,8},{16,20},{20,16},{24,28},{28,24},{32,36},... | collective-permute-start | bytes 393224 | tf_op jit(solution)/shard_map/ppermute | solution.py:25
  24.2 11.1 %collective-permute-start.12 = (bf16[384,256]{0,1:T(8,128)(2,1)S(1)}, bf16[384,256]{0,1:T(8,128)(2,1)S(1)}, u32[]{:S(2)}, u32[]{:S(2)}) collective-permute-start(bf16[384,256]{0,1:T(8,128)(2,1)S(1)} %convolution_convert_fusion.3), channel_id=1, source_target_pairs={{0,64},{4,68},{8,72},{12,76},{16,80},{20,84},{24,88},{28,92},{32,9... | collective-permute-start | bytes 589832 | tf_op jit(solution)/shard_map/ppermute | solution.py:25
  26.1 11.6 %collective-permute-start.13 = (bf16[384,256]{0,1:T(8,128)(2,1)S(1)}, bf16[384,256]{0,1:T(8,128)(2,1)S(1)}, u32[]{:S(2)}, u32[]{:S(2)}) collective-permute-start(bf16[384,256]{0,1:T(8,128)(2,1)S(1)} %convolution_convert_fusion.2), channel_id=1, source_target_pairs={{0,128},{4,132},{8,136},{12,140},{16,144},{20,148},{24,152},{28,15... | collective-permute-start | bytes 589832 | tf_op jit(solution)/shard_map/ppermute | solution.py:25
  28.9 1.3 %collective-permute-start.4 = (bf16[256,256]{1,0:T(8,128)(2,1)S(1)}, bf16[256,256]{1,0:T(8,128)(2,1)S(1)}, u32[]{:S(2)}, u32[]{:S(2)}) collective-permute-start(bf16[256,256]{1,0:T(8,128)(2,1)S(1)} %add_convert_fusion.1), channel_id=1, source_target_pairs={{0,4},{4,0},{8,12},{12,8},{16,20},{20,16},{24,28},{28,24},{32,36},... | collective-permute-start | bytes 393224 | tf_op jit(solution)/shard_map/ppermute | solution.py:25
  29.3 12.4 %collective-permute-start.14 = (bf16[384,256]{0,1:T(8,128)(2,1)S(1)}, bf16[384,256]{0,1:T(8,128)(2,1)S(1)}, u32[]{:S(2)}, u32[]{:S(2)}) collective-permute-start(bf16[384,256]{0,1:T(8,128)(2,1)S(1)} %convolution_convert_fusion.1), channel_id=1, source_target_pairs={{0,192},{4,196},{8,200},{12,204},{16,208},{20,212},{24,216},{28,22... | collective-permute-start | bytes 589832 | tf_op jit(solution)/shard_map/ppermute | solution.py:25
  31.0 11.0 %collective-permute-start.5 = (bf16[384,256]{0,1:T(8,128)(2,1)S(1)}, bf16[384,256]{0,1:T(8,128)(2,1)S(1)}, u32[]{:S(2)}, u32[]{:S(2)}) collective-permute-start(bf16[384,256]{0,1:T(8,128)(2,1)S(1)} %convolution_convert_fusion.6), channel_id=1, source_target_pairs={{0,64},{4,68},{8,72},{12,76},{16,80},{20,84},{24,88},{28,92},{32,9... | collective-permute-start | bytes 589832 | tf_op jit(solution)/shard_map/ppermute | solution.py:25
  31.3 14.0 %collective-permute-start.6 = (bf16[384,256]{0,1:T(8,128)(2,1)S(1)}, bf16[384,256]{0,1:T(8,128)(2,1)S(1)}, u32[]{:S(2)}, u32[]{:S(2)}) collective-permute-start(bf16[384,256]{0,1:T(8,128)(2,1)S(1)} %convolution_convert_fusion.5), channel_id=1, source_target_pairs={{0,128},{4,132},{8,136},{12,140},{16,144},{20,148},{24,152},{28,15... | collective-permute-start | bytes 589832 | tf_op jit(solution)/shard_map/ppermute | solution.py:25
  35.3 13.7 %collective-permute-start.7 = (bf16[384,256]{0,1:T(8,128)(2,1)S(1)}, bf16[384,256]{0,1:T(8,128)(2,1)S(1)}, u32[]{:S(2)}, u32[]{:S(2)}) collective-permute-start(bf16[384,256]{0,1:T(8,128)(2,1)S(1)} %convolution_convert_fusion.4), channel_id=1, source_target_pairs={{0,192},{4,196},{8,200},{12,204},{16,208},{20,212},{24,216},{28,22... | collective-permute-start | bytes 589832 | tf_op jit(solution)/shard_map/ppermute | solution.py:25
  49.6 9.6 %collective-permute-start.15 = (bf16[144,512]{0,1:T(8,128)(2,1)S(1)}, bf16[144,512]{0,1:T(8,128)(2,1)S(1)}, u32[]{:S(2)}, u32[]{:S(2)}) collective-permute-start(bf16[144,512]{0,1:T(8,128)(2,1)S(1)} %slice.49), channel_id=1, source_target_pairs={{0,56},{4,60},{8,0},{12,4},{16,8},{20,12},{24,16},{28,20},{32,24},... | collective-permute-start | bytes 442376 | tf_op jit(solution)/shard_map/ppermute | solution.py:25
  50.0 9.2 %collective-permute-start.16 = (bf16[96,512]{0,1:T(8,128)(2,1)S(1)}, bf16[96,512]{0,1:T(8,128)(2,1)S(1)}, u32[]{:S(2)}, u32[]{:S(2)}) collective-permute-start(bf16[96,512]{0,1:T(8,128)(2,1)S(1)} %slice.51), channel_id=1, source_target_pairs={{0,8},{4,12},{8,16},{12,20},{16,24},{20,28},{24,32},{28,36},{32,40... | collective-permute-start | bytes 294920 | tf_op jit(solution)/shard_map/ppermute | solution.py:25
  59.7 12.1 %collective-permute-start.17 = (bf16[48,512]{0,1:T(8,128)(2,1)S(1)}, bf16[48,512]{0,1:T(8,128)(2,1)S(1)}, u32[]{:S(2)}, u32[]{:S(2)}) collective-permute-start(bf16[48,512]{0,1:T(8,128)(2,1)S(1)} %get-tuple-element.38), channel_id=1, source_target_pairs={{0,40},{4,44},{8,48},{12,52},{16,56},{20,60},{24,0},{28,4},{32,8},... | collective-permute-start | bytes 147464 | tf_op jit(solution)/shard_map/ppermute | solution.py:25
  64.3 12.6 %collective-permute-start.18 = (bf16[48,512]{0,1:T(8,128)(2,1)S(1)}, bf16[48,512]{0,1:T(8,128)(2,1)S(1)}, u32[]{:S(2)}, u32[]{:S(2)}) collective-permute-start(bf16[48,512]{0,1:T(8,128)(2,1)S(1)} %slice.105), channel_id=1, source_target_pairs={{0,24},{4,28},{8,32},{12,36},{16,40},{20,44},{24,48},{28,52},{32,5... | collective-permute-start | bytes 147464 | tf_op jit(solution)/shard_map/ppermute | solution.py:25
  76.9 10.2 %copy-start.3 = (bf16[1,1024,512]{2,1,0:T(8,128)(2,1)S(1)}, bf16[1,1024,512]{2,1,0:T(8,128)(2,1)}, u32[]{:S(2)}) copy-start(bf16[1,1024,512]{2,1,0:T(8,128)(2,1)} %param.8) | copy-start | bytes 3145732
  77.1 6.5 %collective-permute-start.19 = (bf16[43,512]{0,1:T(8,128)(2,1)S(1)}, bf16[43,512]{0,1:T(8,128)(2,1)S(1)}, u32[]{:S(2)}, u32[]{:S(2)}) collective-permute-start(bf16[43,512]{0,1:T(8,128)(2,1)S(1)} %get-tuple-element.30), channel_id=1, source_target_pairs={{0,1},{1,0},{2,3},{3,2},{4,5},{5,4},{6,7},{7,6},{8,9},{9,8},{10,11... | collective-permute-start | bytes 132104 | tf_op jit(solution)/shard_map/ppermute | solution.py:41
  77.5 6.8 %collective-permute-start.20 = (bf16[43,512]{0,1:T(8,128)(2,1)S(1)}, bf16[43,512]{0,1:T(8,128)(2,1)S(1)}, u32[]{:S(2)}, u32[]{:S(2)}) collective-permute-start(bf16[43,512]{0,1:T(8,128)(2,1)S(1)} %get-tuple-element.30), channel_id=1, source_target_pairs={{0,2},{1,3},{2,0},{3,1},{4,6},{5,7},{6,4},{7,5},{8,10},{9,11},{10,... | collective-permute-start | bytes 132104 | tf_op jit(solution)/shard_map/ppermute | solution.py:41
  77.6 9.4 %collective-permute-start.21 = (bf16[43,512]{0,1:T(8,128)(2,1)S(1)}, bf16[43,512]{0,1:T(8,128)(2,1)S(1)}, u32[]{:S(2)}, u32[]{:S(2)}) collective-permute-start(bf16[43,512]{0,1:T(8,128)(2,1)S(1)} %get-tuple-element.30), channel_id=1, source_target_pairs={{0,3},{1,2},{2,1},{3,0},{4,7},{5,6},{6,5},{7,4},{8,11},{9,10},{10,... | collective-permute-start | bytes 132104 | tf_op jit(solution)/shard_map/ppermute | solution.py:41
  (5 other events, 29.4 us)

commit v4 on v0

v4 whole, which is shorter than its diff:
```python
import jax
import jax.numpy as jnp
from jax import lax
from jax.experimental import pallas as pl
from jax.experimental.layout import Layout, with_layout_constraint
from jax.experimental.pallas import tpu as pltpu
from jax.sharding import PartitionSpec as P

NX, NZ, NCORE, NY = 4, 8, 2, 4
OWNED = 43
CHIP, PADDED = NCORE * OWNED, 88
BF, F32 = jnp.bfloat16, jnp.float32

Z_ORDER = (-2, 1, -4, -1, 2, 3, 0, -3)
FIRST, SECOND = 2 * PADDED, 5 * PADDED
X_ORDER = ((2, 1, 3, 0), (2, 3, 1, 0))
PAIRS = ((1, 3), (3, 1))


def send(value, move):
    pairs = []
    for d in range(NX * NZ * NCORE * NY):
        x, z, c, y = d // (NZ * NCORE * NY), d // (NCORE * NY) % NZ, d // NY % NCORE, d % NY
        x, z, c, y = move(x, z, c, y)
        pairs.append((d, ((x * NZ + z) * NCORE + c) * NY + y))
    value = with_layout_constraint(value, Layout(major_to_minor=(0, 1)))
    return lax.ppermute(value, ("dp", "tensor"), pairs)


def swap_core(value):
    return send(value, lambda x, z, c, y: (x, z, 1 - c, y))


def swap_x(value, step):
    return send(value, lambda x, z, c, y: (x ^ PAIRS[c][step], z, c, y))


def swap_y(value, step):
    return send(value, lambda x, z, c, y: (x, z, c, y ^ PAIRS[c][step]))


def swap_z(value, k):
    return send(value, lambda x, z, c, y: (x, (z + k * (1 - 2 * (z % 2))) % NZ, c, y))


def around_y(value, m):
    return send(value, lambda x, z, c, y: (x, z, c, y ^ m))


def arrange_kernel(order_ref, own, came, first, second, blocks):
    rows, tokens = own.shape
    for s, source in enumerate((own, came)):
        for n in range(NX * NZ):
            start = n * CHIP
            low = start // 16 * 16
            high = min(rows, -(-(start + PADDED) // 16) * 16)
            piece = source[low:high, :].astype(F32)
            piece = piece[start - low : min(start - low + PADDED, high - low), :]
            if piece.shape[0] < PADDED:
                fill = jnp.zeros((PADDED - piece.shape[0], tokens), F32)
                piece = jnp.concatenate([piece, fill], axis=0)
            blocks[n, :, s * tokens : (s + 1) * tokens] = piece
    half = NX * NZ // 2
    for k, out in enumerate((first, second)):
        for i in range(0, half, 2):
            pair = [blocks[order_ref[k * half + i + j]] for j in range(2)]
            out[i * PADDED : (i + 2) * PADDED, :] = jnp.concatenate(pair, axis=0).astype(BF)


def arrange(order, own, came):
    tokens = own.shape[1]
    shape = jax.ShapeDtypeStruct((NX * NZ // 2 * PADDED, NCORE * tokens), BF)
    vmem = pl.BlockSpec(memory_space=pltpu.VMEM)
    smem = pl.BlockSpec(memory_space=pltpu.SMEM)
    return pl.pallas_call(
        arrange_kernel,
        out_shape=[shape] * 2,
        in_specs=[smem, vmem, vmem],
        out_specs=[vmem] * 2,
        scratch_shapes=[pltpu.VMEM((NX * NZ, PADDED, NCORE * tokens), F32)],
        compiler_params=pltpu.CompilerParams(vmem_limit_bytes=20 * 1024 * 1024),
        cost_estimate=pl.CostEstimate(flops=0, bytes_accessed=8 * 1024 * 1024, transcendentals=0),
    )(order, own, came)


def dot(a, b):
    out = lax.dot_general(a, b, (((1,), (0,)), ((), ())), preferred_element_type=F32)
    return with_layout_constraint(out, Layout(major_to_minor=(0, 1)))


def local(features, cotangent, basis, first_moment, second_moment):
    lanes = basis.shape[2] // NCORE
    scale = 1.0 / (features.shape[1] * lax.axis_size("dp"))
    dp = lax.axis_index("dp")
    core, z, x = dp & 1, (dp >> 1) & (NZ - 1), dp >> 4
    y = lax.axis_index("tensor")

    columns = cotangent[0].T
    other_columns = swap_core(columns)
    up = 1 - 2 * (z & 1)
    blocks_z = (z + up * jnp.array(Z_ORDER, jnp.int32)) & (NZ - 1)
    blocks_x = x ^ jnp.where(core == 0, jnp.array(X_ORDER[0]), jnp.array(X_ORDER[1]))
    order = (blocks_x[:, None] * NZ + blocks_z[None, :]).reshape(-1)
    first, second = arrange(order, columns, other_columns)

    def lanes_of(c):
        return lax.dynamic_slice(basis[0], (0, c * lanes), (basis.shape[1], lanes))

    theirs = swap_core(dot(features[0], lanes_of(1 - core)).astype(BF))
    partial = jnp.concatenate([dot(features[0], lanes_of(core)), theirs.astype(F32)], axis=0)
    for step in range(2):
        partial = partial + swap_y(partial.astype(BF), step).astype(F32)
    projected, first, second = lax.optimization_barrier((partial.astype(BF), first, second))

    came = swap_x(dot(first, projected).astype(BF), 0)
    term = dot(second, projected) + came.astype(F32)
    rows = NZ * PADDED
    term = term[rows:] + swap_x(term[:rows].astype(BF), 1).astype(F32)
    came = swap_z(term[:FIRST].astype(BF), 1).astype(F32)
    more = swap_z(term[FIRST:SECOND].astype(BF), -1).astype(F32)
    keep = term[SECOND:] + more
    hub_a, own, hub_b = keep[:PADDED], keep[PADDED:FIRST], keep[FIRST:]
    hub_a, own = hub_a + came[:PADDED], own + came[PADDED:]
    came = swap_z(hub_a.astype(BF), 3).astype(F32)
    own = own + swap_z(hub_b.astype(BF), -3).astype(F32) + came
    mine, other = own[:OWNED], own[OWNED:CHIP]
    came = swap_core(jnp.where(core == 0, other, mine))
    mine = jnp.where(core == 0, mine, other)
    grads = jnp.concatenate(
        [jnp.where(core == 0, mine, came), jnp.where(core == 0, came, mine)], axis=1
    )

    grads = (grads * scale)[None]
    new_first = 0.9 * first_moment + 0.1 * grads
    new_second = 0.999 * second_moment + 0.001 * grads * grads
    update = (
        new_first / (1.0 - 0.9**10) / (jnp.sqrt(new_second / (1.0 - 0.999**10)) + 1e-08)
    ).astype(BF)[0]

    around = [update] + [around_y(update, m) for m in (1, 2, 3)]
    ordered = jnp.stack([lax.select_n(y ^ a, *around) for a in range(NY)])
    change = jnp.einsum("dr,acr->dac", basis[0], ordered, preferred_element_type=F32)
    return (new_first, new_second, change.astype(BF)[None])


def solution(mesh):
    return jax.shard_map(
        local,
        mesh=mesh,
        in_specs=(
            P(None, "dp", "tensor"),
            P(None, "dp", "tensor"),
            P(None, "tensor", None),
            P(None, ("tensor", "dp"), None),
            P(None, ("tensor", "dp"), None),
        ),
        out_specs=(
            P(None, ("tensor", "dp"), None),
            P(None, ("tensor", "dp"), None),
            P(None, "tensor", None, "dp"),
        ),
        check_vma=False,
    )
```

time: 236 us -> 76.3 us (0.32)
  the two profiles are of different devices: /device:TPU:38 before, /device:TPU:32 now
where the time goes in v4:
time: 76.3 us; the launch traced here: 76.2 us
  waiting for transfers between devices  37.6 us (49%)
  starting transfers between devices  27.2 us (36%)
  local copies, waits for them, and re-layouts  3.86 us (5%)
  matrix products  3.22 us (4%)
  Pallas kernels  2.12 us (3%)
  other arithmetic  1.28 us (2%)
  between operations  0.9 us (1%)
    ppermute x14, waiting for transfers between devices, send(): return lax.ppermute(value, ('dp', 'tensor'), pairs)  37.6 us
    ppermute x14, starting transfers between devices, send(): return lax.ppermute(value, ('dp', 'tensor'), pairs)  27.2 us
    unnamed x19, local copies, waits for them, and re-layouts  3.71 us
    dot_general x4, matrix products, dot(): lax.dot_general(a, b, (((1,), (0,)), ((), ())), preferred_element_type=F32)  2.71 us
    pallas_call x1, Pallas kernels, arrange(): pl.pallas_call(arrange_kernel, out_shape=[shape] * 2, in_specs=[smem, vme...  2.12 us
  transfers between devices with their start and end apart: 14, of which 11 were waited for; matrix products, arithmetic and copies ran while one was open for 4% of the time, Pallas kernels for 0%

profile of v4, /device:TPU:32, one launch (start us, length us, event | category | flops | bytes accessed | tf_op | source)
XLA Modules:
  0.0 76.2 jit_solution(13185368963584328707)
XLA Ops:
  0.7 1.2 %copy-done = bf16[1,1024,512]{2,1,0:T(8,128)(2,1)S(1)} copy-done((bf16[1,1024,512]{2,1,0:T(8,128)(2,1)S(1)}, bf16[1,1024,512]{2,1,0:T(8,128)(2,1)}, u32[]{:S(2)}) %copy-start) | copy-done | bytes 1048600
  1.9 1.3 %fusion.1 = bf16[256,256]{1,0:T(8,128)(2,1)S(1)} fusion(bf16[1,256,1024]{2,1,0:T(8,128)(2,1)} %param.8, bf16[1,1024,512]{2,1,0:T(8,128)(2,1)S(1)} %copy-done, s32[]{:T(128)S(6)} %select_n.144), kind=kOutput, calls=%fused_computation.6 | convolution fusion | flops 134283264 | bytes 1179652 | tf_op jit(solution)/shard_map/dot_general | solution.py:87
  4.7 1.7 %collective-permute-start.1 = (bf16[512,256]{1,0:T(8,128)(2,1)S(1)}, bf16[512,256]{1,0:T(8,128)(2,1)S(1)}, u32[]{:S(2)}, u32[]{:S(2)}) collective-permute-start(bf16[512,256]{1,0:T(8,128)(2,1)S(1)} %fusion.9), channel_id=1, source_target_pairs={{0,1},{1,0},{2,3},{3,2},{4,7},{5,6},{6,5},{7,4},{8,9},{9,8},{10,11... | collective-permute-start | bytes 786440 | tf_op jit(solution)/shard_map/ppermute | solution.py:27
  6.4 4.8 %collective-permute-done.1 = bf16[512,256]{1,0:T(8,128)(2,1)S(1)} collective-permute-done((bf16[512,256]{1,0:T(8,128)(2,1)S(1)}, bf16[512,256]{1,0:T(8,128)(2,1)S(1)}, u32[]{:S(2)}, u32[]{:S(2)}) %collective-permute-start.1) | collective-permute-done | bytes 262176 | tf_op jit(solution)/shard_map/ppermute | solution.py:27
  11.2 0.8 fusion.10
  12.0 3.0 %collective-permute-start.2 = (bf16[512,256]{1,0:T(8,128)(2,1)}, bf16[512,256]{1,0:T(8,128)(2,1)S(1)}, u32[]{:S(2)}, u32[]{:S(2)}) collective-permute-start(bf16[512,256]{1,0:T(8,128)(2,1)} %fusion.10), channel_id=1, source_target_pairs={{0,3},{1,2},{2,1},{3,0},{4,5},{5,4},{6,7},{7,6},{8,11},{9,10},{10,... | collective-permute-start | bytes 786440 | tf_op jit(solution)/shard_map/ppermute | solution.py:27
  15.1 4.6 %collective-permute-done.2 = bf16[512,256]{1,0:T(8,128)(2,1)S(1)} collective-permute-done((bf16[512,256]{1,0:T(8,128)(2,1)}, bf16[512,256]{1,0:T(8,128)(2,1)S(1)}, u32[]{:S(2)}, u32[]{:S(2)}) %collective-permute-start.2) | collective-permute-done | bytes 262176 | tf_op jit(solution)/shard_map/ppermute | solution.py:27
  19.9 2.1 %shard_map.103 = (bf16[1408,512]{1,0:T(8,128)(2,1)S(1)}, bf16[1408,512]{1,0:T(8,128)(2,1)S(1)}) custom-call(s32[32]{0:T(128)S(1)} %add.77.order_ref, bf16[2752,256]{1,0:T(8,128)(2,1)S(1)} %bitcast.47, bf16[2752,256]{1,0:T(8,128)(2,1)} %collective-permute-done.3.came), custom_call_target="tpu_custom_call" | custom-call | bytes 8388608 | tf_op jit(solution)/shard_map/pallas_call | solution.py:75
  22.5 1.6 %collective-permute-start.4 = (bf16[1408,256]{1,0:T(8,128)(2,1)S(1)}, bf16[1408,256]{1,0:T(8,128)(2,1)S(1)}, u32[]{:S(2)}, u32[]{:S(2)}) collective-permute-start(bf16[1408,256]{1,0:T(8,128)(2,1)S(1)} %convolution_convert_fusion), channel_id=1, source_target_pairs={{0,64},{1,65},{2,66},{3,67},{4,196},{5,197},{6,198},{7,199},{8,72}... | collective-permute-start | bytes 2162696 | tf_op jit(solution)/shard_map/ppermute | solution.py:27
  24.1 9.8 %collective-permute-done.4 = bf16[1408,256]{1,0:T(8,128)(2,1)S(1)} collective-permute-done((bf16[1408,256]{1,0:T(8,128)(2,1)S(1)}, bf16[1408,256]{1,0:T(8,128)(2,1)S(1)}, u32[]{:S(2)}, u32[]{:S(2)}) %collective-permute-start.4) | collective-permute-done | bytes 720928 | tf_op jit(solution)/shard_map/ppermute | solution.py:27
  34.5 2.8 %collective-permute-start.5 = (bf16[704,256]{1,0:T(8,128)(2,1)S(1)}, bf16[704,256]{1,0:T(8,128)(2,1)S(1)}, u32[]{:S(2)}, u32[]{:S(2)}) collective-permute-start(bf16[704,256]{1,0:T(8,128)(2,1)S(1)} %slice.90), channel_id=1, source_target_pairs={{0,192},{1,193},{2,194},{3,195},{4,68},{5,69},{6,70},{7,71},{8,200... | collective-permute-start | bytes 1081352 | tf_op jit(solution)/shard_map/ppermute | solution.py:27
  37.3 5.9 %collective-permute-done.5 = bf16[704,256]{1,0:T(8,128)(2,1)S(1)} collective-permute-done((bf16[704,256]{1,0:T(8,128)(2,1)S(1)}, bf16[704,256]{1,0:T(8,128)(2,1)S(1)}, u32[]{:S(2)}, u32[]{:S(2)}) %collective-permute-start.5) | collective-permute-done | bytes 360480 | tf_op jit(solution)/shard_map/ppermute | solution.py:27
  43.3 2.0 %collective-permute-start.6 = (bf16[264,256]{1,0:T(8,128)(2,1)S(1)}, bf16[264,256]{1,0:T(8,128)(2,1)S(1)}, u32[]{:S(2)}, u32[]{:S(2)}) collective-permute-start(bf16[264,256]{1,0:T(8,128)(2,1)S(1)} %slice.55), channel_id=1, source_target_pairs={{0,56},{1,57},{2,58},{3,59},{4,60},{5,61},{6,62},{7,63},{8,16},{9,... | collective-permute-start | bytes 405512 | tf_op jit(solution)/shard_map/ppermute | solution.py:27
  45.4 4.1 %collective-permute-start.7 = (bf16[176,256]{1,0:T(8,128)(2,1)S(1)}, bf16[176,256]{1,0:T(8,128)(2,1)S(1)}, u32[]{:S(2)}, u32[]{:S(2)}) collective-permute-start(bf16[176,256]{1,0:T(8,128)(2,1)S(1)} %slice.57), channel_id=1, source_target_pairs={{0,8},{1,9},{2,10},{3,11},{4,12},{5,13},{6,14},{7,15},{8,0},{9,1},... | collective-permute-start | bytes 270344 | tf_op jit(solution)/shard_map/ppermute | solution.py:27
  49.4 2.6 %collective-permute-done.7 = bf16[176,256]{1,0:T(8,128)(2,1)S(1)} collective-permute-done((bf16[176,256]{1,0:T(8,128)(2,1)S(1)}, bf16[176,256]{1,0:T(8,128)(2,1)S(1)}, u32[]{:S(2)}, u32[]{:S(2)}) %collective-permute-start.7) | collective-permute-done | bytes 90144 | tf_op jit(solution)/shard_map/ppermute | solution.py:27
  52.0 4.1 %collective-permute-start.8 = (bf16[88,256]{1,0:T(8,128)(2,1)S(1)}, bf16[88,256]{1,0:T(8,128)(2,1)S(1)}, u32[]{:S(2)}, u32[]{:S(2)}) collective-permute-start(bf16[88,256]{1,0:T(8,128)(2,1)S(1)} %slice.91), channel_id=1, source_target_pairs={{0,40},{1,41},{2,42},{3,43},{4,44},{5,45},{6,46},{7,47},{8,32},{9,... | collective-permute-start | bytes 135176 | tf_op jit(solution)/shard_map/ppermute | solution.py:27
  56.1 2.6 %collective-permute-start.9 = (bf16[88,256]{1,0:T(8,128)(2,1)S(1)}, bf16[88,256]{1,0:T(8,128)(2,1)S(1)}, u32[]{:S(2)}, u32[]{:S(2)}) collective-permute-start(bf16[88,256]{1,0:T(8,128)(2,1)S(1)} %fusion.20), channel_id=1, source_target_pairs={{0,24},{1,25},{2,26},{3,27},{4,28},{5,29},{6,30},{7,31},{8,48},{9,... | collective-permute-start | bytes 135176 | tf_op jit(solution)/shard_map/ppermute | solution.py:27
  59.3 4.0 %collective-permute-done.9 = bf16[88,256]{1,0:T(8,128)(2,1)S(1)} collective-permute-done((bf16[88,256]{1,0:T(8,128)(2,1)S(1)}, bf16[88,256]{1,0:T(8,128)(2,1)S(1)}, u32[]{:S(2)}, u32[]{:S(2)}) %collective-permute-start.9) | collective-permute-done | bytes 45088 | tf_op jit(solution)/shard_map/ppermute | solution.py:27
  63.4 1.2 %collective-permute-done.10 = f32[43,256]{1,0:T(8,128)S(1)} collective-permute-done((f32[43,256]{1,0:T(8,128)S(1)}, f32[43,256]{1,0:T(8,128)S(1)}, u32[]{:S(2)}, u32[]{:S(2)}) %collective-permute-start.10) | collective-permute-done | bytes 44064 | tf_op jit(solution)/shard_map/ppermute | solution.py:27
  65.2 4.1 %collective-permute-start.12 = (bf16[43,512]{1,0:T(8,128)(2,1)S(1)}, bf16[43,512]{1,0:T(8,128)(2,1)S(1)}, u32[]{:S(2)}, u32[]{:S(2)}) collective-permute-start(bf16[43,512]{1,0:T(8,128)(2,1)S(1)} %get-tuple-element.16), channel_id=1, source_target_pairs={{0,2},{1,3},{2,0},{3,1},{4,6},{5,7},{6,4},{7,5},{8,10},{9,11},{10,... | collective-permute-start | bytes 132104 | tf_op jit(solution)/shard_map/ppermute | solution.py:27
  69.5 0.7 copy.13
  71.0 1.2 %collective-permute-done.12 = bf16[43,512]{1,0:T(8,128)(2,1)S(1)} collective-permute-done((bf16[43,512]{1,0:T(8,128)(2,1)S(1)}, bf16[43,512]{1,0:T(8,128)(2,1)S(1)}, u32[]{:S(2)}, u32[]{:S(2)}) %collective-permute-start.12) | collective-permute-done | bytes 44064 | tf_op jit(solution)/shard_map/ppermute | solution.py:27
  72.2 2.5 %collective-permute-done.13 = bf16[43,512]{1,0:T(8,128)(2,1)S(1)} collective-permute-done((bf16[43,512]{1,0:T(8,128)(2,1)S(1)}, bf16[43,512]{1,0:T(8,128)(2,1)S(1)}, u32[]{:S(2)}, u32[]{:S(2)}) %collective-permute-start.13) | collective-permute-done | bytes 44064 | tf_op jit(solution)/shard_map/ppermute | solution.py:27
  75.2 1.0 %copy.15 = bf16[1,1024,4,43]{1,2,3,0:T(4,128)(2,1)} copy(bf16[1,1024,4,43]{1,3,2,0:T(8,128)(2,1)S(1)} %fusion) | data formatting | bytes 704512
  (50 shorter events, 5.8 us)
Async XLA Ops:
  0.6 1.2 %copy-start = (bf16[1,1024,512]{2,1,0:T(8,128)(2,1)S(1)}, bf16[1,1024,512]{2,1,0:T(8,128)(2,1)}, u32[]{:S(2)}) copy-start(bf16[1,1024,512]{2,1,0:T(8,128)(2,1)} %param.10) | copy-start | bytes 3145732
  0.6 3.2 %copy-start.2 = (bf16[1,256,1024]{2,1,0:T(8,128)(2,1)S(1)}, bf16[1,256,1024]{2,1,0:T(8,128)(2,1)}, u32[]{:S(2)}) copy-start(bf16[1,256,1024]{2,1,0:T(8,128)(2,1)} %param.8) | copy-start | bytes 1572868
  3.2 3.2 %copy-start.5 = (s32[4]{0:T(128)S(1)}, s32[4]{0:T(128)}, u32[]{:S(2)}) copy-start(s32[4]{0:T(128)} %constant.57.clone) | copy-start | bytes 52
  3.2 3.2 %copy-start.6 = (s32[4]{0:T(128)S(1)}, s32[4]{0:T(128)}, u32[]{:S(2)}) copy-start(s32[4]{0:T(128)} %constant.58.clone) | copy-start | bytes 52
  3.2 1.4 %collective-permute-start = (bf16[256,256]{1,0:T(8,128)(2,1)S(1)}, bf16[256,256]{1,0:T(8,128)(2,1)S(1)}, u32[]{:S(2)}, u32[]{:S(2)}) collective-permute-start(bf16[256,256]{1,0:T(8,128)(2,1)S(1)} %fusion.1), channel_id=1, source_target_pairs={{0,4},{1,5},{2,6},{3,7},{4,0},{5,1},{6,2},{7,3},{8,12},{9,13},{10,... | collective-permute-start | bytes 393224 | tf_op jit(solution)/shard_map/ppermute | solution.py:27
  3.3 16.5 %collective-permute-start.3 = (bf16[2752,256]{1,0:T(8,128)(2,1)}, bf16[2752,256]{1,0:T(8,128)(2,1)}, u32[]{:S(2)}, u32[]{:S(2)}) collective-permute-start(bf16[2752,256]{1,0:T(8,128)(2,1)} %bitcast.46), channel_id=1, source_target_pairs={{0,4},{1,5},{2,6},{3,7},{4,0},{5,1},{6,2},{7,3},{8,12},{9,13},{10,... | collective-permute-start | bytes 4227080 | tf_op jit(solution)/shard_map/ppermute | solution.py:27
  4.1 10.8 %copy-start.7 = (s32[8]{0:T(128)S(1)}, s32[8]{0:T(128)}, u32[]{:S(2)}) copy-start(s32[8]{0:T(128)} %constant.56.clone) | copy-start | bytes 100
  4.7 15.2 %copy-start.1 = (bf16[1,256,2752]{1,2,0:T(8,128)(2,1)S(1)}, bf16[1,256,2752]{1,2,0:T(8,128)(2,1)}, u32[]{:S(2)}) copy-start(bf16[1,256,2752]{1,2,0:T(8,128)(2,1)} %param.9) | copy-start | bytes 4227076
  4.7 6.5 %collective-permute-start.1 = (bf16[512,256]{1,0:T(8,128)(2,1)S(1)}, bf16[512,256]{1,0:T(8,128)(2,1)S(1)}, u32[]{:S(2)}, u32[]{:S(2)}) collective-permute-start(bf16[512,256]{1,0:T(8,128)(2,1)S(1)} %fusion.9), channel_id=1, source_target_pairs={{0,1},{1,0},{2,3},{3,2},{4,7},{5,6},{6,5},{7,4},{8,9},{9,8},{10,11... | collective-permute-start | bytes 786440 | tf_op jit(solution)/shard_map/ppermute | solution.py:27
  12.0 7.8 %collective-permute-start.2 = (bf16[512,256]{1,0:T(8,128)(2,1)}, bf16[512,256]{1,0:T(8,128)(2,1)S(1)}, u32[]{:S(2)}, u32[]{:S(2)}) collective-permute-start(bf16[512,256]{1,0:T(8,128)(2,1)} %fusion.10), channel_id=1, source_target_pairs={{0,3},{1,2},{2,1},{3,0},{4,5},{5,4},{6,7},{7,6},{8,11},{9,10},{10,... | collective-permute-start | bytes 786440 | tf_op jit(solution)/shard_map/ppermute | solution.py:27
  22.5 11.4 %collective-permute-start.4 = (bf16[1408,256]{1,0:T(8,128)(2,1)S(1)}, bf16[1408,256]{1,0:T(8,128)(2,1)S(1)}, u32[]{:S(2)}, u32[]{:S(2)}) collective-permute-start(bf16[1408,256]{1,0:T(8,128)(2,1)S(1)} %convolution_convert_fusion), channel_id=1, source_target_pairs={{0,64},{1,65},{2,66},{3,67},{4,196},{5,197},{6,198},{7,199},{8,72}... | collective-permute-start | bytes 2162696 | tf_op jit(solution)/shard_map/ppermute | solution.py:27
  34.5 8.7 %collective-permute-start.5 = (bf16[704,256]{1,0:T(8,128)(2,1)S(1)}, bf16[704,256]{1,0:T(8,128)(2,1)S(1)}, u32[]{:S(2)}, u32[]{:S(2)}) collective-permute-start(bf16[704,256]{1,0:T(8,128)(2,1)S(1)} %slice.90), channel_id=1, source_target_pairs={{0,192},{1,193},{2,194},{3,195},{4,68},{5,69},{6,70},{7,71},{8,200... | collective-permute-start | bytes 1081352 | tf_op jit(solution)/shard_map/ppermute | solution.py:27
  43.3 21.3 %copy-start.3 = (f32[1,43,512]{2,0,1:T(1,128)S(1)}, f32[1,43,512]{2,0,1:T(1,128)}, u32[]{:S(2)}) copy-start(f32[1,43,512]{2,0,1:T(1,128)} %param.12) | copy-start | bytes 264196
  43.3 21.3 %copy-start.4 = (f32[1,43,512]{2,0,1:T(1,128)S(1)}, f32[1,43,512]{2,0,1:T(1,128)}, u32[]{:S(2)}) copy-start(f32[1,43,512]{2,0,1:T(1,128)} %param.11) | copy-start | bytes 264196
  43.3 8.6 %collective-permute-start.6 = (bf16[264,256]{1,0:T(8,128)(2,1)S(1)}, bf16[264,256]{1,0:T(8,128)(2,1)S(1)}, u32[]{:S(2)}, u32[]{:S(2)}) collective-permute-start(bf16[264,256]{1,0:T(8,128)(2,1)S(1)} %slice.55), channel_id=1, source_target_pairs={{0,56},{1,57},{2,58},{3,59},{4,60},{5,61},{6,62},{7,63},{8,16},{9,... | collective-permute-start | bytes 405512 | tf_op jit(solution)/shard_map/ppermute | solution.py:27
  45.4 6.6 %collective-permute-start.7 = (bf16[176,256]{1,0:T(8,128)(2,1)S(1)}, bf16[176,256]{1,0:T(8,128)(2,1)S(1)}, u32[]{:S(2)}, u32[]{:S(2)}) collective-permute-start(bf16[176,256]{1,0:T(8,128)(2,1)S(1)} %slice.57), channel_id=1, source_target_pairs={{0,8},{1,9},{2,10},{3,11},{4,12},{5,13},{6,14},{7,15},{8,0},{9,1},... | collective-permute-start | bytes 270344 | tf_op jit(solution)/shard_map/ppermute | solution.py:27
  52.0 7.2 %collective-permute-start.8 = (bf16[88,256]{1,0:T(8,128)(2,1)S(1)}, bf16[88,256]{1,0:T(8,128)(2,1)S(1)}, u32[]{:S(2)}, u32[]{:S(2)}) collective-permute-start(bf16[88,256]{1,0:T(8,128)(2,1)S(1)} %slice.91), channel_id=1, source_target_pairs={{0,40},{1,41},{2,42},{3,43},{4,44},{5,45},{6,46},{7,47},{8,32},{9,... | collective-permute-start | bytes 135176 | tf_op jit(solution)/shard_map/ppermute | solution.py:27
  56.1 7.1 %collective-permute-start.9 = (bf16[88,256]{1,0:T(8,128)(2,1)S(1)}, bf16[88,256]{1,0:T(8,128)(2,1)S(1)}, u32[]{:S(2)}, u32[]{:S(2)}) collective-permute-start(bf16[88,256]{1,0:T(8,128)(2,1)S(1)} %fusion.20), channel_id=1, source_target_pairs={{0,24},{1,25},{2,26},{3,27},{4,28},{5,29},{6,30},{7,31},{8,48},{9,... | collective-permute-start | bytes 135176 | tf_op jit(solution)/shard_map/ppermute | solution.py:27
  63.3 1.3 %collective-permute-start.10 = (f32[43,256]{1,0:T(8,128)S(1)}, f32[43,256]{1,0:T(8,128)S(1)}, u32[]{:S(2)}, u32[]{:S(2)}) collective-permute-start(f32[43,256]{1,0:T(8,128)S(1)} %slice_select_fusion), channel_id=1, source_target_pairs={{0,4},{1,5},{2,6},{3,7},{4,0},{5,1},{6,2},{7,3},{8,12},{9,13},{10,... | collective-permute-start | bytes 132104 | tf_op jit(solution)/shard_map/ppermute | solution.py:27
  64.8 6.2 %collective-permute-start.11 = (bf16[43,512]{1,0:T(8,128)(2,1)S(1)}, bf16[43,512]{1,0:T(8,128)(2,1)S(1)}, u32[]{:S(2)}, u32[]{:S(2)}) collective-permute-start(bf16[43,512]{1,0:T(8,128)(2,1)S(1)} %get-tuple-element.16), channel_id=1, source_target_pairs={{0,1},{1,0},{2,3},{3,2},{4,5},{5,4},{6,7},{7,6},{8,9},{9,8},{10,11... | collective-permute-start | bytes 132104 | tf_op jit(solution)/shard_map/ppermute | solution.py:27
  65.2 7.0 %collective-permute-start.12 = (bf16[43,512]{1,0:T(8,128)(2,1)S(1)}, bf16[43,512]{1,0:T(8,128)(2,1)S(1)}, u32[]{:S(2)}, u32[]{:S(2)}) collective-permute-start(bf16[43,512]{1,0:T(8,128)(2,1)S(1)} %get-tuple-element.16), channel_id=1, source_target_pairs={{0,2},{1,3},{2,0},{3,1},{4,6},{5,7},{6,4},{7,5},{8,10},{9,11},{10,... | collective-permute-start | bytes 132104 | tf_op jit(solution)/shard_map/ppermute | solution.py:27
  69.3 5.3 %collective-permute-start.13 = (bf16[43,512]{1,0:T(8,128)(2,1)S(1)}, bf16[43,512]{1,0:T(8,128)(2,1)S(1)}, u32[]{:S(2)}, u32[]{:S(2)}) collective-permute-start(bf16[43,512]{1,0:T(8,128)(2,1)S(1)} %get-tuple-element.16), channel_id=1, source_target_pairs={{0,3},{1,2},{2,1},{3,0},{4,7},{5,6},{6,5},{7,4},{8,11},{9,10},{10,... | collective-permute-start | bytes 132104 | tf_op jit(solution)/shard_map/ppermute | solution.py:27

commit v5 on v4

--- a/solution.py
+++ b/solution.py
@@ -8,6 +8,7 @@
 
 NX, NZ, NCORE, NY = 4, 8, 2, 4
 OWNED = 43
+CHUNKS = 2
 CHIP, PADDED = NCORE * OWNED, 88
 BF, F32 = jnp.bfloat16, jnp.float32
 
@@ -101,21 +102,27 @@
     blocks_z = (z + up * jnp.array(Z_ORDER, jnp.int32)) & (NZ - 1)
     blocks_x = x ^ jnp.where(core == 0, jnp.array(X_ORDER[0]), jnp.array(X_ORDER[1]))
     order = (blocks_x[:, None] * NZ + blocks_z[None, :]).reshape(-1)
-    first, second = arrange(order, columns, other_columns)
 
     def lanes_of(c):
         return lax.dynamic_slice(basis[0], (0, c * lanes), (basis.shape[1], lanes))
 
     theirs = swap_core(dot(features[0], lanes_of(1 - core)).astype(BF))
     partial = jnp.concatenate([dot(features[0], lanes_of(core)), theirs.astype(F32)], axis=0)
-    for step in range(2):
-        partial = partial + swap_y(partial.astype(BF), step).astype(F32)
-    projected, first, second = lax.optimization_barrier((partial.astype(BF), first, second))
+    width = lanes // CHUNKS
+    chunks = [partial[:, c * width : (c + 1) * width] for c in range(CHUNKS)]
+    chunks = [p + swap_y(p.astype(BF), 0).astype(F32) for p in chunks]
+    chunks, other_columns = lax.optimization_barrier((chunks, other_columns))
+    first, second = arrange(order, columns, other_columns)
+    chunks = [(p + swap_y(p.astype(BF), 1).astype(F32)).astype(BF) for p in chunks]
+    chunks[0], first, second = lax.optimization_barrier((chunks[0], first, second))
 
-    came = swap_x(dot(first, projected).astype(BF), 0)
-    term = dot(second, projected) + came.astype(F32)
     rows = NZ * PADDED
-    term = term[rows:] + swap_x(term[:rows].astype(BF), 1).astype(F32)
+    terms = []
+    for projected in chunks:
+        came = swap_x(dot(first, projected).astype(BF), 0)
+        term = dot(second, projected) + came.astype(F32)
+        terms.append(term[rows:] + swap_x(term[:rows].astype(BF), 1).astype(F32))
+    term = jnp.concatenate(terms, axis=1)
     came = swap_z(term[:FIRST].astype(BF), 1).astype(F32)
     more = swap_z(term[FIRST:SECOND].astype(BF), -1).astype(F32)
     keep = term[SECOND:] + more

time: 76.3 us -> 73.7 us (0.966)
  the two profiles are of different devices: /device:TPU:32 before, /device:TPU:1 now
where the time goes in v5:
time: 73.7 us; the launch traced here: 73.6 us
  starting transfers between devices  34.5 us (47%)
  waiting for transfers between devices  28.4 us (39%)
  matrix products  4.33 us (6%)
  local copies, waits for them, and re-layouts  2.67 us (4%)
  Pallas kernels  2.11 us (3%)
  between operations  0.99 us (1%)
    ppermute x18, starting transfers between devices, send(): return lax.ppermute(value, ('dp', 'tensor'), pairs)  34.5 us
    ppermute x18, waiting for transfers between devices, send(): return lax.ppermute(value, ('dp', 'tensor'), pairs)  28.4 us
    dot_general x6, matrix products, dot(): lax.dot_general(a, b, (((1,), (0,)), ((), ())), preferred_element_type=F32)  3.83 us
    unnamed x19, local copies, waits for them, and re-layouts  2.52 us
    pallas_call x1, Pallas kernels, arrange(): pl.pallas_call(arrange_kernel, out_shape=[shape] * 2, in_specs=[smem, vme...  2.11 us
  transfers between devices with their start and end apart: 18, of which 14 were waited for; matrix products, arithmetic and copies ran while one was open for 7% of the time, Pallas kernels for 3%

profile of v5, /device:TPU:1, one launch (start us, length us, event | category | flops | bytes accessed | tf_op | source)
XLA Modules:
  0.0 73.6 jit_solution(143003746723069324)
XLA Ops:
  0.7 3.3 %collective-permute-start.3 = (bf16[2752,256]{1,0:T(8,128)(2,1)}, bf16[2752,256]{1,0:T(8,128)(2,1)}, u32[]{:S(2)}, u32[]{:S(2)}) collective-permute-start(bf16[2752,256]{1,0:T(8,128)(2,1)} %bitcast.48), channel_id=1, source_target_pairs={{0,4},{1,5},{2,6},{3,7},{4,0},{5,1},{6,2},{7,3},{8,12},{9,13},{10,... | collective-permute-start | bytes 4227080 | tf_op jit(solution)/shard_map/ppermute | solution.py:28
  4.0 1.3 %fusion.1 = bf16[256,256]{1,0:T(8,128)(2,1)S(1)} fusion(bf16[1,256,1024]{2,1,0:T(8,128)(2,1)} %param.8, bf16[1,1024,512]{2,1,0:T(8,128)(2,1)S(1)} %copy-done, s32[]{:T(128)S(6)} %select_n.144), kind=kOutput, calls=%fused_computation.7 | convolution fusion | flops 134283264 | bytes 1179652 | tf_op jit(solution)/shard_map/dot_general | solution.py:88
  5.4 1.3 %collective-permute-start = (bf16[256,256]{1,0:T(8,128)(2,1)S(1)}, bf16[256,256]{1,0:T(8,128)(2,1)S(1)}, u32[]{:S(2)}, u32[]{:S(2)}) collective-permute-start(bf16[256,256]{1,0:T(8,128)(2,1)S(1)} %fusion.1), channel_id=1, source_target_pairs={{0,4},{1,5},{2,6},{3,7},{4,0},{5,1},{6,2},{7,3},{8,12},{9,13},{10,... | collective-permute-start | bytes 393224 | tf_op jit(solution)/shard_map/ppermute | solution.py:28
  7.8 1.1 %collective-permute-start.2 = (bf16[512,128]{1,0:T(8,128)(2,1)S(1)}, bf16[512,128]{1,0:T(8,128)(2,1)S(1)}, u32[]{:S(2)}, u32[]{:S(2)}) collective-permute-start(bf16[512,128]{1,0:T(8,128)(2,1)S(1)} %get-tuple-element.27), channel_id=1, source_target_pairs={{0,1},{1,0},{2,3},{3,2},{4,7},{5,6},{6,5},{7,4},{8,9},{9,8},{10,11... | collective-permute-start | bytes 393224 | tf_op jit(solution)/shard_map/ppermute | solution.py:28
  8.9 1.7 %collective-permute-start.1 = (bf16[512,128]{1,0:T(8,128)(2,1)S(1)}, bf16[512,128]{1,0:T(8,128)(2,1)S(1)}, u32[]{:S(2)}, u32[]{:S(2)}) collective-permute-start(bf16[512,128]{1,0:T(8,128)(2,1)S(1)} %get-tuple-element.28), channel_id=1, source_target_pairs={{0,1},{1,0},{2,3},{3,2},{4,7},{5,6},{6,5},{7,4},{8,9},{9,8},{10,11... | collective-permute-start | bytes 393224 | tf_op jit(solution)/shard_map/ppermute | solution.py:28
  10.5 2.3 %collective-permute-done.2 = bf16[512,128]{1,0:T(8,128)(2,1)S(1)} collective-permute-done((bf16[512,128]{1,0:T(8,128)(2,1)S(1)}, bf16[512,128]{1,0:T(8,128)(2,1)S(1)}, u32[]{:S(2)}, u32[]{:S(2)}) %collective-permute-start.2) | collective-permute-done | bytes 131104 | tf_op jit(solution)/shard_map/ppermute | solution.py:28
  12.9 1.4 %collective-permute-done.1 = bf16[512,128]{1,0:T(8,128)(2,1)S(1)} collective-permute-done((bf16[512,128]{1,0:T(8,128)(2,1)S(1)}, bf16[512,128]{1,0:T(8,128)(2,1)S(1)}, u32[]{:S(2)}, u32[]{:S(2)}) %collective-permute-start.1) | collective-permute-done | bytes 131104 | tf_op jit(solution)/shard_map/ppermute | solution.py:28
  14.7 1.5 %collective-permute-start.7 = (bf16[512,128]{1,0:T(8,128)(2,1)S(1)}, bf16[512,128]{1,0:T(8,128)(2,1)S(1)}, u32[]{:S(2)}, u32[]{:S(2)}) collective-permute-start(bf16[512,128]{1,0:T(8,128)(2,1)S(1)} %convert_element_type.95), channel_id=1, source_target_pairs={{0,3},{1,2},{2,1},{3,0},{4,5},{5,4},{6,7},{7,6},{8,11},{9,10},{10,... | collective-permute-start | bytes 393224 | tf_op jit(solution)/shard_map/ppermute | solution.py:28
  16.2 2.1 %shard_map.103 = (bf16[1408,512]{1,0:T(8,128)(2,1)S(1)}, bf16[1408,512]{1,0:T(8,128)(2,1)S(1)}) custom-call(s32[32]{0:T(128)S(1)} %add.90.order_ref, bf16[2752,256]{1,0:T(8,128)(2,1)S(1)} %bitcast.49, bf16[2752,256]{1,0:T(8,128)(2,1)} %collective-permute-done.3.came), custom_call_target="tpu_custom_call" | custom-call | bytes 8388608 | tf_op jit(solution)/shard_map/pallas_call | solution.py:76
  18.4 1.6 %collective-permute-done.7 = bf16[512,128]{1,0:T(8,128)(2,1)S(1)} collective-permute-done((bf16[512,128]{1,0:T(8,128)(2,1)S(1)}, bf16[512,128]{1,0:T(8,128)(2,1)S(1)}, u32[]{:S(2)}, u32[]{:S(2)}) %collective-permute-start.7) | collective-permute-done | bytes 131104 | tf_op jit(solution)/shard_map/ppermute | solution.py:28
  20.5 1.9 %collective-permute-start.8 = (bf16[1408,128]{1,0:T(8,128)(2,1)S(1)}, bf16[1408,128]{1,0:T(8,128)(2,1)S(1)}, u32[]{:S(2)}, u32[]{:S(2)}) collective-permute-start(bf16[1408,128]{1,0:T(8,128)(2,1)S(1)} %convolution_convert_fusion), channel_id=1, source_target_pairs={{0,64},{1,65},{2,66},{3,67},{4,196},{5,197},{6,198},{7,199},{8,72}... | collective-permute-start | bytes 1081352 | tf_op jit(solution)/shard_map/ppermute | solution.py:28
  23.9 4.2 %collective-permute-done.8 = bf16[1408,128]{1,0:T(8,128)(2,1)S(1)} collective-permute-done((bf16[1408,128]{1,0:T(8,128)(2,1)S(1)}, bf16[1408,128]{1,0:T(8,128)(2,1)S(1)}, u32[]{:S(2)}, u32[]{:S(2)}) %collective-permute-start.8) | collective-permute-done | bytes 360480 | tf_op jit(solution)/shard_map/ppermute | solution.py:28
  28.8 3.2 %collective-permute-done.5 = bf16[1408,128]{1,0:T(8,128)(2,1)S(1)} collective-permute-done((bf16[1408,128]{1,0:T(8,128)(2,1)S(1)}, bf16[1408,128]{1,0:T(8,128)(2,1)S(1)}, u32[]{:S(2)}, u32[]{:S(2)}) %collective-permute-start.5) | collective-permute-done | bytes 360480 | tf_op jit(solution)/shard_map/ppermute | solution.py:28
  32.7 2.7 %collective-permute-done.9 = bf16[704,128]{1,0:T(8,128)(2,1)S(1)} collective-permute-done((bf16[704,128]{1,0:T(8,128)(2,1)S(1)}, bf16[704,128]{1,0:T(8,128)(2,1)S(1)}, u32[]{:S(2)}, u32[]{:S(2)}) %collective-permute-start.9) | collective-permute-done | bytes 180256 | tf_op jit(solution)/shard_map/ppermute | solution.py:28
  35.4 2.1 %collective-permute-done.6 = bf16[704,128]{1,0:T(8,128)(2,1)S(1)} collective-permute-done((bf16[704,128]{1,0:T(8,128)(2,1)S(1)}, bf16[704,128]{1,0:T(8,128)(2,1)S(1)}, u32[]{:S(2)}, u32[]{:S(2)}) %collective-permute-start.6) | collective-permute-done | bytes 180256 | tf_op jit(solution)/shard_map/ppermute | solution.py:28
  37.7 5.7 %collective-permute-start.10 = (bf16[264,256]{1,0:T(8,128)(2,1)S(1)}, bf16[264,256]{1,0:T(8,128)(2,1)S(1)}, u32[]{:S(2)}, u32[]{:S(2)}) collective-permute-start(bf16[264,256]{1,0:T(8,128)(2,1)S(1)} %slice.77), channel_id=1, source_target_pairs={{0,56},{1,57},{2,58},{3,59},{4,60},{5,61},{6,62},{7,63},{8,16},{9,... | collective-permute-start | bytes 405512 | tf_op jit(solution)/shard_map/ppermute | solution.py:28
  43.4 3.4 %collective-permute-done.11 = bf16[176,256]{1,0:T(8,128)(2,1)S(1)} collective-permute-done((bf16[176,256]{1,0:T(8,128)(2,1)S(1)}, bf16[176,256]{1,0:T(8,128)(2,1)S(1)}, u32[]{:S(2)}, u32[]{:S(2)}) %collective-permute-start.11) | collective-permute-done | bytes 90144 | tf_op jit(solution)/shard_map/ppermute | solution.py:28
  46.9 2.0 %collective-permute-start.13 = (bf16[88,256]{1,0:T(8,128)(2,1)S(1)}, bf16[88,256]{1,0:T(8,128)(2,1)S(1)}, u32[]{:S(2)}, u32[]{:S(2)}) collective-permute-start(bf16[88,256]{1,0:T(8,128)(2,1)S(1)} %fusion.22), channel_id=1, source_target_pairs={{0,24},{1,25},{2,26},{3,27},{4,28},{5,29},{6,30},{7,31},{8,48},{9,... | collective-permute-start | bytes 135176 | tf_op jit(solution)/shard_map/ppermute | solution.py:28
  48.9 2.1 %collective-permute-start.12 = (bf16[88,256]{1,0:T(8,128)(2,1)S(1)}, bf16[88,256]{1,0:T(8,128)(2,1)S(1)}, u32[]{:S(2)}, u32[]{:S(2)}) collective-permute-start(bf16[88,256]{1,0:T(8,128)(2,1)S(1)} %slice.137), channel_id=1, source_target_pairs={{0,40},{1,41},{2,42},{3,43},{4,44},{5,45},{6,46},{7,47},{8,32},{9,... | collective-permute-start | bytes 135176 | tf_op jit(solution)/shard_map/ppermute | solution.py:28
  51.6 3.5 %collective-permute-done.12 = bf16[88,256]{1,0:T(8,128)(2,1)S(1)} collective-permute-done((bf16[88,256]{1,0:T(8,128)(2,1)S(1)}, bf16[88,256]{1,0:T(8,128)(2,1)S(1)}, u32[]{:S(2)}, u32[]{:S(2)}) %collective-permute-start.12) | collective-permute-done | bytes 45088 | tf_op jit(solution)/shard_map/ppermute | solution.py:28
  55.2 9.9 %collective-permute-start.14 = (f32[43,256]{1,0:T(8,128)S(1)}, f32[43,256]{1,0:T(8,128)S(1)}, u32[]{:S(2)}, u32[]{:S(2)}) collective-permute-start(f32[43,256]{1,0:T(8,128)S(1)} %slice_select_fusion), channel_id=1, source_target_pairs={{0,4},{1,5},{2,6},{3,7},{4,0},{5,1},{6,2},{7,3},{8,12},{9,13},{10,... | collective-permute-start | bytes 132104 | tf_op jit(solution)/shard_map/ppermute | solution.py:28
  66.7 2.2 %collective-permute-start.15 = (bf16[43,512]{1,0:T(8,128)(2,1)S(1)}, bf16[43,512]{1,0:T(8,128)(2,1)S(1)}, u32[]{:S(2)}, u32[]{:S(2)}) collective-permute-start(bf16[43,512]{1,0:T(8,128)(2,1)S(1)} %get-tuple-element.22), channel_id=1, source_target_pairs={{0,1},{1,0},{2,3},{3,2},{4,5},{5,4},{6,7},{7,6},{8,9},{9,8},{10,11... | collective-permute-start | bytes 132104 | tf_op jit(solution)/shard_map/ppermute | solution.py:28
  70.8 1.2 %collective-permute-done.17 = bf16[43,512]{1,0:T(8,128)(2,1)S(1)} collective-permute-done((bf16[43,512]{1,0:T(8,128)(2,1)S(1)}, bf16[43,512]{1,0:T(8,128)(2,1)S(1)}, u32[]{:S(2)}, u32[]{:S(2)}) %collective-permute-start.17) | collective-permute-done | bytes 44064 | tf_op jit(solution)/shard_map/ppermute | solution.py:28
  72.5 1.0 %copy.15 = bf16[1,1024,4,43]{1,2,3,0:T(4,128)(2,1)} copy(bf16[1,1024,4,43]{1,3,2,0:T(8,128)(2,1)S(1)} %fusion) | data formatting | bytes 704512
  (65 shorter events, 9.7 us)
Async XLA Ops:
  0.6 6.4 %copy-start.5 = (s32[4]{0:T(128)S(1)}, s32[4]{0:T(128)}, u32[]{:S(2)}) copy-start(s32[4]{0:T(128)} %constant.57.clone) | copy-start | bytes 52
  0.7 6.4 %copy-start.6 = (s32[4]{0:T(128)S(1)}, s32[4]{0:T(128)}, u32[]{:S(2)}) copy-start(s32[4]{0:T(128)} %constant.58.clone) | copy-start | bytes 52
  0.7 6.0 %copy-start.2 = (bf16[1,256,1024]{2,1,0:T(8,128)(2,1)S(1)}, bf16[1,256,1024]{2,1,0:T(8,128)(2,1)}, u32[]{:S(2)}) copy-start(bf16[1,256,1024]{2,1,0:T(8,128)(2,1)} %param.8) | copy-start | bytes 1572868
  0.7 13.7 %collective-permute-start.3 = (bf16[2752,256]{1,0:T(8,128)(2,1)}, bf16[2752,256]{1,0:T(8,128)(2,1)}, u32[]{:S(2)}, u32[]{:S(2)}) collective-permute-start(bf16[2752,256]{1,0:T(8,128)(2,1)} %bitcast.48), channel_id=1, source_target_pairs={{0,4},{1,5},{2,6},{3,7},{4,0},{5,1},{6,2},{7,3},{8,12},{9,13},{10,... | collective-permute-start | bytes 4227080 | tf_op jit(solution)/shard_map/ppermute | solution.py:28
  5.4 2.3 %collective-permute-start = (bf16[256,256]{1,0:T(8,128)(2,1)S(1)}, bf16[256,256]{1,0:T(8,128)(2,1)S(1)}, u32[]{:S(2)}, u32[]{:S(2)}) collective-permute-start(bf16[256,256]{1,0:T(8,128)(2,1)S(1)} %fusion.1), channel_id=1, source_target_pairs={{0,4},{1,5},{2,6},{3,7},{4,0},{5,1},{6,2},{7,3},{8,12},{9,13},{10,... | collective-permute-start | bytes 393224 | tf_op jit(solution)/shard_map/ppermute | solution.py:28
  7.7 8.5 %copy-start.1 = (bf16[1,256,2752]{1,2,0:T(8,128)(2,1)S(1)}, bf16[1,256,2752]{1,2,0:T(8,128)(2,1)}, u32[]{:S(2)}) copy-start(bf16[1,256,2752]{1,2,0:T(8,128)(2,1)} %param.9) | copy-start | bytes 4227076
  7.8 5.1 %collective-permute-start.2 = (bf16[512,128]{1,0:T(8,128)(2,1)S(1)}, bf16[512,128]{1,0:T(8,128)(2,1)S(1)}, u32[]{:S(2)}, u32[]{:S(2)}) collective-permute-start(bf16[512,128]{1,0:T(8,128)(2,1)S(1)} %get-tuple-element.27), channel_id=1, source_target_pairs={{0,1},{1,0},{2,3},{3,2},{4,7},{5,6},{6,5},{7,4},{8,9},{9,8},{10,11... | collective-permute-start | bytes 393224 | tf_op jit(solution)/shard_map/ppermute | solution.py:28
  8.9 5.4 %collective-permute-start.1 = (bf16[512,128]{1,0:T(8,128)(2,1)S(1)}, bf16[512,128]{1,0:T(8,128)(2,1)S(1)}, u32[]{:S(2)}, u32[]{:S(2)}) collective-permute-start(bf16[512,128]{1,0:T(8,128)(2,1)S(1)} %get-tuple-element.28), channel_id=1, source_target_pairs={{0,1},{1,0},{2,3},{3,2},{4,7},{5,6},{6,5},{7,4},{8,9},{9,8},{10,11... | collective-permute-start | bytes 393224 | tf_op jit(solution)/shard_map/ppermute | solution.py:28
  14.4 3.9 %collective-permute-start.4 = (bf16[512,128]{1,0:T(8,128)(2,1)S(1)}, bf16[512,128]{1,0:T(8,128)(2,1)S(1)}, u32[]{:S(2)}, u32[]{:S(2)}) collective-permute-start(bf16[512,128]{1,0:T(8,128)(2,1)S(1)} %convert_element_type.89), channel_id=1, source_target_pairs={{0,3},{1,2},{2,1},{3,0},{4,5},{5,4},{6,7},{7,6},{8,11},{9,10},{10,... | collective-permute-start | bytes 393224 | tf_op jit(solution)/shard_map/ppermute | solution.py:28
  14.7 5.3 %collective-permute-start.7 = (bf16[512,128]{1,0:T(8,128)(2,1)S(1)}, bf16[512,128]{1,0:T(8,128)(2,1)S(1)}, u32[]{:S(2)}, u32[]{:S(2)}) collective-permute-start(bf16[512,128]{1,0:T(8,128)(2,1)S(1)} %convert_element_type.95), channel_id=1, source_target_pairs={{0,3},{1,2},{2,1},{3,0},{4,5},{5,4},{6,7},{7,6},{8,11},{9,10},{10,... | collective-permute-start | bytes 393224 | tf_op jit(solution)/shard_map/ppermute | solution.py:28
  20.5 7.6 %collective-permute-start.8 = (bf16[1408,128]{1,0:T(8,128)(2,1)S(1)}, bf16[1408,128]{1,0:T(8,128)(2,1)S(1)}, u32[]{:S(2)}, u32[]{:S(2)}) collective-permute-start(bf16[1408,128]{1,0:T(8,128)(2,1)S(1)} %convolution_convert_fusion), channel_id=1, source_target_pairs={{0,64},{1,65},{2,66},{3,67},{4,196},{5,197},{6,198},{7,199},{8,72}... | collective-permute-start | bytes 1081352 | tf_op jit(solution)/shard_map/ppermute | solution.py:28
  22.9 9.0 %collective-permute-start.5 = (bf16[1408,128]{1,0:T(8,128)(2,1)S(1)}, bf16[1408,128]{1,0:T(8,128)(2,1)S(1)}, u32[]{:S(2)}, u32[]{:S(2)}) collective-permute-start(bf16[1408,128]{1,0:T(8,128)(2,1)S(1)} %convolution_convert_fusion.1), channel_id=1, source_target_pairs={{0,64},{1,65},{2,66},{3,67},{4,196},{5,197},{6,198},{7,199},{8,72}... | collective-permute-start | bytes 1081352 | tf_op jit(solution)/shard_map/ppermute | solution.py:28
  28.7 6.7 %collective-permute-start.9 = (bf16[704,128]{1,0:T(8,128)(2,1)S(1)}, bf16[704,128]{1,0:T(8,128)(2,1)S(1)}, u32[]{:S(2)}, u32[]{:S(2)}) collective-permute-start(bf16[704,128]{1,0:T(8,128)(2,1)S(1)} %slice.135), channel_id=1, source_target_pairs={{0,192},{1,193},{2,194},{3,195},{4,68},{5,69},{6,70},{7,71},{8,200... | collective-permute-start | bytes 540680 | tf_op jit(solution)/shard_map/ppermute | solution.py:28
  32.6 5.0 %collective-permute-start.6 = (bf16[704,128]{1,0:T(8,128)(2,1)S(1)}, bf16[704,128]{1,0:T(8,128)(2,1)S(1)}, u32[]{:S(2)}, u32[]{:S(2)}) collective-permute-start(bf16[704,128]{1,0:T(8,128)(2,1)S(1)} %slice.136), channel_id=1, source_target_pairs={{0,192},{1,193},{2,194},{3,195},{4,68},{5,69},{6,70},{7,71},{8,200... | collective-permute-start | bytes 540680 | tf_op jit(solution)/shard_map/ppermute | solution.py:28
  37.7 28.4 %copy-start.3 = (f32[1,43,512]{2,0,1:T(1,128)S(1)}, f32[1,43,512]{2,0,1:T(1,128)}, u32[]{:S(2)}) copy-start(f32[1,43,512]{2,0,1:T(1,128)} %param.12) | copy-start | bytes 264196
  37.7 28.4 %copy-start.4 = (f32[1,43,512]{2,0,1:T(1,128)S(1)}, f32[1,43,512]{2,0,1:T(1,128)}, u32[]{:S(2)}) copy-start(f32[1,43,512]{2,0,1:T(1,128)} %param.11) | copy-start | bytes 264196
  37.7 9.1 %collective-permute-start.10 = (bf16[264,256]{1,0:T(8,128)(2,1)S(1)}, bf16[264,256]{1,0:T(8,128)(2,1)S(1)}, u32[]{:S(2)}, u32[]{:S(2)}) collective-permute-start(bf16[264,256]{1,0:T(8,128)(2,1)S(1)} %slice.77), channel_id=1, source_target_pairs={{0,56},{1,57},{2,58},{3,59},{4,60},{5,61},{6,62},{7,63},{8,16},{9,... | collective-permute-start | bytes 405512 | tf_op jit(solution)/shard_map/ppermute | solution.py:28
  43.4 3.4 %collective-permute-start.11 = (bf16[176,256]{1,0:T(8,128)(2,1)S(1)}, bf16[176,256]{1,0:T(8,128)(2,1)S(1)}, u32[]{:S(2)}, u32[]{:S(2)}) collective-permute-start(bf16[176,256]{1,0:T(8,128)(2,1)S(1)} %slice.79), channel_id=1, source_target_pairs={{0,8},{1,9},{2,10},{3,11},{4,12},{5,13},{6,14},{7,15},{8,0},{9,1},... | collective-permute-start | bytes 270344 | tf_op jit(solution)/shard_map/ppermute | solution.py:28
  46.9 4.8 %collective-permute-start.13 = (bf16[88,256]{1,0:T(8,128)(2,1)S(1)}, bf16[88,256]{1,0:T(8,128)(2,1)S(1)}, u32[]{:S(2)}, u32[]{:S(2)}) collective-permute-start(bf16[88,256]{1,0:T(8,128)(2,1)S(1)} %fusion.22), channel_id=1, source_target_pairs={{0,24},{1,25},{2,26},{3,27},{4,28},{5,29},{6,30},{7,31},{8,48},{9,... | collective-permute-start | bytes 135176 | tf_op jit(solution)/shard_map/ppermute | solution.py:28
  48.9 6.3 %collective-permute-start.12 = (bf16[88,256]{1,0:T(8,128)(2,1)S(1)}, bf16[88,256]{1,0:T(8,128)(2,1)S(1)}, u32[]{:S(2)}, u32[]{:S(2)}) collective-permute-start(bf16[88,256]{1,0:T(8,128)(2,1)S(1)} %slice.137), channel_id=1, source_target_pairs={{0,40},{1,41},{2,42},{3,43},{4,44},{5,45},{6,46},{7,47},{8,32},{9,... | collective-permute-start | bytes 135176 | tf_op jit(solution)/shard_map/ppermute | solution.py:28
  55.2 10.8 %collective-permute-start.14 = (f32[43,256]{1,0:T(8,128)S(1)}, f32[43,256]{1,0:T(8,128)S(1)}, u32[]{:S(2)}, u32[]{:S(2)}) collective-permute-start(f32[43,256]{1,0:T(8,128)S(1)} %slice_select_fusion), channel_id=1, source_target_pairs={{0,4},{1,5},{2,6},{3,7},{4,0},{5,1},{6,2},{7,3},{8,12},{9,13},{10,... | collective-permute-start | bytes 132104 | tf_op jit(solution)/shard_map/ppermute | solution.py:28
  66.2 4.6 %collective-permute-start.16 = (bf16[43,512]{1,0:T(8,128)(2,1)S(1)}, bf16[43,512]{1,0:T(8,128)(2,1)S(1)}, u32[]{:S(2)}, u32[]{:S(2)}) collective-permute-start(bf16[43,512]{1,0:T(8,128)(2,1)S(1)} %get-tuple-element.22), channel_id=1, source_target_pairs={{0,2},{1,3},{2,0},{3,1},{4,6},{5,7},{6,4},{7,5},{8,10},{9,11},{10,... | collective-permute-start | bytes 132104 | tf_op jit(solution)/shard_map/ppermute | solution.py:28
  66.3 5.7 %collective-permute-start.17 = (bf16[43,512]{1,0:T(8,128)(2,1)S(1)}, bf16[43,512]{1,0:T(8,128)(2,1)S(1)}, u32[]{:S(2)}, u32[]{:S(2)}) collective-permute-start(bf16[43,512]{1,0:T(8,128)(2,1)S(1)} %get-tuple-element.22), channel_id=1, source_target_pairs={{0,3},{1,2},{2,1},{3,0},{4,7},{5,6},{6,5},{7,4},{8,11},{9,10},{10,... | collective-permute-start | bytes 132104 | tf_op jit(solution)/shard_map/ppermute | solution.py:28
  66.7 5.3 %collective-permute-start.15 = (bf16[43,512]{1,0:T(8,128)(2,1)S(1)}, bf16[43,512]{1,0:T(8,128)(2,1)S(1)}, u32[]{:S(2)}, u32[]{:S(2)}) collective-permute-start(bf16[43,512]{1,0:T(8,128)(2,1)S(1)} %get-tuple-element.22), channel_id=1, source_target_pairs={{0,1},{1,0},{2,3},{3,2},{4,5},{5,4},{6,7},{7,6},{8,9},{9,8},{10,11... | collective-permute-start | bytes 132104 | tf_op jit(solution)/shard_map/ppermute | solution.py:28
  (2 other events, 8.6 us)

commit v6 on v5

--- a/solution.py
+++ b/solution.py
@@ -32,23 +32,20 @@
     return send(value, lambda x, z, c, y: (x, z, 1 - c, y))
 
 
-def swap_x(value, step):
-    return send(value, lambda x, z, c, y: (x ^ PAIRS[c][step], z, c, y))
-
-
-def swap_y(value, step):
-    return send(value, lambda x, z, c, y: (x, z, c, y ^ PAIRS[c][step]))
+def swap_x(value, m):
+    return send(value, lambda x, z, c, y: (x ^ m, z, c, y))
 
 
 def swap_z(value, k):
     return send(value, lambda x, z, c, y: (x, (z + k * (1 - 2 * (z % 2))) % NZ, c, y))
 
 
-def around_y(value, m):
+def swap_y(value, m):
     return send(value, lambda x, z, c, y: (x, z, c, y ^ m))
 
 
-def arrange_kernel(order_ref, own, came, first, second, blocks):
+def arrange_kernel(order_ref, own, came, *refs):
+    outs, blocks = refs[:-1], refs[-1]
     rows, tokens = own.shape
     for s, source in enumerate((own, came)):
         for n in range(NX * NZ):
@@ -62,7 +59,7 @@
                 piece = jnp.concatenate([piece, fill], axis=0)
             blocks[n, :, s * tokens : (s + 1) * tokens] = piece
     half = NX * NZ // 2
-    for k, out in enumerate((first, second)):
+    for k, out in enumerate(outs):
         for i in range(0, half, 2):
             pair = [blocks[order_ref[k * half + i + j]] for j in range(2)]
             out[i * PADDED : (i + 2) * PADDED, :] = jnp.concatenate(pair, axis=0).astype(BF)
@@ -75,9 +72,9 @@
     smem = pl.BlockSpec(memory_space=pltpu.SMEM)
     return pl.pallas_call(
         arrange_kernel,
-        out_shape=[shape] * 2,
+        out_shape=[shape] * 2 * CHUNKS,
         in_specs=[smem, vmem, vmem],
-        out_specs=[vmem] * 2,
+        out_specs=[vmem] * 2 * CHUNKS,
         scratch_shapes=[pltpu.VMEM((NX * NZ, PADDED, NCORE * tokens), F32)],
         compiler_params=pltpu.CompilerParams(vmem_limit_bytes=20 * 1024 * 1024),
         cost_estimate=pl.CostEstimate(flops=0, bytes_accessed=8 * 1024 * 1024, transcendentals=0),
@@ -100,7 +97,7 @@
     other_columns = swap_core(columns)
     up = 1 - 2 * (z & 1)
     blocks_z = (z + up * jnp.array(Z_ORDER, jnp.int32)) & (NZ - 1)
-    blocks_x = x ^ jnp.where(core == 0, jnp.array(X_ORDER[0]), jnp.array(X_ORDER[1]))
+    blocks_x = x ^ jnp.array(X_ORDER, jnp.int32).reshape(-1)
     order = (blocks_x[:, None] * NZ + blocks_z[None, :]).reshape(-1)
 
     def lanes_of(c):
@@ -110,18 +107,19 @@
     partial = jnp.concatenate([dot(features[0], lanes_of(core)), theirs.astype(F32)], axis=0)
     width = lanes // CHUNKS
     chunks = [partial[:, c * width : (c + 1) * width] for c in range(CHUNKS)]
-    chunks = [p + swap_y(p.astype(BF), 0).astype(F32) for p in chunks]
+    chunks = [p + swap_y(p.astype(BF), m[0]).astype(F32) for p, m in zip(chunks, PAIRS)]
     chunks, other_columns = lax.optimization_barrier((chunks, other_columns))
-    first, second = arrange(order, columns, other_columns)
-    chunks = [(p + swap_y(p.astype(BF), 1).astype(F32)).astype(BF) for p in chunks]
-    chunks[0], first, second = lax.optimization_barrier((chunks[0], first, second))
+    parts = arrange(order, columns, other_columns)
+    chunks = [p + swap_y(p.astype(BF), m[1]).astype(F32) for p, m in zip(chunks, PAIRS)]
+    chunks = [p.astype(BF) for p in chunks]
+    chunks[0], parts = lax.optimization_barrier((chunks[0], parts))
 
     rows = NZ * PADDED
     terms = []
-    for projected in chunks:
-        came = swap_x(dot(first, projected).astype(BF), 0)
-        term = dot(second, projected) + came.astype(F32)
-        terms.append(term[rows:] + swap_x(term[:rows].astype(BF), 1).astype(F32))
+    for c, (projected, m) in enumerate(zip(chunks, PAIRS)):
+        came = swap_x(dot(parts[2 * c], projected).astype(BF), m[0])
+        term = dot(parts[2 * c + 1], projected) + came.astype(F32)
+        terms.append(term[rows:] + swap_x(term[:rows].astype(BF), m[1]).astype(F32))
     term = jnp.concatenate(terms, axis=1)
     came = swap_z(term[:FIRST].astype(BF), 1).astype(F32)
     more = swap_z(term[FIRST:SECOND].astype(BF), -1).astype(F32)
@@ -144,7 +142,7 @@
         new_first / (1.0 - 0.9**10) / (jnp.sqrt(new_second / (1.0 - 0.999**10)) + 1e-08)
     ).astype(BF)[0]
 
-    around = [update] + [around_y(update, m) for m in (1, 2, 3)]
+    around = [update] + [swap_y(update, m) for m in (1, 2, 3)]
     ordered = jnp.stack([lax.select_n(y ^ a, *around) for a in range(NY)])
     change = jnp.einsum("dr,acr->dac", basis[0], ordered, preferred_element_type=F32)
     return (new_first, new_second, change.astype(BF)[None])

time: 73.7 us -> 71.3 us (0.967)
  the two profiles are of different devices: /device:TPU:1 before, /device:TPU:32 now
where the time goes in v6:
time: 71.3 us; the launch traced here: 70.1 us
  waiting for transfers between devices  32.6 us (46%)
  starting transfers between devices  24.8 us (35%)
  matrix products  4.33 us (6%)
  local copies, waits for them, and re-layouts  3.83 us (5%)
  Pallas kernels  2.39 us (3%)
  other arithmetic  1.24 us (2%)
  between operations  0.96 us (1%)
    ppermute x18, waiting for transfers between devices, send(): return lax.ppermute(value, ('dp', 'tensor'), pairs)  32.6 us
    ppermute x18, starting transfers between devices, send(): return lax.ppermute(value, ('dp', 'tensor'), pairs)  24.8 us
    dot_general x6, matrix products, dot(): lax.dot_general(a, b, (((1,), (0,)), ((), ())), preferred_element_type=F32)  3.82 us
    unnamed x15, local copies, waits for them, and re-layouts  3.6 us
    pallas_call x1, Pallas kernels, arrange(): pl.pallas_call(arrange_kernel, out_shape=[shape] * 2 * CHUNKS, in_specs=[...  2.39 us
  transfers between devices with their start and end apart: 18, of which 15 were waited for; matrix products, arithmetic and copies ran while one was open for 8% of the time, Pallas kernels for 3%

profile of v6, /device:TPU:32, one launch (start us, length us, event | category | flops | bytes accessed | tf_op | source)
XLA Modules:
  0.0 70.1 jit_solution(7462929485401757351)
XLA Ops:
  0.8 1.1 %copy-done = bf16[1,1024,512]{2,1,0:T(8,128)(2,1)S(1)} copy-done((bf16[1,1024,512]{2,1,0:T(8,128)(2,1)S(1)}, bf16[1,1024,512]{2,1,0:T(8,128)(2,1)}, u32[]{:S(2)}) %copy-start) | copy-done | bytes 1048600
  1.9 1.3 %fusion.1 = bf16[256,256]{1,0:T(8,128)(2,1)S(1)} fusion(bf16[1,256,1024]{2,1,0:T(8,128)(2,1)} %param.7, bf16[1,1024,512]{2,1,0:T(8,128)(2,1)S(1)} %copy-done, s32[]{:T(128)S(6)} %select_n.136), kind=kOutput, calls=%fused_computation.7 | convolution fusion | flops 134283264 | bytes 1179652 | tf_op jit(solution)/shard_map/dot_general | solution.py:85
  4.7 3.1 %collective-permute-start.2 = (bf16[512,128]{1,0:T(8,128)(2,1)S(1)}, bf16[512,128]{1,0:T(8,128)(2,1)S(1)}, u32[]{:S(2)}, u32[]{:S(2)}) collective-permute-start(bf16[512,128]{1,0:T(8,128)(2,1)S(1)} %get-tuple-element.35), channel_id=1, source_target_pairs={{0,3},{1,2},{2,1},{3,0},{4,7},{5,6},{6,5},{7,4},{8,11},{9,10},{10,... | collective-permute-start | bytes 393224 | tf_op jit(solution)/shard_map/ppermute | solution.py:28
  8.0 3.8 %collective-permute-done.2 = bf16[512,128]{1,0:T(8,128)(2,1)S(1)} collective-permute-done((bf16[512,128]{1,0:T(8,128)(2,1)S(1)}, bf16[512,128]{1,0:T(8,128)(2,1)S(1)}, u32[]{:S(2)}, u32[]{:S(2)}) %collective-permute-start.2) | collective-permute-done | bytes 131104 | tf_op jit(solution)/shard_map/ppermute | solution.py:28
  11.8 1.5 %collective-permute-done.1 = bf16[512,128]{1,0:T(8,128)(2,1)S(1)} collective-permute-done((bf16[512,128]{1,0:T(8,128)(2,1)S(1)}, bf16[512,128]{1,0:T(8,128)(2,1)S(1)}, u32[]{:S(2)}, u32[]{:S(2)}) %collective-permute-start.1) | collective-permute-done | bytes 131104 | tf_op jit(solution)/shard_map/ppermute | solution.py:28
  13.3 1.6 %collective-permute-start.4 = (bf16[512,128]{1,0:T(8,128)(2,1)S(1)}, bf16[512,128]{1,0:T(8,128)(2,1)S(1)}, u32[]{:S(2)}, u32[]{:S(2)}) collective-permute-start(bf16[512,128]{1,0:T(8,128)(2,1)S(1)} %convert_element_type.89), channel_id=1, source_target_pairs={{0,3},{1,2},{2,1},{3,0},{4,7},{5,6},{6,5},{7,4},{8,11},{9,10},{10,... | collective-permute-start | bytes 393224 | tf_op jit(solution)/shard_map/ppermute | solution.py:28
  15.2 2.4 %shard_map.94 = (bf16[1408,512]{1,0:T(8,128)(2,1)S(1)}, bf16[1408,512]{1,0:T(8,128)(2,1)S(1)}, bf16[1408,512]{1,0:T(8,128)(2,1)S(1)}, bf16[1408,512]{1,0:T(8,128)(2,1)S(1)}) custom-call(s32[64]{0:T(128)S(1)} %add.90.order_ref, bf16[2752,256]{1,0:T(8,128)(2,1)S(1)} %bitcast.49, bf16[2752,256]{1,0:T(8,128)(2,1)} %collective-permute-done.3.came), custom_call_target="tpu_custom_call" | custom-call | bytes 8388608 | tf_op jit(solution)/shard_map/pallas_call | solution.py:73
  17.6 2.0 %collective-permute-done.4 = bf16[512,128]{1,0:T(8,128)(2,1)S(1)} collective-permute-done((bf16[512,128]{1,0:T(8,128)(2,1)S(1)}, bf16[512,128]{1,0:T(8,128)(2,1)S(1)}, u32[]{:S(2)}, u32[]{:S(2)}) %collective-permute-start.4) | collective-permute-done | bytes 131104 | tf_op jit(solution)/shard_map/ppermute | solution.py:28
  20.7 2.8 %collective-permute-start.8 = (bf16[1408,128]{1,0:T(8,128)(2,1)S(1)}, bf16[1408,128]{1,0:T(8,128)(2,1)S(1)}, u32[]{:S(2)}, u32[]{:S(2)}) collective-permute-start(bf16[1408,128]{1,0:T(8,128)(2,1)S(1)} %convolution_convert_fusion), channel_id=1, source_target_pairs={{0,192},{1,193},{2,194},{3,195},{4,196},{5,197},{6,198},{7,199},{8... | collective-permute-start | bytes 1081352 | tf_op jit(solution)/shard_map/ppermute | solution.py:28
  24.4 6.2 %collective-permute-done.8 = bf16[1408,128]{1,0:T(8,128)(2,1)S(1)} collective-permute-done((bf16[1408,128]{1,0:T(8,128)(2,1)S(1)}, bf16[1408,128]{1,0:T(8,128)(2,1)S(1)}, u32[]{:S(2)}, u32[]{:S(2)}) %collective-permute-start.8) | collective-permute-done | bytes 360480 | tf_op jit(solution)/shard_map/ppermute | solution.py:28
  31.5 2.1 %collective-permute-done.5 = bf16[1408,128]{1,0:T(8,128)(2,1)S(1)} collective-permute-done((bf16[1408,128]{1,0:T(8,128)(2,1)S(1)}, bf16[1408,128]{1,0:T(8,128)(2,1)S(1)}, u32[]{:S(2)}, u32[]{:S(2)}) %collective-permute-start.5) | collective-permute-done | bytes 360480 | tf_op jit(solution)/shard_map/ppermute | solution.py:28
  34.7 2.0 %collective-permute-done.9 = bf16[704,128]{1,0:T(8,128)(2,1)S(1)} collective-permute-done((bf16[704,128]{1,0:T(8,128)(2,1)S(1)}, bf16[704,128]{1,0:T(8,128)(2,1)S(1)}, u32[]{:S(2)}, u32[]{:S(2)}) %collective-permute-start.9) | collective-permute-done | bytes 180256 | tf_op jit(solution)/shard_map/ppermute | solution.py:28
  36.8 4.3 %collective-permute-done.6 = bf16[704,128]{1,0:T(8,128)(2,1)S(1)} collective-permute-done((bf16[704,128]{1,0:T(8,128)(2,1)S(1)}, bf16[704,128]{1,0:T(8,128)(2,1)S(1)}, u32[]{:S(2)}, u32[]{:S(2)}) %collective-permute-start.6) | collective-permute-done | bytes 180256 | tf_op jit(solution)/shard_map/ppermute | solution.py:28
  41.2 2.0 %collective-permute-start.10 = (bf16[264,256]{1,0:T(8,128)(2,1)S(1)}, bf16[264,256]{1,0:T(8,128)(2,1)S(1)}, u32[]{:S(2)}, u32[]{:S(2)}) collective-permute-start(bf16[264,256]{1,0:T(8,128)(2,1)S(1)} %slice.77), channel_id=1, source_target_pairs={{0,56},{1,57},{2,58},{3,59},{4,60},{5,61},{6,62},{7,63},{8,16},{9,... | collective-permute-start | bytes 405512 | tf_op jit(solution)/shard_map/ppermute | solution.py:28
  43.2 4.0 %collective-permute-start.11 = (bf16[176,256]{1,0:T(8,128)(2,1)S(1)}, bf16[176,256]{1,0:T(8,128)(2,1)S(1)}, u32[]{:S(2)}, u32[]{:S(2)}) collective-permute-start(bf16[176,256]{1,0:T(8,128)(2,1)S(1)} %slice.79), channel_id=1, source_target_pairs={{0,8},{1,9},{2,10},{3,11},{4,12},{5,13},{6,14},{7,15},{8,0},{9,1},... | collective-permute-start | bytes 270344 | tf_op jit(solution)/shard_map/ppermute | solution.py:28
  47.2 3.0 %collective-permute-done.11 = bf16[176,256]{1,0:T(8,128)(2,1)S(1)} collective-permute-done((bf16[176,256]{1,0:T(8,128)(2,1)S(1)}, bf16[176,256]{1,0:T(8,128)(2,1)S(1)}, u32[]{:S(2)}, u32[]{:S(2)}) %collective-permute-start.11) | collective-permute-done | bytes 90144 | tf_op jit(solution)/shard_map/ppermute | solution.py:28
  50.3 3.0 %collective-permute-start.13 = (bf16[88,256]{1,0:T(8,128)(2,1)S(1)}, bf16[88,256]{1,0:T(8,128)(2,1)S(1)}, u32[]{:S(2)}, u32[]{:S(2)}) collective-permute-start(bf16[88,256]{1,0:T(8,128)(2,1)S(1)} %fusion.22), channel_id=1, source_target_pairs={{0,24},{1,25},{2,26},{3,27},{4,28},{5,29},{6,30},{7,31},{8,48},{9,... | collective-permute-start | bytes 135176 | tf_op jit(solution)/shard_map/ppermute | solution.py:28
  53.3 2.8 %collective-permute-start.12 = (bf16[88,256]{1,0:T(8,128)(2,1)S(1)}, bf16[88,256]{1,0:T(8,128)(2,1)S(1)}, u32[]{:S(2)}, u32[]{:S(2)}) collective-permute-start(bf16[88,256]{1,0:T(8,128)(2,1)S(1)} %slice.137), channel_id=1, source_target_pairs={{0,40},{1,41},{2,42},{3,43},{4,44},{5,45},{6,46},{7,47},{8,32},{9,... | collective-permute-start | bytes 135176 | tf_op jit(solution)/shard_map/ppermute | solution.py:28
  56.1 1.3 %collective-permute-done.13 = bf16[88,256]{1,0:T(8,128)(2,1)S(1)} collective-permute-done((bf16[88,256]{1,0:T(8,128)(2,1)S(1)}, bf16[88,256]{1,0:T(8,128)(2,1)S(1)}, u32[]{:S(2)}, u32[]{:S(2)}) %collective-permute-start.13) | collective-permute-done | bytes 45088 | tf_op jit(solution)/shard_map/ppermute | solution.py:28
  57.5 2.9 %collective-permute-done.12 = bf16[88,256]{1,0:T(8,128)(2,1)S(1)} collective-permute-done((bf16[88,256]{1,0:T(8,128)(2,1)S(1)}, bf16[88,256]{1,0:T(8,128)(2,1)S(1)}, u32[]{:S(2)}, u32[]{:S(2)}) %collective-permute-start.12) | collective-permute-done | bytes 45088 | tf_op jit(solution)/shard_map/ppermute | solution.py:28
  60.7 1.2 %collective-permute-done.14 = f32[43,256]{1,0:T(8,128)S(1)} collective-permute-done((f32[43,256]{1,0:T(8,128)S(1)}, f32[43,256]{1,0:T(8,128)S(1)}, u32[]{:S(2)}, u32[]{:S(2)}) %collective-permute-start.14) | collective-permute-done | bytes 44064 | tf_op jit(solution)/shard_map/ppermute | solution.py:28
  62.1 1.2 %collective-permute-start.16 = (bf16[43,512]{1,0:T(8,128)(2,1)S(1)}, bf16[43,512]{1,0:T(8,128)(2,1)S(1)}, u32[]{:S(2)}, u32[]{:S(2)}) collective-permute-start(bf16[43,512]{1,0:T(8,128)(2,1)S(1)} %get-tuple-element.30), channel_id=1, source_target_pairs={{0,2},{1,3},{2,0},{3,1},{4,6},{5,7},{6,4},{7,5},{8,10},{9,11},{10,... | collective-permute-start | bytes 132104 | tf_op jit(solution)/shard_map/ppermute | solution.py:28
  63.3 1.0 %collective-permute-start.17 = (bf16[43,512]{1,0:T(8,128)(2,1)S(1)}, bf16[43,512]{1,0:T(8,128)(2,1)S(1)}, u32[]{:S(2)}, u32[]{:S(2)}) collective-permute-start(bf16[43,512]{1,0:T(8,128)(2,1)S(1)} %get-tuple-element.30), channel_id=1, source_target_pairs={{0,3},{1,2},{2,1},{3,0},{4,7},{5,6},{6,5},{7,4},{8,11},{9,10},{10,... | collective-permute-start | bytes 132104 | tf_op jit(solution)/shard_map/ppermute | solution.py:28
  64.3 1.3 %collective-permute-start.15 = (bf16[43,512]{1,0:T(8,128)(2,1)S(1)}, bf16[43,512]{1,0:T(8,128)(2,1)S(1)}, u32[]{:S(2)}, u32[]{:S(2)}) collective-permute-start(bf16[43,512]{1,0:T(8,128)(2,1)S(1)} %get-tuple-element.30), channel_id=1, source_target_pairs={{0,1},{1,0},{2,3},{3,2},{4,5},{5,4},{6,7},{7,6},{8,9},{9,8},{10,11... | collective-permute-start | bytes 132104 | tf_op jit(solution)/shard_map/ppermute | solution.py:28
  (62 shorter events, 11.0 us)
Async XLA Ops:
  0.6 1.2 %copy-start = (bf16[1,1024,512]{2,1,0:T(8,128)(2,1)S(1)}, bf16[1,1024,512]{2,1,0:T(8,128)(2,1)}, u32[]{:S(2)}) copy-start(bf16[1,1024,512]{2,1,0:T(8,128)(2,1)} %param.9) | copy-start | bytes 3145732
  0.6 3.5 %copy-start.2 = (bf16[1,256,1024]{2,1,0:T(8,128)(2,1)S(1)}, bf16[1,256,1024]{2,1,0:T(8,128)(2,1)}, u32[]{:S(2)}) copy-start(bf16[1,256,1024]{2,1,0:T(8,128)(2,1)} %param.7) | copy-start | bytes 1572868
  0.7 12.6 %collective-permute-start.3 = (bf16[2752,256]{1,0:T(8,128)(2,1)}, bf16[2752,256]{1,0:T(8,128)(2,1)}, u32[]{:S(2)}, u32[]{:S(2)}) collective-permute-start(bf16[2752,256]{1,0:T(8,128)(2,1)} %bitcast.48), channel_id=1, source_target_pairs={{0,4},{1,5},{2,6},{3,7},{4,0},{5,1},{6,2},{7,3},{8,12},{9,13},{10,... | collective-permute-start | bytes 4227080 | tf_op jit(solution)/shard_map/ppermute | solution.py:28
  3.2 4.8 %copy-start.5 = (s32[8]{0:T(128)S(1)}, s32[8]{0:T(128)}, u32[]{:S(2)}) copy-start(s32[8]{0:T(128)} %constant.54.clone) | copy-start | bytes 100
  3.2 1.4 %collective-permute-start = (bf16[256,256]{1,0:T(8,128)(2,1)S(1)}, bf16[256,256]{1,0:T(8,128)(2,1)S(1)}, u32[]{:S(2)}, u32[]{:S(2)}) collective-permute-start(bf16[256,256]{1,0:T(8,128)(2,1)S(1)} %fusion.1), channel_id=1, source_target_pairs={{0,4},{1,5},{2,6},{3,7},{4,0},{5,1},{6,2},{7,3},{8,12},{9,13},{10,... | collective-permute-start | bytes 393224 | tf_op jit(solution)/shard_map/ppermute | solution.py:28
  4.7 10.5 %copy-start.1 = (bf16[1,256,2752]{1,2,0:T(8,128)(2,1)S(1)}, bf16[1,256,2752]{1,2,0:T(8,128)(2,1)}, u32[]{:S(2)}) copy-start(bf16[1,256,2752]{1,2,0:T(8,128)(2,1)} %param.8) | copy-start | bytes 4227076
  4.7 7.0 %collective-permute-start.2 = (bf16[512,128]{1,0:T(8,128)(2,1)S(1)}, bf16[512,128]{1,0:T(8,128)(2,1)S(1)}, u32[]{:S(2)}, u32[]{:S(2)}) collective-permute-start(bf16[512,128]{1,0:T(8,128)(2,1)S(1)} %get-tuple-element.35), channel_id=1, source_target_pairs={{0,3},{1,2},{2,1},{3,0},{4,7},{5,6},{6,5},{7,4},{8,11},{9,10},{10,... | collective-permute-start | bytes 393224 | tf_op jit(solution)/shard_map/ppermute | solution.py:28
  7.8 5.4 %collective-permute-start.1 = (bf16[512,128]{1,0:T(8,128)(2,1)S(1)}, bf16[512,128]{1,0:T(8,128)(2,1)S(1)}, u32[]{:S(2)}, u32[]{:S(2)}) collective-permute-start(bf16[512,128]{1,0:T(8,128)(2,1)S(1)} %get-tuple-element.36), channel_id=1, source_target_pairs={{0,1},{1,0},{2,3},{3,2},{4,5},{5,4},{6,7},{7,6},{8,9},{9,8},{10,11... | collective-permute-start | bytes 393224 | tf_op jit(solution)/shard_map/ppermute | solution.py:28
  13.3 6.3 %collective-permute-start.4 = (bf16[512,128]{1,0:T(8,128)(2,1)S(1)}, bf16[512,128]{1,0:T(8,128)(2,1)S(1)}, u32[]{:S(2)}, u32[]{:S(2)}) collective-permute-start(bf16[512,128]{1,0:T(8,128)(2,1)S(1)} %convert_element_type.89), channel_id=1, source_target_pairs={{0,3},{1,2},{2,1},{3,0},{4,7},{5,6},{6,5},{7,4},{8,11},{9,10},{10,... | collective-permute-start | bytes 393224 | tf_op jit(solution)/shard_map/ppermute | solution.py:28
  15.1 5.1 %collective-permute-start.7 = (bf16[512,128]{1,0:T(8,128)(2,1)S(1)}, bf16[512,128]{1,0:T(8,128)(2,1)S(1)}, u32[]{:S(2)}, u32[]{:S(2)}) collective-permute-start(bf16[512,128]{1,0:T(8,128)(2,1)S(1)} %convert_element_type.95), channel_id=1, source_target_pairs={{0,1},{1,0},{2,3},{3,2},{4,5},{5,4},{6,7},{7,6},{8,9},{9,8},{10,11... | collective-permute-start | bytes 393224 | tf_op jit(solution)/shard_map/ppermute | solution.py:28
  20.7 9.9 %collective-permute-start.8 = (bf16[1408,128]{1,0:T(8,128)(2,1)S(1)}, bf16[1408,128]{1,0:T(8,128)(2,1)S(1)}, u32[]{:S(2)}, u32[]{:S(2)}) collective-permute-start(bf16[1408,128]{1,0:T(8,128)(2,1)S(1)} %convolution_convert_fusion), channel_id=1, source_target_pairs={{0,192},{1,193},{2,194},{3,195},{4,196},{5,197},{6,198},{7,199},{8... | collective-permute-start | bytes 1081352 | tf_op jit(solution)/shard_map/ppermute | solution.py:28
  24.1 9.6 %collective-permute-start.5 = (bf16[1408,128]{1,0:T(8,128)(2,1)S(1)}, bf16[1408,128]{1,0:T(8,128)(2,1)S(1)}, u32[]{:S(2)}, u32[]{:S(2)}) collective-permute-start(bf16[1408,128]{1,0:T(8,128)(2,1)S(1)} %convolution_convert_fusion.1), channel_id=1, source_target_pairs={{0,64},{1,65},{2,66},{3,67},{4,68},{5,69},{6,70},{7,71},{8,72},{9,... | collective-permute-start | bytes 1081352 | tf_op jit(solution)/shard_map/ppermute | solution.py:28
  31.2 5.6 %collective-permute-start.9 = (bf16[704,128]{1,0:T(8,128)(2,1)S(1)}, bf16[704,128]{1,0:T(8,128)(2,1)S(1)}, u32[]{:S(2)}, u32[]{:S(2)}) collective-permute-start(bf16[704,128]{1,0:T(8,128)(2,1)S(1)} %slice.135), channel_id=1, source_target_pairs={{0,64},{1,65},{2,66},{3,67},{4,68},{5,69},{6,70},{7,71},{8,72},{9,... | collective-permute-start | bytes 540680 | tf_op jit(solution)/shard_map/ppermute | solution.py:28
  34.3 6.8 %collective-permute-start.6 = (bf16[704,128]{1,0:T(8,128)(2,1)S(1)}, bf16[704,128]{1,0:T(8,128)(2,1)S(1)}, u32[]{:S(2)}, u32[]{:S(2)}) collective-permute-start(bf16[704,128]{1,0:T(8,128)(2,1)S(1)} %slice.136), channel_id=1, source_target_pairs={{0,192},{1,193},{2,194},{3,195},{4,196},{5,197},{6,198},{7,199},{8... | collective-permute-start | bytes 540680 | tf_op jit(solution)/shard_map/ppermute | solution.py:28
  41.1 20.8 %copy-start.3 = (f32[1,43,512]{2,0,1:T(1,128)S(1)}, f32[1,43,512]{2,0,1:T(1,128)}, u32[]{:S(2)}) copy-start(f32[1,43,512]{2,0,1:T(1,128)} %param.11) | copy-start | bytes 264196
  41.2 20.8 %copy-start.4 = (f32[1,43,512]{2,0,1:T(1,128)S(1)}, f32[1,43,512]{2,0,1:T(1,128)}, u32[]{:S(2)}) copy-start(f32[1,43,512]{2,0,1:T(1,128)} %param.10) | copy-start | bytes 264196
  41.2 9.1 %collective-permute-start.10 = (bf16[264,256]{1,0:T(8,128)(2,1)S(1)}, bf16[264,256]{1,0:T(8,128)(2,1)S(1)}, u32[]{:S(2)}, u32[]{:S(2)}) collective-permute-start(bf16[264,256]{1,0:T(8,128)(2,1)S(1)} %slice.77), channel_id=1, source_target_pairs={{0,56},{1,57},{2,58},{3,59},{4,60},{5,61},{6,62},{7,63},{8,16},{9,... | collective-permute-start | bytes 405512 | tf_op jit(solution)/shard_map/ppermute | solution.py:28
  43.2 7.0 %collective-permute-start.11 = (bf16[176,256]{1,0:T(8,128)(2,1)S(1)}, bf16[176,256]{1,0:T(8,128)(2,1)S(1)}, u32[]{:S(2)}, u32[]{:S(2)}) collective-permute-start(bf16[176,256]{1,0:T(8,128)(2,1)S(1)} %slice.79), channel_id=1, source_target_pairs={{0,8},{1,9},{2,10},{3,11},{4,12},{5,13},{6,14},{7,15},{8,0},{9,1},... | collective-permute-start | bytes 270344 | tf_op jit(solution)/shard_map/ppermute | solution.py:28
  50.3 7.1 %collective-permute-start.13 = (bf16[88,256]{1,0:T(8,128)(2,1)S(1)}, bf16[88,256]{1,0:T(8,128)(2,1)S(1)}, u32[]{:S(2)}, u32[]{:S(2)}) collective-permute-start(bf16[88,256]{1,0:T(8,128)(2,1)S(1)} %fusion.22), channel_id=1, source_target_pairs={{0,24},{1,25},{2,26},{3,27},{4,28},{5,29},{6,30},{7,31},{8,48},{9,... | collective-permute-start | bytes 135176 | tf_op jit(solution)/shard_map/ppermute | solution.py:28
  53.3 7.1 %collective-permute-start.12 = (bf16[88,256]{1,0:T(8,128)(2,1)S(1)}, bf16[88,256]{1,0:T(8,128)(2,1)S(1)}, u32[]{:S(2)}, u32[]{:S(2)}) collective-permute-start(bf16[88,256]{1,0:T(8,128)(2,1)S(1)} %slice.137), channel_id=1, source_target_pairs={{0,40},{1,41},{2,42},{3,43},{4,44},{5,45},{6,46},{7,47},{8,32},{9,... | collective-permute-start | bytes 135176 | tf_op jit(solution)/shard_map/ppermute | solution.py:28
  60.4 1.5 %collective-permute-start.14 = (f32[43,256]{1,0:T(8,128)S(1)}, f32[43,256]{1,0:T(8,128)S(1)}, u32[]{:S(2)}, u32[]{:S(2)}) collective-permute-start(f32[43,256]{1,0:T(8,128)S(1)} %slice_select_fusion), channel_id=1, source_target_pairs={{0,4},{1,5},{2,6},{3,7},{4,0},{5,1},{6,2},{7,3},{8,12},{9,13},{10,... | collective-permute-start | bytes 132104 | tf_op jit(solution)/shard_map/ppermute | solution.py:28
  62.1 5.8 %collective-permute-start.16 = (bf16[43,512]{1,0:T(8,128)(2,1)S(1)}, bf16[43,512]{1,0:T(8,128)(2,1)S(1)}, u32[]{:S(2)}, u32[]{:S(2)}) collective-permute-start(bf16[43,512]{1,0:T(8,128)(2,1)S(1)} %get-tuple-element.30), channel_id=1, source_target_pairs={{0,2},{1,3},{2,0},{3,1},{4,6},{5,7},{6,4},{7,5},{8,10},{9,11},{10,... | collective-permute-start | bytes 132104 | tf_op jit(solution)/shard_map/ppermute | solution.py:28
  63.3 5.3 %collective-permute-start.17 = (bf16[43,512]{1,0:T(8,128)(2,1)S(1)}, bf16[43,512]{1,0:T(8,128)(2,1)S(1)}, u32[]{:S(2)}, u32[]{:S(2)}) collective-permute-start(bf16[43,512]{1,0:T(8,128)(2,1)S(1)} %get-tuple-element.30), channel_id=1, source_target_pairs={{0,3},{1,2},{2,1},{3,0},{4,7},{5,6},{6,5},{7,4},{8,11},{9,10},{10,... | collective-permute-start | bytes 132104 | tf_op jit(solution)/shard_map/ppermute | solution.py:28
  64.3 4.3 %collective-permute-start.15 = (bf16[43,512]{1,0:T(8,128)(2,1)S(1)}, bf16[43,512]{1,0:T(8,128)(2,1)S(1)}, u32[]{:S(2)}, u32[]{:S(2)}) collective-permute-start(bf16[43,512]{1,0:T(8,128)(2,1)S(1)} %get-tuple-element.30), channel_id=1, source_target_pairs={{0,1},{1,0},{2,3},{3,2},{4,5},{5,4},{6,7},{7,6},{8,9},{9,8},{10,11... | collective-permute-start | bytes 132104 | tf_op jit(solution)/shard_map/ppermute | solution.py:28

commit v7 on v6

--- a/solution.py
+++ b/solution.py
@@ -14,8 +14,8 @@
 
 Z_ORDER = (-2, 1, -4, -1, 2, 3, 0, -3)
 FIRST, SECOND = 2 * PADDED, 5 * PADDED
-X_ORDER = ((2, 1, 3, 0), (2, 3, 1, 0))
-PAIRS = ((1, 3), (3, 1))
+X_ORDER = (1, 2, 3, 0)
+Y_PAIRS = ((1, 3), (3, 1))
 
 
 def send(value, move):
@@ -58,23 +58,24 @@
                 fill = jnp.zeros((PADDED - piece.shape[0], tokens), F32)
                 piece = jnp.concatenate([piece, fill], axis=0)
             blocks[n, :, s * tokens : (s + 1) * tokens] = piece
-    half = NX * NZ // 2
-    for k, out in enumerate(outs):
-        for i in range(0, half, 2):
-            pair = [blocks[order_ref[k * half + i + j]] for j in range(2)]
-            out[i * PADDED : (i + 2) * PADDED, :] = jnp.concatenate(pair, axis=0).astype(BF)
+    k = 0
+    for out in outs:
+        for i in range(0, out.shape[0], 2 * PADDED):
+            pair = [blocks[order_ref[k + j]] for j in range(2)]
+            out[i : i + 2 * PADDED, :] = jnp.concatenate(pair, axis=0).astype(BF)
+            k += 2
 
 
 def arrange(order, own, came):
     tokens = own.shape[1]
-    shape = jax.ShapeDtypeStruct((NX * NZ // 2 * PADDED, NCORE * tokens), BF)
+    sizes = [NZ * PADDED] * NX + [NX * n for n in (FIRST, SECOND - FIRST, SECOND - FIRST)]
     vmem = pl.BlockSpec(memory_space=pltpu.VMEM)
     smem = pl.BlockSpec(memory_space=pltpu.SMEM)
     return pl.pallas_call(
         arrange_kernel,
-        out_shape=[shape] * 2 * CHUNKS,
+        out_shape=[jax.ShapeDtypeStruct((n, NCORE * tokens), BF) for n in sizes],
         in_specs=[smem, vmem, vmem],
-        out_specs=[vmem] * 2 * CHUNKS,
+        out_specs=[vmem] * len(sizes),
         scratch_shapes=[pltpu.VMEM((NX * NZ, PADDED, NCORE * tokens), F32)],
         compiler_params=pltpu.CompilerParams(vmem_limit_bytes=20 * 1024 * 1024),
         cost_estimate=pl.CostEstimate(flops=0, bytes_accessed=8 * 1024 * 1024, transcendentals=0),
@@ -97,8 +98,10 @@
     other_columns = swap_core(columns)
     up = 1 - 2 * (z & 1)
     blocks_z = (z + up * jnp.array(Z_ORDER, jnp.int32)) & (NZ - 1)
-    blocks_x = x ^ jnp.array(X_ORDER, jnp.int32).reshape(-1)
-    order = (blocks_x[:, None] * NZ + blocks_z[None, :]).reshape(-1)
+    blocks_x = (x ^ jnp.array(X_ORDER, jnp.int32))[:, None] * NZ
+    order = blocks_x + blocks_z[None, :]
+    order = [order] + [order[:, i:j] for i, j in ((0, 2), (2, 5), (5, 8))]
+    order = jnp.concatenate([part.reshape(-1) for part in order])
 
     def lanes_of(c):
         return lax.dynamic_slice(basis[0], (0, c * lanes), (basis.shape[1], lanes))
@@ -107,25 +110,38 @@
     partial = jnp.concatenate([dot(features[0], lanes_of(core)), theirs.astype(F32)], axis=0)
     width = lanes // CHUNKS
     chunks = [partial[:, c * width : (c + 1) * width] for c in range(CHUNKS)]
-    chunks = [p + swap_y(p.astype(BF), m[0]).astype(F32) for p, m in zip(chunks, PAIRS)]
+    chunks = [p + swap_y(p.astype(BF), m[0]).astype(F32) for p, m in zip(chunks, Y_PAIRS)]
     chunks, other_columns = lax.optimization_barrier((chunks, other_columns))
     parts = arrange(order, columns, other_columns)
-    chunks = [p + swap_y(p.astype(BF), m[1]).astype(F32) for p, m in zip(chunks, PAIRS)]
+    chunks = [p + swap_y(p.astype(BF), m[1]).astype(F32) for p, m in zip(chunks, Y_PAIRS)]
     chunks = [p.astype(BF) for p in chunks]
     chunks[0], parts = lax.optimization_barrier((chunks[0], parts))
 
-    rows = NZ * PADDED
-    terms = []
-    for c, (projected, m) in enumerate(zip(chunks, PAIRS)):
-        came = swap_x(dot(parts[2 * c], projected).astype(BF), m[0])
-        term = dot(parts[2 * c + 1], projected) + came.astype(F32)
-        terms.append(term[rows:] + swap_x(term[:rows].astype(BF), m[1]).astype(F32))
-    term = jnp.concatenate(terms, axis=1)
-    came = swap_z(term[:FIRST].astype(BF), 1).astype(F32)
-    more = swap_z(term[FIRST:SECOND].astype(BF), -1).astype(F32)
-    keep = term[SECOND:] + more
+    def send_x(sent):
+        return [swap_x(value.astype(BF), m) for value, m in zip(sent, X_ORDER)]
+
+    def send_z(first, second):
+        return [swap_z(first.astype(BF), 1), swap_z(second.astype(BF), -1)]
+
+    def add_x(keep, came):
+        return keep + came[0].astype(F32) + came[1].astype(F32) + came[2].astype(F32)
+
+    def add_z(keep, came):
+        keep = (keep + came[1].astype(F32)).reshape(-1, SECOND - FIRST, width)
+        first = came[0].astype(F32).reshape(-1, FIRST, width)
+        return jnp.concatenate([keep[:, :FIRST] + first, keep[:, FIRST:]], axis=1)
+
+    came_x = send_x([dot(part, chunks[0]) for part in parts[:3]])
+    came_z = send_z(dot(parts[4], chunks[1]), dot(parts[5], chunks[1]))
+    came_x, came_z = lax.optimization_barrier((came_x, came_z))
+    a = add_x(dot(parts[3], chunks[0]), came_x)
+    b = add_z(dot(parts[6], chunks[1]), came_z)
+    came_z = send_z(a[:FIRST], a[FIRST:SECOND])
+    came_x = send_x([b[0], b[1], b[2]])
+    a = add_z(a[SECOND:], came_z)[0]
+    b = add_x(b[3], came_x)
+    keep = jnp.concatenate([a, b], axis=1)
     hub_a, own, hub_b = keep[:PADDED], keep[PADDED:FIRST], keep[FIRST:]
-    hub_a, own = hub_a + came[:PADDED], own + came[PADDED:]
     came = swap_z(hub_a.astype(BF), 3).astype(F32)
     own = own + swap_z(hub_b.astype(BF), -3).astype(F32) + came
     mine, other = own[:OWNED], own[OWNED:CHIP]

time: 71.3 us -> 71.4 us (level); the launches traced: 70.1 us -> 71.2 us
  starting transfers between devices: 24.8 us -> 31 us
  waiting for transfers between devices: 32.6 us -> 27.2 us
    ppermute x18 -> x22, starting transfers between devices: 24.8 us -> 31 us  [send(): return lax.ppermute(value, ('dp', 'tensor'), pairs)]
    ppermute x18 -> x22, waiting for transfers between devices: 32.6 us -> 27.2 us  [send(): return lax.ppermute(value, ('dp', 'tensor'), pairs)]
    dot_general x6 -> x9, matrix products: 3.82 us -> 4.27 us  [dot(): lax.dot_general(a, b, (((1,), (0,)), ((), ())), preferred_element_type=F32)]
    unnamed x15 -> x17, local copies, waits for them, and re-layouts: 3.6 us -> 3.59 us
  transfers between devices with their start and end apart: 18 -> 22, of which waited for: 15 -> 14; matrix products, arithmetic and copies ran while one was open for 8% -> 9% of each run, Pallas kernels for 3% -> 3%
where the time goes in v7:
time: 71.4 us; the launch traced here: 71.2 us
  starting transfers between devices  31 us (43%)
  waiting for transfers between devices  27.2 us (38%)
  matrix products  4.77 us (7%)
  local copies, waits for them, and re-layouts  4.04 us (6%)
  Pallas kernels  2.39 us (3%)
  between operations  1.06 us (1%)
  other arithmetic  0.77 us (1%)
    ppermute x22, starting transfers between devices, send(): return lax.ppermute(value, ('dp', 'tensor'), pairs)  31 us
    ppermute x22, waiting for transfers between devices, send(): return lax.ppermute(value, ('dp', 'tensor'), pairs)  27.2 us
    dot_general x9, matrix products, dot(): lax.dot_general(a, b, (((1,), (0,)), ((), ())), preferred_element_type=F32)  4.27 us
    unnamed x17, local copies, waits for them, and re-layouts  3.59 us
    pallas_call x1, Pallas kernels, arrange(): pl.pallas_call(arrange_kernel, out_shape=[jax.ShapeDtypeStruct((n, NCORE...  2.39 us
  transfers between devices with their start and end apart: 22, of which 14 were waited for; matrix products, arithmetic and copies ran while one was open for 9% of the time, Pallas kernels for 3%

profile of v7, /device:TPU:32, one launch (start us, length us, event | category | flops | bytes accessed | tf_op | source)
XLA Modules:
  0.0 71.2 jit_solution(5490957479227888170)
XLA Ops:
  1.9 1.4 %fusion.1 = bf16[256,256]{1,0:T(8,128)(2,1)S(1)} fusion(bf16[1,256,1024]{2,1,0:T(8,128)(2,1)} %param.7, bf16[1,1024,512]{2,1,0:T(8,128)(2,1)S(1)} %copy-done, s32[]{:T(128)S(6)} %select_n.136), kind=kOutput, calls=%fused_computation.10 | convolution fusion | flops 134283264 | bytes 1179652 | tf_op jit(solution)/shard_map/dot_general | solution.py:86
  4.7 3.1 %collective-permute-start.2 = (bf16[512,128]{1,0:T(8,128)(2,1)S(1)}, bf16[512,128]{1,0:T(8,128)(2,1)S(1)}, u32[]{:S(2)}, u32[]{:S(2)}) collective-permute-start(bf16[512,128]{1,0:T(8,128)(2,1)S(1)} %get-tuple-element.62), channel_id=1, source_target_pairs={{0,3},{1,2},{2,1},{3,0},{4,7},{5,6},{6,5},{7,4},{8,11},{9,10},{10,... | collective-permute-start | bytes 393224 | tf_op jit(solution)/shard_map/ppermute | solution.py:28
  8.1 3.6 %collective-permute-done.2 = bf16[512,128]{1,0:T(8,128)(2,1)S(1)} collective-permute-done((bf16[512,128]{1,0:T(8,128)(2,1)S(1)}, bf16[512,128]{1,0:T(8,128)(2,1)S(1)}, u32[]{:S(2)}, u32[]{:S(2)}) %collective-permute-start.2) | collective-permute-done | bytes 131104 | tf_op jit(solution)/shard_map/ppermute | solution.py:28
  11.7 1.5 %collective-permute-done.1 = bf16[512,128]{1,0:T(8,128)(2,1)S(1)} collective-permute-done((bf16[512,128]{1,0:T(8,128)(2,1)S(1)}, bf16[512,128]{1,0:T(8,128)(2,1)S(1)}, u32[]{:S(2)}, u32[]{:S(2)}) %collective-permute-start.1) | collective-permute-done | bytes 131104 | tf_op jit(solution)/shard_map/ppermute | solution.py:28
  13.2 1.6 %collective-permute-start.4 = (bf16[512,128]{1,0:T(8,128)(2,1)S(1)}, bf16[512,128]{1,0:T(8,128)(2,1)S(1)}, u32[]{:S(2)}, u32[]{:S(2)}) collective-permute-start(bf16[512,128]{1,0:T(8,128)(2,1)S(1)} %convert_element_type.114), channel_id=1, source_target_pairs={{0,3},{1,2},{2,1},{3,0},{4,7},{5,6},{6,5},{7,4},{8,11},{9,10},{10,... | collective-permute-start | bytes 393224 | tf_op jit(solution)/shard_map/ppermute | solution.py:28
  15.4 2.4 %shard_map.94 = (bf16[704,512]{1,0:T(8,128)(2,1)S(1)}, bf16[704,512]{1,0:T(8,128)(2,1)S(1)}, bf16[704,512]{1,0:T(8,128)(2,1)S(1)}, bf16[704,512]{1,0:T(8,128)(2,...) custom-call(s32[64]{0:T(128)S(1)} %pad_add_fusion.order_ref, ...), custom_call_target="tpu_custom_call" | custom-call | bytes 8388608 | tf_op jit(solution)/shard_map/pallas_call | solution.py:74
  17.8 1.7 %collective-permute-done.4 = bf16[512,128]{1,0:T(8,128)(2,1)S(1)} collective-permute-done((bf16[512,128]{1,0:T(8,128)(2,1)S(1)}, bf16[512,128]{1,0:T(8,128)(2,1)S(1)}, u32[]{:S(2)}, u32[]{:S(2)}) %collective-permute-start.4) | collective-permute-done | bytes 131104 | tf_op jit(solution)/shard_map/ppermute | solution.py:28
  21.0 2.0 %collective-permute-start.10 = (bf16[1056,128]{1,0:T(8,128)(2,1)S(1)}, bf16[1056,128]{1,0:T(8,128)(2,1)S(1)}, u32[]{:S(2)}, u32[]{:S(2)}) collective-permute-start(bf16[1056,128]{1,0:T(8,128)(2,1)S(1)} %convolution_convert_fusion), channel_id=1, source_target_pairs={{0,56},{1,57},{2,58},{3,59},{4,60},{5,61},{6,62},{7,63},{8,16},{9,... | collective-permute-start | bytes 811016 | tf_op jit(solution)/shard_map/ppermute | solution.py:28
  23.4 4.1 %collective-permute-start.9 = (bf16[704,128]{1,0:T(8,128)(2,1)S(1)}, bf16[704,128]{1,0:T(8,128)(2,1)S(1)}, u32[]{:S(2)}, u32[]{:S(2)}) collective-permute-start(bf16[704,128]{1,0:T(8,128)(2,1)S(1)} %convolution_convert_fusion.2), channel_id=1, source_target_pairs={{0,8},{1,9},{2,10},{3,11},{4,12},{5,13},{6,14},{7,15},{8,0},{9,1},... | collective-permute-start | bytes 540680 | tf_op jit(solution)/shard_map/ppermute | solution.py:28
  27.5 2.8 %collective-permute-start.7 = (bf16[704,128]{1,0:T(8,128)(2,1)S(1)}, bf16[704,128]{1,0:T(8,128)(2,1)S(1)}, u32[]{:S(2)}, u32[]{:S(2)}) collective-permute-start(bf16[704,128]{1,0:T(8,128)(2,1)S(1)} %convolution_convert_fusion.3), channel_id=1, source_target_pairs={{0,192},{1,193},{2,194},{3,195},{4,196},{5,197},{6,198},{7,199},{8... | collective-permute-start | bytes 540680 | tf_op jit(solution)/shard_map/ppermute | solution.py:28
  32.0 3.5 %collective-permute-done.7 = bf16[704,128]{1,0:T(8,128)(2,1)S(1)} collective-permute-done((bf16[704,128]{1,0:T(8,128)(2,1)S(1)}, bf16[704,128]{1,0:T(8,128)(2,1)S(1)}, u32[]{:S(2)}, u32[]{:S(2)}) %collective-permute-start.7) | collective-permute-done | bytes 180256 | tf_op jit(solution)/shard_map/ppermute | solution.py:28
  35.5 1.8 %collective-permute-done.6 = bf16[704,128]{1,0:T(8,128)(2,1)S(1)} collective-permute-done((bf16[704,128]{1,0:T(8,128)(2,1)S(1)}, bf16[704,128]{1,0:T(8,128)(2,1)S(1)}, u32[]{:S(2)}, u32[]{:S(2)}) %collective-permute-start.6) | collective-permute-done | bytes 180256 | tf_op jit(solution)/shard_map/ppermute | solution.py:28
  39.5 1.4 %collective-permute-start.13 = (bf16[264,128]{1,0:T(8,128)(2,1)S(1)}, bf16[264,128]{1,0:T(8,128)(2,1)S(1)}, u32[]{:S(2)}, u32[]{:S(2)}) collective-permute-start(bf16[264,128]{1,0:T(8,128)(2,1)S(1)} %get-tuple-element.64), channel_id=1, source_target_pairs={{0,64},{1,65},{2,66},{3,67},{4,68},{5,69},{6,70},{7,71},{8,72},{9,... | collective-permute-start | bytes 202760 | tf_op jit(solution)/shard_map/ppermute | solution.py:28
  40.9 2.0 %collective-permute-start.15 = (bf16[264,128]{1,0:T(8,128)(2,1)S(1)}, bf16[264,128]{1,0:T(8,128)(2,1)S(1)}, u32[]{:S(2)}, u32[]{:S(2)}) collective-permute-start(bf16[264,128]{1,0:T(8,128)(2,1)S(1)} %get-tuple-element.65), channel_id=1, source_target_pairs={{0,192},{1,193},{2,194},{3,195},{4,196},{5,197},{6,198},{7,199},{8... | collective-permute-start | bytes 202760 | tf_op jit(solution)/shard_map/ppermute | solution.py:28
  43.8 2.5 %collective-permute-done.15 = bf16[264,128]{1,0:T(8,128)(2,1)S(1)} collective-permute-done((bf16[264,128]{1,0:T(8,128)(2,1)S(1)}, bf16[264,128]{1,0:T(8,128)(2,1)S(1)}, u32[]{:S(2)}, u32[]{:S(2)}) %collective-permute-start.15) | collective-permute-done | bytes 67616 | tf_op jit(solution)/shard_map/ppermute | solution.py:28
  46.4 2.3 %collective-permute-done.14 = bf16[264,128]{1,0:T(8,128)(2,1)S(1)} collective-permute-done((bf16[264,128]{1,0:T(8,128)(2,1)S(1)}, bf16[264,128]{1,0:T(8,128)(2,1)S(1)}, u32[]{:S(2)}, u32[]{:S(2)}) %collective-permute-start.14) | collective-permute-done | bytes 67616 | tf_op jit(solution)/shard_map/ppermute | solution.py:28
  48.8 3.8 %collective-permute-start.16 = (bf16[88,256]{1,0:T(8,128)(2,1)S(1)}, bf16[88,256]{1,0:T(8,128)(2,1)S(1)}, u32[]{:S(2)}, u32[]{:S(2)}) collective-permute-start(bf16[88,256]{1,0:T(8,128)(2,1)S(1)} %get-tuple-element.73), channel_id=1, source_target_pairs={{0,40},{1,41},{2,42},{3,43},{4,44},{5,45},{6,46},{7,47},{8,32},{9,... | collective-permute-start | bytes 135176 | tf_op jit(solution)/shard_map/ppermute | solution.py:28
  52.6 1.3 %collective-permute-start.17 = (bf16[88,256]{1,0:T(8,128)(2,1)S(1)}, bf16[88,256]{1,0:T(8,128)(2,1)S(1)}, u32[]{:S(2)}, u32[]{:S(2)}) collective-permute-start(bf16[88,256]{1,0:T(8,128)(2,1)S(1)} %get-tuple-element.74), channel_id=1, source_target_pairs={{0,24},{1,25},{2,26},{3,27},{4,28},{5,29},{6,30},{7,31},{8,48},{9,... | collective-permute-start | bytes 135176 | tf_op jit(solution)/shard_map/ppermute | solution.py:28
  53.9 2.1 %collective-permute-done.16 = bf16[88,256]{1,0:T(8,128)(2,1)S(1)} collective-permute-done((bf16[88,256]{1,0:T(8,128)(2,1)S(1)}, bf16[88,256]{1,0:T(8,128)(2,1)S(1)}, u32[]{:S(2)}, u32[]{:S(2)}) %collective-permute-start.16) | collective-permute-done | bytes 45088 | tf_op jit(solution)/shard_map/ppermute | solution.py:28
  56.0 3.7 %collective-permute-done.17 = bf16[88,256]{1,0:T(8,128)(2,1)S(1)} collective-permute-done((bf16[88,256]{1,0:T(8,128)(2,1)S(1)}, bf16[88,256]{1,0:T(8,128)(2,1)S(1)}, u32[]{:S(2)}, u32[]{:S(2)}) %collective-permute-start.17) | collective-permute-done | bytes 45088 | tf_op jit(solution)/shard_map/ppermute | solution.py:28
  61.1 1.3 %collective-permute-start.19 = (bf16[43,512]{1,0:T(8,128)(2,1)S(1)}, bf16[43,512]{1,0:T(8,128)(2,1)S(1)}, u32[]{:S(2)}, u32[]{:S(2)}) collective-permute-start(bf16[43,512]{1,0:T(8,128)(2,1)S(1)} %get-tuple-element.55), channel_id=1, source_target_pairs={{0,1},{1,0},{2,3},{3,2},{4,5},{5,4},{6,7},{7,6},{8,9},{9,8},{10,11... | collective-permute-start | bytes 132104 | tf_op jit(solution)/shard_map/ppermute | solution.py:28
  62.4 2.0 %collective-permute-start.20 = (bf16[43,512]{1,0:T(8,128)(2,1)S(1)}, bf16[43,512]{1,0:T(8,128)(2,1)S(1)}, u32[]{:S(2)}, u32[]{:S(2)}) collective-permute-start(bf16[43,512]{1,0:T(8,128)(2,1)S(1)} %get-tuple-element.55), channel_id=1, source_target_pairs={{0,2},{1,3},{2,0},{3,1},{4,6},{5,7},{6,4},{7,5},{8,10},{9,11},{10,... | collective-permute-start | bytes 132104 | tf_op jit(solution)/shard_map/ppermute | solution.py:28
  64.4 1.6 %collective-permute-start.21 = (bf16[43,512]{1,0:T(8,128)(2,1)S(1)}, bf16[43,512]{1,0:T(8,128)(2,1)S(1)}, u32[]{:S(2)}, u32[]{:S(2)}) collective-permute-start(bf16[43,512]{1,0:T(8,128)(2,1)S(1)} %get-tuple-element.55), channel_id=1, source_target_pairs={{0,3},{1,2},{2,1},{3,0},{4,7},{5,6},{6,5},{7,4},{8,11},{9,10},{10,... | collective-permute-start | bytes 132104 | tf_op jit(solution)/shard_map/ppermute | solution.py:28
  68.0 1.6 %collective-permute-done.21 = bf16[43,512]{1,0:T(8,128)(2,1)S(1)} collective-permute-done((bf16[43,512]{1,0:T(8,128)(2,1)S(1)}, bf16[43,512]{1,0:T(8,128)(2,1)S(1)}, u32[]{:S(2)}, u32[]{:S(2)}) %collective-permute-start.21) | collective-permute-done | bytes 44064 | tf_op jit(solution)/shard_map/ppermute | solution.py:28
  (83 shorter events, 15.2 us)
Async XLA Ops:
  0.7 12.5 %collective-permute-start.3 = (bf16[2752,256]{1,0:T(8,128)(2,1)}, bf16[2752,256]{1,0:T(8,128)(2,1)}, u32[]{:S(2)}, u32[]{:S(2)}) collective-permute-start(bf16[2752,256]{1,0:T(8,128)(2,1)} %bitcast.81), channel_id=1, source_target_pairs={{0,4},{1,5},{2,6},{3,7},{4,0},{5,1},{6,2},{7,3},{8,12},{9,13},{10,... | collective-permute-start | bytes 4227080 | tf_op jit(solution)/shard_map/ppermute | solution.py:28
  3.2 1.4 %collective-permute-start = (bf16[256,256]{1,0:T(8,128)(2,1)S(1)}, bf16[256,256]{1,0:T(8,128)(2,1)S(1)}, u32[]{:S(2)}, u32[]{:S(2)}) collective-permute-start(bf16[256,256]{1,0:T(8,128)(2,1)S(1)} %fusion.1), channel_id=1, source_target_pairs={{0,4},{1,5},{2,6},{3,7},{4,0},{5,1},{6,2},{7,3},{8,12},{9,13},{10,... | collective-permute-start | bytes 393224 | tf_op jit(solution)/shard_map/ppermute | solution.py:28
  4.7 6.9 %collective-permute-start.2 = (bf16[512,128]{1,0:T(8,128)(2,1)S(1)}, bf16[512,128]{1,0:T(8,128)(2,1)S(1)}, u32[]{:S(2)}, u32[]{:S(2)}) collective-permute-start(bf16[512,128]{1,0:T(8,128)(2,1)S(1)} %get-tuple-element.62), channel_id=1, source_target_pairs={{0,3},{1,2},{2,1},{3,0},{4,7},{5,6},{6,5},{7,4},{8,11},{9,10},{10,... | collective-permute-start | bytes 393224 | tf_op jit(solution)/shard_map/ppermute | solution.py:28
  7.8 5.3 %collective-permute-start.1 = (bf16[512,128]{1,0:T(8,128)(2,1)S(1)}, bf16[512,128]{1,0:T(8,128)(2,1)S(1)}, u32[]{:S(2)}, u32[]{:S(2)}) collective-permute-start(bf16[512,128]{1,0:T(8,128)(2,1)S(1)} %get-tuple-element.63), channel_id=1, source_target_pairs={{0,1},{1,0},{2,3},{3,2},{4,5},{5,4},{6,7},{7,6},{8,9},{9,8},{10,11... | collective-permute-start | bytes 393224 | tf_op jit(solution)/shard_map/ppermute | solution.py:28
  13.2 6.3 %collective-permute-start.4 = (bf16[512,128]{1,0:T(8,128)(2,1)S(1)}, bf16[512,128]{1,0:T(8,128)(2,1)S(1)}, u32[]{:S(2)}, u32[]{:S(2)}) collective-permute-start(bf16[512,128]{1,0:T(8,128)(2,1)S(1)} %convert_element_type.114), channel_id=1, source_target_pairs={{0,3},{1,2},{2,1},{3,0},{4,7},{5,6},{6,5},{7,4},{8,11},{9,10},{10,... | collective-permute-start | bytes 393224 | tf_op jit(solution)/shard_map/ppermute | solution.py:28
  15.3 5.3 %collective-permute-start.8 = (bf16[512,128]{1,0:T(8,128)(2,1)S(1)}, bf16[512,128]{1,0:T(8,128)(2,1)S(1)}, u32[]{:S(2)}, u32[]{:S(2)}) collective-permute-start(bf16[512,128]{1,0:T(8,128)(2,1)S(1)} %convert_element_type.120), channel_id=1, source_target_pairs={{0,1},{1,0},{2,3},{3,2},{4,5},{5,4},{6,7},{7,6},{8,9},{9,8},{10,11... | collective-permute-start | bytes 393224 | tf_op jit(solution)/shard_map/ppermute | solution.py:28
  21.0 16.3 %collective-permute-start.10 = (bf16[1056,128]{1,0:T(8,128)(2,1)S(1)}, bf16[1056,128]{1,0:T(8,128)(2,1)S(1)}, u32[]{:S(2)}, u32[]{:S(2)}) collective-permute-start(bf16[1056,128]{1,0:T(8,128)(2,1)S(1)} %convolution_convert_fusion), channel_id=1, source_target_pairs={{0,56},{1,57},{2,58},{3,59},{4,60},{5,61},{6,62},{7,63},{8,16},{9,... | collective-permute-start | bytes 811016 | tf_op jit(solution)/shard_map/ppermute | solution.py:28
  23.4 8.6 %collective-permute-start.9 = (bf16[704,128]{1,0:T(8,128)(2,1)S(1)}, bf16[704,128]{1,0:T(8,128)(2,1)S(1)}, u32[]{:S(2)}, u32[]{:S(2)}) collective-permute-start(bf16[704,128]{1,0:T(8,128)(2,1)S(1)} %convolution_convert_fusion.2), channel_id=1, source_target_pairs={{0,8},{1,9},{2,10},{3,11},{4,12},{5,13},{6,14},{7,15},{8,0},{9,1},... | collective-permute-start | bytes 540680 | tf_op jit(solution)/shard_map/ppermute | solution.py:28
  27.5 8.0 %collective-permute-start.7 = (bf16[704,128]{1,0:T(8,128)(2,1)S(1)}, bf16[704,128]{1,0:T(8,128)(2,1)S(1)}, u32[]{:S(2)}, u32[]{:S(2)}) collective-permute-start(bf16[704,128]{1,0:T(8,128)(2,1)S(1)} %convolution_convert_fusion.3), channel_id=1, source_target_pairs={{0,192},{1,193},{2,194},{3,195},{4,196},{5,197},{6,198},{7,199},{8... | collective-permute-start | bytes 540680 | tf_op jit(solution)/shard_map/ppermute | solution.py:28
  30.3 7.0 %collective-permute-start.6 = (bf16[704,128]{1,0:T(8,128)(2,1)S(1)}, bf16[704,128]{1,0:T(8,128)(2,1)S(1)}, u32[]{:S(2)}, u32[]{:S(2)}) collective-permute-start(bf16[704,128]{1,0:T(8,128)(2,1)S(1)} %convolution_convert_fusion.4), channel_id=1, source_target_pairs={{0,128},{1,129},{2,130},{3,131},{4,132},{5,133},{6,134},{7,135},{8... | collective-permute-start | bytes 540680 | tf_op jit(solution)/shard_map/ppermute | solution.py:28
  31.1 6.2 %collective-permute-start.5 = (bf16[704,128]{1,0:T(8,128)(2,1)S(1)}, bf16[704,128]{1,0:T(8,128)(2,1)S(1)}, u32[]{:S(2)}, u32[]{:S(2)}) collective-permute-start(bf16[704,128]{1,0:T(8,128)(2,1)S(1)} %convolution_convert_fusion.5), channel_id=1, source_target_pairs={{0,64},{1,65},{2,66},{3,67},{4,68},{5,69},{6,70},{7,71},{8,72},{9,... | collective-permute-start | bytes 540680 | tf_op jit(solution)/shard_map/ppermute | solution.py:28
  37.4 6.3 %collective-permute-start.12 = (bf16[176,128]{1,0:T(8,128)(2,1)S(1)}, bf16[176,128]{1,0:T(8,128)(2,1)S(1)}, u32[]{:S(2)}, u32[]{:S(2)}) collective-permute-start(bf16[176,128]{1,0:T(8,128)(2,1)S(1)} %slice.96), channel_id=1, source_target_pairs={{0,8},{1,9},{2,10},{3,11},{4,12},{5,13},{6,14},{7,15},{8,0},{9,1},... | collective-permute-start | bytes 135176 | tf_op jit(solution)/shard_map/ppermute | solution.py:28
  37.9 5.8 %collective-permute-start.11 = (bf16[264,128]{1,0:T(8,128)(2,1)S(1)}, bf16[264,128]{1,0:T(8,128)(2,1)S(1)}, u32[]{:S(2)}, u32[]{:S(2)}) collective-permute-start(bf16[264,128]{1,0:T(8,128)(2,1)S(1)} %slice.94), channel_id=1, source_target_pairs={{0,56},{1,57},{2,58},{3,59},{4,60},{5,61},{6,62},{7,63},{8,16},{9,... | collective-permute-start | bytes 202760 | tf_op jit(solution)/shard_map/ppermute | solution.py:28
  39.5 4.4 %collective-permute-start.13 = (bf16[264,128]{1,0:T(8,128)(2,1)S(1)}, bf16[264,128]{1,0:T(8,128)(2,1)S(1)}, u32[]{:S(2)}, u32[]{:S(2)}) collective-permute-start(bf16[264,128]{1,0:T(8,128)(2,1)S(1)} %get-tuple-element.64), channel_id=1, source_target_pairs={{0,64},{1,65},{2,66},{3,67},{4,68},{5,69},{6,70},{7,71},{8,72},{9,... | collective-permute-start | bytes 202760 | tf_op jit(solution)/shard_map/ppermute | solution.py:28
  40.9 5.5 %collective-permute-start.15 = (bf16[264,128]{1,0:T(8,128)(2,1)S(1)}, bf16[264,128]{1,0:T(8,128)(2,1)S(1)}, u32[]{:S(2)}, u32[]{:S(2)}) collective-permute-start(bf16[264,128]{1,0:T(8,128)(2,1)S(1)} %get-tuple-element.65), channel_id=1, source_target_pairs={{0,192},{1,193},{2,194},{3,195},{4,196},{5,197},{6,198},{7,199},{8... | collective-permute-start | bytes 202760 | tf_op jit(solution)/shard_map/ppermute | solution.py:28
  42.9 5.8 %collective-permute-start.14 = (bf16[264,128]{1,0:T(8,128)(2,1)S(1)}, bf16[264,128]{1,0:T(8,128)(2,1)S(1)}, u32[]{:S(2)}, u32[]{:S(2)}) collective-permute-start(bf16[264,128]{1,0:T(8,128)(2,1)S(1)} %get-tuple-element.66), channel_id=1, source_target_pairs={{0,128},{1,129},{2,130},{3,131},{4,132},{5,133},{6,134},{7,135},{8... | collective-permute-start | bytes 202760 | tf_op jit(solution)/shard_map/ppermute | solution.py:28
  43.7 17.3 %copy-start.3 = (f32[1,43,512]{2,0,1:T(1,128)S(1)}, f32[1,43,512]{2,0,1:T(1,128)}, u32[]{:S(2)}) copy-start(f32[1,43,512]{2,0,1:T(1,128)} %param.11) | copy-start | bytes 264196
  43.7 17.3 %copy-start.4 = (f32[1,43,512]{2,0,1:T(1,128)S(1)}, f32[1,43,512]{2,0,1:T(1,128)}, u32[]{:S(2)}) copy-start(f32[1,43,512]{2,0,1:T(1,128)} %param.10) | copy-start | bytes 264196
  48.8 7.2 %collective-permute-start.16 = (bf16[88,256]{1,0:T(8,128)(2,1)S(1)}, bf16[88,256]{1,0:T(8,128)(2,1)S(1)}, u32[]{:S(2)}, u32[]{:S(2)}) collective-permute-start(bf16[88,256]{1,0:T(8,128)(2,1)S(1)} %get-tuple-element.73), channel_id=1, source_target_pairs={{0,40},{1,41},{2,42},{3,43},{4,44},{5,45},{6,46},{7,47},{8,32},{9,... | collective-permute-start | bytes 135176 | tf_op jit(solution)/shard_map/ppermute | solution.py:28
  52.6 7.1 %collective-permute-start.17 = (bf16[88,256]{1,0:T(8,128)(2,1)S(1)}, bf16[88,256]{1,0:T(8,128)(2,1)S(1)}, u32[]{:S(2)}, u32[]{:S(2)}) collective-permute-start(bf16[88,256]{1,0:T(8,128)(2,1)S(1)} %get-tuple-element.74), channel_id=1, source_target_pairs={{0,24},{1,25},{2,26},{3,27},{4,28},{5,29},{6,30},{7,31},{8,48},{9,... | collective-permute-start | bytes 135176 | tf_op jit(solution)/shard_map/ppermute | solution.py:28
  59.7 1.3 %collective-permute-start.18 = (f32[43,256]{1,0:T(8,128)S(1)}, f32[43,256]{1,0:T(8,128)S(1)}, u32[]{:S(2)}, u32[]{:S(2)}) collective-permute-start(f32[43,256]{1,0:T(8,128)S(1)} %slice_select_fusion), channel_id=1, source_target_pairs={{0,4},{1,5},{2,6},{3,7},{4,0},{5,1},{6,2},{7,3},{8,12},{9,13},{10,... | collective-permute-start | bytes 132104 | tf_op jit(solution)/shard_map/ppermute | solution.py:28
  61.1 6.2 %collective-permute-start.19 = (bf16[43,512]{1,0:T(8,128)(2,1)S(1)}, bf16[43,512]{1,0:T(8,128)(2,1)S(1)}, u32[]{:S(2)}, u32[]{:S(2)}) collective-permute-start(bf16[43,512]{1,0:T(8,128)(2,1)S(1)} %get-tuple-element.55), channel_id=1, source_target_pairs={{0,1},{1,0},{2,3},{3,2},{4,5},{5,4},{6,7},{7,6},{8,9},{9,8},{10,11... | collective-permute-start | bytes 132104 | tf_op jit(solution)/shard_map/ppermute | solution.py:28
  62.4 5.6 %collective-permute-start.20 = (bf16[43,512]{1,0:T(8,128)(2,1)S(1)}, bf16[43,512]{1,0:T(8,128)(2,1)S(1)}, u32[]{:S(2)}, u32[]{:S(2)}) collective-permute-start(bf16[43,512]{1,0:T(8,128)(2,1)S(1)} %get-tuple-element.55), channel_id=1, source_target_pairs={{0,2},{1,3},{2,0},{3,1},{4,6},{5,7},{6,4},{7,5},{8,10},{9,11},{10,... | collective-permute-start | bytes 132104 | tf_op jit(solution)/shard_map/ppermute | solution.py:28
  64.4 5.3 %collective-permute-start.21 = (bf16[43,512]{1,0:T(8,128)(2,1)S(1)}, bf16[43,512]{1,0:T(8,128)(2,1)S(1)}, u32[]{:S(2)}, u32[]{:S(2)}) collective-permute-start(bf16[43,512]{1,0:T(8,128)(2,1)S(1)} %get-tuple-element.55), channel_id=1, source_target_pairs={{0,3},{1,2},{2,1},{3,0},{4,7},{5,6},{6,5},{7,4},{8,11},{9,10},{10,... | collective-permute-start | bytes 132104 | tf_op jit(solution)/shard_map/ppermute | solution.py:28
  (5 other events, 19.1 us)

commit v8 on v7

--- a/solution.py
+++ b/solution.py
@@ -8,14 +8,12 @@
 
 NX, NZ, NCORE, NY = 4, 8, 2, 4
 OWNED = 43
-CHUNKS = 2
 CHIP, PADDED = NCORE * OWNED, 88
 BF, F32 = jnp.bfloat16, jnp.float32
 
-Z_ORDER = (-2, 1, -4, -1, 2, 3, 0, -3)
-FIRST, SECOND = 2 * PADDED, 5 * PADDED
+Z_ORDER = (3, 1, -1, -3, -2, 0, 2, 4)
+FIRST, SECOND, KEEP = 2 * PADDED, 4 * PADDED, 7 * PADDED
 X_ORDER = (1, 2, 3, 0)
-Y_PAIRS = ((1, 3), (3, 1))
 
 
 def send(value, move):
@@ -38,6 +36,10 @@
 
 def swap_z(value, k):
     return send(value, lambda x, z, c, y: (x, (z + k * (1 - 2 * (z % 2))) % NZ, c, y))
+
+
+def swap_z2(value, shift):
+    return send(value, lambda x, z, c, y: (x, ((z + shift) % NZ ^ 2) - shift & (NZ - 1), c, y))
 
 
 def swap_y(value, m):
@@ -68,7 +70,7 @@
 
 def arrange(order, own, came):
     tokens = own.shape[1]
-    sizes = [NZ * PADDED] * NX + [NX * n for n in (FIRST, SECOND - FIRST, SECOND - FIRST)]
+    sizes = [NZ * PADDED] * NX
     vmem = pl.BlockSpec(memory_space=pltpu.VMEM)
     smem = pl.BlockSpec(memory_space=pltpu.SMEM)
     return pl.pallas_call(
@@ -99,51 +101,35 @@
     up = 1 - 2 * (z & 1)
     blocks_z = (z + up * jnp.array(Z_ORDER, jnp.int32)) & (NZ - 1)
     blocks_x = (x ^ jnp.array(X_ORDER, jnp.int32))[:, None] * NZ
-    order = blocks_x + blocks_z[None, :]
-    order = [order] + [order[:, i:j] for i, j in ((0, 2), (2, 5), (5, 8))]
-    order = jnp.concatenate([part.reshape(-1) for part in order])
+    order = (blocks_x + blocks_z[None, :]).reshape(-1)
 
     def lanes_of(c):
         return lax.dynamic_slice(basis[0], (0, c * lanes), (basis.shape[1], lanes))
 
     theirs = swap_core(dot(features[0], lanes_of(1 - core)).astype(BF))
     partial = jnp.concatenate([dot(features[0], lanes_of(core)), theirs.astype(F32)], axis=0)
-    width = lanes // CHUNKS
-    chunks = [partial[:, c * width : (c + 1) * width] for c in range(CHUNKS)]
-    chunks = [p + swap_y(p.astype(BF), m[0]).astype(F32) for p, m in zip(chunks, Y_PAIRS)]
-    chunks, other_columns = lax.optimization_barrier((chunks, other_columns))
+    sent = partial.astype(BF)
+    came = [swap_y(sent, m) for m in (1, 2, 3)]
+    came[0], other_columns = lax.optimization_barrier((came[0], other_columns))
     parts = arrange(order, columns, other_columns)
-    chunks = [p + swap_y(p.astype(BF), m[1]).astype(F32) for p, m in zip(chunks, Y_PAIRS)]
-    chunks = [p.astype(BF) for p in chunks]
-    chunks[0], parts = lax.optimization_barrier((chunks[0], parts))
+    came[2], parts = lax.optimization_barrier((came[2], parts))
+    partial = partial + came[0].astype(F32) + came[1].astype(F32) + came[2].astype(F32)
+    projected = partial.astype(BF)
 
-    def send_x(sent):
-        return [swap_x(value.astype(BF), m) for value, m in zip(sent, X_ORDER)]
-
-    def send_z(first, second):
-        return [swap_z(first.astype(BF), 1), swap_z(second.astype(BF), -1)]
-
-    def add_x(keep, came):
-        return keep + came[0].astype(F32) + came[1].astype(F32) + came[2].astype(F32)
-
-    def add_z(keep, came):
-        keep = (keep + came[1].astype(F32)).reshape(-1, SECOND - FIRST, width)
-        first = came[0].astype(F32).reshape(-1, FIRST, width)
-        return jnp.concatenate([keep[:, :FIRST] + first, keep[:, FIRST:]], axis=1)
-
-    came_x = send_x([dot(part, chunks[0]) for part in parts[:3]])
-    came_z = send_z(dot(parts[4], chunks[1]), dot(parts[5], chunks[1]))
-    came_x, came_z = lax.optimization_barrier((came_x, came_z))
-    a = add_x(dot(parts[3], chunks[0]), came_x)
-    b = add_z(dot(parts[6], chunks[1]), came_z)
-    came_z = send_z(a[:FIRST], a[FIRST:SECOND])
-    came_x = send_x([b[0], b[1], b[2]])
-    a = add_z(a[SECOND:], came_z)[0]
-    b = add_x(b[3], came_x)
-    keep = jnp.concatenate([a, b], axis=1)
-    hub_a, own, hub_b = keep[:PADDED], keep[PADDED:FIRST], keep[FIRST:]
-    came = swap_z(hub_a.astype(BF), 3).astype(F32)
-    own = own + swap_z(hub_b.astype(BF), -3).astype(F32) + came
+    came = [swap_x(dot(part, projected).astype(BF), m) for part, m in zip(parts, X_ORDER[:3])]
+    term = dot(parts[3], projected)
+    term = term + came[0].astype(F32) + came[1].astype(F32) + came[2].astype(F32)
+    lower, upper = swap_z(term[:FIRST].astype(BF), 1), swap_z(term[FIRST:SECOND].astype(BF), -1)
+    opposite = swap_z(term[KEEP:].astype(BF), 4)
+    keep = term[SECOND:KEEP]
+    lower, upper = lower.astype(F32), upper.astype(F32)
+    hub_a = keep[:PADDED] + lower[:PADDED]
+    own = keep[PADDED:FIRST] + lower[PADDED:] + upper[:PADDED]
+    hub_b = keep[FIRST:] + upper[PADDED:]
+    straight = ((z ^ (z >> 1)) & 1) == 0
+    near, far = jnp.where(straight, hub_b, hub_a), jnp.where(straight, hub_a, hub_b)
+    near, far = swap_z2(near.astype(BF), 0), swap_z2(far.astype(BF), 2)
+    own = own + near.astype(F32) + far.astype(F32) + opposite.astype(F32)
     mine, other = own[:OWNED], own[OWNED:CHIP]
     came = swap_core(jnp.where(core == 0, other, mine))
     mine = jnp.where(core == 0, mine, other)

time: 71.4 us -> 75.7 us (1.060)
  waiting for transfers between devices: 27.2 us -> 34.3 us
  starting transfers between devices: 31 us -> 28.9 us
  matrix products: 4.77 us -> 3.56 us
  other arithmetic: 0.77 us -> 1.54 us
    ppermute x22 -> x17, waiting for transfers between devices: 27.2 us -> 34.3 us  [send(): return lax.ppermute(value, ('dp', 'tensor'), pairs)]
    ppermute x22 -> x17, starting transfers between devices: 31 us -> 28.9 us  [send(): return lax.ppermute(value, ('dp', 'tensor'), pairs)]
    dot_general x9 -> x6, matrix products: 4.27 us -> 3.05 us  [dot(): lax.dot_general(a, b, (((1,), (0,)), ((), ())), preferred_element_type=F32)]
    convert_element_type x5, other arithmetic: 0.14 us -> 1.26 us  [the longest x1 1.17 us: local(): projected = partial.astype(BF)]
  transfers between devices with their start and end apart: 22 -> 17, of which waited for: 14 -> 11; matrix products, arithmetic and copies ran while one was open for 9% -> 5% of each run, Pallas kernels for 3% -> 3%
where the time goes in v8:
time: 75.7 us; the launch traced here: 75.2 us
  waiting for transfers between devices  34.3 us (45%)
  starting transfers between devices  28.9 us (38%)
  local copies, waits for them, and re-layouts  3.85 us (5%)
  matrix products  3.56 us (5%)
  Pallas kernels  2.11 us (3%)
  other arithmetic  1.54 us (2%)
  between operations  0.91 us (1%)
    ppermute x17, waiting for transfers between devices, send(): return lax.ppermute(value, ('dp', 'tensor'), pairs)  34.3 us
    ppermute x17, starting transfers between devices, send(): return lax.ppermute(value, ('dp', 'tensor'), pairs)  28.9 us
    unnamed x17, local copies, waits for them, and re-layouts  3.75 us
    dot_general x6, matrix products, dot(): lax.dot_general(a, b, (((1,), (0,)), ((), ())), preferred_element_type=F32)  3.05 us
    pallas_call x1, Pallas kernels, arrange(): pl.pallas_call(arrange_kernel, out_shape=[jax.ShapeDtypeStruct((n, NCORE...  2.11 us
  transfers between devices with their start and end apart: 17, of which 11 were waited for; matrix products, arithmetic and copies ran while one was open for 5% of the time, Pallas kernels for 3%

profile of v8, /device:TPU:32, one launch (start us, length us, event | category | flops | bytes accessed | tf_op | source)
XLA Modules:
  0.0 75.2 jit_solution(11327559611425861742)
XLA Ops:
  0.8 1.2 %copy-done = bf16[1,1024,512]{2,1,0:T(8,128)(2,1)S(1)} copy-done((bf16[1,1024,512]{2,1,0:T(8,128)(2,1)S(1)}, bf16[1,1024,512]{2,1,0:T(8,128)(2,1)}, u32[]{:S(2)}) %copy-start) | copy-done | bytes 1048600
  2.0 1.3 %fusion.3 = bf16[256,256]{1,0:T(8,128)(2,1)S(1)} fusion(bf16[1,256,1024]{2,1,0:T(8,128)(2,1)} %param.7, bf16[1,1024,512]{2,1,0:T(8,128)(2,1)S(1)} %copy-done, s32[]{:T(128)S(6)} %select_n.148), kind=kOutput, calls=%fused_computation.10 | convolution fusion | flops 134283264 | bytes 1179652 | tf_op jit(solution)/shard_map/dot_general | solution.py:88
  4.9 1.7 %collective-permute-start.2 = (bf16[512,256]{1,0:T(8,128)(2,1)S(1)}, bf16[512,256]{1,0:T(8,128)(2,1)S(1)}, u32[]{:S(2)}, u32[]{:S(2)}) collective-permute-start(bf16[512,256]{1,0:T(8,128)(2,1)S(1)} %fusion.11), channel_id=1, source_target_pairs={{0,1},{1,0},{2,3},{3,2},{4,5},{5,4},{6,7},{7,6},{8,9},{9,8},{10,11... | collective-permute-start | bytes 786440 | tf_op jit(solution)/shard_map/ppermute | solution.py:26
  6.5 2.2 %collective-permute-start.1 = (bf16[512,256]{1,0:T(8,128)(2,1)S(1)}, bf16[512,256]{1,0:T(8,128)(2,1)}, u32[]{:S(2)}, u32[]{:S(2)}) collective-permute-start(bf16[512,256]{1,0:T(8,128)(2,1)S(1)} %fusion.11), channel_id=1, source_target_pairs={{0,3},{1,2},{2,1},{3,0},{4,7},{5,6},{6,5},{7,4},{8,11},{9,10},{10,... | collective-permute-start | bytes 786440 | tf_op jit(solution)/shard_map/ppermute | solution.py:26
  9.6 4.5 %collective-permute-done.2 = bf16[512,256]{1,0:T(8,128)(2,1)S(1)} collective-permute-done((bf16[512,256]{1,0:T(8,128)(2,1)S(1)}, bf16[512,256]{1,0:T(8,128)(2,1)S(1)}, u32[]{:S(2)}, u32[]{:S(2)}) %collective-permute-start.2) | collective-permute-done | bytes 262176 | tf_op jit(solution)/shard_map/ppermute | solution.py:26
  14.1 2.1 %shard_map.94 = (bf16[704,512]{1,0:T(8,128)(2,1)S(1)}, bf16[704,512]{1,0:T(8,128)(2,1)S(1)}, bf16[704,512]{1,0:T(8,128)(2,1)S(1)}, bf16[704,512]{1,0:T(8,128)(2,1)S(1)}) custom-call(s32[32]{0:T(128)S(1)} %add.87.order_ref, bf16[2752,256]{1,0:T(8,128)(2,1)S(1)} %bitcast.51, bf16[2752,256]{1,0:T(8,128)(2,1)} %collective-permute-done.3.came), custom_call_target="tpu_custom_call" | custom-call | bytes 8388608 | tf_op jit(solution)/shard_map/pallas_call | solution.py:76
  16.2 3.7 %collective-permute-done.1 = bf16[512,256]{1,0:T(8,128)(2,1)} collective-permute-done((bf16[512,256]{1,0:T(8,128)(2,1)S(1)}, bf16[512,256]{1,0:T(8,128)(2,1)}, u32[]{:S(2)}, u32[]{:S(2)}) %collective-permute-start.1) | collective-permute-done | bytes 262176 | tf_op jit(solution)/shard_map/ppermute | solution.py:26
  19.9 1.6 %collective-permute-done.4 = bf16[512,256]{1,0:T(8,128)(2,1)} collective-permute-done((bf16[512,256]{1,0:T(8,128)(2,1)S(1)}, bf16[512,256]{1,0:T(8,128)(2,1)}, u32[]{:S(2)}, u32[]{:S(2)}) %collective-permute-start.4) | collective-permute-done | bytes 262176 | tf_op jit(solution)/shard_map/ppermute | solution.py:26
  21.6 1.2 %add_convert_fusion = bf16[512,256]{1,0:T(8,128)(2,1)S(1)} fusion(bf16[512,256]{1,0:T(8,128)(2,1)} %collective-permute-done.1, bf16[512,256]{1,0:T(8,128)(2,1)} %collective-permute-done.4, bf16[512,256]{1,0:T(8,128)(2,1)S(1)} %collective-permute-done.2, f32[256,256]{1,0:T(8,128)S(1)} %convert_element_type.73, f32[256,256]{1,0:T(8,128)S(1)} %convolution_bitcast_fusion.1), kind=kLoop, calls=%fused_computation.17 | loop fusion | flops 1048576 | bytes 1572864 | tf_op jit(solution)/shard_map/convert_element_type | solution.py:117
  23.1 1.6 %collective-permute-start.5 = (bf16[704,256]{1,0:T(8,128)(2,1)S(1)}, bf16[704,256]{1,0:T(8,128)(2,1)S(1)}, u32[]{:S(2)}, u32[]{:S(2)}) collective-permute-start(bf16[704,256]{1,0:T(8,128)(2,1)S(1)} %convolution_convert_fusion.3), channel_id=1, source_target_pairs={{0,64},{1,65},{2,66},{3,67},{4,68},{5,69},{6,70},{7,71},{8,72},{9,... | collective-permute-start | bytes 1081352 | tf_op jit(solution)/shard_map/ppermute | solution.py:26
  25.0 2.8 %collective-permute-start.6 = (bf16[704,256]{1,0:T(8,128)(2,1)S(1)}, bf16[704,256]{1,0:T(8,128)(2,1)S(1)}, u32[]{:S(2)}, u32[]{:S(2)}) collective-permute-start(bf16[704,256]{1,0:T(8,128)(2,1)S(1)} %convolution_convert_fusion.2), channel_id=1, source_target_pairs={{0,128},{1,129},{2,130},{3,131},{4,132},{5,133},{6,134},{7,135},{8... | collective-permute-start | bytes 1081352 | tf_op jit(solution)/shard_map/ppermute | solution.py:26
  28.8 5.8 %collective-permute-done.5 = bf16[704,256]{1,0:T(8,128)(2,1)S(1)} collective-permute-done((bf16[704,256]{1,0:T(8,128)(2,1)S(1)}, bf16[704,256]{1,0:T(8,128)(2,1)S(1)}, u32[]{:S(2)}, u32[]{:S(2)}) %collective-permute-start.5) | collective-permute-done | bytes 360480 | tf_op jit(solution)/shard_map/ppermute | solution.py:26
  34.5 8.3 %collective-permute-done.6 = bf16[704,256]{1,0:T(8,128)(2,1)S(1)} collective-permute-done((bf16[704,256]{1,0:T(8,128)(2,1)S(1)}, bf16[704,256]{1,0:T(8,128)(2,1)S(1)}, u32[]{:S(2)}, u32[]{:S(2)}) %collective-permute-start.6) | collective-permute-done | bytes 360480 | tf_op jit(solution)/shard_map/ppermute | solution.py:26
  42.8 3.4 %collective-permute-done.7 = bf16[704,256]{1,0:T(8,128)(2,1)S(1)} collective-permute-done((bf16[704,256]{1,0:T(8,128)(2,1)S(1)}, bf16[704,256]{1,0:T(8,128)(2,1)S(1)}, u32[]{:S(2)}, u32[]{:S(2)}) %collective-permute-start.7) | collective-permute-done | bytes 360480 | tf_op jit(solution)/shard_map/ppermute | solution.py:26
  46.8 3.7 %collective-permute-start.9 = (bf16[176,256]{1,0:T(8,128)(2,1)S(1)}, bf16[176,256]{1,0:T(8,128)(2,1)S(1)}, u32[]{:S(2)}, u32[]{:S(2)}) collective-permute-start(bf16[176,256]{1,0:T(8,128)(2,1)S(1)} %get-tuple-element.34), channel_id=1, source_target_pairs={{0,56},{1,57},{2,58},{3,59},{4,60},{5,61},{6,62},{7,63},{8,16},{9,... | collective-permute-start | bytes 270344 | tf_op jit(solution)/shard_map/ppermute | solution.py:26
  50.6 4.5 %collective-permute-start.12 = (bf16[88,256]{1,0:T(8,128)(2,1)S(1)}, bf16[88,256]{1,0:T(8,128)(2,1)S(1)}, u32[]{:S(2)}, u32[]{:S(2)}) collective-permute-start(bf16[88,256]{1,0:T(8,128)(2,1)S(1)} %slice.64), channel_id=1, source_target_pairs={{0,32},{1,33},{2,34},{3,35},{4,36},{5,37},{6,38},{7,39},{8,40},{9,... | collective-permute-start | bytes 135176 | tf_op jit(solution)/shard_map/ppermute | solution.py:26
  55.2 1.6 %collective-permute-start.10 = (bf16[88,256]{1,0:T(8,128)(2,1)S(1)}, bf16[88,256]{1,0:T(8,128)(2,1)S(1)}, u32[]{:S(2)}, u32[]{:S(2)}) collective-permute-start(bf16[88,256]{1,0:T(8,128)(2,1)S(1)} %get-tuple-element.31), channel_id=1, source_target_pairs={{0,16},{1,17},{2,18},{3,19},{4,20},{5,21},{6,22},{7,23},{8,24},{9,... | collective-permute-start | bytes 135176 | tf_op jit(solution)/shard_map/ppermute | solution.py:26
  56.8 4.2 %collective-permute-start.11 = (bf16[88,256]{1,0:T(8,128)(2,1)S(1)}, bf16[88,256]{1,0:T(8,128)(2,1)S(1)}, u32[]{:S(2)}, u32[]{:S(2)}) collective-permute-start(bf16[88,256]{1,0:T(8,128)(2,1)S(1)} %get-tuple-element.32), channel_id=1, source_target_pairs={{0,48},{1,49},{2,50},{3,51},{4,52},{5,53},{6,54},{7,55},{8,56},{9,... | collective-permute-start | bytes 135176 | tf_op jit(solution)/shard_map/ppermute | solution.py:26
  61.1 2.2 %collective-permute-done.11 = bf16[88,256]{1,0:T(8,128)(2,1)S(1)} collective-permute-done((bf16[88,256]{1,0:T(8,128)(2,1)S(1)}, bf16[88,256]{1,0:T(8,128)(2,1)S(1)}, u32[]{:S(2)}, u32[]{:S(2)}) %collective-permute-start.11) | collective-permute-done | bytes 45088 | tf_op jit(solution)/shard_map/ppermute | solution.py:26
  63.4 1.2 %collective-permute-done.13 = f32[43,256]{1,0:T(8,128)S(1)} collective-permute-done((f32[43,256]{1,0:T(8,128)S(1)}, f32[43,256]{1,0:T(8,128)S(1)}, u32[]{:S(2)}, u32[]{:S(2)}) %collective-permute-start.13) | collective-permute-done | bytes 44064 | tf_op jit(solution)/shard_map/ppermute | solution.py:26
  65.0 3.4 %collective-permute-start.15 = (bf16[43,512]{1,0:T(8,128)(2,1)S(1)}, bf16[43,512]{1,0:T(8,128)(2,1)S(1)}, u32[]{:S(2)}, u32[]{:S(2)}) collective-permute-start(bf16[43,512]{1,0:T(8,128)(2,1)S(1)} %get-tuple-element.28), channel_id=1, source_target_pairs={{0,2},{1,3},{2,0},{3,1},{4,6},{5,7},{6,4},{7,5},{8,10},{9,11},{10,... | collective-permute-start | bytes 132104 | tf_op jit(solution)/shard_map/ppermute | solution.py:26
  68.3 1.2 %collective-permute-start.16 = (bf16[43,512]{1,0:T(8,128)(2,1)S(1)}, bf16[43,512]{1,0:T(8,128)(2,1)S(1)}, u32[]{:S(2)}, u32[]{:S(2)}) collective-permute-start(bf16[43,512]{1,0:T(8,128)(2,1)S(1)} %get-tuple-element.28), channel_id=1, source_target_pairs={{0,3},{1,2},{2,1},{3,0},{4,7},{5,6},{6,5},{7,4},{8,11},{9,10},{10,... | collective-permute-start | bytes 132104 | tf_op jit(solution)/shard_map/ppermute | solution.py:26
  71.2 2.5 %collective-permute-done.16 = bf16[43,512]{1,0:T(8,128)(2,1)S(1)} collective-permute-done((bf16[43,512]{1,0:T(8,128)(2,1)S(1)}, bf16[43,512]{1,0:T(8,128)(2,1)S(1)}, u32[]{:S(2)}, u32[]{:S(2)}) %collective-permute-start.16) | collective-permute-done | bytes 44064 | tf_op jit(solution)/shard_map/ppermute | solution.py:26
  74.2 1.0 %copy.14 = bf16[1,1024,4,43]{1,2,3,0:T(4,128)(2,1)} copy(bf16[1,1024,4,43]{1,3,2,0:T(8,128)(2,1)S(1)} %fusion.2) | data formatting | bytes 704512
  (52 shorter events, 7.2 us)
Async XLA Ops:
  0.6 1.4 %copy-start = (bf16[1,1024,512]{2,1,0:T(8,128)(2,1)S(1)}, bf16[1,1024,512]{2,1,0:T(8,128)(2,1)}, u32[]{:S(2)}) copy-start(bf16[1,1024,512]{2,1,0:T(8,128)(2,1)} %param.9) | copy-start | bytes 3145732
  0.6 3.2 %copy-start.5 = (s32[8]{0:T(128)S(1)}, s32[8]{0:T(128)}, u32[]{:S(2)}) copy-start(s32[8]{0:T(128)} %constant.54.clone) | copy-start | bytes 100
  0.7 2.8 %copy-start.2 = (bf16[1,256,1024]{2,1,0:T(8,128)(2,1)S(1)}, bf16[1,256,1024]{2,1,0:T(8,128)(2,1)}, u32[]{:S(2)}) copy-start(bf16[1,256,1024]{2,1,0:T(8,128)(2,1)} %param.7) | copy-start | bytes 1572868
  0.7 13.5 %collective-permute-start.3 = (bf16[2752,256]{1,0:T(8,128)(2,1)}, bf16[2752,256]{1,0:T(8,128)(2,1)}, u32[]{:S(2)}, u32[]{:S(2)}) collective-permute-start(bf16[2752,256]{1,0:T(8,128)(2,1)} %bitcast.50), channel_id=1, source_target_pairs={{0,4},{1,5},{2,6},{3,7},{4,0},{5,1},{6,2},{7,3},{8,12},{9,13},{10,... | collective-permute-start | bytes 4227080 | tf_op jit(solution)/shard_map/ppermute | solution.py:26
  3.4 6.1 %copy-start.6 = (s32[4]{0:T(128)S(1)}, s32[4]{0:T(128)}, u32[]{:S(2)}) copy-start(s32[4]{0:T(128)} %constant.55.clone) | copy-start | bytes 52
  3.4 10.7 %copy-start.1 = (bf16[1,256,2752]{1,2,0:T(8,128)(2,1)S(1)}, bf16[1,256,2752]{1,2,0:T(8,128)(2,1)}, u32[]{:S(2)}) copy-start(bf16[1,256,2752]{1,2,0:T(8,128)(2,1)} %param.8) | copy-start | bytes 4227076
  3.4 1.4 %collective-permute-start = (bf16[256,256]{1,0:T(8,128)(2,1)S(1)}, bf16[256,256]{1,0:T(8,128)(2,1)S(1)}, u32[]{:S(2)}, u32[]{:S(2)}) collective-permute-start(bf16[256,256]{1,0:T(8,128)(2,1)S(1)} %fusion.3), channel_id=1, source_target_pairs={{0,4},{1,5},{2,6},{3,7},{4,0},{5,1},{6,2},{7,3},{8,12},{9,13},{10,... | collective-permute-start | bytes 393224 | tf_op jit(solution)/shard_map/ppermute | solution.py:26
  4.9 9.2 %collective-permute-start.2 = (bf16[512,256]{1,0:T(8,128)(2,1)S(1)}, bf16[512,256]{1,0:T(8,128)(2,1)S(1)}, u32[]{:S(2)}, u32[]{:S(2)}) collective-permute-start(bf16[512,256]{1,0:T(8,128)(2,1)S(1)} %fusion.11), channel_id=1, source_target_pairs={{0,1},{1,0},{2,3},{3,2},{4,5},{5,4},{6,7},{7,6},{8,9},{9,8},{10,11... | collective-permute-start | bytes 786440 | tf_op jit(solution)/shard_map/ppermute | solution.py:26
  6.5 13.4 %collective-permute-start.1 = (bf16[512,256]{1,0:T(8,128)(2,1)S(1)}, bf16[512,256]{1,0:T(8,128)(2,1)}, u32[]{:S(2)}, u32[]{:S(2)}) collective-permute-start(bf16[512,256]{1,0:T(8,128)(2,1)S(1)} %fusion.11), channel_id=1, source_target_pairs={{0,3},{1,2},{2,1},{3,0},{4,7},{5,6},{6,5},{7,4},{8,11},{9,10},{10,... | collective-permute-start | bytes 786440 | tf_op jit(solution)/shard_map/ppermute | solution.py:26
  8.7 12.8 %collective-permute-start.4 = (bf16[512,256]{1,0:T(8,128)(2,1)S(1)}, bf16[512,256]{1,0:T(8,128)(2,1)}, u32[]{:S(2)}, u32[]{:S(2)}) collective-permute-start(bf16[512,256]{1,0:T(8,128)(2,1)S(1)} %fusion.11), channel_id=1, source_target_pairs={{0,2},{1,3},{2,0},{3,1},{4,6},{5,7},{6,4},{7,5},{8,10},{9,11},{10,... | collective-permute-start | bytes 786440 | tf_op jit(solution)/shard_map/ppermute | solution.py:26
  23.1 11.4 %collective-permute-start.5 = (bf16[704,256]{1,0:T(8,128)(2,1)S(1)}, bf16[704,256]{1,0:T(8,128)(2,1)S(1)}, u32[]{:S(2)}, u32[]{:S(2)}) collective-permute-start(bf16[704,256]{1,0:T(8,128)(2,1)S(1)} %convolution_convert_fusion.3), channel_id=1, source_target_pairs={{0,64},{1,65},{2,66},{3,67},{4,68},{5,69},{6,70},{7,71},{8,72},{9,... | collective-permute-start | bytes 1081352 | tf_op jit(solution)/shard_map/ppermute | solution.py:26
  25.0 17.8 %collective-permute-start.6 = (bf16[704,256]{1,0:T(8,128)(2,1)S(1)}, bf16[704,256]{1,0:T(8,128)(2,1)S(1)}, u32[]{:S(2)}, u32[]{:S(2)}) collective-permute-start(bf16[704,256]{1,0:T(8,128)(2,1)S(1)} %convolution_convert_fusion.2), channel_id=1, source_target_pairs={{0,128},{1,129},{2,130},{3,131},{4,132},{5,133},{6,134},{7,135},{8... | collective-permute-start | bytes 1081352 | tf_op jit(solution)/shard_map/ppermute | solution.py:26
  28.2 18.0 %collective-permute-start.7 = (bf16[704,256]{1,0:T(8,128)(2,1)S(1)}, bf16[704,256]{1,0:T(8,128)(2,1)S(1)}, u32[]{:S(2)}, u32[]{:S(2)}) collective-permute-start(bf16[704,256]{1,0:T(8,128)(2,1)S(1)} %convolution_convert_fusion.1), channel_id=1, source_target_pairs={{0,192},{1,193},{2,194},{3,195},{4,196},{5,197},{6,198},{7,199},{8... | collective-permute-start | bytes 1081352 | tf_op jit(solution)/shard_map/ppermute | solution.py:26
  46.6 18.1 %copy-start.3 = (f32[1,43,512]{2,0,1:T(1,128)S(1)}, f32[1,43,512]{2,0,1:T(1,128)}, u32[]{:S(2)}) copy-start(f32[1,43,512]{2,0,1:T(1,128)} %param.11) | copy-start | bytes 264196
  46.6 18.1 %copy-start.4 = (f32[1,43,512]{2,0,1:T(1,128)S(1)}, f32[1,43,512]{2,0,1:T(1,128)}, u32[]{:S(2)}) copy-start(f32[1,43,512]{2,0,1:T(1,128)} %param.10) | copy-start | bytes 264196
  46.6 8.4 %collective-permute-start.8 = (bf16[176,256]{1,0:T(8,128)(2,1)S(1)}, bf16[176,256]{1,0:T(8,128)(2,1)S(1)}, u32[]{:S(2)}, u32[]{:S(2)}) collective-permute-start(bf16[176,256]{1,0:T(8,128)(2,1)S(1)} %get-tuple-element.33), channel_id=1, source_target_pairs={{0,8},{1,9},{2,10},{3,11},{4,12},{5,13},{6,14},{7,15},{8,0},{9,1},... | collective-permute-start | bytes 270344 | tf_op jit(solution)/shard_map/ppermute | solution.py:26
  46.8 8.2 %collective-permute-start.9 = (bf16[176,256]{1,0:T(8,128)(2,1)S(1)}, bf16[176,256]{1,0:T(8,128)(2,1)S(1)}, u32[]{:S(2)}, u32[]{:S(2)}) collective-permute-start(bf16[176,256]{1,0:T(8,128)(2,1)S(1)} %get-tuple-element.34), channel_id=1, source_target_pairs={{0,56},{1,57},{2,58},{3,59},{4,60},{5,61},{6,62},{7,63},{8,16},{9,... | collective-permute-start | bytes 270344 | tf_op jit(solution)/shard_map/ppermute | solution.py:26
  50.6 10.5 %collective-permute-start.12 = (bf16[88,256]{1,0:T(8,128)(2,1)S(1)}, bf16[88,256]{1,0:T(8,128)(2,1)S(1)}, u32[]{:S(2)}, u32[]{:S(2)}) collective-permute-start(bf16[88,256]{1,0:T(8,128)(2,1)S(1)} %slice.64), channel_id=1, source_target_pairs={{0,32},{1,33},{2,34},{3,35},{4,36},{5,37},{6,38},{7,39},{8,40},{9,... | collective-permute-start | bytes 135176 | tf_op jit(solution)/shard_map/ppermute | solution.py:26
  55.2 5.9 %collective-permute-start.10 = (bf16[88,256]{1,0:T(8,128)(2,1)S(1)}, bf16[88,256]{1,0:T(8,128)(2,1)S(1)}, u32[]{:S(2)}, u32[]{:S(2)}) collective-permute-start(bf16[88,256]{1,0:T(8,128)(2,1)S(1)} %get-tuple-element.31), channel_id=1, source_target_pairs={{0,16},{1,17},{2,18},{3,19},{4,20},{5,21},{6,22},{7,23},{8,24},{9,... | collective-permute-start | bytes 135176 | tf_op jit(solution)/shard_map/ppermute | solution.py:26
  56.8 6.5 %collective-permute-start.11 = (bf16[88,256]{1,0:T(8,128)(2,1)S(1)}, bf16[88,256]{1,0:T(8,128)(2,1)S(1)}, u32[]{:S(2)}, u32[]{:S(2)}) collective-permute-start(bf16[88,256]{1,0:T(8,128)(2,1)S(1)} %get-tuple-element.32), channel_id=1, source_target_pairs={{0,48},{1,49},{2,50},{3,51},{4,52},{5,53},{6,54},{7,55},{8,56},{9,... | collective-permute-start | bytes 135176 | tf_op jit(solution)/shard_map/ppermute | solution.py:26
  63.3 1.3 %collective-permute-start.13 = (f32[43,256]{1,0:T(8,128)S(1)}, f32[43,256]{1,0:T(8,128)S(1)}, u32[]{:S(2)}, u32[]{:S(2)}) collective-permute-start(f32[43,256]{1,0:T(8,128)S(1)} %slice_select_fusion), channel_id=1, source_target_pairs={{0,4},{1,5},{2,6},{3,7},{4,0},{5,1},{6,2},{7,3},{8,12},{9,13},{10,... | collective-permute-start | bytes 132104 | tf_op jit(solution)/shard_map/ppermute | solution.py:26
  64.8 6.2 %collective-permute-start.14 = (bf16[43,512]{1,0:T(8,128)(2,1)S(1)}, bf16[43,512]{1,0:T(8,128)(2,1)S(1)}, u32[]{:S(2)}, u32[]{:S(2)}) collective-permute-start(bf16[43,512]{1,0:T(8,128)(2,1)S(1)} %get-tuple-element.28), channel_id=1, source_target_pairs={{0,1},{1,0},{2,3},{3,2},{4,5},{5,4},{6,7},{7,6},{8,9},{9,8},{10,11... | collective-permute-start | bytes 132104 | tf_op jit(solution)/shard_map/ppermute | solution.py:26
  65.0 6.2 %collective-permute-start.15 = (bf16[43,512]{1,0:T(8,128)(2,1)S(1)}, bf16[43,512]{1,0:T(8,128)(2,1)S(1)}, u32[]{:S(2)}, u32[]{:S(2)}) collective-permute-start(bf16[43,512]{1,0:T(8,128)(2,1)S(1)} %get-tuple-element.28), channel_id=1, source_target_pairs={{0,2},{1,3},{2,0},{3,1},{4,6},{5,7},{6,4},{7,5},{8,10},{9,11},{10,... | collective-permute-start | bytes 132104 | tf_op jit(solution)/shard_map/ppermute | solution.py:26
  68.3 5.3 %collective-permute-start.16 = (bf16[43,512]{1,0:T(8,128)(2,1)S(1)}, bf16[43,512]{1,0:T(8,128)(2,1)S(1)}, u32[]{:S(2)}, u32[]{:S(2)}) collective-permute-start(bf16[43,512]{1,0:T(8,128)(2,1)S(1)} %get-tuple-element.28), channel_id=1, source_target_pairs={{0,3},{1,2},{2,1},{3,0},{4,7},{5,6},{6,5},{7,4},{8,11},{9,10},{10,... | collective-permute-start | bytes 132104 | tf_op jit(solution)/shard_map/ppermute | solution.py:26

commit v9 on v6

--- a/solution.py
+++ b/solution.py
@@ -12,8 +12,8 @@
 CHIP, PADDED = NCORE * OWNED, 88
 BF, F32 = jnp.bfloat16, jnp.float32
 
-Z_ORDER = (-2, 1, -4, -1, 2, 3, 0, -3)
-FIRST, SECOND = 2 * PADDED, 5 * PADDED
+Z_ORDER = (3, 1, -1, -3, -2, 0, 2, 4)
+FIRST, SECOND, KEEP = 2 * PADDED, 4 * PADDED, 7 * PADDED
 X_ORDER = ((2, 1, 3, 0), (2, 3, 1, 0))
 PAIRS = ((1, 3), (3, 1))
 
@@ -38,6 +38,10 @@
 
 def swap_z(value, k):
     return send(value, lambda x, z, c, y: (x, (z + k * (1 - 2 * (z % 2))) % NZ, c, y))
+
+
+def swap_z2(value, shift):
+    return send(value, lambda x, z, c, y: (x, ((z + shift) % NZ ^ 2) - shift & (NZ - 1), c, y))
 
 
 def swap_y(value, m):
@@ -115,19 +119,25 @@
     chunks[0], parts = lax.optimization_barrier((chunks[0], parts))
 
     rows = NZ * PADDED
-    terms = []
-    for c, (projected, m) in enumerate(zip(chunks, PAIRS)):
-        came = swap_x(dot(parts[2 * c], projected).astype(BF), m[0])
-        term = dot(parts[2 * c + 1], projected) + came.astype(F32)
-        terms.append(term[rows:] + swap_x(term[:rows].astype(BF), m[1]).astype(F32))
+    sent = [dot(parts[2 * c], p).astype(BF) for c, p in enumerate(chunks)]
+    came = [swap_x(value, m[0]) for value, m in zip(sent, PAIRS)]
+    chunks, sent = lax.optimization_barrier((chunks, sent))
+    kept = [dot(parts[2 * c + 1], p) for c, p in enumerate(chunks)]
+    terms = [k + c.astype(F32) for k, c in zip(lax.optimization_barrier(kept), came)]
+    came = [swap_x(t[:rows].astype(BF), m[1]) for t, m in zip(terms, PAIRS)]
+    terms = [t[rows:] + c.astype(F32) for t, c in zip(terms, came)]
     term = jnp.concatenate(terms, axis=1)
-    came = swap_z(term[:FIRST].astype(BF), 1).astype(F32)
-    more = swap_z(term[FIRST:SECOND].astype(BF), -1).astype(F32)
-    keep = term[SECOND:] + more
-    hub_a, own, hub_b = keep[:PADDED], keep[PADDED:FIRST], keep[FIRST:]
-    hub_a, own = hub_a + came[:PADDED], own + came[PADDED:]
-    came = swap_z(hub_a.astype(BF), 3).astype(F32)
-    own = own + swap_z(hub_b.astype(BF), -3).astype(F32) + came
+    lower, upper = swap_z(term[:FIRST].astype(BF), 1), swap_z(term[FIRST:SECOND].astype(BF), -1)
+    opposite = swap_z(term[KEEP:].astype(BF), 4)
+    keep = term[SECOND:KEEP]
+    lower, upper = lower.astype(F32), upper.astype(F32)
+    hub_a = keep[:PADDED] + lower[:PADDED]
+    own = keep[PADDED:FIRST] + lower[PADDED:] + upper[:PADDED]
+    hub_b = keep[FIRST:] + upper[PADDED:]
+    straight = ((z ^ (z >> 1)) & 1) == 0
+    near, far = jnp.where(straight, hub_b, hub_a), jnp.where(straight, hub_a, hub_b)
+    near, far = swap_z2(near.astype(BF), 0), swap_z2(far.astype(BF), 2)
+    own = own + near.astype(F32) + far.astype(F32) + opposite.astype(F32)
     mine, other = own[:OWNED], own[OWNED:CHIP]
     came = swap_core(jnp.where(core == 0, other, mine))
     mine = jnp.where(core == 0, mine, other)
@@ -143,9 +153,10 @@
     ).astype(BF)[0]
 
     around = [update] + [swap_y(update, m) for m in (1, 2, 3)]
-    ordered = jnp.stack([lax.select_n(y ^ a, *around) for a in range(NY)])
-    change = jnp.einsum("dr,acr->dac", basis[0], ordered, preferred_element_type=F32)
-    return (new_first, new_second, change.astype(BF)[None])
+    ordered = jnp.stack([lax.select_n(y ^ a, *around) for a in range(NY)], axis=1)
+    rows = lax.optimization_barrier(ordered.reshape(-1, ordered.shape[2]))
+    change = dot(rows, basis[0].T).reshape(OWNED, NY, -1)
+    return (new_first, new_second, change.astype(BF).transpose(2, 1, 0)[None])
 
 
 def solution(mesh):

time: 71.3 us -> 70.1 us (0.983); the launches traced: 70.1 us -> 69.7 us
  waiting for transfers between devices: 32.6 us -> 30.3 us
  starting transfers between devices: 24.8 us -> 26.3 us
    ppermute x18 -> x19, waiting for transfers between devices: 32.6 us -> 30.3 us  [send(): return lax.ppermute(value, ('dp', 'tensor'), pairs)]
    ppermute x18 -> x19, starting transfers between devices: 24.8 us -> 26.3 us  [send(): return lax.ppermute(value, ('dp', 'tensor'), pairs)]
    unnamed x15 -> x14, local copies, waits for them, and re-layouts: 3.6 us -> 2.59 us
    convert_element_type x0 -> x1, local copies, waits for them, and re-layouts: none -> 0.89 us  [local(): return (new_first, new_second, change.astype(BF).transpose(2, 1, 0)[None])]
    dot_general x6 -> x7, matrix products: 3.82 us -> 4.27 us  [dot(): lax.dot_general(a, b, (((1,), (0,)), ((), ())), preferred_element_type=F32)]
  transfers between devices with their start and end apart: 18 -> 19, of which waited for: 15 -> 13; matrix products, arithmetic and copies ran while one was open for 8% -> 9% of each run, Pallas kernels for 3% -> 3%
where the time goes in v9:
time: 70.1 us; the launch traced here: 69.7 us
  waiting for transfers between devices  30.3 us (43%)
  starting transfers between devices  26.3 us (38%)
  matrix products  4.27 us (6%)
  local copies, waits for them, and re-layouts  3.88 us (6%)
  Pallas kernels  2.39 us (3%)
  other arithmetic  1.47 us (2%)
  between operations  0.98 us (1%)
    ppermute x19, waiting for transfers between devices, send(): return lax.ppermute(value, ('dp', 'tensor'), pairs)  30.3 us
    ppermute x19, starting transfers between devices, send(): return lax.ppermute(value, ('dp', 'tensor'), pairs)  26.3 us
    dot_general x7, matrix products, dot(): lax.dot_general(a, b, (((1,), (0,)), ((), ())), preferred_element_type=F32)  4.27 us
    unnamed x14, local copies, waits for them, and re-layouts  2.59 us
    pallas_call x1, Pallas kernels, arrange(): pl.pallas_call(arrange_kernel, out_shape=[shape] * 2 * CHUNKS, in_specs=[...  2.39 us
  transfers between devices with their start and end apart: 19, of which 13 were waited for; matrix products, arithmetic and copies ran while one was open for 9% of the time, Pallas kernels for 3%

profile of v9, /device:TPU:32, one launch (start us, length us, event | category | flops | bytes accessed | tf_op | source)
XLA Modules:
  0.0 69.7 jit_solution(18293145966823847660)
XLA Ops:
  0.8 1.1 %copy-done = bf16[1,1024,512]{2,1,0:T(8,128)(2,1)S(1)} copy-done((bf16[1,1024,512]{2,1,0:T(8,128)(2,1)S(1)}, bf16[1,1024,512]{2,1,0:T(8,128)(2,1)}, u32[]{:S(2)}) %copy-start) | copy-done | bytes 1048600
  1.9 1.3 %fusion = bf16[256,256]{1,0:T(8,128)(2,1)S(1)} fusion(bf16[1,256,1024]{2,1,0:T(8,128)(2,1)} %param.7, bf16[1,1024,512]{2,1,0:T(8,128)(2,1)S(1)} %copy-done, s32[]{:T(128)S(6)} %select_n.148), kind=kOutput, calls=%fused_computation.5 | convolution fusion | flops 134283264 | bytes 1179652 | tf_op jit(solution)/shard_map/dot_general | solution.py:89
  4.7 3.1 %collective-permute-start.2 = (bf16[512,128]{1,0:T(8,128)(2,1)S(1)}, bf16[512,128]{1,0:T(8,128)(2,1)S(1)}, u32[]{:S(2)}, u32[]{:S(2)}) collective-permute-start(bf16[512,128]{1,0:T(8,128)(2,1)S(1)} %get-tuple-element.48), channel_id=1, source_target_pairs={{0,3},{1,2},{2,1},{3,0},{4,7},{5,6},{6,5},{7,4},{8,11},{9,10},{10,... | collective-permute-start | bytes 393224 | tf_op jit(solution)/shard_map/ppermute | solution.py:28
  8.0 3.8 %collective-permute-done.2 = bf16[512,128]{1,0:T(8,128)(2,1)S(1)} collective-permute-done((bf16[512,128]{1,0:T(8,128)(2,1)S(1)}, bf16[512,128]{1,0:T(8,128)(2,1)S(1)}, u32[]{:S(2)}, u32[]{:S(2)}) %collective-permute-start.2) | collective-permute-done | bytes 131104 | tf_op jit(solution)/shard_map/ppermute | solution.py:28
  11.8 1.5 %collective-permute-done.1 = bf16[512,128]{1,0:T(8,128)(2,1)S(1)} collective-permute-done((bf16[512,128]{1,0:T(8,128)(2,1)S(1)}, bf16[512,128]{1,0:T(8,128)(2,1)S(1)}, u32[]{:S(2)}, u32[]{:S(2)}) %collective-permute-start.1) | collective-permute-done | bytes 131104 | tf_op jit(solution)/shard_map/ppermute | solution.py:28
  13.3 1.6 %collective-permute-start.4 = (bf16[512,128]{1,0:T(8,128)(2,1)S(1)}, bf16[512,128]{1,0:T(8,128)(2,1)S(1)}, u32[]{:S(2)}, u32[]{:S(2)}) collective-permute-start(bf16[512,128]{1,0:T(8,128)(2,1)S(1)} %convert_element_type.95), channel_id=1, source_target_pairs={{0,3},{1,2},{2,1},{3,0},{4,7},{5,6},{6,5},{7,4},{8,11},{9,10},{10,... | collective-permute-start | bytes 393224 | tf_op jit(solution)/shard_map/ppermute | solution.py:28
  15.2 2.4 %shard_map.94 = (bf16[1408,512]{1,0:T(8,128)(2,1)S(1)}, bf16[1408,512]{1,0:T(8,128)(2,1)S(1)}, bf16[1408,512]{1,0:T(8,128)(2,1)S(1)}, bf16[1408,512]{1,0:T(8,128)(2,1)S(1)}) custom-call(s32[64]{0:T(128)S(1)} %add.96.order_ref, bf16[2752,256]{1,0:T(8,128)(2,1)S(1)} %bitcast.50, bf16[2752,256]{1,0:T(8,128)(2,1)} %collective-permute-done.3.came), custom_call_target="tpu_custom_call" | custom-call | bytes 8388608 | tf_op jit(solution)/shard_map/pallas_call | solution.py:77
  17.6 2.0 %collective-permute-done.4 = bf16[512,128]{1,0:T(8,128)(2,1)S(1)} collective-permute-done((bf16[512,128]{1,0:T(8,128)(2,1)S(1)}, bf16[512,128]{1,0:T(8,128)(2,1)S(1)}, u32[]{:S(2)}, u32[]{:S(2)}) %collective-permute-start.4) | collective-permute-done | bytes 131104 | tf_op jit(solution)/shard_map/ppermute | solution.py:28
  20.7 2.8 %collective-permute-start.8 = (bf16[1408,128]{1,0:T(8,128)(2,1)S(1)}, bf16[1408,128]{1,0:T(8,128)(2,1)S(1)}, u32[]{:S(2)}, u32[]{:S(2)}) collective-permute-start(bf16[1408,128]{1,0:T(8,128)(2,1)S(1)} %convolution_convert_fusion), channel_id=1, source_target_pairs={{0,192},{1,193},{2,194},{3,195},{4,196},{5,197},{6,198},{7,199},{8... | collective-permute-start | bytes 1081352 | tf_op jit(solution)/shard_map/ppermute | solution.py:28
  25.5 5.2 %collective-permute-done.8 = bf16[1408,128]{1,0:T(8,128)(2,1)S(1)} collective-permute-done((bf16[1408,128]{1,0:T(8,128)(2,1)S(1)}, bf16[1408,128]{1,0:T(8,128)(2,1)S(1)}, u32[]{:S(2)}, u32[]{:S(2)}) %collective-permute-start.8) | collective-permute-done | bytes 360480 | tf_op jit(solution)/shard_map/ppermute | solution.py:28
  31.1 3.1 %collective-permute-done.6 = bf16[1408,128]{1,0:T(8,128)(2,1)S(1)} collective-permute-done((bf16[1408,128]{1,0:T(8,128)(2,1)S(1)}, bf16[1408,128]{1,0:T(8,128)(2,1)S(1)}, u32[]{:S(2)}, u32[]{:S(2)}) %collective-permute-start.6) | collective-permute-done | bytes 360480 | tf_op jit(solution)/shard_map/ppermute | solution.py:28
  34.4 2.0 %collective-permute-done.9 = bf16[704,128]{1,0:T(8,128)(2,1)S(1)} collective-permute-done((bf16[704,128]{1,0:T(8,128)(2,1)S(1)}, bf16[704,128]{1,0:T(8,128)(2,1)S(1)}, u32[]{:S(2)}, u32[]{:S(2)}) %collective-permute-start.9) | collective-permute-done | bytes 180256 | tf_op jit(solution)/shard_map/ppermute | solution.py:28
  36.4 4.7 %collective-permute-done.7 = bf16[704,128]{1,0:T(8,128)(2,1)S(1)} collective-permute-done((bf16[704,128]{1,0:T(8,128)(2,1)S(1)}, bf16[704,128]{1,0:T(8,128)(2,1)S(1)}, u32[]{:S(2)}, u32[]{:S(2)}) %collective-permute-start.7) | collective-permute-done | bytes 180256 | tf_op jit(solution)/shard_map/ppermute | solution.py:28
  41.6 3.6 %collective-permute-start.11 = (bf16[176,256]{1,0:T(8,128)(2,1)S(1)}, bf16[176,256]{1,0:T(8,128)(2,1)S(1)}, u32[]{:S(2)}, u32[]{:S(2)}) collective-permute-start(bf16[176,256]{1,0:T(8,128)(2,1)S(1)} %get-tuple-element.51), channel_id=1, source_target_pairs={{0,56},{1,57},{2,58},{3,59},{4,60},{5,61},{6,62},{7,63},{8,16},{9,... | collective-permute-start | bytes 270344 | tf_op jit(solution)/shard_map/ppermute | solution.py:28
  45.1 4.5 %collective-permute-start.14 = (bf16[88,256]{1,0:T(8,128)(2,1)S(1)}, bf16[88,256]{1,0:T(8,128)(2,1)S(1)}, u32[]{:S(2)}, u32[]{:S(2)}) collective-permute-start(bf16[88,256]{1,0:T(8,128)(2,1)S(1)} %slice.99), channel_id=1, source_target_pairs={{0,32},{1,33},{2,34},{3,35},{4,36},{5,37},{6,38},{7,39},{8,40},{9,... | collective-permute-start | bytes 135176 | tf_op jit(solution)/shard_map/ppermute | solution.py:28
  49.7 2.2 %collective-permute-start.12 = (bf16[88,256]{1,0:T(8,128)(2,1)S(1)}, bf16[88,256]{1,0:T(8,128)(2,1)S(1)}, u32[]{:S(2)}, u32[]{:S(2)}) collective-permute-start(bf16[88,256]{1,0:T(8,128)(2,1)S(1)} %get-tuple-element.44), channel_id=1, source_target_pairs={{0,16},{1,17},{2,18},{3,19},{4,20},{5,21},{6,22},{7,23},{8,24},{9,... | collective-permute-start | bytes 135176 | tf_op jit(solution)/shard_map/ppermute | solution.py:28
  51.9 2.2 %collective-permute-start.13 = (bf16[88,256]{1,0:T(8,128)(2,1)S(1)}, bf16[88,256]{1,0:T(8,128)(2,1)S(1)}, u32[]{:S(2)}, u32[]{:S(2)}) collective-permute-start(bf16[88,256]{1,0:T(8,128)(2,1)S(1)} %get-tuple-element.45), channel_id=1, source_target_pairs={{0,48},{1,49},{2,50},{3,51},{4,52},{5,53},{6,54},{7,55},{8,56},{9,... | collective-permute-start | bytes 135176 | tf_op jit(solution)/shard_map/ppermute | solution.py:28
  54.8 3.5 %collective-permute-done.13 = bf16[88,256]{1,0:T(8,128)(2,1)S(1)} collective-permute-done((bf16[88,256]{1,0:T(8,128)(2,1)S(1)}, bf16[88,256]{1,0:T(8,128)(2,1)S(1)}, u32[]{:S(2)}, u32[]{:S(2)}) %collective-permute-start.13) | collective-permute-done | bytes 45088 | tf_op jit(solution)/shard_map/ppermute | solution.py:28
  58.4 1.2 %collective-permute-done.15 = f32[43,256]{1,0:T(8,128)S(1)} collective-permute-done((f32[43,256]{1,0:T(8,128)S(1)}, f32[43,256]{1,0:T(8,128)S(1)}, u32[]{:S(2)}, u32[]{:S(2)}) %collective-permute-start.15) | collective-permute-done | bytes 44064 | tf_op jit(solution)/shard_map/ppermute | solution.py:28
  60.1 2.7 %collective-permute-start.17 = (bf16[43,512]{1,0:T(8,128)(2,1)S(1)}, bf16[43,512]{1,0:T(8,128)(2,1)S(1)}, u32[]{:S(2)}, u32[]{:S(2)}) collective-permute-start(bf16[43,512]{1,0:T(8,128)(2,1)S(1)} %get-tuple-element.41), channel_id=1, source_target_pairs={{0,2},{1,3},{2,0},{3,1},{4,6},{5,7},{6,4},{7,5},{8,10},{9,11},{10,... | collective-permute-start | bytes 132104 | tf_op jit(solution)/shard_map/ppermute | solution.py:28
  62.7 1.8 %collective-permute-start.18 = (bf16[43,512]{1,0:T(8,128)(2,1)S(1)}, bf16[43,512]{1,0:T(8,128)(2,1)S(1)}, u32[]{:S(2)}, u32[]{:S(2)}) collective-permute-start(bf16[43,512]{1,0:T(8,128)(2,1)S(1)} %get-tuple-element.41), channel_id=1, source_target_pairs={{0,3},{1,2},{2,1},{3,0},{4,7},{5,6},{6,5},{7,4},{8,11},{9,10},{10,... | collective-permute-start | bytes 132104 | tf_op jit(solution)/shard_map/ppermute | solution.py:28
  65.3 0.7 %copy.17 = f32[1,43,512]{2,0,1:T(1,128)} copy(f32[1,43,512]{2,1,0:T(8,128)S(1)} %get-tuple-element.43) | data formatting | bytes 176128
  66.0 2.0 %collective-permute-done.18 = bf16[43,512]{1,0:T(8,128)(2,1)S(1)} collective-permute-done((bf16[43,512]{1,0:T(8,128)(2,1)S(1)}, bf16[43,512]{1,0:T(8,128)(2,1)S(1)}, u32[]{:S(2)}, u32[]{:S(2)}) %collective-permute-start.18) | collective-permute-done | bytes 44064 | tf_op jit(solution)/shard_map/ppermute | solution.py:28
  68.8 0.9 %convert_element_type.116 = bf16[43,4,1024]{2,1,0:T(4,128)(2,1)} reshape(bf16[172,1024]{1,0:T(8,128)(2,1)S(1)} %convolution_convert_fusion.2) | data formatting | bytes 704512 | tf_op jit(solution)/shard_map/convert_element_type | solution.py:159
  (69 shorter events, 9.0 us)
Async XLA Ops:
  0.6 3.5 %copy-start.2 = (bf16[1,256,1024]{2,1,0:T(8,128)(2,1)S(1)}, bf16[1,256,1024]{2,1,0:T(8,128)(2,1)}, u32[]{:S(2)}) copy-start(bf16[1,256,1024]{2,1,0:T(8,128)(2,1)} %param.7) | copy-start | bytes 1572868
  0.7 12.6 %collective-permute-start.3 = (bf16[2752,256]{1,0:T(8,128)(2,1)}, bf16[2752,256]{1,0:T(8,128)(2,1)}, u32[]{:S(2)}, u32[]{:S(2)}) collective-permute-start(bf16[2752,256]{1,0:T(8,128)(2,1)} %bitcast.49), channel_id=1, source_target_pairs={{0,4},{1,5},{2,6},{3,7},{4,0},{5,1},{6,2},{7,3},{8,12},{9,13},{10,... | collective-permute-start | bytes 4227080 | tf_op jit(solution)/shard_map/ppermute | solution.py:28
  3.2 4.8 %copy-start.5 = (s32[8]{0:T(128)S(1)}, s32[8]{0:T(128)}, u32[]{:S(2)}) copy-start(s32[8]{0:T(128)} %constant.54.clone) | copy-start | bytes 100
  3.2 1.4 %collective-permute-start = (bf16[256,256]{1,0:T(8,128)(2,1)S(1)}, bf16[256,256]{1,0:T(8,128)(2,1)S(1)}, u32[]{:S(2)}, u32[]{:S(2)}) collective-permute-start(bf16[256,256]{1,0:T(8,128)(2,1)S(1)} %fusion), channel_id=1, source_target_pairs={{0,4},{1,5},{2,6},{3,7},{4,0},{5,1},{6,2},{7,3},{8,12},{9,13},{10,... | collective-permute-start | bytes 393224 | tf_op jit(solution)/shard_map/ppermute | solution.py:28
  4.7 10.5 %copy-start.1 = (bf16[1,256,2752]{1,2,0:T(8,128)(2,1)S(1)}, bf16[1,256,2752]{1,2,0:T(8,128)(2,1)}, u32[]{:S(2)}) copy-start(bf16[1,256,2752]{1,2,0:T(8,128)(2,1)} %param.8) | copy-start | bytes 4227076
  4.7 7.0 %collective-permute-start.2 = (bf16[512,128]{1,0:T(8,128)(2,1)S(1)}, bf16[512,128]{1,0:T(8,128)(2,1)S(1)}, u32[]{:S(2)}, u32[]{:S(2)}) collective-permute-start(bf16[512,128]{1,0:T(8,128)(2,1)S(1)} %get-tuple-element.48), channel_id=1, source_target_pairs={{0,3},{1,2},{2,1},{3,0},{4,7},{5,6},{6,5},{7,4},{8,11},{9,10},{10,... | collective-permute-start | bytes 393224 | tf_op jit(solution)/shard_map/ppermute | solution.py:28
  7.8 5.4 %collective-permute-start.1 = (bf16[512,128]{1,0:T(8,128)(2,1)S(1)}, bf16[512,128]{1,0:T(8,128)(2,1)S(1)}, u32[]{:S(2)}, u32[]{:S(2)}) collective-permute-start(bf16[512,128]{1,0:T(8,128)(2,1)S(1)} %get-tuple-element.49), channel_id=1, source_target_pairs={{0,1},{1,0},{2,3},{3,2},{4,5},{5,4},{6,7},{7,6},{8,9},{9,8},{10,11... | collective-permute-start | bytes 393224 | tf_op jit(solution)/shard_map/ppermute | solution.py:28
  13.3 6.3 %collective-permute-start.4 = (bf16[512,128]{1,0:T(8,128)(2,1)S(1)}, bf16[512,128]{1,0:T(8,128)(2,1)S(1)}, u32[]{:S(2)}, u32[]{:S(2)}) collective-permute-start(bf16[512,128]{1,0:T(8,128)(2,1)S(1)} %convert_element_type.95), channel_id=1, source_target_pairs={{0,3},{1,2},{2,1},{3,0},{4,7},{5,6},{6,5},{7,4},{8,11},{9,10},{10,... | collective-permute-start | bytes 393224 | tf_op jit(solution)/shard_map/ppermute | solution.py:28
  15.1 5.1 %collective-permute-start.5 = (bf16[512,128]{1,0:T(8,128)(2,1)S(1)}, bf16[512,128]{1,0:T(8,128)(2,1)S(1)}, u32[]{:S(2)}, u32[]{:S(2)}) collective-permute-start(bf16[512,128]{1,0:T(8,128)(2,1)S(1)} %convert_element_type.98), channel_id=1, source_target_pairs={{0,1},{1,0},{2,3},{3,2},{4,5},{5,4},{6,7},{7,6},{8,9},{9,8},{10,11... | collective-permute-start | bytes 393224 | tf_op jit(solution)/shard_map/ppermute | solution.py:28
  20.7 9.9 %collective-permute-start.8 = (bf16[1408,128]{1,0:T(8,128)(2,1)S(1)}, bf16[1408,128]{1,0:T(8,128)(2,1)S(1)}, u32[]{:S(2)}, u32[]{:S(2)}) collective-permute-start(bf16[1408,128]{1,0:T(8,128)(2,1)S(1)} %convolution_convert_fusion), channel_id=1, source_target_pairs={{0,192},{1,193},{2,194},{3,195},{4,196},{5,197},{6,198},{7,199},{8... | collective-permute-start | bytes 1081352 | tf_op jit(solution)/shard_map/ppermute | solution.py:28
  24.1 10.1 %collective-permute-start.6 = (bf16[1408,128]{1,0:T(8,128)(2,1)S(1)}, bf16[1408,128]{1,0:T(8,128)(2,1)S(1)}, u32[]{:S(2)}, u32[]{:S(2)}) collective-permute-start(bf16[1408,128]{1,0:T(8,128)(2,1)S(1)} %convolution_convert_fusion.1), channel_id=1, source_target_pairs={{0,64},{1,65},{2,66},{3,67},{4,68},{5,69},{6,70},{7,71},{8,72},{9,... | collective-permute-start | bytes 1081352 | tf_op jit(solution)/shard_map/ppermute | solution.py:28
  30.7 5.7 %collective-permute-start.9 = (bf16[704,128]{1,0:T(8,128)(2,1)S(1)}, bf16[704,128]{1,0:T(8,128)(2,1)S(1)}, u32[]{:S(2)}, u32[]{:S(2)}) collective-permute-start(bf16[704,128]{1,0:T(8,128)(2,1)S(1)} %slice.192), channel_id=1, source_target_pairs={{0,64},{1,65},{2,66},{3,67},{4,68},{5,69},{6,70},{7,71},{8,72},{9,... | collective-permute-start | bytes 540680 | tf_op jit(solution)/shard_map/ppermute | solution.py:28
  34.3 6.8 %collective-permute-start.7 = (bf16[704,128]{1,0:T(8,128)(2,1)S(1)}, bf16[704,128]{1,0:T(8,128)(2,1)S(1)}, u32[]{:S(2)}, u32[]{:S(2)}) collective-permute-start(bf16[704,128]{1,0:T(8,128)(2,1)S(1)} %slice.193), channel_id=1, source_target_pairs={{0,192},{1,193},{2,194},{3,195},{4,196},{5,197},{6,198},{7,199},{8... | collective-permute-start | bytes 540680 | tf_op jit(solution)/shard_map/ppermute | solution.py:28
  41.2 8.4 %collective-permute-start.10 = (bf16[176,256]{1,0:T(8,128)(2,1)S(1)}, bf16[176,256]{1,0:T(8,128)(2,1)S(1)}, u32[]{:S(2)}, u32[]{:S(2)}) collective-permute-start(bf16[176,256]{1,0:T(8,128)(2,1)S(1)} %get-tuple-element.50), channel_id=1, source_target_pairs={{0,8},{1,9},{2,10},{3,11},{4,12},{5,13},{6,14},{7,15},{8,0},{9,1},... | collective-permute-start | bytes 270344 | tf_op jit(solution)/shard_map/ppermute | solution.py:28
  41.6 8.1 %collective-permute-start.11 = (bf16[176,256]{1,0:T(8,128)(2,1)S(1)}, bf16[176,256]{1,0:T(8,128)(2,1)S(1)}, u32[]{:S(2)}, u32[]{:S(2)}) collective-permute-start(bf16[176,256]{1,0:T(8,128)(2,1)S(1)} %get-tuple-element.51), channel_id=1, source_target_pairs={{0,56},{1,57},{2,58},{3,59},{4,60},{5,61},{6,62},{7,63},{8,16},{9,... | collective-permute-start | bytes 270344 | tf_op jit(solution)/shard_map/ppermute | solution.py:28
  45.1 8.9 %collective-permute-start.14 = (bf16[88,256]{1,0:T(8,128)(2,1)S(1)}, bf16[88,256]{1,0:T(8,128)(2,1)S(1)}, u32[]{:S(2)}, u32[]{:S(2)}) collective-permute-start(bf16[88,256]{1,0:T(8,128)(2,1)S(1)} %slice.99), channel_id=1, source_target_pairs={{0,32},{1,33},{2,34},{3,35},{4,36},{5,37},{6,38},{7,39},{8,40},{9,... | collective-permute-start | bytes 135176 | tf_op jit(solution)/shard_map/ppermute | solution.py:28
  49.6 10.0 %copy-start.3 = (f32[1,43,512]{2,0,1:T(1,128)S(1)}, f32[1,43,512]{2,0,1:T(1,128)}, u32[]{:S(2)}) copy-start(f32[1,43,512]{2,0,1:T(1,128)} %param.11) | copy-start | bytes 264196
  49.6 10.0 %copy-start.4 = (f32[1,43,512]{2,0,1:T(1,128)S(1)}, f32[1,43,512]{2,0,1:T(1,128)}, u32[]{:S(2)}) copy-start(f32[1,43,512]{2,0,1:T(1,128)} %param.10) | copy-start | bytes 264196
  49.7 5.0 %collective-permute-start.12 = (bf16[88,256]{1,0:T(8,128)(2,1)S(1)}, bf16[88,256]{1,0:T(8,128)(2,1)S(1)}, u32[]{:S(2)}, u32[]{:S(2)}) collective-permute-start(bf16[88,256]{1,0:T(8,128)(2,1)S(1)} %get-tuple-element.44), channel_id=1, source_target_pairs={{0,16},{1,17},{2,18},{3,19},{4,20},{5,21},{6,22},{7,23},{8,24},{9,... | collective-permute-start | bytes 135176 | tf_op jit(solution)/shard_map/ppermute | solution.py:28
  51.9 6.4 %collective-permute-start.13 = (bf16[88,256]{1,0:T(8,128)(2,1)S(1)}, bf16[88,256]{1,0:T(8,128)(2,1)S(1)}, u32[]{:S(2)}, u32[]{:S(2)}) collective-permute-start(bf16[88,256]{1,0:T(8,128)(2,1)S(1)} %get-tuple-element.45), channel_id=1, source_target_pairs={{0,48},{1,49},{2,50},{3,51},{4,52},{5,53},{6,54},{7,55},{8,56},{9,... | collective-permute-start | bytes 135176 | tf_op jit(solution)/shard_map/ppermute | solution.py:28
  58.3 1.3 %collective-permute-start.15 = (f32[43,256]{1,0:T(8,128)S(1)}, f32[43,256]{1,0:T(8,128)S(1)}, u32[]{:S(2)}, u32[]{:S(2)}) collective-permute-start(f32[43,256]{1,0:T(8,128)S(1)} %slice_select_fusion), channel_id=1, source_target_pairs={{0,4},{1,5},{2,6},{3,7},{4,0},{5,1},{6,2},{7,3},{8,12},{9,13},{10,... | collective-permute-start | bytes 132104 | tf_op jit(solution)/shard_map/ppermute | solution.py:28
  59.8 6.2 %collective-permute-start.16 = (bf16[43,512]{1,0:T(8,128)(2,1)S(1)}, bf16[43,512]{1,0:T(8,128)(2,1)S(1)}, u32[]{:S(2)}, u32[]{:S(2)}) collective-permute-start(bf16[43,512]{1,0:T(8,128)(2,1)S(1)} %get-tuple-element.41), channel_id=1, source_target_pairs={{0,1},{1,0},{2,3},{3,2},{4,5},{5,4},{6,7},{7,6},{8,9},{9,8},{10,11... | collective-permute-start | bytes 132104 | tf_op jit(solution)/shard_map/ppermute | solution.py:28
  60.1 6.0 %collective-permute-start.17 = (bf16[43,512]{1,0:T(8,128)(2,1)S(1)}, bf16[43,512]{1,0:T(8,128)(2,1)S(1)}, u32[]{:S(2)}, u32[]{:S(2)}) collective-permute-start(bf16[43,512]{1,0:T(8,128)(2,1)S(1)} %get-tuple-element.41), channel_id=1, source_target_pairs={{0,2},{1,3},{2,0},{3,1},{4,6},{5,7},{6,4},{7,5},{8,10},{9,11},{10,... | collective-permute-start | bytes 132104 | tf_op jit(solution)/shard_map/ppermute | solution.py:28
  62.7 5.3 %collective-permute-start.18 = (bf16[43,512]{1,0:T(8,128)(2,1)S(1)}, bf16[43,512]{1,0:T(8,128)(2,1)S(1)}, u32[]{:S(2)}, u32[]{:S(2)}) collective-permute-start(bf16[43,512]{1,0:T(8,128)(2,1)S(1)} %get-tuple-element.41), channel_id=1, source_target_pairs={{0,3},{1,2},{2,1},{3,0},{4,7},{5,6},{6,5},{7,4},{8,11},{9,10},{10,... | collective-permute-start | bytes 132104 | tf_op jit(solution)/shard_map/ppermute | solution.py:28
  (1 other events, 1.2 us)

commit v10 on v9

--- a/solution.py
+++ b/solution.py
@@ -8,7 +8,7 @@
 
 NX, NZ, NCORE, NY = 4, 8, 2, 4
 OWNED = 43
-CHUNKS = 2
+CHUNKS, PIECES = 2, 4
 CHIP, PADDED = NCORE * OWNED, 88
 BF, F32 = jnp.bfloat16, jnp.float32
 
@@ -85,6 +85,56 @@
     )(order, own, came)
 
 
+def project_kernel(core_ref, features, basis, own, theirs, f_buf, b_buf, total, sems):
+    pieces, tokens, depth = f_buf.shape
+    lanes = own.shape[1]
+    copies = []
+    for k in range(pieces):
+        part = pl.ds(k * depth, depth)
+        copies.append(pltpu.make_async_copy(features.at[:, part], f_buf.at[k], sems.at[0, k]))
+        copies.append(pltpu.make_async_copy(basis.at[part, :], b_buf.at[k], sems.at[1, k]))
+    for copy in copies:
+        copy.start()
+    for k in range(pieces):
+        copies[2 * k].wait()
+        copies[2 * k + 1].wait()
+        term = jnp.dot(f_buf[k], b_buf[k], preferred_element_type=F32)
+        total[...] = term if k == 0 else total[...] + term
+    for core in range(NCORE):
+
+        @pl.when(core_ref[0] == core)
+        def _(core=core):
+            own[...] = total[:, core * lanes : (core + 1) * lanes]
+            theirs[...] = total[:, (1 - core) * lanes : (2 - core) * lanes].astype(BF)
+
+
+def project(core, features, basis):
+    tokens, depth = features.shape
+    rank = basis.shape[1]
+    step = depth // PIECES
+    vmem = pl.BlockSpec(memory_space=pltpu.VMEM)
+    hbm = pl.BlockSpec(memory_space=pltpu.HBM)
+    return pl.pallas_call(
+        project_kernel,
+        out_shape=[
+            jax.ShapeDtypeStruct((tokens, rank // NCORE), F32),
+            jax.ShapeDtypeStruct((tokens, rank // NCORE), BF),
+        ],
+        in_specs=[pl.BlockSpec(memory_space=pltpu.SMEM), hbm, hbm],
+        out_specs=[vmem] * 2,
+        scratch_shapes=[
+            pltpu.VMEM((PIECES, tokens, step), BF),
+            pltpu.VMEM((PIECES, step, rank), BF),
+            pltpu.VMEM((tokens, rank), F32),
+            pltpu.SemaphoreType.DMA((2, PIECES)),
+        ],
+        compiler_params=pltpu.CompilerParams(vmem_limit_bytes=8 * 1024 * 1024),
+        cost_estimate=pl.CostEstimate(
+            flops=2 * tokens * depth * rank, bytes_accessed=3 * 1024 * 1024, transcendentals=0
+        ),
+    )(core, features, basis)
+
+
 def dot(a, b):
     out = lax.dot_general(a, b, (((1,), (0,)), ((), ())), preferred_element_type=F32)
     return with_layout_constraint(out, Layout(major_to_minor=(0, 1)))
@@ -104,11 +154,8 @@
     blocks_x = x ^ jnp.array(X_ORDER, jnp.int32).reshape(-1)
     order = (blocks_x[:, None] * NZ + blocks_z[None, :]).reshape(-1)
 
-    def lanes_of(c):
-        return lax.dynamic_slice(basis[0], (0, c * lanes), (basis.shape[1], lanes))
-
-    theirs = swap_core(dot(features[0], lanes_of(1 - core)).astype(BF))
-    partial = jnp.concatenate([dot(features[0], lanes_of(core)), theirs.astype(F32)], axis=0)
+    own, theirs = project(core.reshape(1), features[0], basis[0])
+    partial = jnp.concatenate([own, swap_core(theirs).astype(F32)], axis=0)
     width = lanes // CHUNKS
     chunks = [partial[:, c * width : (c + 1) * width] for c in range(CHUNKS)]
     chunks = [p + swap_y(p.astype(BF), m[0]).astype(F32) for p, m in zip(chunks, PAIRS)]
@@ -152,7 +199,9 @@
         new_first / (1.0 - 0.9**10) / (jnp.sqrt(new_second / (1.0 - 0.999**10)) + 1e-08)
     ).astype(BF)[0]
 
-    around = [update] + [swap_y(update, m) for m in (1, 2, 3)]
+    around = [update]
+    for m, more in ((1, 0), (2, 5), (3, 21)):
+        around.append(swap_y(jnp.pad(update, ((0, more), (0, 0))), m)[:OWNED])
     ordered = jnp.stack([lax.select_n(y ^ a, *around) for a in range(NY)], axis=1)
     rows = lax.optimization_barrier(ordered.reshape(-1, ordered.shape[2]))
     change = dot(rows, basis[0].T).reshape(OWNED, NY, -1)

time: 70.1 us -> 70.2 us (level)
  matrix products: 4.27 us -> 2.62 us
  local copies, waits for them, and re-layouts: 3.88 us -> 5.08 us
  waiting for transfers between devices: 30.3 us -> 31.5 us
    dot_general x7 -> x5, matrix products: 4.27 us -> 2.62 us  [dot(): lax.dot_general(a, b, (((1,), (0,)), ((), ())), preferred_element_type=F32)]
    unnamed x14 -> x22, local copies, waits for them, and re-layouts: 2.59 us -> 3.77 us
    ppermute x19, waiting for transfers between devices: 30.3 us -> 31.5 us  [send(): return lax.ppermute(value, ('dp', 'tensor'), pairs)]
    pallas_call x0 -> x1, Pallas kernels: none -> 0.83 us  [project(): pl.pallas_call(project_kernel, out_shape=[jax.ShapeDtypeStruct((tokens, r...]
    pallas_call x1, Pallas kernels: 2.39 us -> 1.57 us  [arrange(): pl.pallas_call(arrange_kernel, out_shape=[shape] * 2 * CHUNKS, in_specs=[...]
  transfers between devices with their start and end apart: 19 -> 19, of which waited for: 13 -> 14; matrix products, arithmetic and copies ran while one was open for 9% -> 5% of each run, Pallas kernels for 3% -> 3%
where the time goes in v10:
time: 70.2 us; the launch traced here: 69.6 us
  waiting for transfers between devices  31.5 us (45%)
  starting transfers between devices  26.2 us (37%)
  local copies, waits for them, and re-layouts  5.08 us (7%)
  matrix products  2.62 us (4%)
  Pallas kernels  2.4 us (3%)
  between operations  1.01 us (1%)
  other arithmetic  0.8 us (1%)
    ppermute x19, waiting for transfers between devices, send(): return lax.ppermute(value, ('dp', 'tensor'), pairs)  31.5 us
    ppermute x19, starting transfers between devices, send(): return lax.ppermute(value, ('dp', 'tensor'), pairs)  26.2 us
    unnamed x22, local copies, waits for them, and re-layouts  3.77 us
    dot_general x5, matrix products, dot(): lax.dot_general(a, b, (((1,), (0,)), ((), ())), preferred_element_type=F32)  2.62 us
    pallas_call x1, Pallas kernels, arrange(): pl.pallas_call(arrange_kernel, out_shape=[shape] * 2 * CHUNKS, in_specs=[...  1.57 us
  transfers between devices with their start and end apart: 19, of which 14 were waited for; matrix products, arithmetic and copies ran while one was open for 5% of the time, Pallas kernels for 3%

profile of v10, /device:TPU:32, one launch (start us, length us, event | category | flops | bytes accessed | tf_op | source)
XLA Modules:
  0.0 69.6 jit_solution(7740498358888213330)
XLA Ops:
  0.8 1.2 %copy-done = bf16[1,1024,512]{2,1,0:T(8,128)(2,1)S(1)} copy-done((bf16[1,1024,512]{2,1,0:T(8,128)(2,1)S(1)}, bf16[1,1024,512]{2,1,0:T(8,128)(2,1)}, u32[]{:S(2)}) %copy-start) | copy-done | bytes 1048600
  2.0 1.0 %copy-done.3 = bf16[1,256,1024]{2,1,0:T(8,128)(2,1)S(1)} copy-done((bf16[1,256,1024]{2,1,0:T(8,128)(2,1)S(1)}, bf16[1,256,1024]{2,1,0:T(8,128)(2,1)}, u32[]{:S(2)}) %copy-start.3) | copy-done | bytes 524312
  4.5 0.9 %collective-permute-done = bf16[256,256]{1,0:T(8,128)(2,1)S(1)} collective-permute-done((bf16[256,256]{1,0:T(8,128)(2,1)S(1)}, bf16[256,256]{1,0:T(8,128)(2,1)S(1)}, u32[]{:S(2)}, u32[]{:S(2)}) %collective-permute-start) | collective-permute-done | bytes 131104 | tf_op jit(solution)/shard_map/ppermute | solution.py:28
  5.5 3.1 %collective-permute-start.2 = (bf16[512,128]{1,0:T(8,128)(2,1)S(1)}, bf16[512,128]{1,0:T(8,128)(2,1)S(1)}, u32[]{:S(2)}, u32[]{:S(2)}) collective-permute-start(bf16[512,128]{1,0:T(8,128)(2,1)S(1)} %get-tuple-element.52), channel_id=1, source_target_pairs={{0,3},{1,2},{2,1},{3,0},{4,7},{5,6},{6,5},{7,4},{8,11},{9,10},{10,... | collective-permute-start | bytes 393224 | tf_op jit(solution)/shard_map/ppermute | solution.py:28
  8.8 3.9 %collective-permute-done.2 = bf16[512,128]{1,0:T(8,128)(2,1)S(1)} collective-permute-done((bf16[512,128]{1,0:T(8,128)(2,1)S(1)}, bf16[512,128]{1,0:T(8,128)(2,1)S(1)}, u32[]{:S(2)}, u32[]{:S(2)}) %collective-permute-start.2) | collective-permute-done | bytes 131104 | tf_op jit(solution)/shard_map/ppermute | solution.py:28
  12.6 1.5 %collective-permute-done.1 = bf16[512,128]{1,0:T(8,128)(2,1)S(1)} collective-permute-done((bf16[512,128]{1,0:T(8,128)(2,1)S(1)}, bf16[512,128]{1,0:T(8,128)(2,1)S(1)}, u32[]{:S(2)}, u32[]{:S(2)}) %collective-permute-start.1) | collective-permute-done | bytes 131104 | tf_op jit(solution)/shard_map/ppermute | solution.py:28
  14.2 1.6 %collective-permute-start.4 = (bf16[512,128]{1,0:T(8,128)(2,1)S(1)}, bf16[512,128]{1,0:T(8,128)(2,1)S(1)}, u32[]{:S(2)}, u32[]{:S(2)}) collective-permute-start(bf16[512,128]{1,0:T(8,128)(2,1)S(1)} %convert_element_type.95), channel_id=1, source_target_pairs={{0,3},{1,2},{2,1},{3,0},{4,7},{5,6},{6,5},{7,4},{8,11},{9,10},{10,... | collective-permute-start | bytes 393224 | tf_op jit(solution)/shard_map/ppermute | solution.py:28
  16.1 1.6 %shard_map.95 = (bf16[1408,512]{1,0:T(8,128)(2,1)S(1)}, bf16[1408,512]{1,0:T(8,128)(2,1)S(1)}, bf16[1408,512]{1,0:T(8,128)(2,1)S(1)}, bf16[1408,512]{1,0:T(8,128)(2,1)S(1)}) custom-call(s32[64]{0:T(128)S(1)} %add.92.order_ref, bf16[2752,256]{1,0:T(8,128)(2,1)S(1)} %bitcast.36, bf16[2752,256]{1,0:T(8,128)(2,1)S(1)} %collective-permute-done.3.came), custom_call_target="tpu_custom_call" | custom-call | bytes 8388608 | tf_op jit(solution)/shard_map/pallas_call | solution.py:77
  17.7 2.8 %collective-permute-done.4 = bf16[512,128]{1,0:T(8,128)(2,1)S(1)} collective-permute-done((bf16[512,128]{1,0:T(8,128)(2,1)S(1)}, bf16[512,128]{1,0:T(8,128)(2,1)S(1)}, u32[]{:S(2)}, u32[]{:S(2)}) %collective-permute-start.4) | collective-permute-done | bytes 131104 | tf_op jit(solution)/shard_map/ppermute | solution.py:28
  21.6 2.9 %collective-permute-start.8 = (bf16[1408,128]{1,0:T(8,128)(2,1)S(1)}, bf16[1408,128]{1,0:T(8,128)(2,1)S(1)}, u32[]{:S(2)}, u32[]{:S(2)}) collective-permute-start(bf16[1408,128]{1,0:T(8,128)(2,1)S(1)} %convolution_convert_fusion), channel_id=1, source_target_pairs={{0,192},{1,193},{2,194},{3,195},{4,196},{5,197},{6,198},{7,199},{8... | collective-permute-start | bytes 1081352 | tf_op jit(solution)/shard_map/ppermute | solution.py:28
  26.4 5.3 %collective-permute-done.8 = bf16[1408,128]{1,0:T(8,128)(2,1)S(1)} collective-permute-done((bf16[1408,128]{1,0:T(8,128)(2,1)S(1)}, bf16[1408,128]{1,0:T(8,128)(2,1)S(1)}, u32[]{:S(2)}, u32[]{:S(2)}) %collective-permute-start.8) | collective-permute-done | bytes 360480 | tf_op jit(solution)/shard_map/ppermute | solution.py:28
  32.1 3.0 %collective-permute-done.6 = bf16[1408,128]{1,0:T(8,128)(2,1)S(1)} collective-permute-done((bf16[1408,128]{1,0:T(8,128)(2,1)S(1)}, bf16[1408,128]{1,0:T(8,128)(2,1)S(1)}, u32[]{:S(2)}, u32[]{:S(2)}) %collective-permute-start.6) | collective-permute-done | bytes 360480 | tf_op jit(solution)/shard_map/ppermute | solution.py:28
  35.3 2.1 %collective-permute-done.9 = bf16[704,128]{1,0:T(8,128)(2,1)S(1)} collective-permute-done((bf16[704,128]{1,0:T(8,128)(2,1)S(1)}, bf16[704,128]{1,0:T(8,128)(2,1)S(1)}, u32[]{:S(2)}, u32[]{:S(2)}) %collective-permute-start.9) | collective-permute-done | bytes 180256 | tf_op jit(solution)/shard_map/ppermute | solution.py:28
  37.4 4.6 %collective-permute-done.7 = bf16[704,128]{1,0:T(8,128)(2,1)S(1)} collective-permute-done((bf16[704,128]{1,0:T(8,128)(2,1)S(1)}, bf16[704,128]{1,0:T(8,128)(2,1)S(1)}, u32[]{:S(2)}, u32[]{:S(2)}) %collective-permute-start.7) | collective-permute-done | bytes 180256 | tf_op jit(solution)/shard_map/ppermute | solution.py:28
  42.5 3.5 %collective-permute-start.11 = (bf16[176,256]{1,0:T(8,128)(2,1)S(1)}, bf16[176,256]{1,0:T(8,128)(2,1)S(1)}, u32[]{:S(2)}, u32[]{:S(2)}) collective-permute-start(bf16[176,256]{1,0:T(8,128)(2,1)S(1)} %get-tuple-element.55), channel_id=1, source_target_pairs={{0,56},{1,57},{2,58},{3,59},{4,60},{5,61},{6,62},{7,63},{8,16},{9,... | collective-permute-start | bytes 270344 | tf_op jit(solution)/shard_map/ppermute | solution.py:28
  46.0 4.5 %collective-permute-start.14 = (bf16[88,256]{1,0:T(8,128)(2,1)S(1)}, bf16[88,256]{1,0:T(8,128)(2,1)S(1)}, u32[]{:S(2)}, u32[]{:S(2)}) collective-permute-start(bf16[88,256]{1,0:T(8,128)(2,1)S(1)} %slice.107), channel_id=1, source_target_pairs={{0,32},{1,33},{2,34},{3,35},{4,36},{5,37},{6,38},{7,39},{8,40},{9,... | collective-permute-start | bytes 135176 | tf_op jit(solution)/shard_map/ppermute | solution.py:28
  50.6 2.4 %collective-permute-start.12 = (bf16[88,256]{1,0:T(8,128)(2,1)S(1)}, bf16[88,256]{1,0:T(8,128)(2,1)S(1)}, u32[]{:S(2)}, u32[]{:S(2)}) collective-permute-start(bf16[88,256]{1,0:T(8,128)(2,1)S(1)} %get-tuple-element.48), channel_id=1, source_target_pairs={{0,16},{1,17},{2,18},{3,19},{4,20},{5,21},{6,22},{7,23},{8,24},{9,... | collective-permute-start | bytes 135176 | tf_op jit(solution)/shard_map/ppermute | solution.py:28
  53.0 2.0 %collective-permute-start.13 = (bf16[88,256]{1,0:T(8,128)(2,1)S(1)}, bf16[88,256]{1,0:T(8,128)(2,1)S(1)}, u32[]{:S(2)}, u32[]{:S(2)}) collective-permute-start(bf16[88,256]{1,0:T(8,128)(2,1)S(1)} %get-tuple-element.49), channel_id=1, source_target_pairs={{0,48},{1,49},{2,50},{3,51},{4,52},{5,53},{6,54},{7,55},{8,56},{9,... | collective-permute-start | bytes 135176 | tf_op jit(solution)/shard_map/ppermute | solution.py:28
  55.6 3.6 %collective-permute-done.13 = bf16[88,256]{1,0:T(8,128)(2,1)S(1)} collective-permute-done((bf16[88,256]{1,0:T(8,128)(2,1)S(1)}, bf16[88,256]{1,0:T(8,128)(2,1)S(1)}, u32[]{:S(2)}, u32[]{:S(2)}) %collective-permute-start.13) | collective-permute-done | bytes 45088 | tf_op jit(solution)/shard_map/ppermute | solution.py:28
  59.4 1.2 %collective-permute-done.15 = f32[43,256]{1,0:T(8,128)S(1)} collective-permute-done((f32[43,256]{1,0:T(8,128)S(1)}, f32[43,256]{1,0:T(8,128)S(1)}, u32[]{:S(2)}, u32[]{:S(2)}) %collective-permute-start.15) | collective-permute-done | bytes 44064 | tf_op jit(solution)/shard_map/ppermute | solution.py:28
  60.8 1.6 %collective-permute-start.18 = (bf16[64,512]{1,0:T(8,128)(2,1)S(1)}, bf16[64,512]{1,0:T(8,128)(2,1)S(1)}, u32[]{:S(2)}, u32[]{:S(2)}) collective-permute-start(bf16[64,512]{1,0:T(8,128)(2,1)S(1)} %pad.9), channel_id=1, source_target_pairs={{0,3},{1,2},{2,1},{3,0},{4,7},{5,6},{6,5},{7,4},{8,11},{9,10},{10,... | collective-permute-start | bytes 196616 | tf_op jit(solution)/shard_map/ppermute | solution.py:28
  63.1 1.8 %collective-permute-start.16 = (bf16[43,512]{1,0:T(8,128)(2,1)S(1)}, bf16[43,512]{1,0:T(8,128)(2,1)S(1)}, u32[]{:S(2)}, u32[]{:S(2)}) collective-permute-start(bf16[43,512]{1,0:T(8,128)(2,1)S(1)} %get-tuple-element.45), channel_id=1, source_target_pairs={{0,1},{1,0},{2,3},{3,2},{4,5},{5,4},{6,7},{7,6},{8,9},{9,8},{10,11... | collective-permute-start | bytes 132104 | tf_op jit(solution)/shard_map/ppermute | solution.py:28
  66.4 1.1 %collective-permute-done.16 = bf16[43,512]{1,0:T(8,128)(2,1)S(1)} collective-permute-done((bf16[43,512]{1,0:T(8,128)(2,1)S(1)}, bf16[43,512]{1,0:T(8,128)(2,1)S(1)}, u32[]{:S(2)}, u32[]{:S(2)}) %collective-permute-start.16) | collective-permute-done | bytes 44064 | tf_op jit(solution)/shard_map/ppermute | solution.py:28
  68.7 0.9 %convert_element_type.116 = bf16[43,4,1024]{2,1,0:T(4,128)(2,1)} reshape(bf16[172,1024]{1,0:T(8,128)(2,1)S(1)} %convolution_convert_fusion.2) | data formatting | bytes 704512 | tf_op jit(solution)/shard_map/convert_element_type | solution.py:208
  (79 shorter events, 10.7 us)
Async XLA Ops:
  0.6 8.1 %copy-start.9 = (s32[8]{0:T(128)S(1)}, s32[8]{0:T(128)}, u32[]{:S(2)}) copy-start(s32[8]{0:T(128)} %constant.50.clone) | copy-start | bytes 100
  0.7 13.5 %collective-permute-start.3 = (bf16[2752,256]{1,0:T(8,128)(2,1)}, bf16[2752,256]{1,0:T(8,128)(2,1)S(1)}, u32[]{:S(2)}, u32[]{:S(2)}) collective-permute-start(bf16[2752,256]{1,0:T(8,128)(2,1)} %bitcast.35), channel_id=1, source_target_pairs={{0,4},{1,5},{2,6},{3,7},{4,0},{5,1},{6,2},{7,3},{8,12},{9,13},{10,... | collective-permute-start | bytes 4227080 | tf_op jit(solution)/shard_map/ppermute | solution.py:28
  3.9 1.6 %collective-permute-start = (bf16[256,256]{1,0:T(8,128)(2,1)S(1)}, bf16[256,256]{1,0:T(8,128)(2,1)S(1)}, u32[]{:S(2)}, u32[]{:S(2)}) collective-permute-start(bf16[256,256]{1,0:T(8,128)(2,1)S(1)} %get-tuple-element.22), channel_id=1, source_target_pairs={{0,4},{1,5},{2,6},{3,7},{4,0},{5,1},{6,2},{7,3},{8,12},{9,13},{10,... | collective-permute-start | bytes 393224 | tf_op jit(solution)/shard_map/ppermute | solution.py:28
  5.4 10.6 %copy-start.2 = (bf16[1,256,2752]{1,2,0:T(8,128)(2,1)S(1)}, bf16[1,256,2752]{1,2,0:T(8,128)(2,1)}, u32[]{:S(2)}) copy-start(bf16[1,256,2752]{1,2,0:T(8,128)(2,1)} %param.8) | copy-start | bytes 4227076
  5.5 7.1 %collective-permute-start.2 = (bf16[512,128]{1,0:T(8,128)(2,1)S(1)}, bf16[512,128]{1,0:T(8,128)(2,1)S(1)}, u32[]{:S(2)}, u32[]{:S(2)}) collective-permute-start(bf16[512,128]{1,0:T(8,128)(2,1)S(1)} %get-tuple-element.52), channel_id=1, source_target_pairs={{0,3},{1,2},{2,1},{3,0},{4,7},{5,6},{6,5},{7,4},{8,11},{9,10},{10,... | collective-permute-start | bytes 393224 | tf_op jit(solution)/shard_map/ppermute | solution.py:28
  8.6 5.5 %collective-permute-start.1 = (bf16[512,128]{1,0:T(8,128)(2,1)S(1)}, bf16[512,128]{1,0:T(8,128)(2,1)S(1)}, u32[]{:S(2)}, u32[]{:S(2)}) collective-permute-start(bf16[512,128]{1,0:T(8,128)(2,1)S(1)} %get-tuple-element.53), channel_id=1, source_target_pairs={{0,1},{1,0},{2,3},{3,2},{4,5},{5,4},{6,7},{7,6},{8,9},{9,8},{10,11... | collective-permute-start | bytes 393224 | tf_op jit(solution)/shard_map/ppermute | solution.py:28
  14.2 6.3 %collective-permute-start.4 = (bf16[512,128]{1,0:T(8,128)(2,1)S(1)}, bf16[512,128]{1,0:T(8,128)(2,1)S(1)}, u32[]{:S(2)}, u32[]{:S(2)}) collective-permute-start(bf16[512,128]{1,0:T(8,128)(2,1)S(1)} %convert_element_type.95), channel_id=1, source_target_pairs={{0,3},{1,2},{2,1},{3,0},{4,7},{5,6},{6,5},{7,4},{8,11},{9,10},{10,... | collective-permute-start | bytes 393224 | tf_op jit(solution)/shard_map/ppermute | solution.py:28
  16.0 5.1 %collective-permute-start.5 = (bf16[512,128]{1,0:T(8,128)(2,1)S(1)}, bf16[512,128]{1,0:T(8,128)(2,1)S(1)}, u32[]{:S(2)}, u32[]{:S(2)}) collective-permute-start(bf16[512,128]{1,0:T(8,128)(2,1)S(1)} %convert_element_type.98), channel_id=1, source_target_pairs={{0,1},{1,0},{2,3},{3,2},{4,5},{5,4},{6,7},{7,6},{8,9},{9,8},{10,11... | collective-permute-start | bytes 393224 | tf_op jit(solution)/shard_map/ppermute | solution.py:28
  21.6 10.0 %collective-permute-start.8 = (bf16[1408,128]{1,0:T(8,128)(2,1)S(1)}, bf16[1408,128]{1,0:T(8,128)(2,1)S(1)}, u32[]{:S(2)}, u32[]{:S(2)}) collective-permute-start(bf16[1408,128]{1,0:T(8,128)(2,1)S(1)} %convolution_convert_fusion), channel_id=1, source_target_pairs={{0,192},{1,193},{2,194},{3,195},{4,196},{5,197},{6,198},{7,199},{8... | collective-permute-start | bytes 1081352 | tf_op jit(solution)/shard_map/ppermute | solution.py:28
  25.0 10.1 %collective-permute-start.6 = (bf16[1408,128]{1,0:T(8,128)(2,1)S(1)}, bf16[1408,128]{1,0:T(8,128)(2,1)S(1)}, u32[]{:S(2)}, u32[]{:S(2)}) collective-permute-start(bf16[1408,128]{1,0:T(8,128)(2,1)S(1)} %convolution_convert_fusion.1), channel_id=1, source_target_pairs={{0,64},{1,65},{2,66},{3,67},{4,68},{5,69},{6,70},{7,71},{8,72},{9,... | collective-permute-start | bytes 1081352 | tf_op jit(solution)/shard_map/ppermute | solution.py:28
  31.7 5.7 %collective-permute-start.9 = (bf16[704,128]{1,0:T(8,128)(2,1)S(1)}, bf16[704,128]{1,0:T(8,128)(2,1)S(1)}, u32[]{:S(2)}, u32[]{:S(2)}) collective-permute-start(bf16[704,128]{1,0:T(8,128)(2,1)S(1)} %slice.210), channel_id=1, source_target_pairs={{0,64},{1,65},{2,66},{3,67},{4,68},{5,69},{6,70},{7,71},{8,72},{9,... | collective-permute-start | bytes 540680 | tf_op jit(solution)/shard_map/ppermute | solution.py:28
  35.2 6.8 %collective-permute-start.7 = (bf16[704,128]{1,0:T(8,128)(2,1)S(1)}, bf16[704,128]{1,0:T(8,128)(2,1)S(1)}, u32[]{:S(2)}, u32[]{:S(2)}) collective-permute-start(bf16[704,128]{1,0:T(8,128)(2,1)S(1)} %slice.211), channel_id=1, source_target_pairs={{0,192},{1,193},{2,194},{3,195},{4,196},{5,197},{6,198},{7,199},{8... | collective-permute-start | bytes 540680 | tf_op jit(solution)/shard_map/ppermute | solution.py:28
  42.1 8.4 %collective-permute-start.10 = (bf16[176,256]{1,0:T(8,128)(2,1)S(1)}, bf16[176,256]{1,0:T(8,128)(2,1)S(1)}, u32[]{:S(2)}, u32[]{:S(2)}) collective-permute-start(bf16[176,256]{1,0:T(8,128)(2,1)S(1)} %get-tuple-element.54), channel_id=1, source_target_pairs={{0,8},{1,9},{2,10},{3,11},{4,12},{5,13},{6,14},{7,15},{8,0},{9,1},... | collective-permute-start | bytes 270344 | tf_op jit(solution)/shard_map/ppermute | solution.py:28
  42.5 8.1 %collective-permute-start.11 = (bf16[176,256]{1,0:T(8,128)(2,1)S(1)}, bf16[176,256]{1,0:T(8,128)(2,1)S(1)}, u32[]{:S(2)}, u32[]{:S(2)}) collective-permute-start(bf16[176,256]{1,0:T(8,128)(2,1)S(1)} %get-tuple-element.55), channel_id=1, source_target_pairs={{0,56},{1,57},{2,58},{3,59},{4,60},{5,61},{6,62},{7,63},{8,16},{9,... | collective-permute-start | bytes 270344 | tf_op jit(solution)/shard_map/ppermute | solution.py:28
  46.0 8.9 %collective-permute-start.14 = (bf16[88,256]{1,0:T(8,128)(2,1)S(1)}, bf16[88,256]{1,0:T(8,128)(2,1)S(1)}, u32[]{:S(2)}, u32[]{:S(2)}) collective-permute-start(bf16[88,256]{1,0:T(8,128)(2,1)S(1)} %slice.107), channel_id=1, source_target_pairs={{0,32},{1,33},{2,34},{3,35},{4,36},{5,37},{6,38},{7,39},{8,40},{9,... | collective-permute-start | bytes 135176 | tf_op jit(solution)/shard_map/ppermute | solution.py:28
  50.5 10.1 %copy-start.6 = (f32[1,43,512]{2,0,1:T(1,128)S(1)}, f32[1,43,512]{2,0,1:T(1,128)}, u32[]{:S(2)}) copy-start(f32[1,43,512]{2,0,1:T(1,128)} %param.11) | copy-start | bytes 264196
  50.5 10.1 %copy-start.7 = (f32[1,43,512]{2,0,1:T(1,128)S(1)}, f32[1,43,512]{2,0,1:T(1,128)}, u32[]{:S(2)}) copy-start(f32[1,43,512]{2,0,1:T(1,128)} %param.10) | copy-start | bytes 264196
  50.6 5.0 %collective-permute-start.12 = (bf16[88,256]{1,0:T(8,128)(2,1)S(1)}, bf16[88,256]{1,0:T(8,128)(2,1)S(1)}, u32[]{:S(2)}, u32[]{:S(2)}) collective-permute-start(bf16[88,256]{1,0:T(8,128)(2,1)S(1)} %get-tuple-element.48), channel_id=1, source_target_pairs={{0,16},{1,17},{2,18},{3,19},{4,20},{5,21},{6,22},{7,23},{8,24},{9,... | collective-permute-start | bytes 135176 | tf_op jit(solution)/shard_map/ppermute | solution.py:28
  53.0 6.3 %collective-permute-start.13 = (bf16[88,256]{1,0:T(8,128)(2,1)S(1)}, bf16[88,256]{1,0:T(8,128)(2,1)S(1)}, u32[]{:S(2)}, u32[]{:S(2)}) collective-permute-start(bf16[88,256]{1,0:T(8,128)(2,1)S(1)} %get-tuple-element.49), channel_id=1, source_target_pairs={{0,48},{1,49},{2,50},{3,51},{4,52},{5,53},{6,54},{7,55},{8,56},{9,... | collective-permute-start | bytes 135176 | tf_op jit(solution)/shard_map/ppermute | solution.py:28
  59.3 1.3 %collective-permute-start.15 = (f32[43,256]{1,0:T(8,128)S(1)}, f32[43,256]{1,0:T(8,128)S(1)}, u32[]{:S(2)}, u32[]{:S(2)}) collective-permute-start(f32[43,256]{1,0:T(8,128)S(1)} %slice_select_fusion), channel_id=1, source_target_pairs={{0,4},{1,5},{2,6},{3,7},{4,0},{5,1},{6,2},{7,3},{8,12},{9,13},{10,... | collective-permute-start | bytes 132104 | tf_op jit(solution)/shard_map/ppermute | solution.py:28
  60.6 7.6 %copy-start.1 = (bf16[1,1024,512]{2,1,0:T(8,128)(2,1)S(1)}, bf16[1,1024,512]{2,1,0:T(8,128)(2,1)}, u32[]{:S(2)}) copy-start(bf16[1,1024,512]{2,1,0:T(8,128)(2,1)} %param.9) | copy-start | bytes 3145732
  60.8 7.2 %collective-permute-start.18 = (bf16[64,512]{1,0:T(8,128)(2,1)S(1)}, bf16[64,512]{1,0:T(8,128)(2,1)S(1)}, u32[]{:S(2)}, u32[]{:S(2)}) collective-permute-start(bf16[64,512]{1,0:T(8,128)(2,1)S(1)} %pad.9), channel_id=1, source_target_pairs={{0,3},{1,2},{2,1},{3,0},{4,7},{5,6},{6,5},{7,4},{8,11},{9,10},{10,... | collective-permute-start | bytes 196616 | tf_op jit(solution)/shard_map/ppermute | solution.py:28
  62.4 5.6 %collective-permute-start.17 = (bf16[48,512]{1,0:T(8,128)(2,1)S(1)}, bf16[48,512]{1,0:T(8,128)(2,1)S(1)}, u32[]{:S(2)}, u32[]{:S(2)}) collective-permute-start(bf16[48,512]{1,0:T(8,128)(2,1)S(1)} %pad.8), channel_id=1, source_target_pairs={{0,2},{1,3},{2,0},{3,1},{4,6},{5,7},{6,4},{7,5},{8,10},{9,11},{10,... | collective-permute-start | bytes 147464 | tf_op jit(solution)/shard_map/ppermute | solution.py:28
  63.1 4.4 %collective-permute-start.16 = (bf16[43,512]{1,0:T(8,128)(2,1)S(1)}, bf16[43,512]{1,0:T(8,128)(2,1)S(1)}, u32[]{:S(2)}, u32[]{:S(2)}) collective-permute-start(bf16[43,512]{1,0:T(8,128)(2,1)S(1)} %get-tuple-element.45), channel_id=1, source_target_pairs={{0,1},{1,0},{2,3},{3,2},{4,5},{5,4},{6,7},{7,6},{8,9},{9,8},{10,11... | collective-permute-start | bytes 132104 | tf_op jit(solution)/shard_map/ppermute | solution.py:28
  (5 other events, 12.2 us)

commit v11 on v8

--- a/solution.py
+++ b/solution.py
@@ -12,8 +12,9 @@
 BF, F32 = jnp.bfloat16, jnp.float32
 
 Z_ORDER = (3, 1, -1, -3, -2, 0, 2, 4)
-FIRST, SECOND, KEEP = 2 * PADDED, 4 * PADDED, 7 * PADDED
-X_ORDER = (1, 2, 3, 0)
+FIRST, HALF = 2 * PADDED, 4 * PADDED
+X_ORDER = ((2, 1, 3, 0), (2, 3, 1, 0))
+PAIRS = ((1, 3), (3, 1))
 
 
 def send(value, move):
@@ -70,14 +71,14 @@
 
 def arrange(order, own, came):
     tokens = own.shape[1]
-    sizes = [NZ * PADDED] * NX
+    shape = jax.ShapeDtypeStruct((2 * HALF, NCORE * tokens), BF)
     vmem = pl.BlockSpec(memory_space=pltpu.VMEM)
     smem = pl.BlockSpec(memory_space=pltpu.SMEM)
     return pl.pallas_call(
         arrange_kernel,
-        out_shape=[jax.ShapeDtypeStruct((n, NCORE * tokens), BF) for n in sizes],
+        out_shape=[shape] * 4,
         in_specs=[smem, vmem, vmem],
-        out_specs=[vmem] * len(sizes),
+        out_specs=[vmem] * 4,
         scratch_shapes=[pltpu.VMEM((NX * NZ, PADDED, NCORE * tokens), F32)],
         compiler_params=pltpu.CompilerParams(vmem_limit_bytes=20 * 1024 * 1024),
         cost_estimate=pl.CostEstimate(flops=0, bytes_accessed=8 * 1024 * 1024, transcendentals=0),
@@ -96,36 +97,40 @@
     core, z, x = dp & 1, (dp >> 1) & (NZ - 1), dp >> 4
     y = lax.axis_index("tensor")
 
-    columns = cotangent[0].T
-    other_columns = swap_core(columns)
     up = 1 - 2 * (z & 1)
     blocks_z = (z + up * jnp.array(Z_ORDER, jnp.int32)) & (NZ - 1)
-    blocks_x = (x ^ jnp.array(X_ORDER, jnp.int32))[:, None] * NZ
-    order = (blocks_x + blocks_z[None, :]).reshape(-1)
+    blocks_z = blocks_z.reshape(2, 1, NZ // 2)
+    blocks_x = (x ^ jnp.array(X_ORDER, jnp.int32)) * NZ
+    order = (blocks_x[:, :, None] + blocks_z).reshape(-1)
 
     def lanes_of(c):
         return lax.dynamic_slice(basis[0], (0, c * lanes), (basis.shape[1], lanes))
 
-    theirs = swap_core(dot(features[0], lanes_of(1 - core)).astype(BF))
-    partial = jnp.concatenate([dot(features[0], lanes_of(core)), theirs.astype(F32)], axis=0)
-    sent = partial.astype(BF)
-    came = [swap_y(sent, m) for m in (1, 2, 3)]
-    came[0], other_columns = lax.optimization_barrier((came[0], other_columns))
+    theirs = dot(features[0], lanes_of(1 - core)).astype(BF)
+    columns = cotangent[0].T
+    theirs, sent = lax.optimization_barrier((theirs, columns))
+    other_columns = swap_core(sent)
+    chunks = [dot(features[0], lanes_of(core)), swap_core(theirs).astype(F32)]
+    chunks = [p + swap_y(p.astype(BF), m[0]).astype(F32) for p, m in zip(chunks, PAIRS)]
+    chunks, other_columns = lax.optimization_barrier((chunks, other_columns))
     parts = arrange(order, columns, other_columns)
-    came[2], parts = lax.optimization_barrier((came[2], parts))
-    partial = partial + came[0].astype(F32) + came[1].astype(F32) + came[2].astype(F32)
-    projected = partial.astype(BF)
+    chunks = [p + swap_y(p.astype(BF), m[1]).astype(F32) for p, m in zip(chunks, PAIRS)]
+    projected = jnp.concatenate([p.astype(BF) for p in chunks], axis=0)
+    projected, parts = lax.optimization_barrier((projected, parts))
 
-    came = [swap_x(dot(part, projected).astype(BF), m) for part, m in zip(parts, X_ORDER[:3])]
-    term = dot(parts[3], projected)
-    term = term + came[0].astype(F32) + came[1].astype(F32) + came[2].astype(F32)
-    lower, upper = swap_z(term[:FIRST].astype(BF), 1), swap_z(term[FIRST:SECOND].astype(BF), -1)
-    opposite = swap_z(term[KEEP:].astype(BF), 4)
-    keep = term[SECOND:KEEP]
+    sent = [dot(part, projected).astype(BF) for part in parts[::2]]
+    came = [swap_x(value, m[0]) for value, m in zip(sent, PAIRS)]
+    projected, sent = lax.optimization_barrier((projected, sent))
+    kept = lax.optimization_barrier([dot(part, projected) for part in parts[1::2]])
+    kept = [k + c.astype(F32) for k, c in zip(kept, came)]
+    came = [swap_x(k[:HALF].astype(BF), m[1]) for k, m in zip(kept, PAIRS)]
+    leave, keep = [k[HALF:] + c.astype(F32) for k, c in zip(kept, came)]
+    lower, upper = swap_z(leave[:FIRST].astype(BF), 1), swap_z(leave[FIRST:].astype(BF), -1)
+    opposite = swap_z(keep[3 * PADDED :].astype(BF), 4)
     lower, upper = lower.astype(F32), upper.astype(F32)
     hub_a = keep[:PADDED] + lower[:PADDED]
     own = keep[PADDED:FIRST] + lower[PADDED:] + upper[:PADDED]
-    hub_b = keep[FIRST:] + upper[PADDED:]
+    hub_b = keep[FIRST : 3 * PADDED] + upper[PADDED:]
     straight = ((z ^ (z >> 1)) & 1) == 0
     near, far = jnp.where(straight, hub_b, hub_a), jnp.where(straight, hub_a, hub_b)
     near, far = swap_z2(near.astype(BF), 0), swap_z2(far.astype(BF), 2)
@@ -144,10 +149,13 @@
         new_first / (1.0 - 0.9**10) / (jnp.sqrt(new_second / (1.0 - 0.999**10)) + 1e-08)
     ).astype(BF)[0]
 
-    around = [update] + [swap_y(update, m) for m in (1, 2, 3)]
-    ordered = jnp.stack([lax.select_n(y ^ a, *around) for a in range(NY)])
-    change = jnp.einsum("dr,acr->dac", basis[0], ordered, preferred_element_type=F32)
-    return (new_first, new_second, change.astype(BF)[None])
+    around = [update]
+    for m, more in ((1, 0), (2, 5), (3, 21)):
+        around.append(swap_y(jnp.pad(update, ((0, more), (0, 0))), m)[:OWNED])
+    ordered = jnp.stack([lax.select_n(y ^ a, *around) for a in range(NY)], axis=1)
+    rows = lax.optimization_barrier(ordered.reshape(-1, ordered.shape[2]))
+    change = dot(rows, basis[0].T).reshape(OWNED, NY, -1)
+    return (new_first, new_second, change.astype(BF).transpose(2, 1, 0)[None])
 
 
 def solution(mesh):

time: 75.7 us -> 68.6 us (0.906)
  waiting for transfers between devices: 34.3 us -> 26.2 us
  starting transfers between devices: 28.9 us -> 29.7 us
  other arithmetic: 1.54 us -> 0.77 us
    ppermute x17 -> x19, waiting for transfers between devices: 34.3 us -> 26.2 us  [send(): return lax.ppermute(value, ('dp', 'tensor'), pairs)]
    dot_general x6 -> x7, matrix products: 3.05 us -> 4.19 us  [dot(): lax.dot_general(a, b, (((1,), (0,)), ((), ())), preferred_element_type=F32)]
    convert_element_type x3 -> x4, other arithmetic: 1.22 us -> 0.09 us  [the longest x2 0.05 us: local(): projected = jnp.concatenate([p.astype(BF) for p in chunks], axis=0)]
    unnamed x17 -> x16, local copies, waits for them, and re-layouts: 3.75 us -> 2.82 us
    convert_element_type x0 -> x1, local copies, waits for them, and re-layouts: none -> 0.89 us  [local(): return (new_first, new_second, change.astype(BF).transpose(2, 1, 0)[None])]
    ppermute x17 -> x19, starting transfers between devices: 28.9 us -> 29.7 us  [send(): return lax.ppermute(value, ('dp', 'tensor'), pairs)]
  transfers between devices with their start and end apart: 17 -> 19, of which waited for: 11 -> 10; matrix products, arithmetic and copies ran while one was open for 5% -> 6% of each run, Pallas kernels for 3% -> 3%
where the time goes in v11:
time: 68.6 us; the launch traced here: 68.1 us
  starting transfers between devices  29.7 us (43%)
  waiting for transfers between devices  26.2 us (38%)
  matrix products  4.19 us (6%)
  local copies, waits for them, and re-layouts  4.14 us (6%)
  Pallas kernels  2.12 us (3%)
  between operations  0.96 us (1%)
  other arithmetic  0.77 us (1%)
    ppermute x19, starting transfers between devices, send(): return lax.ppermute(value, ('dp', 'tensor'), pairs)  29.7 us
    ppermute x19, waiting for transfers between devices, send(): return lax.ppermute(value, ('dp', 'tensor'), pairs)  26.2 us
    dot_general x7, matrix products, dot(): lax.dot_general(a, b, (((1,), (0,)), ((), ())), preferred_element_type=F32)  4.19 us
    unnamed x16, local copies, waits for them, and re-layouts  2.82 us
    pallas_call x1, Pallas kernels, arrange(): pl.pallas_call(arrange_kernel, out_shape=[shape] * 4, in_specs=[smem, vme...  2.12 us
  transfers between devices with their start and end apart: 19, of which 10 were waited for; matrix products, arithmetic and copies ran while one was open for 6% of the time, Pallas kernels for 3%

profile of v11, /device:TPU:32, one launch (start us, length us, event | category | flops | bytes accessed | tf_op | source)
XLA Modules:
  0.0 68.1 jit_solution(14443373699706284942)
XLA Ops:
  0.7 1.3 %copy-done = bf16[1,1024,512]{2,1,0:T(8,128)(2,1)S(1)} copy-done((bf16[1,1024,512]{2,1,0:T(8,128)(2,1)S(1)}, bf16[1,1024,512]{2,1,0:T(8,128)(2,1)}, u32[]{:S(2)}) %copy-start) | copy-done | bytes 1048600
  2.0 1.3 %fusion = bf16[256,256]{1,0:T(8,128)(2,1)S(1)} fusion(bf16[1,256,1024]{2,1,0:T(8,128)(2,1)} %param.7, bf16[1,1024,512]{2,1,0:T(8,128)(2,1)S(1)} %copy-done, s32[]{:T(128)S(6)} %select_n.148), kind=kOutput, calls=%fused_computation.5 | convolution fusion | flops 134283264 | bytes 1179652 | tf_op jit(solution)/shard_map/dot_general | solution.py:89
  4.0 1.0 %fusion.20 = (bf16[256,256]{1,0:T(8,128)(2,1)}, f32[256,256]{1,0:T(8,128)S(1)}) fusion(bf16[1,1024,512]{2,1,0:T(8,128)(2,1)S(1)} %copy-done, s32[]{:T(128)S(6)} %select_n.147, bf16[1,256,1024]{2,1,0:T(8,128)(2,1)S(1)} %copy-done.2), kind=kOutput, calls=%fused_computation.57 | convolution fusion | flops 134283264 | bytes 1441796 | tf_op jit(solution)/shard_map/dot_general | solution.py:89
  4.9 1.6 %collective-permute-start = (bf16[256,256]{1,0:T(8,128)(2,1)}, bf16[256,256]{1,0:T(8,128)(2,1)S(1)}, u32[]{:S(2)}, u32[]{:S(2)}) collective-permute-start(bf16[256,256]{1,0:T(8,128)(2,1)} %get-tuple-element.55), channel_id=1, source_target_pairs={{0,1},{1,0},{2,3},{3,2},{4,5},{5,4},{6,7},{7,6},{8,9},{9,8},{10,11... | collective-permute-start | bytes 393224 | tf_op jit(solution)/shard_map/ppermute | solution.py:27
  6.6 2.9 %collective-permute-start.2 = (bf16[256,256]{1,0:T(8,128)(2,1)S(1)}, bf16[256,256]{1,0:T(8,128)(2,1)S(1)}, u32[]{:S(2)}, u32[]{:S(2)}) collective-permute-start(bf16[256,256]{1,0:T(8,128)(2,1)S(1)} %collective-permute-done.1), channel_id=1, source_target_pairs={{0,3},{1,2},{2,1},{3,0},{4,7},{5,6},{6,5},{7,4},{8,11},{9,10},{10,... | collective-permute-start | bytes 393224 | tf_op jit(solution)/shard_map/ppermute | solution.py:27
  9.5 1.2 %collective-permute-done = bf16[256,256]{1,0:T(8,128)(2,1)S(1)} collective-permute-done((bf16[256,256]{1,0:T(8,128)(2,1)}, bf16[256,256]{1,0:T(8,128)(2,1)S(1)}, u32[]{:S(2)}, u32[]{:S(2)}) %collective-permute-start) | collective-permute-done | bytes 131104 | tf_op jit(solution)/shard_map/ppermute | solution.py:27
  10.7 2.8 %collective-permute-done.2 = bf16[256,256]{1,0:T(8,128)(2,1)S(1)} collective-permute-done((bf16[256,256]{1,0:T(8,128)(2,1)S(1)}, bf16[256,256]{1,0:T(8,128)(2,1)S(1)}, u32[]{:S(2)}, u32[]{:S(2)}) %collective-permute-start.2) | collective-permute-done | bytes 131104 | tf_op jit(solution)/shard_map/ppermute | solution.py:27
  13.6 3.0 %collective-permute-start.4 = (bf16[256,256]{1,0:T(8,128)(2,1)S(1)}, bf16[256,256]{1,0:T(8,128)(2,1)S(1)}, u32[]{:S(2)}, u32[]{:S(2)}) collective-permute-start(bf16[256,256]{1,0:T(8,128)(2,1)S(1)} %convert_element_type.96), channel_id=1, source_target_pairs={{0,3},{1,2},{2,1},{3,0},{4,7},{5,6},{6,5},{7,4},{8,11},{9,10},{10,... | collective-permute-start | bytes 393224 | tf_op jit(solution)/shard_map/ppermute | solution.py:27
  16.9 2.1 %shard_map.94 = (bf16[704,512]{1,0:T(8,128)(2,1)S(1)}, bf16[704,512]{1,0:T(8,128)(2,1)S(1)}, bf16[704,512]{1,0:T(8,128)(2,1)S(1)}, bf16[704,512]{1,0:T(8,128)(2,1)S(1)}) custom-call(s32[32]{0:T(128)S(1)} %add.104.order_ref, bf16[2752,256]{1,0:T(8,128)(2,1)S(1)} %bitcast.54, bf16[2752,256]{1,0:T(8,128)(2,1)} %collective-permute-done.3.came), custom_call_target="tpu_custom_call" | custom-call | bytes 8388608 | tf_op jit(solution)/shard_map/pallas_call | solution.py:77
  19.9 2.0 %collective-permute-done.5 = bf16[256,256]{1,0:T(8,128)(2,1)S(1)} collective-permute-done((bf16[256,256]{1,0:T(8,128)(2,1)S(1)}, bf16[256,256]{1,0:T(8,128)(2,1)S(1)}, u32[]{:S(2)}, u32[]{:S(2)}) %collective-permute-start.5) | collective-permute-done | bytes 131104 | tf_op jit(solution)/shard_map/ppermute | solution.py:27
  22.6 2.8 %collective-permute-start.6 = (bf16[704,256]{1,0:T(8,128)(2,1)S(1)}, bf16[704,256]{1,0:T(8,128)(2,1)S(1)}, u32[]{:S(2)}, u32[]{:S(2)}) collective-permute-start(bf16[704,256]{1,0:T(8,128)(2,1)S(1)} %convolution_convert_fusion.1), channel_id=1, source_target_pairs={{0,192},{1,193},{2,194},{3,195},{4,196},{5,197},{6,198},{7,199},{8... | collective-permute-start | bytes 1081352 | tf_op jit(solution)/shard_map/ppermute | solution.py:27
  26.4 7.2 %collective-permute-done.8 = bf16[704,256]{1,0:T(8,128)(2,1)S(1)} collective-permute-done((bf16[704,256]{1,0:T(8,128)(2,1)S(1)}, bf16[704,256]{1,0:T(8,128)(2,1)S(1)}, u32[]{:S(2)}, u32[]{:S(2)}) %collective-permute-start.8) | collective-permute-done | bytes 360480 | tf_op jit(solution)/shard_map/ppermute | solution.py:27
  34.8 5.8 %collective-permute-done.9 = bf16[352,256]{1,0:T(8,128)(2,1)S(1)} collective-permute-done((bf16[352,256]{1,0:T(8,128)(2,1)S(1)}, bf16[352,256]{1,0:T(8,128)(2,1)S(1)}, u32[]{:S(2)}, u32[]{:S(2)}) %collective-permute-start.9) | collective-permute-done | bytes 180256 | tf_op jit(solution)/shard_map/ppermute | solution.py:27
  40.8 3.7 %collective-permute-start.11 = (bf16[176,256]{1,0:T(8,128)(2,1)S(1)}, bf16[176,256]{1,0:T(8,128)(2,1)S(1)}, u32[]{:S(2)}, u32[]{:S(2)}) collective-permute-start(bf16[176,256]{1,0:T(8,128)(2,1)S(1)} %get-tuple-element.52), channel_id=1, source_target_pairs={{0,56},{1,57},{2,58},{3,59},{4,60},{5,61},{6,62},{7,63},{8,16},{9,... | collective-permute-start | bytes 270344 | tf_op jit(solution)/shard_map/ppermute | solution.py:27
  44.6 4.6 %collective-permute-start.14 = (bf16[88,256]{1,0:T(8,128)(2,1)S(1)}, bf16[88,256]{1,0:T(8,128)(2,1)S(1)}, u32[]{:S(2)}, u32[]{:S(2)}) collective-permute-start(bf16[88,256]{1,0:T(8,128)(2,1)S(1)} %slice.155), channel_id=1, source_target_pairs={{0,32},{1,33},{2,34},{3,35},{4,36},{5,37},{6,38},{7,39},{8,40},{9,... | collective-permute-start | bytes 135176 | tf_op jit(solution)/shard_map/ppermute | solution.py:27
  49.3 2.2 %collective-permute-start.12 = (bf16[88,256]{1,0:T(8,128)(2,1)S(1)}, bf16[88,256]{1,0:T(8,128)(2,1)S(1)}, u32[]{:S(2)}, u32[]{:S(2)}) collective-permute-start(bf16[88,256]{1,0:T(8,128)(2,1)S(1)} %get-tuple-element.46), channel_id=1, source_target_pairs={{0,16},{1,17},{2,18},{3,19},{4,20},{5,21},{6,22},{7,23},{8,24},{9,... | collective-permute-start | bytes 135176 | tf_op jit(solution)/shard_map/ppermute | solution.py:27
  51.5 2.6 %collective-permute-start.13 = (bf16[88,256]{1,0:T(8,128)(2,1)S(1)}, bf16[88,256]{1,0:T(8,128)(2,1)S(1)}, u32[]{:S(2)}, u32[]{:S(2)}) collective-permute-start(bf16[88,256]{1,0:T(8,128)(2,1)S(1)} %get-tuple-element.47), channel_id=1, source_target_pairs={{0,48},{1,49},{2,50},{3,51},{4,52},{5,53},{6,54},{7,55},{8,56},{9,... | collective-permute-start | bytes 135176 | tf_op jit(solution)/shard_map/ppermute | solution.py:27
  54.3 3.8 %collective-permute-done.13 = bf16[88,256]{1,0:T(8,128)(2,1)S(1)} collective-permute-done((bf16[88,256]{1,0:T(8,128)(2,1)S(1)}, bf16[88,256]{1,0:T(8,128)(2,1)S(1)}, u32[]{:S(2)}, u32[]{:S(2)}) %collective-permute-start.13) | collective-permute-done | bytes 45088 | tf_op jit(solution)/shard_map/ppermute | solution.py:27
  58.3 1.2 %collective-permute-done.15 = f32[43,256]{1,0:T(8,128)S(1)} collective-permute-done((f32[43,256]{1,0:T(8,128)S(1)}, f32[43,256]{1,0:T(8,128)S(1)}, u32[]{:S(2)}, u32[]{:S(2)}) %collective-permute-start.15) | collective-permute-done | bytes 44064 | tf_op jit(solution)/shard_map/ppermute | solution.py:27
  59.7 1.1 %collective-permute-start.18 = (bf16[64,512]{1,0:T(8,128)(2,1)S(1)}, bf16[64,512]{1,0:T(8,128)(2,1)S(1)}, u32[]{:S(2)}, u32[]{:S(2)}) collective-permute-start(bf16[64,512]{1,0:T(8,128)(2,1)S(1)} %pad.9), channel_id=1, source_target_pairs={{0,3},{1,2},{2,1},{3,0},{4,7},{5,6},{6,5},{7,4},{8,11},{9,10},{10,... | collective-permute-start | bytes 196616 | tf_op jit(solution)/shard_map/ppermute | solution.py:27
  60.8 1.1 %collective-permute-start.17 = (bf16[48,512]{1,0:T(8,128)(2,1)S(1)}, bf16[48,512]{1,0:T(8,128)(2,1)S(1)}, u32[]{:S(2)}, u32[]{:S(2)}) collective-permute-start(bf16[48,512]{1,0:T(8,128)(2,1)S(1)} %pad.8), channel_id=1, source_target_pairs={{0,2},{1,3},{2,0},{3,1},{4,6},{5,7},{6,4},{7,5},{8,10},{9,11},{10,... | collective-permute-start | bytes 147464 | tf_op jit(solution)/shard_map/ppermute | solution.py:27
  61.8 2.0 %collective-permute-start.16 = (bf16[43,512]{1,0:T(8,128)(2,1)S(1)}, bf16[43,512]{1,0:T(8,128)(2,1)S(1)}, u32[]{:S(2)}, u32[]{:S(2)}) collective-permute-start(bf16[43,512]{1,0:T(8,128)(2,1)S(1)} %get-tuple-element.43), channel_id=1, source_target_pairs={{0,1},{1,0},{2,3},{3,2},{4,5},{5,4},{6,7},{7,6},{8,9},{9,8},{10,11... | collective-permute-start | bytes 132104 | tf_op jit(solution)/shard_map/ppermute | solution.py:27
  65.3 1.1 %collective-permute-done.16 = bf16[43,512]{1,0:T(8,128)(2,1)S(1)} collective-permute-done((bf16[43,512]{1,0:T(8,128)(2,1)S(1)}, bf16[43,512]{1,0:T(8,128)(2,1)S(1)}, u32[]{:S(2)}, u32[]{:S(2)}) %collective-permute-start.16) | collective-permute-done | bytes 44064 | tf_op jit(solution)/shard_map/ppermute | solution.py:27
  67.2 0.9 %convert_element_type.117 = bf16[43,4,1024]{2,1,0:T(4,128)(2,1)} reshape(bf16[172,1024]{1,0:T(8,128)(2,1)S(1)} %convolution_convert_fusion) | data formatting | bytes 704512 | tf_op jit(solution)/shard_map/convert_element_type | solution.py:158
  (73 shorter events, 7.8 us)
Async XLA Ops:
  0.6 5.9 %copy-start.6 = (s32[8]{0:T(128)S(1)}, s32[8]{0:T(128)}, u32[]{:S(2)}) copy-start(s32[8]{0:T(128)} %constant.56.clone) | copy-start | bytes 100
  0.7 5.9 %copy-start.5 = (s32[2,4]{1,0:T(2,128)S(1)}, s32[2,4]{1,0:T(2,128)}, u32[]{:S(2)}) copy-start(s32[2,4]{1,0:T(2,128)} %constant.57.clone) | copy-start | bytes 100
  3.4 10.2 %collective-permute-start.3 = (bf16[2752,256]{1,0:T(8,128)(2,1)}, bf16[2752,256]{1,0:T(8,128)(2,1)}, u32[]{:S(2)}, u32[]{:S(2)}) collective-permute-start(bf16[2752,256]{1,0:T(8,128)(2,1)} %bitcast.53), channel_id=1, source_target_pairs={{0,4},{1,5},{2,6},{3,7},{4,0},{5,1},{6,2},{7,3},{8,12},{9,13},{10,... | collective-permute-start | bytes 4227080 | tf_op jit(solution)/shard_map/ppermute | solution.py:27
  3.5 3.1 %collective-permute-start.1 = (bf16[256,256]{1,0:T(8,128)(2,1)S(1)}, bf16[256,256]{1,0:T(8,128)(2,1)S(1)}, u32[]{:S(2)}, u32[]{:S(2)}) collective-permute-start(bf16[256,256]{1,0:T(8,128)(2,1)S(1)} %fusion), channel_id=1, source_target_pairs={{0,4},{1,5},{2,6},{3,7},{4,0},{5,1},{6,2},{7,3},{8,12},{9,13},{10,... | collective-permute-start | bytes 393224 | tf_op jit(solution)/shard_map/ppermute | solution.py:27
  4.0 12.9 %copy-start.1 = (bf16[1,256,2752]{1,2,0:T(8,128)(2,1)S(1)}, bf16[1,256,2752]{1,2,0:T(8,128)(2,1)}, u32[]{:S(2)}) copy-start(bf16[1,256,2752]{1,2,0:T(8,128)(2,1)} %param.8) | copy-start | bytes 4227076
  4.9 5.7 %collective-permute-start = (bf16[256,256]{1,0:T(8,128)(2,1)}, bf16[256,256]{1,0:T(8,128)(2,1)S(1)}, u32[]{:S(2)}, u32[]{:S(2)}) collective-permute-start(bf16[256,256]{1,0:T(8,128)(2,1)} %get-tuple-element.55), channel_id=1, source_target_pairs={{0,1},{1,0},{2,3},{3,2},{4,5},{5,4},{6,7},{7,6},{8,9},{9,8},{10,11... | collective-permute-start | bytes 393224 | tf_op jit(solution)/shard_map/ppermute | solution.py:27
  6.6 6.9 %collective-permute-start.2 = (bf16[256,256]{1,0:T(8,128)(2,1)S(1)}, bf16[256,256]{1,0:T(8,128)(2,1)S(1)}, u32[]{:S(2)}, u32[]{:S(2)}) collective-permute-start(bf16[256,256]{1,0:T(8,128)(2,1)S(1)} %collective-permute-done.1), channel_id=1, source_target_pairs={{0,3},{1,2},{2,1},{3,0},{4,7},{5,6},{6,5},{7,4},{8,11},{9,10},{10,... | collective-permute-start | bytes 393224 | tf_op jit(solution)/shard_map/ppermute | solution.py:27
  13.6 6.3 %collective-permute-start.4 = (bf16[256,256]{1,0:T(8,128)(2,1)S(1)}, bf16[256,256]{1,0:T(8,128)(2,1)S(1)}, u32[]{:S(2)}, u32[]{:S(2)}) collective-permute-start(bf16[256,256]{1,0:T(8,128)(2,1)S(1)} %convert_element_type.96), channel_id=1, source_target_pairs={{0,3},{1,2},{2,1},{3,0},{4,7},{5,6},{6,5},{7,4},{8,11},{9,10},{10,... | collective-permute-start | bytes 393224 | tf_op jit(solution)/shard_map/ppermute | solution.py:27
  16.8 5.1 %collective-permute-start.5 = (bf16[256,256]{1,0:T(8,128)(2,1)S(1)}, bf16[256,256]{1,0:T(8,128)(2,1)S(1)}, u32[]{:S(2)}, u32[]{:S(2)}) collective-permute-start(bf16[256,256]{1,0:T(8,128)(2,1)S(1)} %convert_element_type.99), channel_id=1, source_target_pairs={{0,1},{1,0},{2,3},{3,2},{4,5},{5,4},{6,7},{7,6},{8,9},{9,8},{10,11... | collective-permute-start | bytes 393224 | tf_op jit(solution)/shard_map/ppermute | solution.py:27
  22.6 11.7 %collective-permute-start.6 = (bf16[704,256]{1,0:T(8,128)(2,1)S(1)}, bf16[704,256]{1,0:T(8,128)(2,1)S(1)}, u32[]{:S(2)}, u32[]{:S(2)}) collective-permute-start(bf16[704,256]{1,0:T(8,128)(2,1)S(1)} %convolution_convert_fusion.1), channel_id=1, source_target_pairs={{0,192},{1,193},{2,194},{3,195},{4,196},{5,197},{6,198},{7,199},{8... | collective-permute-start | bytes 1081352 | tf_op jit(solution)/shard_map/ppermute | solution.py:27
  25.5 8.2 %collective-permute-start.8 = (bf16[704,256]{1,0:T(8,128)(2,1)S(1)}, bf16[704,256]{1,0:T(8,128)(2,1)S(1)}, u32[]{:S(2)}, u32[]{:S(2)}) collective-permute-start(bf16[704,256]{1,0:T(8,128)(2,1)S(1)} %convolution_convert_fusion.2), channel_id=1, source_target_pairs={{0,64},{1,65},{2,66},{3,67},{4,68},{5,69},{6,70},{7,71},{8,72},{9,... | collective-permute-start | bytes 1081352 | tf_op jit(solution)/shard_map/ppermute | solution.py:27
  33.7 6.8 %collective-permute-start.9 = (bf16[352,256]{1,0:T(8,128)(2,1)S(1)}, bf16[352,256]{1,0:T(8,128)(2,1)S(1)}, u32[]{:S(2)}, u32[]{:S(2)}) collective-permute-start(bf16[352,256]{1,0:T(8,128)(2,1)S(1)} %slice.153), channel_id=1, source_target_pairs={{0,192},{1,193},{2,194},{3,195},{4,196},{5,197},{6,198},{7,199},{8... | collective-permute-start | bytes 540680 | tf_op jit(solution)/shard_map/ppermute | solution.py:27
  34.4 10.1 %collective-permute-start.7 = (bf16[352,256]{1,0:T(8,128)(2,1)S(1)}, bf16[352,256]{1,0:T(8,128)(2,1)S(1)}, u32[]{:S(2)}, u32[]{:S(2)}) collective-permute-start(bf16[352,256]{1,0:T(8,128)(2,1)S(1)} %slice.154), channel_id=1, source_target_pairs={{0,64},{1,65},{2,66},{3,67},{4,68},{5,69},{6,70},{7,71},{8,72},{9,... | collective-permute-start | bytes 540680 | tf_op jit(solution)/shard_map/ppermute | solution.py:27
  40.6 8.6 %collective-permute-start.10 = (bf16[176,256]{1,0:T(8,128)(2,1)S(1)}, bf16[176,256]{1,0:T(8,128)(2,1)S(1)}, u32[]{:S(2)}, u32[]{:S(2)}) collective-permute-start(bf16[176,256]{1,0:T(8,128)(2,1)S(1)} %get-tuple-element.51), channel_id=1, source_target_pairs={{0,8},{1,9},{2,10},{3,11},{4,12},{5,13},{6,14},{7,15},{8,0},{9,1},... | collective-permute-start | bytes 270344 | tf_op jit(solution)/shard_map/ppermute | solution.py:27
  40.8 18.7 %copy-start.3 = (f32[1,43,512]{2,0,1:T(1,128)S(1)}, f32[1,43,512]{2,0,1:T(1,128)}, u32[]{:S(2)}) copy-start(f32[1,43,512]{2,0,1:T(1,128)} %param.11) | copy-start | bytes 264196
  40.8 18.7 %copy-start.4 = (f32[1,43,512]{2,0,1:T(1,128)S(1)}, f32[1,43,512]{2,0,1:T(1,128)}, u32[]{:S(2)}) copy-start(f32[1,43,512]{2,0,1:T(1,128)} %param.10) | copy-start | bytes 264196
  40.8 8.4 %collective-permute-start.11 = (bf16[176,256]{1,0:T(8,128)(2,1)S(1)}, bf16[176,256]{1,0:T(8,128)(2,1)S(1)}, u32[]{:S(2)}, u32[]{:S(2)}) collective-permute-start(bf16[176,256]{1,0:T(8,128)(2,1)S(1)} %get-tuple-element.52), channel_id=1, source_target_pairs={{0,56},{1,57},{2,58},{3,59},{4,60},{5,61},{6,62},{7,63},{8,16},{9,... | collective-permute-start | bytes 270344 | tf_op jit(solution)/shard_map/ppermute | solution.py:27
  44.6 9.5 %collective-permute-start.14 = (bf16[88,256]{1,0:T(8,128)(2,1)S(1)}, bf16[88,256]{1,0:T(8,128)(2,1)S(1)}, u32[]{:S(2)}, u32[]{:S(2)}) collective-permute-start(bf16[88,256]{1,0:T(8,128)(2,1)S(1)} %slice.155), channel_id=1, source_target_pairs={{0,32},{1,33},{2,34},{3,35},{4,36},{5,37},{6,38},{7,39},{8,40},{9,... | collective-permute-start | bytes 135176 | tf_op jit(solution)/shard_map/ppermute | solution.py:27
  49.3 5.1 %collective-permute-start.12 = (bf16[88,256]{1,0:T(8,128)(2,1)S(1)}, bf16[88,256]{1,0:T(8,128)(2,1)S(1)}, u32[]{:S(2)}, u32[]{:S(2)}) collective-permute-start(bf16[88,256]{1,0:T(8,128)(2,1)S(1)} %get-tuple-element.46), channel_id=1, source_target_pairs={{0,16},{1,17},{2,18},{3,19},{4,20},{5,21},{6,22},{7,23},{8,24},{9,... | collective-permute-start | bytes 135176 | tf_op jit(solution)/shard_map/ppermute | solution.py:27
  51.5 6.6 %collective-permute-start.13 = (bf16[88,256]{1,0:T(8,128)(2,1)S(1)}, bf16[88,256]{1,0:T(8,128)(2,1)S(1)}, u32[]{:S(2)}, u32[]{:S(2)}) collective-permute-start(bf16[88,256]{1,0:T(8,128)(2,1)S(1)} %get-tuple-element.47), channel_id=1, source_target_pairs={{0,48},{1,49},{2,50},{3,51},{4,52},{5,53},{6,54},{7,55},{8,56},{9,... | collective-permute-start | bytes 135176 | tf_op jit(solution)/shard_map/ppermute | solution.py:27
  58.2 1.3 %collective-permute-start.15 = (f32[43,256]{1,0:T(8,128)S(1)}, f32[43,256]{1,0:T(8,128)S(1)}, u32[]{:S(2)}, u32[]{:S(2)}) collective-permute-start(f32[43,256]{1,0:T(8,128)S(1)} %slice_select_fusion), channel_id=1, source_target_pairs={{0,4},{1,5},{2,6},{3,7},{4,0},{5,1},{6,2},{7,3},{8,12},{9,13},{10,... | collective-permute-start | bytes 132104 | tf_op jit(solution)/shard_map/ppermute | solution.py:27
  59.7 6.8 %collective-permute-start.18 = (bf16[64,512]{1,0:T(8,128)(2,1)S(1)}, bf16[64,512]{1,0:T(8,128)(2,1)S(1)}, u32[]{:S(2)}, u32[]{:S(2)}) collective-permute-start(bf16[64,512]{1,0:T(8,128)(2,1)S(1)} %pad.9), channel_id=1, source_target_pairs={{0,3},{1,2},{2,1},{3,0},{4,7},{5,6},{6,5},{7,4},{8,11},{9,10},{10,... | collective-permute-start | bytes 196616 | tf_op jit(solution)/shard_map/ppermute | solution.py:27
  60.8 5.7 %collective-permute-start.17 = (bf16[48,512]{1,0:T(8,128)(2,1)S(1)}, bf16[48,512]{1,0:T(8,128)(2,1)S(1)}, u32[]{:S(2)}, u32[]{:S(2)}) collective-permute-start(bf16[48,512]{1,0:T(8,128)(2,1)S(1)} %pad.8), channel_id=1, source_target_pairs={{0,2},{1,3},{2,0},{3,1},{4,6},{5,7},{6,4},{7,5},{8,10},{9,11},{10,... | collective-permute-start | bytes 147464 | tf_op jit(solution)/shard_map/ppermute | solution.py:27
  61.8 4.6 %collective-permute-start.16 = (bf16[43,512]{1,0:T(8,128)(2,1)S(1)}, bf16[43,512]{1,0:T(8,128)(2,1)S(1)}, u32[]{:S(2)}, u32[]{:S(2)}) collective-permute-start(bf16[43,512]{1,0:T(8,128)(2,1)S(1)} %get-tuple-element.43), channel_id=1, source_target_pairs={{0,1},{1,0},{2,3},{3,2},{4,5},{5,4},{6,7},{7,6},{8,9},{9,8},{10,11... | collective-permute-start | bytes 132104 | tf_op jit(solution)/shard_map/ppermute | solution.py:27
  (2 other events, 4.7 us)

commit v12 on v11

--- a/solution.py
+++ b/solution.py
@@ -85,13 +85,40 @@
     )(order, own, came)
 
 
+def project_kernel(core_ref, features, basis, own, own_sent, theirs):
+    lanes = own.shape[1]
+    total = jnp.dot(features[...], basis[...], preferred_element_type=F32)
+    halves = total[:, :lanes], total[:, lanes:]
+    for core in range(NCORE):
+
+        @pl.when(core_ref[0] == core)
+        def _(core=core):
+            own[...] = halves[core]
+            own_sent[...] = halves[core].astype(BF)
+            theirs[...] = halves[1 - core].astype(BF)
+
+
+def project(core, features, basis):
+    shape = features.shape[0], basis.shape[1] // NCORE
+    vmem = pl.BlockSpec(memory_space=pltpu.VMEM)
+    return pl.pallas_call(
+        project_kernel,
+        out_shape=[jax.ShapeDtypeStruct(shape, dtype) for dtype in (F32, BF, BF)],
+        in_specs=[pl.BlockSpec(memory_space=pltpu.SMEM), vmem, vmem],
+        out_specs=[vmem] * 3,
+        compiler_params=pltpu.CompilerParams(vmem_limit_bytes=8 * 1024 * 1024),
+        cost_estimate=pl.CostEstimate(
+            flops=2 * features.size * basis.shape[1], bytes_accessed=2 * 1024 * 1024, transcendentals=0
+        ),
+    )(core, features, basis)
+
+
 def dot(a, b):
     out = lax.dot_general(a, b, (((1,), (0,)), ((), ())), preferred_element_type=F32)
     return with_layout_constraint(out, Layout(major_to_minor=(0, 1)))
 
 
 def local(features, cotangent, basis, first_moment, second_moment):
-    lanes = basis.shape[2] // NCORE
     scale = 1.0 / (features.shape[1] * lax.axis_size("dp"))
     dp = lax.axis_index("dp")
     core, z, x = dp & 1, (dp >> 1) & (NZ - 1), dp >> 4
@@ -103,20 +130,17 @@
     blocks_x = (x ^ jnp.array(X_ORDER, jnp.int32)) * NZ
     order = (blocks_x[:, :, None] + blocks_z).reshape(-1)
 
-    def lanes_of(c):
-        return lax.dynamic_slice(basis[0], (0, c * lanes), (basis.shape[1], lanes))
-
-    theirs = dot(features[0], lanes_of(1 - core)).astype(BF)
+    mine, mine_sent, theirs = project(core.reshape(1), features[0], basis[0])
     columns = cotangent[0].T
-    theirs, sent = lax.optimization_barrier((theirs, columns))
+    theirs, sent = lax.optimization_barrier((swap_core(theirs), columns))
     other_columns = swap_core(sent)
-    chunks = [dot(features[0], lanes_of(core)), swap_core(theirs).astype(F32)]
-    chunks = [p + swap_y(p.astype(BF), m[0]).astype(F32) for p, m in zip(chunks, PAIRS)]
-    chunks, other_columns = lax.optimization_barrier((chunks, other_columns))
+    came = [swap_y(p, m[0]) for p, m in zip((mine_sent, theirs), PAIRS)]
+    chunks = [p.astype(F32) + c.astype(F32) for p, c in zip((mine, theirs), came)]
+    came = [swap_y(p.astype(BF), m[1]) for p, m in zip(chunks, PAIRS)]
     parts = arrange(order, columns, other_columns)
-    chunks = [p + swap_y(p.astype(BF), m[1]).astype(F32) for p, m in zip(chunks, PAIRS)]
+    came[1], parts = lax.optimization_barrier((came[1], parts))
+    chunks = [p + c.astype(F32) for p, c in zip(chunks, came)]
     projected = jnp.concatenate([p.astype(BF) for p in chunks], axis=0)
-    projected, parts = lax.optimization_barrier((projected, parts))
 
     sent = [dot(part, projected).astype(BF) for part in parts[::2]]
     came = [swap_x(value, m[0]) for value, m in zip(sent, PAIRS)]

time: 68.6 us -> 67.3 us (0.981)
  waiting for transfers between devices: 26.2 us -> 29.6 us
  starting transfers between devices: 29.7 us -> 27.1 us
  matrix products: 4.19 us -> 1.89 us
  local copies, waits for them, and re-layouts: 4.14 us -> 5.07 us
    ppermute x19, waiting for transfers between devices: 26.2 us -> 29.6 us  [send(): return lax.ppermute(value, ('dp', 'tensor'), pairs)]
    ppermute x19, starting transfers between devices: 29.7 us -> 27.1 us  [send(): return lax.ppermute(value, ('dp', 'tensor'), pairs)]
    dot_general x7 -> x5, matrix products: 4.19 us -> 1.89 us  [dot(): lax.dot_general(a, b, (((1,), (0,)), ((), ())), preferred_element_type=F32)]
    unnamed x16 -> x18, local copies, waits for them, and re-layouts: 2.82 us -> 3.75 us
    pallas_call x1, Pallas kernels: 2.12 us -> 1.3 us  [arrange(): pl.pallas_call(arrange_kernel, out_shape=[shape] * 4, in_specs=[smem, vme...]
  transfers between devices with their start and end apart: 19 -> 19, of which waited for: 10 -> 12; matrix products, arithmetic and copies ran while one was open for 6% -> 4% of each run, Pallas kernels for 3% -> 2%
where the time goes in v12:
time: 67.3 us; the launch traced here: 67.1 us
  waiting for transfers between devices  29.6 us (44%)
  starting transfers between devices  27.1 us (40%)
  local copies, waits for them, and re-layouts  5.07 us (8%)
  matrix products  1.89 us (3%)
  Pallas kernels  1.76 us (3%)
  between operations  0.93 us (1%)
  other arithmetic  0.79 us (1%)
    ppermute x19, waiting for transfers between devices, send(): return lax.ppermute(value, ('dp', 'tensor'), pairs)  29.6 us
    ppermute x19, starting transfers between devices, send(): return lax.ppermute(value, ('dp', 'tensor'), pairs)  27.1 us
    unnamed x18, local copies, waits for them, and re-layouts  3.75 us
    dot_general x5, matrix products, dot(): lax.dot_general(a, b, (((1,), (0,)), ((), ())), preferred_element_type=F32)  1.89 us
  transfers between devices with their start and end apart: 19, of which 12 were waited for; matrix products, arithmetic and copies ran while one was open for 4% of the time, Pallas kernels for 2%

profile of v12, /device:TPU:32, one launch (start us, length us, event | category | flops | bytes accessed | tf_op | source)
XLA Modules:
  0.0 67.1 jit_solution(13113325805184800478)
XLA Ops:
  0.7 1.2 %copy-done = bf16[1,1024,512]{2,1,0:T(8,128)(2,1)S(1)} copy-done((bf16[1,1024,512]{2,1,0:T(8,128)(2,1)S(1)}, bf16[1,1024,512]{2,1,0:T(8,128)(2,1)}, u32[]{:S(2)}) %copy-start) | copy-done | bytes 1048600
  3.5 1.3 %collective-permute-done = bf16[256,256]{1,0:T(8,128)(2,1)S(1)} collective-permute-done((bf16[256,256]{1,0:T(8,128)(2,1)S(1)}, bf16[256,256]{1,0:T(8,128)(2,1)S(1)}, u32[]{:S(2)}, u32[]{:S(2)}) %collective-permute-start) | collective-permute-done | bytes 131104 | tf_op jit(solution)/shard_map/ppermute | solution.py:27
  5.0 1.6 %collective-permute-start.4 = (bf16[256,256]{1,0:T(8,128)(2,1)S(1)}, bf16[256,256]{1,0:T(8,128)(2,1)S(1)}, u32[]{:S(2)}, u32[]{:S(2)}) collective-permute-start(bf16[256,256]{1,0:T(8,128)(2,1)S(1)} %get-tuple-element.29), channel_id=1, source_target_pairs={{0,1},{1,0},{2,3},{3,2},{4,5},{5,4},{6,7},{7,6},{8,9},{9,8},{10,11... | collective-permute-start | bytes 393224 | tf_op jit(solution)/shard_map/ppermute | solution.py:27
  6.8 2.2 %collective-permute-start.1 = (bf16[256,256]{1,0:T(8,128)(2,1)S(1)}, bf16[256,256]{1,0:T(8,128)(2,1)S(1)}, u32[]{:S(2)}, u32[]{:S(2)}) collective-permute-start(bf16[256,256]{1,0:T(8,128)(2,1)S(1)} %collective-permute-done), channel_id=1, source_target_pairs={{0,3},{1,2},{2,1},{3,0},{4,7},{5,6},{6,5},{7,4},{8,11},{9,10},{10,... | collective-permute-start | bytes 393224 | tf_op jit(solution)/shard_map/ppermute | solution.py:27
  9.1 1.7 %collective-permute-done.4 = bf16[256,256]{1,0:T(8,128)(2,1)S(1)} collective-permute-done((bf16[256,256]{1,0:T(8,128)(2,1)S(1)}, bf16[256,256]{1,0:T(8,128)(2,1)S(1)}, u32[]{:S(2)}, u32[]{:S(2)}) %collective-permute-start.4) | collective-permute-done | bytes 131104 | tf_op jit(solution)/shard_map/ppermute | solution.py:27
  10.8 3.1 %collective-permute-start.5 = (bf16[256,256]{1,0:T(8,128)(2,1)S(1)}, bf16[256,256]{1,0:T(8,128)(2,1)S(1)}, u32[]{:S(2)}, u32[]{:S(2)}) collective-permute-start(bf16[256,256]{1,0:T(8,128)(2,1)S(1)} %fusion.2), channel_id=1, source_target_pairs={{0,3},{1,2},{2,1},{3,0},{4,7},{5,6},{6,5},{7,4},{8,11},{9,10},{10,... | collective-permute-start | bytes 393224 | tf_op jit(solution)/shard_map/ppermute | solution.py:27
  14.2 2.9 %collective-permute-done.5 = bf16[256,256]{1,0:T(8,128)(2,1)S(1)} collective-permute-done((bf16[256,256]{1,0:T(8,128)(2,1)S(1)}, bf16[256,256]{1,0:T(8,128)(2,1)S(1)}, u32[]{:S(2)}, u32[]{:S(2)}) %collective-permute-start.5) | collective-permute-done | bytes 131104 | tf_op jit(solution)/shard_map/ppermute | solution.py:27
  17.2 1.3 %shard_map.95 = (bf16[704,512]{1,0:T(8,128)(2,1)S(1)}, bf16[704,512]{1,0:T(8,128)(2,1)S(1)}, bf16[704,512]{1,0:T(8,128)(2,1)S(1)}, bf16[704,512]{1,0:T(8,128)(2,1)S(1)}) custom-call(s32[32]{0:T(128)S(1)} %add.93.order_ref, bf16[2752,256]{1,0:T(8,128)(2,1)S(1)} %bitcast.34, bf16[2752,256]{1,0:T(8,128)(2,1)S(1)} %collective-permute-done.3.came), custom_call_target="tpu_custom_call" | custom-call | bytes 8388608 | tf_op jit(solution)/shard_map/pallas_call | solution.py:77
  19.8 2.8 %collective-permute-start.6 = (bf16[704,256]{1,0:T(8,128)(2,1)S(1)}, bf16[704,256]{1,0:T(8,128)(2,1)S(1)}, u32[]{:S(2)}, u32[]{:S(2)}) collective-permute-start(bf16[704,256]{1,0:T(8,128)(2,1)S(1)} %convolution_convert_fusion.1), channel_id=1, source_target_pairs={{0,192},{1,193},{2,194},{3,195},{4,196},{5,197},{6,198},{7,199},{8... | collective-permute-start | bytes 1081352 | tf_op jit(solution)/shard_map/ppermute | solution.py:27
  23.6 7.3 %collective-permute-done.8 = bf16[704,256]{1,0:T(8,128)(2,1)S(1)} collective-permute-done((bf16[704,256]{1,0:T(8,128)(2,1)S(1)}, bf16[704,256]{1,0:T(8,128)(2,1)S(1)}, u32[]{:S(2)}, u32[]{:S(2)}) %collective-permute-start.8) | collective-permute-done | bytes 360480 | tf_op jit(solution)/shard_map/ppermute | solution.py:27
  32.1 5.7 %collective-permute-done.9 = bf16[352,256]{1,0:T(8,128)(2,1)S(1)} collective-permute-done((bf16[352,256]{1,0:T(8,128)(2,1)S(1)}, bf16[352,256]{1,0:T(8,128)(2,1)S(1)}, u32[]{:S(2)}, u32[]{:S(2)}) %collective-permute-start.9) | collective-permute-done | bytes 180256 | tf_op jit(solution)/shard_map/ppermute | solution.py:27
  37.9 2.0 %collective-permute-start.11 = (bf16[176,256]{1,0:T(8,128)(2,1)S(1)}, bf16[176,256]{1,0:T(8,128)(2,1)S(1)}, u32[]{:S(2)}, u32[]{:S(2)}) collective-permute-start(bf16[176,256]{1,0:T(8,128)(2,1)S(1)} %get-tuple-element.52), channel_id=1, source_target_pairs={{0,56},{1,57},{2,58},{3,59},{4,60},{5,61},{6,62},{7,63},{8,16},{9,... | collective-permute-start | bytes 270344 | tf_op jit(solution)/shard_map/ppermute | solution.py:27
  39.9 4.0 %collective-permute-start.10 = (bf16[176,256]{1,0:T(8,128)(2,1)S(1)}, bf16[176,256]{1,0:T(8,128)(2,1)S(1)}, u32[]{:S(2)}, u32[]{:S(2)}) collective-permute-start(bf16[176,256]{1,0:T(8,128)(2,1)S(1)} %get-tuple-element.51), channel_id=1, source_target_pairs={{0,8},{1,9},{2,10},{3,11},{4,12},{5,13},{6,14},{7,15},{8,0},{9,1},... | collective-permute-start | bytes 270344 | tf_op jit(solution)/shard_map/ppermute | solution.py:27
  44.0 1.5 %collective-permute-start.14 = (bf16[88,256]{1,0:T(8,128)(2,1)S(1)}, bf16[88,256]{1,0:T(8,128)(2,1)S(1)}, u32[]{:S(2)}, u32[]{:S(2)}) collective-permute-start(bf16[88,256]{1,0:T(8,128)(2,1)S(1)} %slice.155), channel_id=1, source_target_pairs={{0,32},{1,33},{2,34},{3,35},{4,36},{5,37},{6,38},{7,39},{8,40},{9,... | collective-permute-start | bytes 135176 | tf_op jit(solution)/shard_map/ppermute | solution.py:27
  45.6 1.3 %collective-permute-done.10 = bf16[176,256]{1,0:T(8,128)(2,1)S(1)} collective-permute-done((bf16[176,256]{1,0:T(8,128)(2,1)S(1)}, bf16[176,256]{1,0:T(8,128)(2,1)S(1)}, u32[]{:S(2)}, u32[]{:S(2)}) %collective-permute-start.10) | collective-permute-done | bytes 90144 | tf_op jit(solution)/shard_map/ppermute | solution.py:27
  47.0 2.5 %collective-permute-start.12 = (bf16[88,256]{1,0:T(8,128)(2,1)S(1)}, bf16[88,256]{1,0:T(8,128)(2,1)S(1)}, u32[]{:S(2)}, u32[]{:S(2)}) collective-permute-start(bf16[88,256]{1,0:T(8,128)(2,1)S(1)} %get-tuple-element.46), channel_id=1, source_target_pairs={{0,16},{1,17},{2,18},{3,19},{4,20},{5,21},{6,22},{7,23},{8,24},{9,... | collective-permute-start | bytes 135176 | tf_op jit(solution)/shard_map/ppermute | solution.py:27
  49.5 1.3 %collective-permute-start.13 = (bf16[88,256]{1,0:T(8,128)(2,1)S(1)}, bf16[88,256]{1,0:T(8,128)(2,1)S(1)}, u32[]{:S(2)}, u32[]{:S(2)}) collective-permute-start(bf16[88,256]{1,0:T(8,128)(2,1)S(1)} %get-tuple-element.47), channel_id=1, source_target_pairs={{0,48},{1,49},{2,50},{3,51},{4,52},{5,53},{6,54},{7,55},{8,56},{9,... | collective-permute-start | bytes 135176 | tf_op jit(solution)/shard_map/ppermute | solution.py:27
  50.8 1.7 %collective-permute-done.14 = bf16[88,256]{1,0:T(8,128)(2,1)S(1)} collective-permute-done((bf16[88,256]{1,0:T(8,128)(2,1)S(1)}, bf16[88,256]{1,0:T(8,128)(2,1)S(1)}, u32[]{:S(2)}, u32[]{:S(2)}) %collective-permute-start.14) | collective-permute-done | bytes 45088 | tf_op jit(solution)/shard_map/ppermute | solution.py:27
  52.5 3.1 %collective-permute-done.13 = bf16[88,256]{1,0:T(8,128)(2,1)S(1)} collective-permute-done((bf16[88,256]{1,0:T(8,128)(2,1)S(1)}, bf16[88,256]{1,0:T(8,128)(2,1)S(1)}, u32[]{:S(2)}, u32[]{:S(2)}) %collective-permute-start.13) | collective-permute-done | bytes 45088 | tf_op jit(solution)/shard_map/ppermute | solution.py:27
  55.8 1.2 %collective-permute-done.15 = f32[43,256]{1,0:T(8,128)S(1)} collective-permute-done((f32[43,256]{1,0:T(8,128)S(1)}, f32[43,256]{1,0:T(8,128)S(1)}, u32[]{:S(2)}, u32[]{:S(2)}) %collective-permute-start.15) | collective-permute-done | bytes 44064 | tf_op jit(solution)/shard_map/ppermute | solution.py:27
  57.1 2.7 %collective-permute-start.18 = (bf16[64,512]{1,0:T(8,128)(2,1)S(1)}, bf16[64,512]{1,0:T(8,128)(2,1)S(1)}, u32[]{:S(2)}, u32[]{:S(2)}) collective-permute-start(bf16[64,512]{1,0:T(8,128)(2,1)S(1)} %pad.9), channel_id=1, source_target_pairs={{0,3},{1,2},{2,1},{3,0},{4,7},{5,6},{6,5},{7,4},{8,11},{9,10},{10,... | collective-permute-start | bytes 196616 | tf_op jit(solution)/shard_map/ppermute | solution.py:27
  59.9 1.5 %collective-permute-start.16 = (bf16[43,512]{1,0:T(8,128)(2,1)S(1)}, bf16[43,512]{1,0:T(8,128)(2,1)S(1)}, u32[]{:S(2)}, u32[]{:S(2)}) collective-permute-start(bf16[43,512]{1,0:T(8,128)(2,1)S(1)} %get-tuple-element.43), channel_id=1, source_target_pairs={{0,1},{1,0},{2,3},{3,2},{4,5},{5,4},{6,7},{7,6},{8,9},{9,8},{10,11... | collective-permute-start | bytes 132104 | tf_op jit(solution)/shard_map/ppermute | solution.py:27
  62.8 1.3 %collective-permute-done.16 = bf16[43,512]{1,0:T(8,128)(2,1)S(1)} collective-permute-done((bf16[43,512]{1,0:T(8,128)(2,1)S(1)}, bf16[43,512]{1,0:T(8,128)(2,1)S(1)}, u32[]{:S(2)}, u32[]{:S(2)}) %collective-permute-start.16) | collective-permute-done | bytes 44064 | tf_op jit(solution)/shard_map/ppermute | solution.py:27
  64.0 1.4 %collective-permute-done.17 = bf16[48,512]{1,0:T(8,128)(2,1)S(1)} collective-permute-done((bf16[48,512]{1,0:T(8,128)(2,1)S(1)}, bf16[48,512]{1,0:T(8,128)(2,1)S(1)}, u32[]{:S(2)}, u32[]{:S(2)}) %collective-permute-start.17) | collective-permute-done | bytes 49184 | tf_op jit(solution)/shard_map/ppermute | solution.py:27
  (72 shorter events, 9.3 us)
Async XLA Ops:
  0.6 6.0 %copy-start.7 = (s32[8]{0:T(128)S(1)}, s32[8]{0:T(128)}, u32[]{:S(2)}) copy-start(s32[8]{0:T(128)} %constant.50.clone) | copy-start | bytes 100
  0.6 6.0 %copy-start.6 = (s32[2,4]{1,0:T(2,128)S(1)}, s32[2,4]{1,0:T(2,128)}, u32[]{:S(2)}) copy-start(s32[2,4]{1,0:T(2,128)} %constant.51.clone) | copy-start | bytes 100
  3.4 1.4 %collective-permute-start = (bf16[256,256]{1,0:T(8,128)(2,1)S(1)}, bf16[256,256]{1,0:T(8,128)(2,1)S(1)}, u32[]{:S(2)}, u32[]{:S(2)}) collective-permute-start(bf16[256,256]{1,0:T(8,128)(2,1)S(1)} %get-tuple-element.20), channel_id=1, source_target_pairs={{0,4},{1,5},{2,6},{3,7},{4,0},{5,1},{6,2},{7,3},{8,12},{9,13},{10,... | collective-permute-start | bytes 393224 | tf_op jit(solution)/shard_map/ppermute | solution.py:27
  4.8 12.3 %collective-permute-start.3 = (bf16[2752,256]{1,0:T(8,128)(2,1)S(1)}, bf16[2752,256]{1,0:T(8,128)(2,1)S(1)}, u32[]{:S(2)}, u32[]{:S(2)}) collective-permute-start(bf16[2752,256]{1,0:T(8,128)(2,1)S(1)} %bitcast.33), channel_id=1, source_target_pairs={{0,4},{1,5},{2,6},{3,7},{4,0},{5,1},{6,2},{7,3},{8,12},{9,13},{10,... | collective-permute-start | bytes 4227080 | tf_op jit(solution)/shard_map/ppermute | solution.py:27
  5.0 5.8 %collective-permute-start.4 = (bf16[256,256]{1,0:T(8,128)(2,1)S(1)}, bf16[256,256]{1,0:T(8,128)(2,1)S(1)}, u32[]{:S(2)}, u32[]{:S(2)}) collective-permute-start(bf16[256,256]{1,0:T(8,128)(2,1)S(1)} %get-tuple-element.29), channel_id=1, source_target_pairs={{0,1},{1,0},{2,3},{3,2},{4,5},{5,4},{6,7},{7,6},{8,9},{9,8},{10,11... | collective-permute-start | bytes 393224 | tf_op jit(solution)/shard_map/ppermute | solution.py:27
  6.8 7.1 %collective-permute-start.1 = (bf16[256,256]{1,0:T(8,128)(2,1)S(1)}, bf16[256,256]{1,0:T(8,128)(2,1)S(1)}, u32[]{:S(2)}, u32[]{:S(2)}) collective-permute-start(bf16[256,256]{1,0:T(8,128)(2,1)S(1)} %collective-permute-done), channel_id=1, source_target_pairs={{0,3},{1,2},{2,1},{3,0},{4,7},{5,6},{6,5},{7,4},{8,11},{9,10},{10,... | collective-permute-start | bytes 393224 | tf_op jit(solution)/shard_map/ppermute | solution.py:27
  10.8 6.3 %collective-permute-start.5 = (bf16[256,256]{1,0:T(8,128)(2,1)S(1)}, bf16[256,256]{1,0:T(8,128)(2,1)S(1)}, u32[]{:S(2)}, u32[]{:S(2)}) collective-permute-start(bf16[256,256]{1,0:T(8,128)(2,1)S(1)} %fusion.2), channel_id=1, source_target_pairs={{0,3},{1,2},{2,1},{3,0},{4,7},{5,6},{6,5},{7,4},{8,11},{9,10},{10,... | collective-permute-start | bytes 393224 | tf_op jit(solution)/shard_map/ppermute | solution.py:27
  13.9 5.1 %collective-permute-start.2 = (bf16[256,256]{1,0:T(8,128)(2,1)S(1)}, bf16[256,256]{1,0:T(8,128)(2,1)S(1)}, u32[]{:S(2)}, u32[]{:S(2)}) collective-permute-start(bf16[256,256]{1,0:T(8,128)(2,1)S(1)} %fusion.1), channel_id=1, source_target_pairs={{0,1},{1,0},{2,3},{3,2},{4,5},{5,4},{6,7},{7,6},{8,9},{9,8},{10,11... | collective-permute-start | bytes 393224 | tf_op jit(solution)/shard_map/ppermute | solution.py:27
  19.8 11.8 %collective-permute-start.6 = (bf16[704,256]{1,0:T(8,128)(2,1)S(1)}, bf16[704,256]{1,0:T(8,128)(2,1)S(1)}, u32[]{:S(2)}, u32[]{:S(2)}) collective-permute-start(bf16[704,256]{1,0:T(8,128)(2,1)S(1)} %convolution_convert_fusion.1), channel_id=1, source_target_pairs={{0,192},{1,193},{2,194},{3,195},{4,196},{5,197},{6,198},{7,199},{8... | collective-permute-start | bytes 1081352 | tf_op jit(solution)/shard_map/ppermute | solution.py:27
  22.6 8.3 %collective-permute-start.8 = (bf16[704,256]{1,0:T(8,128)(2,1)S(1)}, bf16[704,256]{1,0:T(8,128)(2,1)S(1)}, u32[]{:S(2)}, u32[]{:S(2)}) collective-permute-start(bf16[704,256]{1,0:T(8,128)(2,1)S(1)} %convolution_convert_fusion.2), channel_id=1, source_target_pairs={{0,64},{1,65},{2,66},{3,67},{4,68},{5,69},{6,70},{7,71},{8,72},{9,... | collective-permute-start | bytes 1081352 | tf_op jit(solution)/shard_map/ppermute | solution.py:27
  31.0 6.8 %collective-permute-start.9 = (bf16[352,256]{1,0:T(8,128)(2,1)S(1)}, bf16[352,256]{1,0:T(8,128)(2,1)S(1)}, u32[]{:S(2)}, u32[]{:S(2)}) collective-permute-start(bf16[352,256]{1,0:T(8,128)(2,1)S(1)} %slice.153), channel_id=1, source_target_pairs={{0,192},{1,193},{2,194},{3,195},{4,196},{5,197},{6,198},{7,199},{8... | collective-permute-start | bytes 540680 | tf_op jit(solution)/shard_map/ppermute | solution.py:27
  31.7 12.3 %collective-permute-start.7 = (bf16[352,256]{1,0:T(8,128)(2,1)S(1)}, bf16[352,256]{1,0:T(8,128)(2,1)S(1)}, u32[]{:S(2)}, u32[]{:S(2)}) collective-permute-start(bf16[352,256]{1,0:T(8,128)(2,1)S(1)} %slice.154), channel_id=1, source_target_pairs={{0,64},{1,65},{2,66},{3,67},{4,68},{5,69},{6,70},{7,71},{8,72},{9,... | collective-permute-start | bytes 540680 | tf_op jit(solution)/shard_map/ppermute | solution.py:27
  37.9 7.7 %collective-permute-start.11 = (bf16[176,256]{1,0:T(8,128)(2,1)S(1)}, bf16[176,256]{1,0:T(8,128)(2,1)S(1)}, u32[]{:S(2)}, u32[]{:S(2)}) collective-permute-start(bf16[176,256]{1,0:T(8,128)(2,1)S(1)} %get-tuple-element.52), channel_id=1, source_target_pairs={{0,56},{1,57},{2,58},{3,59},{4,60},{5,61},{6,62},{7,63},{8,16},{9,... | collective-permute-start | bytes 270344 | tf_op jit(solution)/shard_map/ppermute | solution.py:27
  39.9 17.1 %copy-start.4 = (f32[1,43,512]{2,0,1:T(1,128)S(1)}, f32[1,43,512]{2,0,1:T(1,128)}, u32[]{:S(2)}) copy-start(f32[1,43,512]{2,0,1:T(1,128)} %param.11) | copy-start | bytes 264196
  39.9 17.1 %copy-start.5 = (f32[1,43,512]{2,0,1:T(1,128)S(1)}, f32[1,43,512]{2,0,1:T(1,128)}, u32[]{:S(2)}) copy-start(f32[1,43,512]{2,0,1:T(1,128)} %param.10) | copy-start | bytes 264196
  39.9 7.0 %collective-permute-start.10 = (bf16[176,256]{1,0:T(8,128)(2,1)S(1)}, bf16[176,256]{1,0:T(8,128)(2,1)S(1)}, u32[]{:S(2)}, u32[]{:S(2)}) collective-permute-start(bf16[176,256]{1,0:T(8,128)(2,1)S(1)} %get-tuple-element.51), channel_id=1, source_target_pairs={{0,8},{1,9},{2,10},{3,11},{4,12},{5,13},{6,14},{7,15},{8,0},{9,1},... | collective-permute-start | bytes 270344 | tf_op jit(solution)/shard_map/ppermute | solution.py:27
  44.0 8.5 %collective-permute-start.14 = (bf16[88,256]{1,0:T(8,128)(2,1)S(1)}, bf16[88,256]{1,0:T(8,128)(2,1)S(1)}, u32[]{:S(2)}, u32[]{:S(2)}) collective-permute-start(bf16[88,256]{1,0:T(8,128)(2,1)S(1)} %slice.155), channel_id=1, source_target_pairs={{0,32},{1,33},{2,34},{3,35},{4,36},{5,37},{6,38},{7,39},{8,40},{9,... | collective-permute-start | bytes 135176 | tf_op jit(solution)/shard_map/ppermute | solution.py:27
  47.0 5.6 %collective-permute-start.12 = (bf16[88,256]{1,0:T(8,128)(2,1)S(1)}, bf16[88,256]{1,0:T(8,128)(2,1)S(1)}, u32[]{:S(2)}, u32[]{:S(2)}) collective-permute-start(bf16[88,256]{1,0:T(8,128)(2,1)S(1)} %get-tuple-element.46), channel_id=1, source_target_pairs={{0,16},{1,17},{2,18},{3,19},{4,20},{5,21},{6,22},{7,23},{8,24},{9,... | collective-permute-start | bytes 135176 | tf_op jit(solution)/shard_map/ppermute | solution.py:27
  49.5 6.2 %collective-permute-start.13 = (bf16[88,256]{1,0:T(8,128)(2,1)S(1)}, bf16[88,256]{1,0:T(8,128)(2,1)S(1)}, u32[]{:S(2)}, u32[]{:S(2)}) collective-permute-start(bf16[88,256]{1,0:T(8,128)(2,1)S(1)} %get-tuple-element.47), channel_id=1, source_target_pairs={{0,48},{1,49},{2,50},{3,51},{4,52},{5,53},{6,54},{7,55},{8,56},{9,... | collective-permute-start | bytes 135176 | tf_op jit(solution)/shard_map/ppermute | solution.py:27
  55.7 1.3 %collective-permute-start.15 = (f32[43,256]{1,0:T(8,128)S(1)}, f32[43,256]{1,0:T(8,128)S(1)}, u32[]{:S(2)}, u32[]{:S(2)}) collective-permute-start(f32[43,256]{1,0:T(8,128)S(1)} %slice_select_fusion), channel_id=1, source_target_pairs={{0,4},{1,5},{2,6},{3,7},{4,0},{5,1},{6,2},{7,3},{8,12},{9,13},{10,... | collective-permute-start | bytes 132104 | tf_op jit(solution)/shard_map/ppermute | solution.py:27
  57.0 8.7 %copy-start.1 = (bf16[1,1024,512]{2,1,0:T(8,128)(2,1)S(1)}, bf16[1,1024,512]{2,1,0:T(8,128)(2,1)}, u32[]{:S(2)}) copy-start(bf16[1,1024,512]{2,1,0:T(8,128)(2,1)} %param.9) | copy-start | bytes 3145732
  57.1 8.3 %collective-permute-start.18 = (bf16[64,512]{1,0:T(8,128)(2,1)S(1)}, bf16[64,512]{1,0:T(8,128)(2,1)S(1)}, u32[]{:S(2)}, u32[]{:S(2)}) collective-permute-start(bf16[64,512]{1,0:T(8,128)(2,1)S(1)} %pad.9), channel_id=1, source_target_pairs={{0,3},{1,2},{2,1},{3,0},{4,7},{5,6},{6,5},{7,4},{8,11},{9,10},{10,... | collective-permute-start | bytes 196616 | tf_op jit(solution)/shard_map/ppermute | solution.py:27
  59.9 5.6 %collective-permute-start.17 = (bf16[48,512]{1,0:T(8,128)(2,1)S(1)}, bf16[48,512]{1,0:T(8,128)(2,1)S(1)}, u32[]{:S(2)}, u32[]{:S(2)}) collective-permute-start(bf16[48,512]{1,0:T(8,128)(2,1)S(1)} %pad.8), channel_id=1, source_target_pairs={{0,2},{1,3},{2,0},{3,1},{4,6},{5,7},{6,4},{7,5},{8,10},{9,11},{10,... | collective-permute-start | bytes 147464 | tf_op jit(solution)/shard_map/ppermute | solution.py:27
  59.9 4.2 %collective-permute-start.16 = (bf16[43,512]{1,0:T(8,128)(2,1)S(1)}, bf16[43,512]{1,0:T(8,128)(2,1)S(1)}, u32[]{:S(2)}, u32[]{:S(2)}) collective-permute-start(bf16[43,512]{1,0:T(8,128)(2,1)S(1)} %get-tuple-element.43), channel_id=1, source_target_pairs={{0,1},{1,0},{2,3},{3,2},{4,5},{5,4},{6,7},{7,6},{8,9},{9,8},{10,11... | collective-permute-start | bytes 132104 | tf_op jit(solution)/shard_map/ppermute | solution.py:27
  (3 other events, 4.2 us)

commit v13 on v12

--- a/solution.py
+++ b/solution.py
@@ -132,8 +132,8 @@
 
     mine, mine_sent, theirs = project(core.reshape(1), features[0], basis[0])
     columns = cotangent[0].T
-    theirs, sent = lax.optimization_barrier((swap_core(theirs), columns))
-    other_columns = swap_core(sent)
+    other_columns = swap_core(columns)
+    theirs = swap_core(theirs)
     came = [swap_y(p, m[0]) for p, m in zip((mine_sent, theirs), PAIRS)]
     chunks = [p.astype(F32) + c.astype(F32) for p, c in zip((mine, theirs), came)]
     came = [swap_y(p.astype(BF), m[1]) for p, m in zip(chunks, PAIRS)]
@@ -144,7 +144,7 @@
 
     sent = [dot(part, projected).astype(BF) for part in parts[::2]]
     came = [swap_x(value, m[0]) for value, m in zip(sent, PAIRS)]
-    projected, sent = lax.optimization_barrier((projected, sent))
+    projected, sent[1] = lax.optimization_barrier((projected, sent[1]))
     kept = lax.optimization_barrier([dot(part, projected) for part in parts[1::2]])
     kept = [k + c.astype(F32) for k, c in zip(kept, came)]
     came = [swap_x(k[:HALF].astype(BF), m[1]) for k, m in zip(kept, PAIRS)]

time: 67.3 us -> 67.9 us (level)
  other arithmetic: 0.79 us -> 2.57 us
  waiting for transfers between devices: 29.6 us -> 27.9 us
    ppermute x19, waiting for transfers between devices: 29.6 us -> 27.9 us  [send(): return lax.ppermute(value, ('dp', 'tensor'), pairs)]
    convert_element_type x2, other arithmetic: 0.1 us -> 1.01 us  [local(): projected = jnp.concatenate([p.astype(BF) for p in chunks], axis=0)]
    convert_element_type x2, other arithmetic: 0.07 us -> 0.96 us  [local(): came = [swap_y(p.astype(BF), m[1]) for p, m in zip(chunks, PAIRS)]]
  transfers between devices with their start and end apart: 19 -> 19, of which waited for: 12 -> 10; matrix products, arithmetic and copies ran while one was open for 4% -> 7% of each run, Pallas kernels for 2% -> 3%
where the time goes in v13:
time: 67.9 us; the launch traced here: 67.7 us
  waiting for transfers between devices  27.9 us (41%)
  starting transfers between devices  27.6 us (41%)
  local copies, waits for them, and re-layouts  5.07 us (7%)
  other arithmetic  2.57 us (4%)
  matrix products  1.88 us (3%)
  Pallas kernels  1.76 us (3%)
  between operations  0.95 us (1%)
    ppermute x19, waiting for transfers between devices, send(): return lax.ppermute(value, ('dp', 'tensor'), pairs)  27.9 us
    ppermute x19, starting transfers between devices, send(): return lax.ppermute(value, ('dp', 'tensor'), pairs)  27.6 us
    unnamed x18, local copies, waits for them, and re-layouts  3.75 us
    dot_general x5, matrix products, dot(): lax.dot_general(a, b, (((1,), (0,)), ((), ())), preferred_element_type=F32)  1.88 us
  transfers between devices with their start and end apart: 19, of which 10 were waited for; matrix products, arithmetic and copies ran while one was open for 7% of the time, Pallas kernels for 3%

profile of v13, /device:TPU:32, one launch (start us, length us, event | category | flops | bytes accessed | tf_op | source)
XLA Modules:
  0.0 67.7 jit_solution(12903738683967821748)
XLA Ops:
  0.8 1.2 %copy-done = bf16[1,1024,512]{2,1,0:T(8,128)(2,1)S(1)} copy-done((bf16[1,1024,512]{2,1,0:T(8,128)(2,1)S(1)}, bf16[1,1024,512]{2,1,0:T(8,128)(2,1)}, u32[]{:S(2)}) %copy-start) | copy-done | bytes 1048600
  2.0 1.0 %copy-done.3 = bf16[1,256,1024]{2,1,0:T(8,128)(2,1)S(1)} copy-done((bf16[1,256,1024]{2,1,0:T(8,128)(2,1)S(1)}, bf16[1,256,1024]{2,1,0:T(8,128)(2,1)}, u32[]{:S(2)}) %copy-start.3) | copy-done | bytes 524312
  4.1 1.6 %collective-permute-start.4 = (bf16[256,256]{1,0:T(8,128)(2,1)S(1)}, bf16[256,256]{1,0:T(8,128)(2,1)}, u32[]{:S(2)}, u32[]{:S(2)}) collective-permute-start(bf16[256,256]{1,0:T(8,128)(2,1)S(1)} %get-tuple-element.25), channel_id=1, source_target_pairs={{0,1},{1,0},{2,3},{3,2},{4,5},{5,4},{6,7},{7,6},{8,9},{9,8},{10,11... | collective-permute-start | bytes 393224 | tf_op jit(solution)/shard_map/ppermute | solution.py:27
  5.9 2.3 %collective-permute-start.1 = (bf16[256,256]{1,0:T(8,128)(2,1)S(1)}, bf16[256,256]{1,0:T(8,128)(2,1)S(1)}, u32[]{:S(2)}, u32[]{:S(2)}) collective-permute-start(bf16[256,256]{1,0:T(8,128)(2,1)S(1)} %collective-permute-done), channel_id=1, source_target_pairs={{0,3},{1,2},{2,1},{3,0},{4,7},{5,6},{6,5},{7,4},{8,11},{9,10},{10,... | collective-permute-start | bytes 393224 | tf_op jit(solution)/shard_map/ppermute | solution.py:27
  8.2 1.5 %collective-permute-done.4 = bf16[256,256]{1,0:T(8,128)(2,1)} collective-permute-done((bf16[256,256]{1,0:T(8,128)(2,1)S(1)}, bf16[256,256]{1,0:T(8,128)(2,1)}, u32[]{:S(2)}, u32[]{:S(2)}) %collective-permute-start.4) | collective-permute-done | bytes 131104 | tf_op jit(solution)/shard_map/ppermute | solution.py:27
  10.6 3.1 %collective-permute-start.5 = (bf16[256,256]{1,0:T(8,128)(2,1)S(1)}, bf16[256,256]{1,0:T(8,128)(2,1)S(1)}, u32[]{:S(2)}, u32[]{:S(2)}) collective-permute-start(bf16[256,256]{1,0:T(8,128)(2,1)S(1)} %fusion.2), channel_id=1, source_target_pairs={{0,3},{1,2},{2,1},{3,0},{4,7},{5,6},{6,5},{7,4},{8,11},{9,10},{10,... | collective-permute-start | bytes 393224 | tf_op jit(solution)/shard_map/ppermute | solution.py:27
  14.0 2.9 %collective-permute-done.5 = bf16[256,256]{1,0:T(8,128)(2,1)S(1)} collective-permute-done((bf16[256,256]{1,0:T(8,128)(2,1)S(1)}, bf16[256,256]{1,0:T(8,128)(2,1)S(1)}, u32[]{:S(2)}, u32[]{:S(2)}) %collective-permute-start.5) | collective-permute-done | bytes 131104 | tf_op jit(solution)/shard_map/ppermute | solution.py:27
  17.9 1.3 %shard_map.95 = (bf16[704,512]{1,0:T(8,128)(2,1)S(1)}, bf16[704,512]{1,0:T(8,128)(2,1)S(1)}, bf16[704,512]{1,0:T(8,128)(2,1)S(1)}, bf16[704,512]{1,0:T(8,128)(2,1)S(1)}) custom-call(s32[32]{0:T(128)S(1)} %add.93.order_ref, bf16[2752,256]{1,0:T(8,128)(2,1)S(1)} %bitcast.34, bf16[2752,256]{1,0:T(8,128)(2,1)S(1)} %collective-permute-done.3.came), custom_call_target="tpu_custom_call" | custom-call | bytes 8388608 | tf_op jit(solution)/shard_map/pallas_call | solution.py:77
  19.6 2.8 %collective-permute-start.6 = (bf16[704,256]{1,0:T(8,128)(2,1)S(1)}, bf16[704,256]{1,0:T(8,128)(2,1)S(1)}, u32[]{:S(2)}, u32[]{:S(2)}) collective-permute-start(bf16[704,256]{1,0:T(8,128)(2,1)S(1)} %convolution_convert_fusion.2), channel_id=1, source_target_pairs={{0,192},{1,193},{2,194},{3,195},{4,196},{5,197},{6,198},{7,199},{8... | collective-permute-start | bytes 1081352 | tf_op jit(solution)/shard_map/ppermute | solution.py:27
  23.8 7.3 %collective-permute-done.8 = bf16[704,256]{1,0:T(8,128)(2,1)S(1)} collective-permute-done((bf16[704,256]{1,0:T(8,128)(2,1)S(1)}, bf16[704,256]{1,0:T(8,128)(2,1)S(1)}, u32[]{:S(2)}, u32[]{:S(2)}) %collective-permute-start.8) | collective-permute-done | bytes 360480 | tf_op jit(solution)/shard_map/ppermute | solution.py:27
  32.3 5.8 %collective-permute-done.9 = bf16[352,256]{1,0:T(8,128)(2,1)S(1)} collective-permute-done((bf16[352,256]{1,0:T(8,128)(2,1)S(1)}, bf16[352,256]{1,0:T(8,128)(2,1)S(1)}, u32[]{:S(2)}, u32[]{:S(2)}) %collective-permute-start.9) | collective-permute-done | bytes 180256 | tf_op jit(solution)/shard_map/ppermute | solution.py:27
  38.1 2.0 %collective-permute-start.11 = (bf16[176,256]{1,0:T(8,128)(2,1)S(1)}, bf16[176,256]{1,0:T(8,128)(2,1)S(1)}, u32[]{:S(2)}, u32[]{:S(2)}) collective-permute-start(bf16[176,256]{1,0:T(8,128)(2,1)S(1)} %get-tuple-element.48), channel_id=1, source_target_pairs={{0,56},{1,57},{2,58},{3,59},{4,60},{5,61},{6,62},{7,63},{8,16},{9,... | collective-permute-start | bytes 270344 | tf_op jit(solution)/shard_map/ppermute | solution.py:27
  40.1 4.0 %collective-permute-start.10 = (bf16[176,256]{1,0:T(8,128)(2,1)S(1)}, bf16[176,256]{1,0:T(8,128)(2,1)S(1)}, u32[]{:S(2)}, u32[]{:S(2)}) collective-permute-start(bf16[176,256]{1,0:T(8,128)(2,1)S(1)} %get-tuple-element.47), channel_id=1, source_target_pairs={{0,8},{1,9},{2,10},{3,11},{4,12},{5,13},{6,14},{7,15},{8,0},{9,1},... | collective-permute-start | bytes 270344 | tf_op jit(solution)/shard_map/ppermute | solution.py:27
  44.2 1.5 %collective-permute-start.14 = (bf16[88,256]{1,0:T(8,128)(2,1)S(1)}, bf16[88,256]{1,0:T(8,128)(2,1)S(1)}, u32[]{:S(2)}, u32[]{:S(2)}) collective-permute-start(bf16[88,256]{1,0:T(8,128)(2,1)S(1)} %slice.155), channel_id=1, source_target_pairs={{0,32},{1,33},{2,34},{3,35},{4,36},{5,37},{6,38},{7,39},{8,40},{9,... | collective-permute-start | bytes 135176 | tf_op jit(solution)/shard_map/ppermute | solution.py:27
  45.8 1.4 %collective-permute-done.10 = bf16[176,256]{1,0:T(8,128)(2,1)S(1)} collective-permute-done((bf16[176,256]{1,0:T(8,128)(2,1)S(1)}, bf16[176,256]{1,0:T(8,128)(2,1)S(1)}, u32[]{:S(2)}, u32[]{:S(2)}) %collective-permute-start.10) | collective-permute-done | bytes 90144 | tf_op jit(solution)/shard_map/ppermute | solution.py:27
  47.2 2.6 %collective-permute-start.12 = (bf16[88,256]{1,0:T(8,128)(2,1)S(1)}, bf16[88,256]{1,0:T(8,128)(2,1)S(1)}, u32[]{:S(2)}, u32[]{:S(2)}) collective-permute-start(bf16[88,256]{1,0:T(8,128)(2,1)S(1)} %get-tuple-element.42), channel_id=1, source_target_pairs={{0,16},{1,17},{2,18},{3,19},{4,20},{5,21},{6,22},{7,23},{8,24},{9,... | collective-permute-start | bytes 135176 | tf_op jit(solution)/shard_map/ppermute | solution.py:27
  49.7 1.2 %collective-permute-start.13 = (bf16[88,256]{1,0:T(8,128)(2,1)S(1)}, bf16[88,256]{1,0:T(8,128)(2,1)S(1)}, u32[]{:S(2)}, u32[]{:S(2)}) collective-permute-start(bf16[88,256]{1,0:T(8,128)(2,1)S(1)} %get-tuple-element.43), channel_id=1, source_target_pairs={{0,48},{1,49},{2,50},{3,51},{4,52},{5,53},{6,54},{7,55},{8,56},{9,... | collective-permute-start | bytes 135176 | tf_op jit(solution)/shard_map/ppermute | solution.py:27
  51.0 1.8 %collective-permute-done.14 = bf16[88,256]{1,0:T(8,128)(2,1)S(1)} collective-permute-done((bf16[88,256]{1,0:T(8,128)(2,1)S(1)}, bf16[88,256]{1,0:T(8,128)(2,1)S(1)}, u32[]{:S(2)}, u32[]{:S(2)}) %collective-permute-start.14) | collective-permute-done | bytes 45088 | tf_op jit(solution)/shard_map/ppermute | solution.py:27
  52.7 3.1 %collective-permute-done.13 = bf16[88,256]{1,0:T(8,128)(2,1)S(1)} collective-permute-done((bf16[88,256]{1,0:T(8,128)(2,1)S(1)}, bf16[88,256]{1,0:T(8,128)(2,1)S(1)}, u32[]{:S(2)}, u32[]{:S(2)}) %collective-permute-start.13) | collective-permute-done | bytes 45088 | tf_op jit(solution)/shard_map/ppermute | solution.py:27
  56.0 1.2 %collective-permute-done.15 = f32[43,256]{1,0:T(8,128)S(1)} collective-permute-done((f32[43,256]{1,0:T(8,128)S(1)}, f32[43,256]{1,0:T(8,128)S(1)}, u32[]{:S(2)}, u32[]{:S(2)}) %collective-permute-start.15) | collective-permute-done | bytes 44064 | tf_op jit(solution)/shard_map/ppermute | solution.py:27
  57.4 3.0 %collective-permute-start.18 = (bf16[64,512]{1,0:T(8,128)(2,1)S(1)}, bf16[64,512]{1,0:T(8,128)(2,1)S(1)}, u32[]{:S(2)}, u32[]{:S(2)}) collective-permute-start(bf16[64,512]{1,0:T(8,128)(2,1)S(1)} %pad.9), channel_id=1, source_target_pairs={{0,3},{1,2},{2,1},{3,0},{4,7},{5,6},{6,5},{7,4},{8,11},{9,10},{10,... | collective-permute-start | bytes 196616 | tf_op jit(solution)/shard_map/ppermute | solution.py:27
  60.5 1.1 %collective-permute-start.16 = (bf16[43,512]{1,0:T(8,128)(2,1)S(1)}, bf16[43,512]{1,0:T(8,128)(2,1)S(1)}, u32[]{:S(2)}, u32[]{:S(2)}) collective-permute-start(bf16[43,512]{1,0:T(8,128)(2,1)S(1)} %get-tuple-element.39), channel_id=1, source_target_pairs={{0,1},{1,0},{2,3},{3,2},{4,5},{5,4},{6,7},{7,6},{8,9},{9,8},{10,11... | collective-permute-start | bytes 132104 | tf_op jit(solution)/shard_map/ppermute | solution.py:27
  63.1 1.6 %collective-permute-done.16 = bf16[43,512]{1,0:T(8,128)(2,1)S(1)} collective-permute-done((bf16[43,512]{1,0:T(8,128)(2,1)S(1)}, bf16[43,512]{1,0:T(8,128)(2,1)S(1)}, u32[]{:S(2)}, u32[]{:S(2)}) %collective-permute-start.16) | collective-permute-done | bytes 44064 | tf_op jit(solution)/shard_map/ppermute | solution.py:27
  64.7 1.4 %collective-permute-done.17 = bf16[48,512]{1,0:T(8,128)(2,1)S(1)} collective-permute-done((bf16[48,512]{1,0:T(8,128)(2,1)S(1)}, bf16[48,512]{1,0:T(8,128)(2,1)S(1)}, u32[]{:S(2)}, u32[]{:S(2)}) %collective-permute-start.17) | collective-permute-done | bytes 49184 | tf_op jit(solution)/shard_map/ppermute | solution.py:27
  (72 shorter events, 10.0 us)
Async XLA Ops:
  0.6 5.1 %copy-start.6 = (s32[2,4]{1,0:T(2,128)S(1)}, s32[2,4]{1,0:T(2,128)}, u32[]{:S(2)}) copy-start(s32[2,4]{1,0:T(2,128)} %constant.51.clone) | copy-start | bytes 100
  0.7 17.2 %collective-permute-start.3 = (bf16[2752,256]{1,0:T(8,128)(2,1)}, bf16[2752,256]{1,0:T(8,128)(2,1)S(1)}, u32[]{:S(2)}, u32[]{:S(2)}) collective-permute-start(bf16[2752,256]{1,0:T(8,128)(2,1)} %bitcast.33), channel_id=1, source_target_pairs={{0,4},{1,5},{2,6},{3,7},{4,0},{5,1},{6,2},{7,3},{8,12},{9,13},{10,... | collective-permute-start | bytes 4227080 | tf_op jit(solution)/shard_map/ppermute | solution.py:27
  3.0 14.8 %copy-start.2 = (bf16[1,256,2752]{1,2,0:T(8,128)(2,1)S(1)}, bf16[1,256,2752]{1,2,0:T(8,128)(2,1)}, u32[]{:S(2)}) copy-start(bf16[1,256,2752]{1,2,0:T(8,128)(2,1)} %param.8) | copy-start | bytes 4227076
  3.5 2.4 %collective-permute-start = (bf16[256,256]{1,0:T(8,128)(2,1)S(1)}, bf16[256,256]{1,0:T(8,128)(2,1)S(1)}, u32[]{:S(2)}, u32[]{:S(2)}) collective-permute-start(bf16[256,256]{1,0:T(8,128)(2,1)S(1)} %get-tuple-element.18), channel_id=1, source_target_pairs={{0,4},{1,5},{2,6},{3,7},{4,0},{5,1},{6,2},{7,3},{8,12},{9,13},{10,... | collective-permute-start | bytes 393224 | tf_op jit(solution)/shard_map/ppermute | solution.py:27
  4.1 5.6 %collective-permute-start.4 = (bf16[256,256]{1,0:T(8,128)(2,1)S(1)}, bf16[256,256]{1,0:T(8,128)(2,1)}, u32[]{:S(2)}, u32[]{:S(2)}) collective-permute-start(bf16[256,256]{1,0:T(8,128)(2,1)S(1)} %get-tuple-element.25), channel_id=1, source_target_pairs={{0,1},{1,0},{2,3},{3,2},{4,5},{5,4},{6,7},{7,6},{8,9},{9,8},{10,11... | collective-permute-start | bytes 393224 | tf_op jit(solution)/shard_map/ppermute | solution.py:27
  5.9 7.8 %collective-permute-start.1 = (bf16[256,256]{1,0:T(8,128)(2,1)S(1)}, bf16[256,256]{1,0:T(8,128)(2,1)S(1)}, u32[]{:S(2)}, u32[]{:S(2)}) collective-permute-start(bf16[256,256]{1,0:T(8,128)(2,1)S(1)} %collective-permute-done), channel_id=1, source_target_pairs={{0,3},{1,2},{2,1},{3,0},{4,7},{5,6},{6,5},{7,4},{8,11},{9,10},{10,... | collective-permute-start | bytes 393224 | tf_op jit(solution)/shard_map/ppermute | solution.py:27
  10.6 6.3 %collective-permute-start.5 = (bf16[256,256]{1,0:T(8,128)(2,1)S(1)}, bf16[256,256]{1,0:T(8,128)(2,1)S(1)}, u32[]{:S(2)}, u32[]{:S(2)}) collective-permute-start(bf16[256,256]{1,0:T(8,128)(2,1)S(1)} %fusion.2), channel_id=1, source_target_pairs={{0,3},{1,2},{2,1},{3,0},{4,7},{5,6},{6,5},{7,4},{8,11},{9,10},{10,... | collective-permute-start | bytes 393224 | tf_op jit(solution)/shard_map/ppermute | solution.py:27
  13.8 5.4 %collective-permute-start.2 = (bf16[256,256]{1,0:T(8,128)(2,1)S(1)}, bf16[256,256]{1,0:T(8,128)(2,1)S(1)}, u32[]{:S(2)}, u32[]{:S(2)}) collective-permute-start(bf16[256,256]{1,0:T(8,128)(2,1)S(1)} %fusion.1), channel_id=1, source_target_pairs={{0,1},{1,0},{2,3},{3,2},{4,5},{5,4},{6,7},{7,6},{8,9},{9,8},{10,11... | collective-permute-start | bytes 393224 | tf_op jit(solution)/shard_map/ppermute | solution.py:27
  19.6 12.2 %collective-permute-start.6 = (bf16[704,256]{1,0:T(8,128)(2,1)S(1)}, bf16[704,256]{1,0:T(8,128)(2,1)S(1)}, u32[]{:S(2)}, u32[]{:S(2)}) collective-permute-start(bf16[704,256]{1,0:T(8,128)(2,1)S(1)} %convolution_convert_fusion.2), channel_id=1, source_target_pairs={{0,192},{1,193},{2,194},{3,195},{4,196},{5,197},{6,198},{7,199},{8... | collective-permute-start | bytes 1081352 | tf_op jit(solution)/shard_map/ppermute | solution.py:27
  22.8 8.3 %collective-permute-start.8 = (bf16[704,256]{1,0:T(8,128)(2,1)S(1)}, bf16[704,256]{1,0:T(8,128)(2,1)S(1)}, u32[]{:S(2)}, u32[]{:S(2)}) collective-permute-start(bf16[704,256]{1,0:T(8,128)(2,1)S(1)} %convolution_convert_fusion.1), channel_id=1, source_target_pairs={{0,64},{1,65},{2,66},{3,67},{4,68},{5,69},{6,70},{7,71},{8,72},{9,... | collective-permute-start | bytes 1081352 | tf_op jit(solution)/shard_map/ppermute | solution.py:27
  31.2 6.8 %collective-permute-start.9 = (bf16[352,256]{1,0:T(8,128)(2,1)S(1)}, bf16[352,256]{1,0:T(8,128)(2,1)S(1)}, u32[]{:S(2)}, u32[]{:S(2)}) collective-permute-start(bf16[352,256]{1,0:T(8,128)(2,1)S(1)} %slice.153), channel_id=1, source_target_pairs={{0,192},{1,193},{2,194},{3,195},{4,196},{5,197},{6,198},{7,199},{8... | collective-permute-start | bytes 540680 | tf_op jit(solution)/shard_map/ppermute | solution.py:27
  31.9 12.2 %collective-permute-start.7 = (bf16[352,256]{1,0:T(8,128)(2,1)S(1)}, bf16[352,256]{1,0:T(8,128)(2,1)S(1)}, u32[]{:S(2)}, u32[]{:S(2)}) collective-permute-start(bf16[352,256]{1,0:T(8,128)(2,1)S(1)} %slice.154), channel_id=1, source_target_pairs={{0,64},{1,65},{2,66},{3,67},{4,68},{5,69},{6,70},{7,71},{8,72},{9,... | collective-permute-start | bytes 540680 | tf_op jit(solution)/shard_map/ppermute | solution.py:27
  38.1 7.7 %collective-permute-start.11 = (bf16[176,256]{1,0:T(8,128)(2,1)S(1)}, bf16[176,256]{1,0:T(8,128)(2,1)S(1)}, u32[]{:S(2)}, u32[]{:S(2)}) collective-permute-start(bf16[176,256]{1,0:T(8,128)(2,1)S(1)} %get-tuple-element.48), channel_id=1, source_target_pairs={{0,56},{1,57},{2,58},{3,59},{4,60},{5,61},{6,62},{7,63},{8,16},{9,... | collective-permute-start | bytes 270344 | tf_op jit(solution)/shard_map/ppermute | solution.py:27
  40.1 17.2 %copy-start.4 = (f32[1,43,512]{2,0,1:T(1,128)S(1)}, f32[1,43,512]{2,0,1:T(1,128)}, u32[]{:S(2)}) copy-start(f32[1,43,512]{2,0,1:T(1,128)} %param.11) | copy-start | bytes 264196
  40.1 17.2 %copy-start.5 = (f32[1,43,512]{2,0,1:T(1,128)S(1)}, f32[1,43,512]{2,0,1:T(1,128)}, u32[]{:S(2)}) copy-start(f32[1,43,512]{2,0,1:T(1,128)} %param.10) | copy-start | bytes 264196
  40.1 7.0 %collective-permute-start.10 = (bf16[176,256]{1,0:T(8,128)(2,1)S(1)}, bf16[176,256]{1,0:T(8,128)(2,1)S(1)}, u32[]{:S(2)}, u32[]{:S(2)}) collective-permute-start(bf16[176,256]{1,0:T(8,128)(2,1)S(1)} %get-tuple-element.47), channel_id=1, source_target_pairs={{0,8},{1,9},{2,10},{3,11},{4,12},{5,13},{6,14},{7,15},{8,0},{9,1},... | collective-permute-start | bytes 270344 | tf_op jit(solution)/shard_map/ppermute | solution.py:27
  44.2 8.5 %collective-permute-start.14 = (bf16[88,256]{1,0:T(8,128)(2,1)S(1)}, bf16[88,256]{1,0:T(8,128)(2,1)S(1)}, u32[]{:S(2)}, u32[]{:S(2)}) collective-permute-start(bf16[88,256]{1,0:T(8,128)(2,1)S(1)} %slice.155), channel_id=1, source_target_pairs={{0,32},{1,33},{2,34},{3,35},{4,36},{5,37},{6,38},{7,39},{8,40},{9,... | collective-permute-start | bytes 135176 | tf_op jit(solution)/shard_map/ppermute | solution.py:27
  47.2 5.6 %collective-permute-start.12 = (bf16[88,256]{1,0:T(8,128)(2,1)S(1)}, bf16[88,256]{1,0:T(8,128)(2,1)S(1)}, u32[]{:S(2)}, u32[]{:S(2)}) collective-permute-start(bf16[88,256]{1,0:T(8,128)(2,1)S(1)} %get-tuple-element.42), channel_id=1, source_target_pairs={{0,16},{1,17},{2,18},{3,19},{4,20},{5,21},{6,22},{7,23},{8,24},{9,... | collective-permute-start | bytes 135176 | tf_op jit(solution)/shard_map/ppermute | solution.py:27
  49.7 6.2 %collective-permute-start.13 = (bf16[88,256]{1,0:T(8,128)(2,1)S(1)}, bf16[88,256]{1,0:T(8,128)(2,1)S(1)}, u32[]{:S(2)}, u32[]{:S(2)}) collective-permute-start(bf16[88,256]{1,0:T(8,128)(2,1)S(1)} %get-tuple-element.43), channel_id=1, source_target_pairs={{0,48},{1,49},{2,50},{3,51},{4,52},{5,53},{6,54},{7,55},{8,56},{9,... | collective-permute-start | bytes 135176 | tf_op jit(solution)/shard_map/ppermute | solution.py:27
  55.9 1.3 %collective-permute-start.15 = (f32[43,256]{1,0:T(8,128)S(1)}, f32[43,256]{1,0:T(8,128)S(1)}, u32[]{:S(2)}, u32[]{:S(2)}) collective-permute-start(f32[43,256]{1,0:T(8,128)S(1)} %slice_select_fusion), channel_id=1, source_target_pairs={{0,4},{1,5},{2,6},{3,7},{4,0},{5,1},{6,2},{7,3},{8,12},{9,13},{10,... | collective-permute-start | bytes 132104 | tf_op jit(solution)/shard_map/ppermute | solution.py:27
  57.3 9.1 %copy-start.1 = (bf16[1,1024,512]{2,1,0:T(8,128)(2,1)S(1)}, bf16[1,1024,512]{2,1,0:T(8,128)(2,1)}, u32[]{:S(2)}) copy-start(bf16[1,1024,512]{2,1,0:T(8,128)(2,1)} %param.9) | copy-start | bytes 3145732
  57.4 8.7 %collective-permute-start.18 = (bf16[64,512]{1,0:T(8,128)(2,1)S(1)}, bf16[64,512]{1,0:T(8,128)(2,1)S(1)}, u32[]{:S(2)}, u32[]{:S(2)}) collective-permute-start(bf16[64,512]{1,0:T(8,128)(2,1)S(1)} %pad.9), channel_id=1, source_target_pairs={{0,3},{1,2},{2,1},{3,0},{4,7},{5,6},{6,5},{7,4},{8,11},{9,10},{10,... | collective-permute-start | bytes 196616 | tf_op jit(solution)/shard_map/ppermute | solution.py:27
  60.5 5.6 %collective-permute-start.17 = (bf16[48,512]{1,0:T(8,128)(2,1)S(1)}, bf16[48,512]{1,0:T(8,128)(2,1)S(1)}, u32[]{:S(2)}, u32[]{:S(2)}) collective-permute-start(bf16[48,512]{1,0:T(8,128)(2,1)S(1)} %pad.8), channel_id=1, source_target_pairs={{0,2},{1,3},{2,0},{3,1},{4,6},{5,7},{6,4},{7,5},{8,10},{9,11},{10,... | collective-permute-start | bytes 147464 | tf_op jit(solution)/shard_map/ppermute | solution.py:27
  60.5 4.2 %collective-permute-start.16 = (bf16[43,512]{1,0:T(8,128)(2,1)S(1)}, bf16[43,512]{1,0:T(8,128)(2,1)S(1)}, u32[]{:S(2)}, u32[]{:S(2)}) collective-permute-start(bf16[43,512]{1,0:T(8,128)(2,1)S(1)} %get-tuple-element.39), channel_id=1, source_target_pairs={{0,1},{1,0},{2,3},{3,2},{4,5},{5,4},{6,7},{7,6},{8,9},{9,8},{10,11... | collective-permute-start | bytes 132104 | tf_op jit(solution)/shard_map/ppermute | solution.py:27
  (3 other events, 7.3 us)

commit v14 on v13

--- a/solution.py
+++ b/solution.py
@@ -85,7 +85,7 @@
     )(order, own, came)
 
 
-def project_kernel(core_ref, features, basis, own, own_sent, theirs):
+def project_kernel(core_ref, features, basis, own, theirs):
     lanes = own.shape[1]
     total = jnp.dot(features[...], basis[...], preferred_element_type=F32)
     halves = total[:, :lanes], total[:, lanes:]
@@ -94,7 +94,6 @@
         @pl.when(core_ref[0] == core)
         def _(core=core):
             own[...] = halves[core]
-            own_sent[...] = halves[core].astype(BF)
             theirs[...] = halves[1 - core].astype(BF)
 
 
@@ -103,9 +102,9 @@
     vmem = pl.BlockSpec(memory_space=pltpu.VMEM)
     return pl.pallas_call(
         project_kernel,
-        out_shape=[jax.ShapeDtypeStruct(shape, dtype) for dtype in (F32, BF, BF)],
+        out_shape=[jax.ShapeDtypeStruct(shape, dtype) for dtype in (F32, BF)],
         in_specs=[pl.BlockSpec(memory_space=pltpu.SMEM), vmem, vmem],
-        out_specs=[vmem] * 3,
+        out_specs=[vmem] * 2,
         compiler_params=pltpu.CompilerParams(vmem_limit_bytes=8 * 1024 * 1024),
         cost_estimate=pl.CostEstimate(
             flops=2 * features.size * basis.shape[1], bytes_accessed=2 * 1024 * 1024, transcendentals=0
@@ -130,11 +129,11 @@
     blocks_x = (x ^ jnp.array(X_ORDER, jnp.int32)) * NZ
     order = (blocks_x[:, :, None] + blocks_z).reshape(-1)
 
-    mine, mine_sent, theirs = project(core.reshape(1), features[0], basis[0])
+    mine, theirs = project(core.reshape(1), features[0], basis[0])
     columns = cotangent[0].T
     other_columns = swap_core(columns)
     theirs = swap_core(theirs)
-    came = [swap_y(p, m[0]) for p, m in zip((mine_sent, theirs), PAIRS)]
+    came = [swap_y(p, m[0]) for p, m in zip((mine.astype(BF), theirs), PAIRS)]
     chunks = [p.astype(F32) + c.astype(F32) for p, c in zip((mine, theirs), came)]
     came = [swap_y(p.astype(BF), m[1]) for p, m in zip(chunks, PAIRS)]
     parts = arrange(order, columns, other_columns)

time: 67.9 us -> 66.6 us (0.981)
  waiting for transfers between devices: 27.9 us -> 25.9 us
  starting transfers between devices: 27.6 us -> 29.5 us
  other arithmetic: 2.57 us -> 1.44 us
    ppermute x19, waiting for transfers between devices: 27.9 us -> 25.9 us  [send(): return lax.ppermute(value, ('dp', 'tensor'), pairs)]
    ppermute x19, starting transfers between devices: 27.6 us -> 29.5 us  [send(): return lax.ppermute(value, ('dp', 'tensor'), pairs)]
    convert_element_type x2, other arithmetic: 1.01 us -> 0.1 us  [local(): projected = jnp.concatenate([p.astype(BF) for p in chunks], axis=0)]
    convert_element_type x2, other arithmetic: 0.96 us -> 0.07 us  [local(): came = [swap_y(p.astype(BF), m[1]) for p, m in zip(chunks, PAIRS)]]
  transfers between devices with their start and end apart: 19 -> 19, of which waited for: 10 -> 10; matrix products, arithmetic and copies ran while one was open for 7% -> 6% of each run, Pallas kernels for 3% -> 3%
where the time goes in v14:
time: 66.6 us; the launch traced here: 66.4 us
  starting transfers between devices  29.5 us (44%)
  waiting for transfers between devices  25.9 us (39%)
  local copies, waits for them, and re-layouts  5.07 us (8%)
  matrix products  1.89 us (3%)
  Pallas kernels  1.75 us (3%)
  other arithmetic  1.44 us (2%)
  between operations  0.96 us (1%)
    ppermute x19, starting transfers between devices, send(): return lax.ppermute(value, ('dp', 'tensor'), pairs)  29.5 us
    ppermute x19, waiting for transfers between devices, send(): return lax.ppermute(value, ('dp', 'tensor'), pairs)  25.9 us
    unnamed x18, local copies, waits for them, and re-layouts  3.75 us
    dot_general x5, matrix products, dot(): lax.dot_general(a, b, (((1,), (0,)), ((), ())), preferred_element_type=F32)  1.89 us
  transfers between devices with their start and end apart: 19, of which 10 were waited for; matrix products, arithmetic and copies ran while one was open for 6% of the time, Pallas kernels for 3%

profile of v14, /device:TPU:32, one launch (start us, length us, event | category | flops | bytes accessed | tf_op | source)
XLA Modules:
  0.0 66.4 jit_solution(7487743359877769353)
XLA Ops:
  0.8 1.2 %copy-done = bf16[1,1024,512]{2,1,0:T(8,128)(2,1)S(1)} copy-done((bf16[1,1024,512]{2,1,0:T(8,128)(2,1)S(1)}, bf16[1,1024,512]{2,1,0:T(8,128)(2,1)}, u32[]{:S(2)}) %copy-start) | copy-done | bytes 1048600
  2.0 1.0 %copy-done.3 = bf16[1,256,1024]{2,1,0:T(8,128)(2,1)S(1)} copy-done((bf16[1,256,1024]{2,1,0:T(8,128)(2,1)S(1)}, bf16[1,256,1024]{2,1,0:T(8,128)(2,1)}, u32[]{:S(2)}) %copy-start.3) | copy-done | bytes 524312
  4.7 1.6 %collective-permute-start.4 = (bf16[256,256]{1,0:T(8,128)(2,1)}, bf16[256,256]{1,0:T(8,128)(2,1)S(1)}, u32[]{:S(2)}, u32[]{:S(2)}) collective-permute-start(bf16[256,256]{1,0:T(8,128)(2,1)} %convert_element_type.90), channel_id=1, source_target_pairs={{0,1},{1,0},{2,3},{3,2},{4,5},{5,4},{6,7},{7,6},{8,9},{9,8},{10,11... | collective-permute-start | bytes 393224 | tf_op jit(solution)/shard_map/ppermute | solution.py:27
  6.6 2.3 %collective-permute-start.1 = (bf16[256,256]{1,0:T(8,128)(2,1)S(1)}, bf16[256,256]{1,0:T(8,128)(2,1)S(1)}, u32[]{:S(2)}, u32[]{:S(2)}) collective-permute-start(bf16[256,256]{1,0:T(8,128)(2,1)S(1)} %collective-permute-done), channel_id=1, source_target_pairs={{0,3},{1,2},{2,1},{3,0},{4,7},{5,6},{6,5},{7,4},{8,11},{9,10},{10,... | collective-permute-start | bytes 393224 | tf_op jit(solution)/shard_map/ppermute | solution.py:27
  8.9 1.5 %collective-permute-done.4 = bf16[256,256]{1,0:T(8,128)(2,1)S(1)} collective-permute-done((bf16[256,256]{1,0:T(8,128)(2,1)}, bf16[256,256]{1,0:T(8,128)(2,1)S(1)}, u32[]{:S(2)}, u32[]{:S(2)}) %collective-permute-start.4) | collective-permute-done | bytes 131104 | tf_op jit(solution)/shard_map/ppermute | solution.py:27
  10.4 3.1 %collective-permute-start.5 = (bf16[256,256]{1,0:T(8,128)(2,1)S(1)}, bf16[256,256]{1,0:T(8,128)(2,1)S(1)}, u32[]{:S(2)}, u32[]{:S(2)}) collective-permute-start(bf16[256,256]{1,0:T(8,128)(2,1)S(1)} %fusion.2), channel_id=1, source_target_pairs={{0,3},{1,2},{2,1},{3,0},{4,7},{5,6},{6,5},{7,4},{8,11},{9,10},{10,... | collective-permute-start | bytes 393224 | tf_op jit(solution)/shard_map/ppermute | solution.py:27
  13.8 2.9 %collective-permute-done.5 = bf16[256,256]{1,0:T(8,128)(2,1)S(1)} collective-permute-done((bf16[256,256]{1,0:T(8,128)(2,1)S(1)}, bf16[256,256]{1,0:T(8,128)(2,1)S(1)}, u32[]{:S(2)}, u32[]{:S(2)}) %collective-permute-start.5) | collective-permute-done | bytes 131104 | tf_op jit(solution)/shard_map/ppermute | solution.py:27
  16.8 1.3 %shard_map.95 = (bf16[704,512]{1,0:T(8,128)(2,1)S(1)}, bf16[704,512]{1,0:T(8,128)(2,1)S(1)}, bf16[704,512]{1,0:T(8,128)(2,1)S(1)}, bf16[704,512]{1,0:T(8,128)(2,1)S(1)}) custom-call(s32[32]{0:T(128)S(1)} %add.93.order_ref, bf16[2752,256]{1,0:T(8,128)(2,1)S(1)} %bitcast.34, bf16[2752,256]{1,0:T(8,128)(2,1)S(1)} %collective-permute-done.3.came), custom_call_target="tpu_custom_call" | custom-call | bytes 8388608 | tf_op jit(solution)/shard_map/pallas_call | solution.py:77
  19.0 2.8 %collective-permute-start.6 = (bf16[704,256]{1,0:T(8,128)(2,1)S(1)}, bf16[704,256]{1,0:T(8,128)(2,1)S(1)}, u32[]{:S(2)}, u32[]{:S(2)}) collective-permute-start(bf16[704,256]{1,0:T(8,128)(2,1)S(1)} %convolution_convert_fusion.2), channel_id=1, source_target_pairs={{0,192},{1,193},{2,194},{3,195},{4,196},{5,197},{6,198},{7,199},{8... | collective-permute-start | bytes 1081352 | tf_op jit(solution)/shard_map/ppermute | solution.py:27
  23.3 7.1 %collective-permute-done.8 = bf16[704,256]{1,0:T(8,128)(2,1)S(1)} collective-permute-done((bf16[704,256]{1,0:T(8,128)(2,1)S(1)}, bf16[704,256]{1,0:T(8,128)(2,1)S(1)}, u32[]{:S(2)}, u32[]{:S(2)}) %collective-permute-start.8) | collective-permute-done | bytes 360480 | tf_op jit(solution)/shard_map/ppermute | solution.py:27
  31.5 5.8 %collective-permute-done.9 = bf16[352,256]{1,0:T(8,128)(2,1)S(1)} collective-permute-done((bf16[352,256]{1,0:T(8,128)(2,1)S(1)}, bf16[352,256]{1,0:T(8,128)(2,1)S(1)}, u32[]{:S(2)}, u32[]{:S(2)}) %collective-permute-start.9) | collective-permute-done | bytes 180256 | tf_op jit(solution)/shard_map/ppermute | solution.py:27
  37.6 3.7 %collective-permute-start.11 = (bf16[176,256]{1,0:T(8,128)(2,1)S(1)}, bf16[176,256]{1,0:T(8,128)(2,1)S(1)}, u32[]{:S(2)}, u32[]{:S(2)}) collective-permute-start(bf16[176,256]{1,0:T(8,128)(2,1)S(1)} %get-tuple-element.46), channel_id=1, source_target_pairs={{0,56},{1,57},{2,58},{3,59},{4,60},{5,61},{6,62},{7,63},{8,16},{9,... | collective-permute-start | bytes 270344 | tf_op jit(solution)/shard_map/ppermute | solution.py:27
  41.4 4.6 %collective-permute-start.14 = (bf16[88,256]{1,0:T(8,128)(2,1)S(1)}, bf16[88,256]{1,0:T(8,128)(2,1)S(1)}, u32[]{:S(2)}, u32[]{:S(2)}) collective-permute-start(bf16[88,256]{1,0:T(8,128)(2,1)S(1)} %slice.155), channel_id=1, source_target_pairs={{0,32},{1,33},{2,34},{3,35},{4,36},{5,37},{6,38},{7,39},{8,40},{9,... | collective-permute-start | bytes 135176 | tf_op jit(solution)/shard_map/ppermute | solution.py:27
  46.0 2.4 %collective-permute-start.12 = (bf16[88,256]{1,0:T(8,128)(2,1)S(1)}, bf16[88,256]{1,0:T(8,128)(2,1)S(1)}, u32[]{:S(2)}, u32[]{:S(2)}) collective-permute-start(bf16[88,256]{1,0:T(8,128)(2,1)S(1)} %get-tuple-element.40), channel_id=1, source_target_pairs={{0,16},{1,17},{2,18},{3,19},{4,20},{5,21},{6,22},{7,23},{8,24},{9,... | collective-permute-start | bytes 135176 | tf_op jit(solution)/shard_map/ppermute | solution.py:27
  48.4 2.4 %collective-permute-start.13 = (bf16[88,256]{1,0:T(8,128)(2,1)S(1)}, bf16[88,256]{1,0:T(8,128)(2,1)S(1)}, u32[]{:S(2)}, u32[]{:S(2)}) collective-permute-start(bf16[88,256]{1,0:T(8,128)(2,1)S(1)} %get-tuple-element.41), channel_id=1, source_target_pairs={{0,48},{1,49},{2,50},{3,51},{4,52},{5,53},{6,54},{7,55},{8,56},{9,... | collective-permute-start | bytes 135176 | tf_op jit(solution)/shard_map/ppermute | solution.py:27
  51.1 4.0 %collective-permute-done.13 = bf16[88,256]{1,0:T(8,128)(2,1)S(1)} collective-permute-done((bf16[88,256]{1,0:T(8,128)(2,1)S(1)}, bf16[88,256]{1,0:T(8,128)(2,1)S(1)}, u32[]{:S(2)}, u32[]{:S(2)}) %collective-permute-start.13) | collective-permute-done | bytes 45088 | tf_op jit(solution)/shard_map/ppermute | solution.py:27
  55.2 1.2 %collective-permute-done.15 = f32[43,256]{1,0:T(8,128)S(1)} collective-permute-done((f32[43,256]{1,0:T(8,128)S(1)}, f32[43,256]{1,0:T(8,128)S(1)}, u32[]{:S(2)}, u32[]{:S(2)}) %collective-permute-start.15) | collective-permute-done | bytes 44064 | tf_op jit(solution)/shard_map/ppermute | solution.py:27
  56.6 2.6 %collective-permute-start.18 = (bf16[64,512]{1,0:T(8,128)(2,1)S(1)}, bf16[64,512]{1,0:T(8,128)(2,1)S(1)}, u32[]{:S(2)}, u32[]{:S(2)}) collective-permute-start(bf16[64,512]{1,0:T(8,128)(2,1)S(1)} %pad.9), channel_id=1, source_target_pairs={{0,3},{1,2},{2,1},{3,0},{4,7},{5,6},{6,5},{7,4},{8,11},{9,10},{10,... | collective-permute-start | bytes 196616 | tf_op jit(solution)/shard_map/ppermute | solution.py:27
  59.1 1.6 %collective-permute-start.16 = (bf16[43,512]{1,0:T(8,128)(2,1)S(1)}, bf16[43,512]{1,0:T(8,128)(2,1)S(1)}, u32[]{:S(2)}, u32[]{:S(2)}) collective-permute-start(bf16[43,512]{1,0:T(8,128)(2,1)S(1)} %get-tuple-element.37), channel_id=1, source_target_pairs={{0,1},{1,0},{2,3},{3,2},{4,5},{5,4},{6,7},{7,6},{8,9},{9,8},{10,11... | collective-permute-start | bytes 132104 | tf_op jit(solution)/shard_map/ppermute | solution.py:27
  60.8 0.7 %copy.17 = f32[1,43,512]{2,0,1:T(1,128)} copy(f32[1,43,512]{2,1,0:T(8,128)S(1)} %get-tuple-element.39) | data formatting | bytes 176128
  61.5 0.7 %copy.18 = f32[1,43,512]{2,0,1:T(1,128)} copy(f32[1,43,512]{2,1,0:T(8,128)S(1)} %get-tuple-element.38) | data formatting | bytes 176128
  62.2 1.1 %collective-permute-done.16 = bf16[43,512]{1,0:T(8,128)(2,1)S(1)} collective-permute-done((bf16[43,512]{1,0:T(8,128)(2,1)S(1)}, bf16[43,512]{1,0:T(8,128)(2,1)S(1)}, u32[]{:S(2)}, u32[]{:S(2)}) %collective-permute-start.16) | collective-permute-done | bytes 44064 | tf_op jit(solution)/shard_map/ppermute | solution.py:27
  63.3 1.4 %collective-permute-done.17 = bf16[48,512]{1,0:T(8,128)(2,1)S(1)} collective-permute-done((bf16[48,512]{1,0:T(8,128)(2,1)S(1)}, bf16[48,512]{1,0:T(8,128)(2,1)S(1)}, u32[]{:S(2)}, u32[]{:S(2)}) %collective-permute-start.17) | collective-permute-done | bytes 49184 | tf_op jit(solution)/shard_map/ppermute | solution.py:27
  65.5 0.9 %convert_element_type.112 = bf16[43,4,1024]{2,1,0:T(4,128)(2,1)} reshape(bf16[172,1024]{1,0:T(8,128)(2,1)S(1)} %convolution_convert_fusion) | data formatting | bytes 704512 | tf_op jit(solution)/shard_map/convert_element_type | solution.py:181
  (73 shorter events, 7.5 us)
Async XLA Ops:
  0.6 5.8 %copy-start.6 = (s32[2,4]{1,0:T(2,128)S(1)}, s32[2,4]{1,0:T(2,128)}, u32[]{:S(2)}) copy-start(s32[2,4]{1,0:T(2,128)} %constant.51.clone) | copy-start | bytes 100
  0.7 16.1 %collective-permute-start.3 = (bf16[2752,256]{1,0:T(8,128)(2,1)}, bf16[2752,256]{1,0:T(8,128)(2,1)S(1)}, u32[]{:S(2)}, u32[]{:S(2)}) collective-permute-start(bf16[2752,256]{1,0:T(8,128)(2,1)} %bitcast.33), channel_id=1, source_target_pairs={{0,4},{1,5},{2,6},{3,7},{4,0},{5,1},{6,2},{7,3},{8,12},{9,13},{10,... | collective-permute-start | bytes 4227080 | tf_op jit(solution)/shard_map/ppermute | solution.py:27
  3.0 13.7 %copy-start.2 = (bf16[1,256,2752]{1,2,0:T(8,128)(2,1)S(1)}, bf16[1,256,2752]{1,2,0:T(8,128)(2,1)}, u32[]{:S(2)}) copy-start(bf16[1,256,2752]{1,2,0:T(8,128)(2,1)} %param.8) | copy-start | bytes 4227076
  3.5 3.1 %collective-permute-start = (bf16[256,256]{1,0:T(8,128)(2,1)S(1)}, bf16[256,256]{1,0:T(8,128)(2,1)S(1)}, u32[]{:S(2)}, u32[]{:S(2)}) collective-permute-start(bf16[256,256]{1,0:T(8,128)(2,1)S(1)} %get-tuple-element.17), channel_id=1, source_target_pairs={{0,4},{1,5},{2,6},{3,7},{4,0},{5,1},{6,2},{7,3},{8,12},{9,13},{10,... | collective-permute-start | bytes 393224 | tf_op jit(solution)/shard_map/ppermute | solution.py:27
  4.7 5.6 %collective-permute-start.4 = (bf16[256,256]{1,0:T(8,128)(2,1)}, bf16[256,256]{1,0:T(8,128)(2,1)S(1)}, u32[]{:S(2)}, u32[]{:S(2)}) collective-permute-start(bf16[256,256]{1,0:T(8,128)(2,1)} %convert_element_type.90), channel_id=1, source_target_pairs={{0,1},{1,0},{2,3},{3,2},{4,5},{5,4},{6,7},{7,6},{8,9},{9,8},{10,11... | collective-permute-start | bytes 393224 | tf_op jit(solution)/shard_map/ppermute | solution.py:27
  6.6 6.9 %collective-permute-start.1 = (bf16[256,256]{1,0:T(8,128)(2,1)S(1)}, bf16[256,256]{1,0:T(8,128)(2,1)S(1)}, u32[]{:S(2)}, u32[]{:S(2)}) collective-permute-start(bf16[256,256]{1,0:T(8,128)(2,1)S(1)} %collective-permute-done), channel_id=1, source_target_pairs={{0,3},{1,2},{2,1},{3,0},{4,7},{5,6},{6,5},{7,4},{8,11},{9,10},{10,... | collective-permute-start | bytes 393224 | tf_op jit(solution)/shard_map/ppermute | solution.py:27
  10.4 6.3 %collective-permute-start.5 = (bf16[256,256]{1,0:T(8,128)(2,1)S(1)}, bf16[256,256]{1,0:T(8,128)(2,1)S(1)}, u32[]{:S(2)}, u32[]{:S(2)}) collective-permute-start(bf16[256,256]{1,0:T(8,128)(2,1)S(1)} %fusion.2), channel_id=1, source_target_pairs={{0,3},{1,2},{2,1},{3,0},{4,7},{5,6},{6,5},{7,4},{8,11},{9,10},{10,... | collective-permute-start | bytes 393224 | tf_op jit(solution)/shard_map/ppermute | solution.py:27
  13.6 5.1 %collective-permute-start.2 = (bf16[256,256]{1,0:T(8,128)(2,1)S(1)}, bf16[256,256]{1,0:T(8,128)(2,1)S(1)}, u32[]{:S(2)}, u32[]{:S(2)}) collective-permute-start(bf16[256,256]{1,0:T(8,128)(2,1)S(1)} %fusion.1), channel_id=1, source_target_pairs={{0,1},{1,0},{2,3},{3,2},{4,5},{5,4},{6,7},{7,6},{8,9},{9,8},{10,11... | collective-permute-start | bytes 393224 | tf_op jit(solution)/shard_map/ppermute | solution.py:27
  19.0 12.0 %collective-permute-start.6 = (bf16[704,256]{1,0:T(8,128)(2,1)S(1)}, bf16[704,256]{1,0:T(8,128)(2,1)S(1)}, u32[]{:S(2)}, u32[]{:S(2)}) collective-permute-start(bf16[704,256]{1,0:T(8,128)(2,1)S(1)} %convolution_convert_fusion.2), channel_id=1, source_target_pairs={{0,192},{1,193},{2,194},{3,195},{4,196},{5,197},{6,198},{7,199},{8... | collective-permute-start | bytes 1081352 | tf_op jit(solution)/shard_map/ppermute | solution.py:27
  22.2 8.2 %collective-permute-start.8 = (bf16[704,256]{1,0:T(8,128)(2,1)S(1)}, bf16[704,256]{1,0:T(8,128)(2,1)S(1)}, u32[]{:S(2)}, u32[]{:S(2)}) collective-permute-start(bf16[704,256]{1,0:T(8,128)(2,1)S(1)} %convolution_convert_fusion.1), channel_id=1, source_target_pairs={{0,64},{1,65},{2,66},{3,67},{4,68},{5,69},{6,70},{7,71},{8,72},{9,... | collective-permute-start | bytes 1081352 | tf_op jit(solution)/shard_map/ppermute | solution.py:27
  30.5 6.8 %collective-permute-start.9 = (bf16[352,256]{1,0:T(8,128)(2,1)S(1)}, bf16[352,256]{1,0:T(8,128)(2,1)S(1)}, u32[]{:S(2)}, u32[]{:S(2)}) collective-permute-start(bf16[352,256]{1,0:T(8,128)(2,1)S(1)} %slice.153), channel_id=1, source_target_pairs={{0,192},{1,193},{2,194},{3,195},{4,196},{5,197},{6,198},{7,199},{8... | collective-permute-start | bytes 540680 | tf_op jit(solution)/shard_map/ppermute | solution.py:27
  31.2 10.1 %collective-permute-start.7 = (bf16[352,256]{1,0:T(8,128)(2,1)S(1)}, bf16[352,256]{1,0:T(8,128)(2,1)S(1)}, u32[]{:S(2)}, u32[]{:S(2)}) collective-permute-start(bf16[352,256]{1,0:T(8,128)(2,1)S(1)} %slice.154), channel_id=1, source_target_pairs={{0,64},{1,65},{2,66},{3,67},{4,68},{5,69},{6,70},{7,71},{8,72},{9,... | collective-permute-start | bytes 540680 | tf_op jit(solution)/shard_map/ppermute | solution.py:27
  37.4 8.6 %collective-permute-start.10 = (bf16[176,256]{1,0:T(8,128)(2,1)S(1)}, bf16[176,256]{1,0:T(8,128)(2,1)S(1)}, u32[]{:S(2)}, u32[]{:S(2)}) collective-permute-start(bf16[176,256]{1,0:T(8,128)(2,1)S(1)} %get-tuple-element.45), channel_id=1, source_target_pairs={{0,8},{1,9},{2,10},{3,11},{4,12},{5,13},{6,14},{7,15},{8,0},{9,1},... | collective-permute-start | bytes 270344 | tf_op jit(solution)/shard_map/ppermute | solution.py:27
  37.6 18.9 %copy-start.4 = (f32[1,43,512]{2,0,1:T(1,128)S(1)}, f32[1,43,512]{2,0,1:T(1,128)}, u32[]{:S(2)}) copy-start(f32[1,43,512]{2,0,1:T(1,128)} %param.11) | copy-start | bytes 264196
  37.6 18.9 %copy-start.5 = (f32[1,43,512]{2,0,1:T(1,128)S(1)}, f32[1,43,512]{2,0,1:T(1,128)}, u32[]{:S(2)}) copy-start(f32[1,43,512]{2,0,1:T(1,128)} %param.10) | copy-start | bytes 264196
  37.6 8.4 %collective-permute-start.11 = (bf16[176,256]{1,0:T(8,128)(2,1)S(1)}, bf16[176,256]{1,0:T(8,128)(2,1)S(1)}, u32[]{:S(2)}, u32[]{:S(2)}) collective-permute-start(bf16[176,256]{1,0:T(8,128)(2,1)S(1)} %get-tuple-element.46), channel_id=1, source_target_pairs={{0,56},{1,57},{2,58},{3,59},{4,60},{5,61},{6,62},{7,63},{8,16},{9,... | collective-permute-start | bytes 270344 | tf_op jit(solution)/shard_map/ppermute | solution.py:27
  41.4 9.5 %collective-permute-start.14 = (bf16[88,256]{1,0:T(8,128)(2,1)S(1)}, bf16[88,256]{1,0:T(8,128)(2,1)S(1)}, u32[]{:S(2)}, u32[]{:S(2)}) collective-permute-start(bf16[88,256]{1,0:T(8,128)(2,1)S(1)} %slice.155), channel_id=1, source_target_pairs={{0,32},{1,33},{2,34},{3,35},{4,36},{5,37},{6,38},{7,39},{8,40},{9,... | collective-permute-start | bytes 135176 | tf_op jit(solution)/shard_map/ppermute | solution.py:27
  46.0 5.0 %collective-permute-start.12 = (bf16[88,256]{1,0:T(8,128)(2,1)S(1)}, bf16[88,256]{1,0:T(8,128)(2,1)S(1)}, u32[]{:S(2)}, u32[]{:S(2)}) collective-permute-start(bf16[88,256]{1,0:T(8,128)(2,1)S(1)} %get-tuple-element.40), channel_id=1, source_target_pairs={{0,16},{1,17},{2,18},{3,19},{4,20},{5,21},{6,22},{7,23},{8,24},{9,... | collective-permute-start | bytes 135176 | tf_op jit(solution)/shard_map/ppermute | solution.py:27
  48.4 6.6 %collective-permute-start.13 = (bf16[88,256]{1,0:T(8,128)(2,1)S(1)}, bf16[88,256]{1,0:T(8,128)(2,1)S(1)}, u32[]{:S(2)}, u32[]{:S(2)}) collective-permute-start(bf16[88,256]{1,0:T(8,128)(2,1)S(1)} %get-tuple-element.41), channel_id=1, source_target_pairs={{0,48},{1,49},{2,50},{3,51},{4,52},{5,53},{6,54},{7,55},{8,56},{9,... | collective-permute-start | bytes 135176 | tf_op jit(solution)/shard_map/ppermute | solution.py:27
  55.1 1.3 %collective-permute-start.15 = (f32[43,256]{1,0:T(8,128)S(1)}, f32[43,256]{1,0:T(8,128)S(1)}, u32[]{:S(2)}, u32[]{:S(2)}) collective-permute-start(f32[43,256]{1,0:T(8,128)S(1)} %slice_select_fusion), channel_id=1, source_target_pairs={{0,4},{1,5},{2,6},{3,7},{4,0},{5,1},{6,2},{7,3},{8,12},{9,13},{10,... | collective-permute-start | bytes 132104 | tf_op jit(solution)/shard_map/ppermute | solution.py:27
  56.4 8.6 %copy-start.1 = (bf16[1,1024,512]{2,1,0:T(8,128)(2,1)S(1)}, bf16[1,1024,512]{2,1,0:T(8,128)(2,1)}, u32[]{:S(2)}) copy-start(bf16[1,1024,512]{2,1,0:T(8,128)(2,1)} %param.9) | copy-start | bytes 3145732
  56.6 8.2 %collective-permute-start.18 = (bf16[64,512]{1,0:T(8,128)(2,1)S(1)}, bf16[64,512]{1,0:T(8,128)(2,1)S(1)}, u32[]{:S(2)}, u32[]{:S(2)}) collective-permute-start(bf16[64,512]{1,0:T(8,128)(2,1)S(1)} %pad.9), channel_id=1, source_target_pairs={{0,3},{1,2},{2,1},{3,0},{4,7},{5,6},{6,5},{7,4},{8,11},{9,10},{10,... | collective-permute-start | bytes 196616 | tf_op jit(solution)/shard_map/ppermute | solution.py:27
  59.1 5.6 %collective-permute-start.17 = (bf16[48,512]{1,0:T(8,128)(2,1)S(1)}, bf16[48,512]{1,0:T(8,128)(2,1)S(1)}, u32[]{:S(2)}, u32[]{:S(2)}) collective-permute-start(bf16[48,512]{1,0:T(8,128)(2,1)S(1)} %pad.8), channel_id=1, source_target_pairs={{0,2},{1,3},{2,0},{3,1},{4,6},{5,7},{6,4},{7,5},{8,10},{9,11},{10,... | collective-permute-start | bytes 147464 | tf_op jit(solution)/shard_map/ppermute | solution.py:27
  59.1 4.2 %collective-permute-start.16 = (bf16[43,512]{1,0:T(8,128)(2,1)S(1)}, bf16[43,512]{1,0:T(8,128)(2,1)S(1)}, u32[]{:S(2)}, u32[]{:S(2)}) collective-permute-start(bf16[43,512]{1,0:T(8,128)(2,1)S(1)} %get-tuple-element.37), channel_id=1, source_target_pairs={{0,1},{1,0},{2,3},{3,2},{4,5},{5,4},{6,7},{7,6},{8,9},{9,8},{10,11... | collective-permute-start | bytes 132104 | tf_op jit(solution)/shard_map/ppermute | solution.py:27
  (3 other events, 8.0 us)

commit v15 on v14

--- a/solution.py
+++ b/solution.py
@@ -8,6 +8,7 @@
 
 NX, NZ, NCORE, NY = 4, 8, 2, 4
 OWNED = 43
+PIECES = 4
 CHIP, PADDED = NCORE * OWNED, 88
 BF, F32 = jnp.bfloat16, jnp.float32
 
@@ -85,29 +86,52 @@
     )(order, own, came)
 
 
-def project_kernel(core_ref, features, basis, own, theirs):
+def project_kernel(core_ref, features, basis, own, theirs, f_buf, b_buf, total, sems):
+    pieces, tokens, depth = f_buf.shape
     lanes = own.shape[1]
-    total = jnp.dot(features[...], basis[...], preferred_element_type=F32)
-    halves = total[:, :lanes], total[:, lanes:]
+    copies = []
+    for k in range(pieces):
+        part = pl.ds(k * depth, depth)
+        copies.append(pltpu.make_async_copy(features.at[:, part], f_buf.at[k], sems.at[0, k]))
+        copies.append(pltpu.make_async_copy(basis.at[part, :], b_buf.at[k], sems.at[1, k]))
+    for copy in copies:
+        copy.start()
+    for k in range(pieces):
+        copies[2 * k].wait()
+        copies[2 * k + 1].wait()
+        term = jnp.dot(f_buf[k], b_buf[k], preferred_element_type=F32)
+        total[...] = term if k == 0 else total[...] + term
     for core in range(NCORE):
 
         @pl.when(core_ref[0] == core)
         def _(core=core):
-            own[...] = halves[core]
-            theirs[...] = halves[1 - core].astype(BF)
+            own[...] = total[:, core * lanes : (core + 1) * lanes]
+            theirs[...] = total[:, (1 - core) * lanes : (2 - core) * lanes].astype(BF)
 
 
 def project(core, features, basis):
-    shape = features.shape[0], basis.shape[1] // NCORE
+    tokens, depth = features.shape
+    rank = basis.shape[1]
+    step = depth // PIECES
     vmem = pl.BlockSpec(memory_space=pltpu.VMEM)
+    hbm = pl.BlockSpec(memory_space=pltpu.HBM)
     return pl.pallas_call(
         project_kernel,
-        out_shape=[jax.ShapeDtypeStruct(shape, dtype) for dtype in (F32, BF)],
-        in_specs=[pl.BlockSpec(memory_space=pltpu.SMEM), vmem, vmem],
+        out_shape=[
+            jax.ShapeDtypeStruct((tokens, rank // NCORE), F32),
+            jax.ShapeDtypeStruct((tokens, rank // NCORE), BF),
+        ],
+        in_specs=[pl.BlockSpec(memory_space=pltpu.SMEM), hbm, hbm],
         out_specs=[vmem] * 2,
-        compiler_params=pltpu.CompilerParams(vmem_limit_bytes=8 * 1024 * 1024),
+        scratch_shapes=[
+            pltpu.VMEM((PIECES, tokens, step), BF),
+            pltpu.VMEM((PIECES, step, rank), BF),
+            pltpu.VMEM((tokens, rank), F32),
+            pltpu.SemaphoreType.DMA((2, PIECES)),
+        ],
+        compiler_params=pltpu.CompilerParams(vmem_limit_bytes=60 * 1024 * 1024),
         cost_estimate=pl.CostEstimate(
-            flops=2 * features.size * basis.shape[1], bytes_accessed=2 * 1024 * 1024, transcendentals=0
+            flops=2 * tokens * depth * rank, bytes_accessed=3 * 1024 * 1024, transcendentals=0
         ),
     )(core, features, basis)
 
@@ -133,7 +157,8 @@
     columns = cotangent[0].T
     other_columns = swap_core(columns)
     theirs = swap_core(theirs)
-    came = [swap_y(p, m[0]) for p, m in zip((mine.astype(BF), theirs), PAIRS)]
+    mine = lax.optimization_barrier(mine.astype(BF))
+    came = [swap_y(p, m[0]) for p, m in zip((mine, theirs), PAIRS)]
     chunks = [p.astype(F32) + c.astype(F32) for p, c in zip((mine, theirs), came)]
     came = [swap_y(p.astype(BF), m[1]) for p, m in zip(chunks, PAIRS)]
     parts = arrange(order, columns, other_columns)

time: 66.6 us -> 66.6 us (level)
  local copies, waits for them, and re-layouts: 5.07 us -> 2.81 us
  Pallas kernels: 1.75 us -> 3.86 us
    unnamed x18 -> x14, local copies, waits for them, and re-layouts: 3.75 us -> 1.49 us
    pallas_call x1, Pallas kernels: 0.45 us -> 2.56 us  [project(): pl.pallas_call(project_kernel, out_shape=[jax.ShapeDtypeStruct((tokens, r...]
  transfers between devices with their start and end apart: 19 -> 19, of which waited for: 10 -> 10; matrix products, arithmetic and copies ran while one was open for 6% -> 6% of each run, Pallas kernels for 3% -> 6%
where the time goes in v15:
time: 66.6 us; the launch traced here: 66.4 us
  starting transfers between devices  29.6 us (44%)
  waiting for transfers between devices  25.6 us (38%)
  Pallas kernels  3.86 us (6%)
  local copies, waits for them, and re-layouts  2.81 us (4%)
  matrix products  1.89 us (3%)
  other arithmetic  1.74 us (3%)
  between operations  0.96 us (1%)
    ppermute x19, starting transfers between devices, send(): return lax.ppermute(value, ('dp', 'tensor'), pairs)  29.6 us
    ppermute x19, waiting for transfers between devices, send(): return lax.ppermute(value, ('dp', 'tensor'), pairs)  25.6 us
    pallas_call x1, Pallas kernels, project(): pl.pallas_call(project_kernel, out_shape=[jax.ShapeDtypeStruct((tokens, r...  2.56 us
    dot_general x5, matrix products, dot(): lax.dot_general(a, b, (((1,), (0,)), ((), ())), preferred_element_type=F32)  1.89 us
    unnamed x14, local copies, waits for them, and re-layouts  1.49 us
  transfers between devices with their start and end apart: 19, of which 10 were waited for; matrix products, arithmetic and copies ran while one was open for 6% of the time, Pallas kernels for 6%

profile of v15, /device:TPU:32, one launch (start us, length us, event | category | flops | bytes accessed | tf_op | source)
XLA Modules:
  0.0 66.4 jit_solution(16299103096517309477)
XLA Ops:
  0.8 2.6 %shard_map.94 = (f32[256,256]{1,0:T(8,128)}, bf16[256,256]{1,0:T(8,128)(2,1)}) custom-call(s32[1]{0:T(128)} %bitcast.core_ref, bf16[256,1024]{1,0:T(8,128)(2,1)} %bitcast.35, bf16[1024,512]{1,0:T(8,128)(2,1)} %bitcast.34), custom_call_target="tpu_custom_call" | custom-call | flops 268435456 | bytes 3145728 | tf_op jit(solution)/shard_map/pallas_call | solution.py:118
  3.9 1.0 %convert_element_type.93 = bf16[256,256]{1,0:T(8,128)(2,1)S(1)} convert(f32[256,256]{1,0:T(8,128)} %get-tuple-element.23) | non-fusion elementwise | flops 65536 | bytes 393216 | tf_op jit(solution)/shard_map/convert_element_type | solution.py:160
  4.9 1.7 %collective-permute-start.4 = (bf16[256,256]{1,0:T(8,128)(2,1)S(1)}, bf16[256,256]{1,0:T(8,128)(2,1)S(1)}, u32[]{:S(2)}, u32[]{:S(2)}) collective-permute-start(bf16[256,256]{1,0:T(8,128)(2,1)S(1)} %convert_element_type.93), channel_id=1, source_target_pairs={{0,1},{1,0},{2,3},{3,2},{4,5},{5,4},{6,7},{7,6},{8,9},{9,8},{10,11... | collective-permute-start | bytes 393224 | tf_op jit(solution)/shard_map/ppermute | solution.py:28
  6.8 2.3 %collective-permute-start.1 = (bf16[256,256]{1,0:T(8,128)(2,1)S(1)}, bf16[256,256]{1,0:T(8,128)(2,1)S(1)}, u32[]{:S(2)}, u32[]{:S(2)}) collective-permute-start(bf16[256,256]{1,0:T(8,128)(2,1)S(1)} %collective-permute-done), channel_id=1, source_target_pairs={{0,3},{1,2},{2,1},{3,0},{4,7},{5,6},{6,5},{7,4},{8,11},{9,10},{10,... | collective-permute-start | bytes 393224 | tf_op jit(solution)/shard_map/ppermute | solution.py:28
  9.1 1.3 %collective-permute-done.4 = bf16[256,256]{1,0:T(8,128)(2,1)S(1)} collective-permute-done((bf16[256,256]{1,0:T(8,128)(2,1)S(1)}, bf16[256,256]{1,0:T(8,128)(2,1)S(1)}, u32[]{:S(2)}, u32[]{:S(2)}) %collective-permute-start.4) | collective-permute-done | bytes 131104 | tf_op jit(solution)/shard_map/ppermute | solution.py:28
  10.4 3.1 %collective-permute-start.5 = (bf16[256,256]{1,0:T(8,128)(2,1)S(1)}, bf16[256,256]{1,0:T(8,128)(2,1)S(1)}, u32[]{:S(2)}, u32[]{:S(2)}) collective-permute-start(bf16[256,256]{1,0:T(8,128)(2,1)S(1)} %fusion.2), channel_id=1, source_target_pairs={{0,3},{1,2},{2,1},{3,0},{4,7},{5,6},{6,5},{7,4},{8,11},{9,10},{10,... | collective-permute-start | bytes 393224 | tf_op jit(solution)/shard_map/ppermute | solution.py:28
  13.8 2.9 %collective-permute-done.5 = bf16[256,256]{1,0:T(8,128)(2,1)S(1)} collective-permute-done((bf16[256,256]{1,0:T(8,128)(2,1)S(1)}, bf16[256,256]{1,0:T(8,128)(2,1)S(1)}, u32[]{:S(2)}, u32[]{:S(2)}) %collective-permute-start.5) | collective-permute-done | bytes 131104 | tf_op jit(solution)/shard_map/ppermute | solution.py:28
  16.8 1.3 %shard_map.95 = (bf16[704,512]{1,0:T(8,128)(2,1)S(1)}, bf16[704,512]{1,0:T(8,128)(2,1)S(1)}, bf16[704,512]{1,0:T(8,128)(2,1)S(1)}, bf16[704,512]{1,0:T(8,128)(2,1)S(1)}) custom-call(s32[32]{0:T(128)S(1)} %add.93.order_ref, bf16[2752,256]{1,0:T(8,128)(2,1)S(1)} %bitcast.33, bf16[2752,256]{1,0:T(8,128)(2,1)S(1)} %collective-permute-done.3.came), custom_call_target="tpu_custom_call" | custom-call | bytes 8388608 | tf_op jit(solution)/shard_map/pallas_call | solution.py:78
  19.1 2.8 %collective-permute-start.6 = (bf16[704,256]{1,0:T(8,128)(2,1)S(1)}, bf16[704,256]{1,0:T(8,128)(2,1)S(1)}, u32[]{:S(2)}, u32[]{:S(2)}) collective-permute-start(bf16[704,256]{1,0:T(8,128)(2,1)S(1)} %convolution_convert_fusion.2), channel_id=1, source_target_pairs={{0,192},{1,193},{2,194},{3,195},{4,196},{5,197},{6,198},{7,199},{8... | collective-permute-start | bytes 1081352 | tf_op jit(solution)/shard_map/ppermute | solution.py:28
  23.3 7.1 %collective-permute-done.8 = bf16[704,256]{1,0:T(8,128)(2,1)S(1)} collective-permute-done((bf16[704,256]{1,0:T(8,128)(2,1)S(1)}, bf16[704,256]{1,0:T(8,128)(2,1)S(1)}, u32[]{:S(2)}, u32[]{:S(2)}) %collective-permute-start.8) | collective-permute-done | bytes 360480 | tf_op jit(solution)/shard_map/ppermute | solution.py:28
  31.6 5.7 %collective-permute-done.9 = bf16[352,256]{1,0:T(8,128)(2,1)S(1)} collective-permute-done((bf16[352,256]{1,0:T(8,128)(2,1)S(1)}, bf16[352,256]{1,0:T(8,128)(2,1)S(1)}, u32[]{:S(2)}, u32[]{:S(2)}) %collective-permute-start.9) | collective-permute-done | bytes 180256 | tf_op jit(solution)/shard_map/ppermute | solution.py:28
  37.6 3.7 %collective-permute-start.11 = (bf16[176,256]{1,0:T(8,128)(2,1)S(1)}, bf16[176,256]{1,0:T(8,128)(2,1)S(1)}, u32[]{:S(2)}, u32[]{:S(2)}) collective-permute-start(bf16[176,256]{1,0:T(8,128)(2,1)S(1)} %get-tuple-element.46), channel_id=1, source_target_pairs={{0,56},{1,57},{2,58},{3,59},{4,60},{5,61},{6,62},{7,63},{8,16},{9,... | collective-permute-start | bytes 270344 | tf_op jit(solution)/shard_map/ppermute | solution.py:28
  41.4 4.6 %collective-permute-start.14 = (bf16[88,256]{1,0:T(8,128)(2,1)S(1)}, bf16[88,256]{1,0:T(8,128)(2,1)S(1)}, u32[]{:S(2)}, u32[]{:S(2)}) collective-permute-start(bf16[88,256]{1,0:T(8,128)(2,1)S(1)} %slice.155), channel_id=1, source_target_pairs={{0,32},{1,33},{2,34},{3,35},{4,36},{5,37},{6,38},{7,39},{8,40},{9,... | collective-permute-start | bytes 135176 | tf_op jit(solution)/shard_map/ppermute | solution.py:28
  46.1 2.3 %collective-permute-start.12 = (bf16[88,256]{1,0:T(8,128)(2,1)S(1)}, bf16[88,256]{1,0:T(8,128)(2,1)S(1)}, u32[]{:S(2)}, u32[]{:S(2)}) collective-permute-start(bf16[88,256]{1,0:T(8,128)(2,1)S(1)} %get-tuple-element.40), channel_id=1, source_target_pairs={{0,16},{1,17},{2,18},{3,19},{4,20},{5,21},{6,22},{7,23},{8,24},{9,... | collective-permute-start | bytes 135176 | tf_op jit(solution)/shard_map/ppermute | solution.py:28
  48.4 2.4 %collective-permute-start.13 = (bf16[88,256]{1,0:T(8,128)(2,1)S(1)}, bf16[88,256]{1,0:T(8,128)(2,1)S(1)}, u32[]{:S(2)}, u32[]{:S(2)}) collective-permute-start(bf16[88,256]{1,0:T(8,128)(2,1)S(1)} %get-tuple-element.41), channel_id=1, source_target_pairs={{0,48},{1,49},{2,50},{3,51},{4,52},{5,53},{6,54},{7,55},{8,56},{9,... | collective-permute-start | bytes 135176 | tf_op jit(solution)/shard_map/ppermute | solution.py:28
  51.1 3.9 %collective-permute-done.13 = bf16[88,256]{1,0:T(8,128)(2,1)S(1)} collective-permute-done((bf16[88,256]{1,0:T(8,128)(2,1)S(1)}, bf16[88,256]{1,0:T(8,128)(2,1)S(1)}, u32[]{:S(2)}, u32[]{:S(2)}) %collective-permute-start.13) | collective-permute-done | bytes 45088 | tf_op jit(solution)/shard_map/ppermute | solution.py:28
  55.2 1.2 %collective-permute-done.15 = f32[43,256]{1,0:T(8,128)S(1)} collective-permute-done((f32[43,256]{1,0:T(8,128)S(1)}, f32[43,256]{1,0:T(8,128)S(1)}, u32[]{:S(2)}, u32[]{:S(2)}) %collective-permute-start.15) | collective-permute-done | bytes 44064 | tf_op jit(solution)/shard_map/ppermute | solution.py:28
  56.6 2.6 %collective-permute-start.18 = (bf16[64,512]{1,0:T(8,128)(2,1)S(1)}, bf16[64,512]{1,0:T(8,128)(2,1)S(1)}, u32[]{:S(2)}, u32[]{:S(2)}) collective-permute-start(bf16[64,512]{1,0:T(8,128)(2,1)S(1)} %pad.9), channel_id=1, source_target_pairs={{0,3},{1,2},{2,1},{3,0},{4,7},{5,6},{6,5},{7,4},{8,11},{9,10},{10,... | collective-permute-start | bytes 196616 | tf_op jit(solution)/shard_map/ppermute | solution.py:28
  59.1 1.6 %collective-permute-start.16 = (bf16[43,512]{1,0:T(8,128)(2,1)S(1)}, bf16[43,512]{1,0:T(8,128)(2,1)S(1)}, u32[]{:S(2)}, u32[]{:S(2)}) collective-permute-start(bf16[43,512]{1,0:T(8,128)(2,1)S(1)} %get-tuple-element.37), channel_id=1, source_target_pairs={{0,1},{1,0},{2,3},{3,2},{4,5},{5,4},{6,7},{7,6},{8,9},{9,8},{10,11... | collective-permute-start | bytes 132104 | tf_op jit(solution)/shard_map/ppermute | solution.py:28
  60.8 0.7 %copy.17 = f32[1,43,512]{2,0,1:T(1,128)} copy(f32[1,43,512]{2,1,0:T(8,128)S(1)} %get-tuple-element.39) | data formatting | bytes 176128
  61.5 0.7 %copy.18 = f32[1,43,512]{2,0,1:T(1,128)} copy(f32[1,43,512]{2,1,0:T(8,128)S(1)} %get-tuple-element.38) | data formatting | bytes 176128
  62.2 1.1 %collective-permute-done.16 = bf16[43,512]{1,0:T(8,128)(2,1)S(1)} collective-permute-done((bf16[43,512]{1,0:T(8,128)(2,1)S(1)}, bf16[43,512]{1,0:T(8,128)(2,1)S(1)}, u32[]{:S(2)}, u32[]{:S(2)}) %collective-permute-start.16) | collective-permute-done | bytes 44064 | tf_op jit(solution)/shard_map/ppermute | solution.py:28
  63.3 1.4 %collective-permute-done.17 = bf16[48,512]{1,0:T(8,128)(2,1)S(1)} collective-permute-done((bf16[48,512]{1,0:T(8,128)(2,1)S(1)}, bf16[48,512]{1,0:T(8,128)(2,1)S(1)}, u32[]{:S(2)}, u32[]{:S(2)}) %collective-permute-start.17) | collective-permute-done | bytes 49184 | tf_op jit(solution)/shard_map/ppermute | solution.py:28
  65.5 0.9 %convert_element_type.116 = bf16[43,4,1024]{2,1,0:T(4,128)(2,1)} reshape(bf16[172,1024]{1,0:T(8,128)(2,1)S(1)} %convolution_convert_fusion) | data formatting | bytes 704512 | tf_op jit(solution)/shard_map/convert_element_type | solution.py:206
  (69 shorter events, 6.4 us)
Async XLA Ops:
  0.6 6.0 %copy-start.4 = (s32[2,4]{1,0:T(2,128)S(1)}, s32[2,4]{1,0:T(2,128)}, u32[]{:S(2)}) copy-start(s32[2,4]{1,0:T(2,128)} %constant.51.clone) | copy-start | bytes 100
  0.7 16.1 %collective-permute-start.3 = (bf16[2752,256]{1,0:T(8,128)(2,1)}, bf16[2752,256]{1,0:T(8,128)(2,1)S(1)}, u32[]{:S(2)}, u32[]{:S(2)}) collective-permute-start(bf16[2752,256]{1,0:T(8,128)(2,1)} %bitcast.32), channel_id=1, source_target_pairs={{0,4},{1,5},{2,6},{3,7},{4,0},{5,1},{6,2},{7,3},{8,12},{9,13},{10,... | collective-permute-start | bytes 4227080 | tf_op jit(solution)/shard_map/ppermute | solution.py:28
  0.8 16.0 %copy-start = (bf16[1,256,2752]{1,2,0:T(8,128)(2,1)S(1)}, bf16[1,256,2752]{1,2,0:T(8,128)(2,1)}, u32[]{:S(2)}) copy-start(bf16[1,256,2752]{1,2,0:T(8,128)(2,1)} %param.8) | copy-start | bytes 4227076
  3.3 3.5 %collective-permute-start = (bf16[256,256]{1,0:T(8,128)(2,1)}, bf16[256,256]{1,0:T(8,128)(2,1)S(1)}, u32[]{:S(2)}, u32[]{:S(2)}) collective-permute-start(bf16[256,256]{1,0:T(8,128)(2,1)} %get-tuple-element.17), channel_id=1, source_target_pairs={{0,4},{1,5},{2,6},{3,7},{4,0},{5,1},{6,2},{7,3},{8,12},{9,13},{10,... | collective-permute-start | bytes 393224 | tf_op jit(solution)/shard_map/ppermute | solution.py:28
  4.9 5.5 %collective-permute-start.4 = (bf16[256,256]{1,0:T(8,128)(2,1)S(1)}, bf16[256,256]{1,0:T(8,128)(2,1)S(1)}, u32[]{:S(2)}, u32[]{:S(2)}) collective-permute-start(bf16[256,256]{1,0:T(8,128)(2,1)S(1)} %convert_element_type.93), channel_id=1, source_target_pairs={{0,1},{1,0},{2,3},{3,2},{4,5},{5,4},{6,7},{7,6},{8,9},{9,8},{10,11... | collective-permute-start | bytes 393224 | tf_op jit(solution)/shard_map/ppermute | solution.py:28
  6.8 6.7 %collective-permute-start.1 = (bf16[256,256]{1,0:T(8,128)(2,1)S(1)}, bf16[256,256]{1,0:T(8,128)(2,1)S(1)}, u32[]{:S(2)}, u32[]{:S(2)}) collective-permute-start(bf16[256,256]{1,0:T(8,128)(2,1)S(1)} %collective-permute-done), channel_id=1, source_target_pairs={{0,3},{1,2},{2,1},{3,0},{4,7},{5,6},{6,5},{7,4},{8,11},{9,10},{10,... | collective-permute-start | bytes 393224 | tf_op jit(solution)/shard_map/ppermute | solution.py:28
  10.4 6.3 %collective-permute-start.5 = (bf16[256,256]{1,0:T(8,128)(2,1)S(1)}, bf16[256,256]{1,0:T(8,128)(2,1)S(1)}, u32[]{:S(2)}, u32[]{:S(2)}) collective-permute-start(bf16[256,256]{1,0:T(8,128)(2,1)S(1)} %fusion.2), channel_id=1, source_target_pairs={{0,3},{1,2},{2,1},{3,0},{4,7},{5,6},{6,5},{7,4},{8,11},{9,10},{10,... | collective-permute-start | bytes 393224 | tf_op jit(solution)/shard_map/ppermute | solution.py:28
  13.6 5.1 %collective-permute-start.2 = (bf16[256,256]{1,0:T(8,128)(2,1)S(1)}, bf16[256,256]{1,0:T(8,128)(2,1)S(1)}, u32[]{:S(2)}, u32[]{:S(2)}) collective-permute-start(bf16[256,256]{1,0:T(8,128)(2,1)S(1)} %fusion.1), channel_id=1, source_target_pairs={{0,1},{1,0},{2,3},{3,2},{4,5},{5,4},{6,7},{7,6},{8,9},{9,8},{10,11... | collective-permute-start | bytes 393224 | tf_op jit(solution)/shard_map/ppermute | solution.py:28
  19.1 12.0 %collective-permute-start.6 = (bf16[704,256]{1,0:T(8,128)(2,1)S(1)}, bf16[704,256]{1,0:T(8,128)(2,1)S(1)}, u32[]{:S(2)}, u32[]{:S(2)}) collective-permute-start(bf16[704,256]{1,0:T(8,128)(2,1)S(1)} %convolution_convert_fusion.2), channel_id=1, source_target_pairs={{0,192},{1,193},{2,194},{3,195},{4,196},{5,197},{6,198},{7,199},{8... | collective-permute-start | bytes 1081352 | tf_op jit(solution)/shard_map/ppermute | solution.py:28
  22.3 8.2 %collective-permute-start.8 = (bf16[704,256]{1,0:T(8,128)(2,1)S(1)}, bf16[704,256]{1,0:T(8,128)(2,1)S(1)}, u32[]{:S(2)}, u32[]{:S(2)}) collective-permute-start(bf16[704,256]{1,0:T(8,128)(2,1)S(1)} %convolution_convert_fusion.1), channel_id=1, source_target_pairs={{0,64},{1,65},{2,66},{3,67},{4,68},{5,69},{6,70},{7,71},{8,72},{9,... | collective-permute-start | bytes 1081352 | tf_op jit(solution)/shard_map/ppermute | solution.py:28
  30.5 6.8 %collective-permute-start.9 = (bf16[352,256]{1,0:T(8,128)(2,1)S(1)}, bf16[352,256]{1,0:T(8,128)(2,1)S(1)}, u32[]{:S(2)}, u32[]{:S(2)}) collective-permute-start(bf16[352,256]{1,0:T(8,128)(2,1)S(1)} %slice.153), channel_id=1, source_target_pairs={{0,192},{1,193},{2,194},{3,195},{4,196},{5,197},{6,198},{7,199},{8... | collective-permute-start | bytes 540680 | tf_op jit(solution)/shard_map/ppermute | solution.py:28
  31.2 10.1 %collective-permute-start.7 = (bf16[352,256]{1,0:T(8,128)(2,1)S(1)}, bf16[352,256]{1,0:T(8,128)(2,1)S(1)}, u32[]{:S(2)}, u32[]{:S(2)}) collective-permute-start(bf16[352,256]{1,0:T(8,128)(2,1)S(1)} %slice.154), channel_id=1, source_target_pairs={{0,64},{1,65},{2,66},{3,67},{4,68},{5,69},{6,70},{7,71},{8,72},{9,... | collective-permute-start | bytes 540680 | tf_op jit(solution)/shard_map/ppermute | solution.py:28
  37.4 8.6 %collective-permute-start.10 = (bf16[176,256]{1,0:T(8,128)(2,1)S(1)}, bf16[176,256]{1,0:T(8,128)(2,1)S(1)}, u32[]{:S(2)}, u32[]{:S(2)}) collective-permute-start(bf16[176,256]{1,0:T(8,128)(2,1)S(1)} %get-tuple-element.45), channel_id=1, source_target_pairs={{0,8},{1,9},{2,10},{3,11},{4,12},{5,13},{6,14},{7,15},{8,0},{9,1},... | collective-permute-start | bytes 270344 | tf_op jit(solution)/shard_map/ppermute | solution.py:28
  37.6 18.8 %copy-start.2 = (f32[1,43,512]{2,0,1:T(1,128)S(1)}, f32[1,43,512]{2,0,1:T(1,128)}, u32[]{:S(2)}) copy-start(f32[1,43,512]{2,0,1:T(1,128)} %param.11) | copy-start | bytes 264196
  37.6 18.8 %copy-start.3 = (f32[1,43,512]{2,0,1:T(1,128)S(1)}, f32[1,43,512]{2,0,1:T(1,128)}, u32[]{:S(2)}) copy-start(f32[1,43,512]{2,0,1:T(1,128)} %param.10) | copy-start | bytes 264196
  37.6 8.4 %collective-permute-start.11 = (bf16[176,256]{1,0:T(8,128)(2,1)S(1)}, bf16[176,256]{1,0:T(8,128)(2,1)S(1)}, u32[]{:S(2)}, u32[]{:S(2)}) collective-permute-start(bf16[176,256]{1,0:T(8,128)(2,1)S(1)} %get-tuple-element.46), channel_id=1, source_target_pairs={{0,56},{1,57},{2,58},{3,59},{4,60},{5,61},{6,62},{7,63},{8,16},{9,... | collective-permute-start | bytes 270344 | tf_op jit(solution)/shard_map/ppermute | solution.py:28
  41.4 9.5 %collective-permute-start.14 = (bf16[88,256]{1,0:T(8,128)(2,1)S(1)}, bf16[88,256]{1,0:T(8,128)(2,1)S(1)}, u32[]{:S(2)}, u32[]{:S(2)}) collective-permute-start(bf16[88,256]{1,0:T(8,128)(2,1)S(1)} %slice.155), channel_id=1, source_target_pairs={{0,32},{1,33},{2,34},{3,35},{4,36},{5,37},{6,38},{7,39},{8,40},{9,... | collective-permute-start | bytes 135176 | tf_op jit(solution)/shard_map/ppermute | solution.py:28
  46.1 5.0 %collective-permute-start.12 = (bf16[88,256]{1,0:T(8,128)(2,1)S(1)}, bf16[88,256]{1,0:T(8,128)(2,1)S(1)}, u32[]{:S(2)}, u32[]{:S(2)}) collective-permute-start(bf16[88,256]{1,0:T(8,128)(2,1)S(1)} %get-tuple-element.40), channel_id=1, source_target_pairs={{0,16},{1,17},{2,18},{3,19},{4,20},{5,21},{6,22},{7,23},{8,24},{9,... | collective-permute-start | bytes 135176 | tf_op jit(solution)/shard_map/ppermute | solution.py:28
  48.4 6.6 %collective-permute-start.13 = (bf16[88,256]{1,0:T(8,128)(2,1)S(1)}, bf16[88,256]{1,0:T(8,128)(2,1)S(1)}, u32[]{:S(2)}, u32[]{:S(2)}) collective-permute-start(bf16[88,256]{1,0:T(8,128)(2,1)S(1)} %get-tuple-element.41), channel_id=1, source_target_pairs={{0,48},{1,49},{2,50},{3,51},{4,52},{5,53},{6,54},{7,55},{8,56},{9,... | collective-permute-start | bytes 135176 | tf_op jit(solution)/shard_map/ppermute | solution.py:28
  55.1 1.3 %collective-permute-start.15 = (f32[43,256]{1,0:T(8,128)S(1)}, f32[43,256]{1,0:T(8,128)S(1)}, u32[]{:S(2)}, u32[]{:S(2)}) collective-permute-start(f32[43,256]{1,0:T(8,128)S(1)} %slice_select_fusion), channel_id=1, source_target_pairs={{0,4},{1,5},{2,6},{3,7},{4,0},{5,1},{6,2},{7,3},{8,12},{9,13},{10,... | collective-permute-start | bytes 132104 | tf_op jit(solution)/shard_map/ppermute | solution.py:28
  56.4 8.6 %copy-start.1 = (bf16[1,1024,512]{2,1,0:T(8,128)(2,1)S(1)}, bf16[1,1024,512]{2,1,0:T(8,128)(2,1)}, u32[]{:S(2)}) copy-start(bf16[1,1024,512]{2,1,0:T(8,128)(2,1)} %param.9) | copy-start | bytes 3145732
  56.6 8.2 %collective-permute-start.18 = (bf16[64,512]{1,0:T(8,128)(2,1)S(1)}, bf16[64,512]{1,0:T(8,128)(2,1)S(1)}, u32[]{:S(2)}, u32[]{:S(2)}) collective-permute-start(bf16[64,512]{1,0:T(8,128)(2,1)S(1)} %pad.9), channel_id=1, source_target_pairs={{0,3},{1,2},{2,1},{3,0},{4,7},{5,6},{6,5},{7,4},{8,11},{9,10},{10,... | collective-permute-start | bytes 196616 | tf_op jit(solution)/shard_map/ppermute | solution.py:28
  59.1 5.6 %collective-permute-start.17 = (bf16[48,512]{1,0:T(8,128)(2,1)S(1)}, bf16[48,512]{1,0:T(8,128)(2,1)S(1)}, u32[]{:S(2)}, u32[]{:S(2)}) collective-permute-start(bf16[48,512]{1,0:T(8,128)(2,1)S(1)} %pad.8), channel_id=1, source_target_pairs={{0,2},{1,3},{2,0},{3,1},{4,6},{5,7},{6,4},{7,5},{8,10},{9,11},{10,... | collective-permute-start | bytes 147464 | tf_op jit(solution)/shard_map/ppermute | solution.py:28
  59.1 4.2 %collective-permute-start.16 = (bf16[43,512]{1,0:T(8,128)(2,1)S(1)}, bf16[43,512]{1,0:T(8,128)(2,1)S(1)}, u32[]{:S(2)}, u32[]{:S(2)}) collective-permute-start(bf16[43,512]{1,0:T(8,128)(2,1)S(1)} %get-tuple-element.37), channel_id=1, source_target_pairs={{0,1},{1,0},{2,3},{3,2},{4,5},{5,4},{6,7},{7,6},{8,9},{9,8},{10,11... | collective-permute-start | bytes 132104 | tf_op jit(solution)/shard_map/ppermute | solution.py:28
  (1 other events, 5.9 us)

commit v16 on v15

--- a/solution.py
+++ b/solution.py
@@ -105,7 +105,7 @@
 
         @pl.when(core_ref[0] == core)
         def _(core=core):
-            own[...] = total[:, core * lanes : (core + 1) * lanes]
+            own[...] = total[:, core * lanes : (core + 1) * lanes].astype(BF)
             theirs[...] = total[:, (1 - core) * lanes : (2 - core) * lanes].astype(BF)
 
 
@@ -117,10 +117,7 @@
     hbm = pl.BlockSpec(memory_space=pltpu.HBM)
     return pl.pallas_call(
         project_kernel,
-        out_shape=[
-            jax.ShapeDtypeStruct((tokens, rank // NCORE), F32),
-            jax.ShapeDtypeStruct((tokens, rank // NCORE), BF),
-        ],
+        out_shape=[jax.ShapeDtypeStruct((tokens, rank // NCORE), BF)] * 2,
         in_specs=[pl.BlockSpec(memory_space=pltpu.SMEM), hbm, hbm],
         out_specs=[vmem] * 2,
         scratch_shapes=[
@@ -157,9 +154,9 @@
     columns = cotangent[0].T
     other_columns = swap_core(columns)
     theirs = swap_core(theirs)
-    mine = lax.optimization_barrier(mine.astype(BF))
     came = [swap_y(p, m[0]) for p, m in zip((mine, theirs), PAIRS)]
     chunks = [p.astype(F32) + c.astype(F32) for p, c in zip((mine, theirs), came)]
+    chunks[0] = lax.optimization_barrier(chunks[0])
     came = [swap_y(p.astype(BF), m[1]) for p, m in zip(chunks, PAIRS)]
     parts = arrange(order, columns, other_columns)
     came[1], parts = lax.optimization_barrier((came[1], parts))

time: 66.6 us -> 66.7 us (level)
    convert_element_type x1 -> x0, other arithmetic: 0.96 us -> none  [local(): mine = lax.optimization_barrier(mine.astype(BF))]
    add x0 -> x1, other arithmetic: none -> 0.94 us  [local(): p.astype(F32) + c.astype(F32)]
where the time goes in v16:
time: 66.7 us; the launch traced here: 66.5 us
  starting transfers between devices  29.6 us (44%)
  waiting for transfers between devices  25.8 us (39%)
  Pallas kernels  3.82 us (6%)
  local copies, waits for them, and re-layouts  2.81 us (4%)
  matrix products  1.88 us (3%)
  other arithmetic  1.67 us (3%)
  between operations  0.96 us (1%)
    ppermute x19, starting transfers between devices, send(): return lax.ppermute(value, ('dp', 'tensor'), pairs)  29.6 us
    ppermute x19, waiting for transfers between devices, send(): return lax.ppermute(value, ('dp', 'tensor'), pairs)  25.8 us
    pallas_call x1, Pallas kernels, project(): pl.pallas_call(project_kernel, out_shape=[jax.ShapeDtypeStruct((tokens, r...  2.53 us
    dot_general x5, matrix products, dot(): lax.dot_general(a, b, (((1,), (0,)), ((), ())), preferred_element_type=F32)  1.88 us
    unnamed x14, local copies, waits for them, and re-layouts  1.49 us
  transfers between devices with their start and end apart: 19, of which 10 were waited for; matrix products, arithmetic and copies ran while one was open for 6% of the time, Pallas kernels for 6%

profile of v16, /device:TPU:32, one launch (start us, length us, event | category | flops | bytes accessed | tf_op | source)
XLA Modules:
  0.0 66.5 jit_solution(5099815618798871353)
XLA Ops:
  0.8 2.5 %shard_map.94 = (bf16[256,256]{1,0:T(8,128)(2,1)}, bf16[256,256]{1,0:T(8,128)(2,1)}) custom-call(s32[1]{0:T(128)} %bitcast.core_ref, bf16[256,1024]{1,0:T(8,128)(2,1)} %bitcast.35, bf16[1024,512]{1,0:T(8,128)(2,1)} %bitcast.34), custom_call_target="tpu_custom_call" | custom-call | flops 268435456 | bytes 3145728 | tf_op jit(solution)/shard_map/pallas_call | solution.py:118
  3.9 1.6 %collective-permute-start.4 = (bf16[256,256]{1,0:T(8,128)(2,1)}, bf16[256,256]{1,0:T(8,128)(2,1)S(1)}, u32[]{:S(2)}, u32[]{:S(2)}) collective-permute-start(bf16[256,256]{1,0:T(8,128)(2,1)} %get-tuple-element.23), channel_id=1, source_target_pairs={{0,1},{1,0},{2,3},{3,2},{4,5},{5,4},{6,7},{7,6},{8,9},{9,8},{10,11... | collective-permute-start | bytes 393224 | tf_op jit(solution)/shard_map/ppermute | solution.py:28
  5.7 2.4 %collective-permute-start.1 = (bf16[256,256]{1,0:T(8,128)(2,1)S(1)}, bf16[256,256]{1,0:T(8,128)(2,1)S(1)}, u32[]{:S(2)}, u32[]{:S(2)}) collective-permute-start(bf16[256,256]{1,0:T(8,128)(2,1)S(1)} %collective-permute-done), channel_id=1, source_target_pairs={{0,3},{1,2},{2,1},{3,0},{4,7},{5,6},{6,5},{7,4},{8,11},{9,10},{10,... | collective-permute-start | bytes 393224 | tf_op jit(solution)/shard_map/ppermute | solution.py:28
  8.1 1.5 %collective-permute-done.4 = bf16[256,256]{1,0:T(8,128)(2,1)S(1)} collective-permute-done((bf16[256,256]{1,0:T(8,128)(2,1)}, bf16[256,256]{1,0:T(8,128)(2,1)S(1)}, u32[]{:S(2)}, u32[]{:S(2)}) %collective-permute-start.4) | collective-permute-done | bytes 131104 | tf_op jit(solution)/shard_map/ppermute | solution.py:28
  9.6 0.9 %convert_add_fusion.2 = f32[256,256]{1,0:T(8,128)S(1)} fusion(bf16[256,256]{1,0:T(8,128)(2,1)S(1)} %collective-permute-done.4, bf16[256,256]{1,0:T(8,128)(2,1)} %get-tuple-element.23), kind=kLoop, calls=%fused_computation.13 | loop fusion | flops 196608 | bytes 524288 | tf_op jit(solution)/shard_map/add | solution.py:158
  10.6 3.1 %collective-permute-start.5 = (bf16[256,256]{1,0:T(8,128)(2,1)S(1)}, bf16[256,256]{1,0:T(8,128)(2,1)S(1)}, u32[]{:S(2)}, u32[]{:S(2)}) collective-permute-start(bf16[256,256]{1,0:T(8,128)(2,1)S(1)} %convert_element_type.92), channel_id=1, source_target_pairs={{0,3},{1,2},{2,1},{3,0},{4,7},{5,6},{6,5},{7,4},{8,11},{9,10},{10,... | collective-permute-start | bytes 393224 | tf_op jit(solution)/shard_map/ppermute | solution.py:28
  13.9 2.9 %collective-permute-done.5 = bf16[256,256]{1,0:T(8,128)(2,1)S(1)} collective-permute-done((bf16[256,256]{1,0:T(8,128)(2,1)S(1)}, bf16[256,256]{1,0:T(8,128)(2,1)S(1)}, u32[]{:S(2)}, u32[]{:S(2)}) %collective-permute-start.5) | collective-permute-done | bytes 131104 | tf_op jit(solution)/shard_map/ppermute | solution.py:28
  16.9 1.3 %shard_map.95 = (bf16[704,512]{1,0:T(8,128)(2,1)S(1)}, bf16[704,512]{1,0:T(8,128)(2,1)S(1)}, bf16[704,512]{1,0:T(8,128)(2,1)S(1)}, bf16[704,512]{1,0:T(8,128)(2,1)S(1)}) custom-call(s32[32]{0:T(128)S(1)} %add.93.order_ref, bf16[2752,256]{1,0:T(8,128)(2,1)S(1)} %bitcast.33, bf16[2752,256]{1,0:T(8,128)(2,1)S(1)} %collective-permute-done.3.came), custom_call_target="tpu_custom_call" | custom-call | bytes 8388608 | tf_op jit(solution)/shard_map/pallas_call | solution.py:78
  19.2 2.8 %collective-permute-start.6 = (bf16[704,256]{1,0:T(8,128)(2,1)S(1)}, bf16[704,256]{1,0:T(8,128)(2,1)S(1)}, u32[]{:S(2)}, u32[]{:S(2)}) collective-permute-start(bf16[704,256]{1,0:T(8,128)(2,1)S(1)} %convolution_convert_fusion.2), channel_id=1, source_target_pairs={{0,192},{1,193},{2,194},{3,195},{4,196},{5,197},{6,198},{7,199},{8... | collective-permute-start | bytes 1081352 | tf_op jit(solution)/shard_map/ppermute | solution.py:28
  23.4 7.2 %collective-permute-done.8 = bf16[704,256]{1,0:T(8,128)(2,1)S(1)} collective-permute-done((bf16[704,256]{1,0:T(8,128)(2,1)S(1)}, bf16[704,256]{1,0:T(8,128)(2,1)S(1)}, u32[]{:S(2)}, u32[]{:S(2)}) %collective-permute-start.8) | collective-permute-done | bytes 360480 | tf_op jit(solution)/shard_map/ppermute | solution.py:28
  31.8 5.7 %collective-permute-done.9 = bf16[352,256]{1,0:T(8,128)(2,1)S(1)} collective-permute-done((bf16[352,256]{1,0:T(8,128)(2,1)S(1)}, bf16[352,256]{1,0:T(8,128)(2,1)S(1)}, u32[]{:S(2)}, u32[]{:S(2)}) %collective-permute-start.9) | collective-permute-done | bytes 180256 | tf_op jit(solution)/shard_map/ppermute | solution.py:28
  37.8 3.7 %collective-permute-start.11 = (bf16[176,256]{1,0:T(8,128)(2,1)S(1)}, bf16[176,256]{1,0:T(8,128)(2,1)S(1)}, u32[]{:S(2)}, u32[]{:S(2)}) collective-permute-start(bf16[176,256]{1,0:T(8,128)(2,1)S(1)} %get-tuple-element.46), channel_id=1, source_target_pairs={{0,56},{1,57},{2,58},{3,59},{4,60},{5,61},{6,62},{7,63},{8,16},{9,... | collective-permute-start | bytes 270344 | tf_op jit(solution)/shard_map/ppermute | solution.py:28
  41.6 4.6 %collective-permute-start.14 = (bf16[88,256]{1,0:T(8,128)(2,1)S(1)}, bf16[88,256]{1,0:T(8,128)(2,1)S(1)}, u32[]{:S(2)}, u32[]{:S(2)}) collective-permute-start(bf16[88,256]{1,0:T(8,128)(2,1)S(1)} %slice.155), channel_id=1, source_target_pairs={{0,32},{1,33},{2,34},{3,35},{4,36},{5,37},{6,38},{7,39},{8,40},{9,... | collective-permute-start | bytes 135176 | tf_op jit(solution)/shard_map/ppermute | solution.py:28
  46.3 2.2 %collective-permute-start.12 = (bf16[88,256]{1,0:T(8,128)(2,1)S(1)}, bf16[88,256]{1,0:T(8,128)(2,1)S(1)}, u32[]{:S(2)}, u32[]{:S(2)}) collective-permute-start(bf16[88,256]{1,0:T(8,128)(2,1)S(1)} %get-tuple-element.40), channel_id=1, source_target_pairs={{0,16},{1,17},{2,18},{3,19},{4,20},{5,21},{6,22},{7,23},{8,24},{9,... | collective-permute-start | bytes 135176 | tf_op jit(solution)/shard_map/ppermute | solution.py:28
  48.5 2.5 %collective-permute-start.13 = (bf16[88,256]{1,0:T(8,128)(2,1)S(1)}, bf16[88,256]{1,0:T(8,128)(2,1)S(1)}, u32[]{:S(2)}, u32[]{:S(2)}) collective-permute-start(bf16[88,256]{1,0:T(8,128)(2,1)S(1)} %get-tuple-element.41), channel_id=1, source_target_pairs={{0,48},{1,49},{2,50},{3,51},{4,52},{5,53},{6,54},{7,55},{8,56},{9,... | collective-permute-start | bytes 135176 | tf_op jit(solution)/shard_map/ppermute | solution.py:28
  51.3 3.8 %collective-permute-done.13 = bf16[88,256]{1,0:T(8,128)(2,1)S(1)} collective-permute-done((bf16[88,256]{1,0:T(8,128)(2,1)S(1)}, bf16[88,256]{1,0:T(8,128)(2,1)S(1)}, u32[]{:S(2)}, u32[]{:S(2)}) %collective-permute-start.13) | collective-permute-done | bytes 45088 | tf_op jit(solution)/shard_map/ppermute | solution.py:28
  55.3 1.2 %collective-permute-done.15 = f32[43,256]{1,0:T(8,128)S(1)} collective-permute-done((f32[43,256]{1,0:T(8,128)S(1)}, f32[43,256]{1,0:T(8,128)S(1)}, u32[]{:S(2)}, u32[]{:S(2)}) %collective-permute-start.15) | collective-permute-done | bytes 44064 | tf_op jit(solution)/shard_map/ppermute | solution.py:28
  56.7 2.5 %collective-permute-start.18 = (bf16[64,512]{1,0:T(8,128)(2,1)S(1)}, bf16[64,512]{1,0:T(8,128)(2,1)S(1)}, u32[]{:S(2)}, u32[]{:S(2)}) collective-permute-start(bf16[64,512]{1,0:T(8,128)(2,1)S(1)} %pad.9), channel_id=1, source_target_pairs={{0,3},{1,2},{2,1},{3,0},{4,7},{5,6},{6,5},{7,4},{8,11},{9,10},{10,... | collective-permute-start | bytes 196616 | tf_op jit(solution)/shard_map/ppermute | solution.py:28
  59.2 1.6 %collective-permute-start.16 = (bf16[43,512]{1,0:T(8,128)(2,1)S(1)}, bf16[43,512]{1,0:T(8,128)(2,1)S(1)}, u32[]{:S(2)}, u32[]{:S(2)}) collective-permute-start(bf16[43,512]{1,0:T(8,128)(2,1)S(1)} %get-tuple-element.37), channel_id=1, source_target_pairs={{0,1},{1,0},{2,3},{3,2},{4,5},{5,4},{6,7},{7,6},{8,9},{9,8},{10,11... | collective-permute-start | bytes 132104 | tf_op jit(solution)/shard_map/ppermute | solution.py:28
  60.9 0.7 %copy.17 = f32[1,43,512]{2,0,1:T(1,128)} copy(f32[1,43,512]{2,1,0:T(8,128)S(1)} %get-tuple-element.39) | data formatting | bytes 176128
  61.6 0.7 %copy.18 = f32[1,43,512]{2,0,1:T(1,128)} copy(f32[1,43,512]{2,1,0:T(8,128)S(1)} %get-tuple-element.38) | data formatting | bytes 176128
  62.3 1.1 %collective-permute-done.16 = bf16[43,512]{1,0:T(8,128)(2,1)S(1)} collective-permute-done((bf16[43,512]{1,0:T(8,128)(2,1)S(1)}, bf16[43,512]{1,0:T(8,128)(2,1)S(1)}, u32[]{:S(2)}, u32[]{:S(2)}) %collective-permute-start.16) | collective-permute-done | bytes 44064 | tf_op jit(solution)/shard_map/ppermute | solution.py:28
  63.5 1.4 %collective-permute-done.17 = bf16[48,512]{1,0:T(8,128)(2,1)S(1)} collective-permute-done((bf16[48,512]{1,0:T(8,128)(2,1)S(1)}, bf16[48,512]{1,0:T(8,128)(2,1)S(1)}, u32[]{:S(2)}, u32[]{:S(2)}) %collective-permute-start.17) | collective-permute-done | bytes 49184 | tf_op jit(solution)/shard_map/ppermute | solution.py:28
  65.6 0.9 %convert_element_type.112 = bf16[43,4,1024]{2,1,0:T(4,128)(2,1)} reshape(bf16[172,1024]{1,0:T(8,128)(2,1)S(1)} %convolution_convert_fusion) | data formatting | bytes 704512 | tf_op jit(solution)/shard_map/convert_element_type | solution.py:203
  (69 shorter events, 6.4 us)
Async XLA Ops:
  0.6 4.9 %copy-start.4 = (s32[2,4]{1,0:T(2,128)S(1)}, s32[2,4]{1,0:T(2,128)}, u32[]{:S(2)}) copy-start(s32[2,4]{1,0:T(2,128)} %constant.51.clone) | copy-start | bytes 100
  0.7 16.2 %collective-permute-start.3 = (bf16[2752,256]{1,0:T(8,128)(2,1)}, bf16[2752,256]{1,0:T(8,128)(2,1)S(1)}, u32[]{:S(2)}, u32[]{:S(2)}) collective-permute-start(bf16[2752,256]{1,0:T(8,128)(2,1)} %bitcast.32), channel_id=1, source_target_pairs={{0,4},{1,5},{2,6},{3,7},{4,0},{5,1},{6,2},{7,3},{8,12},{9,13},{10,... | collective-permute-start | bytes 4227080 | tf_op jit(solution)/shard_map/ppermute | solution.py:28
  0.8 16.1 %copy-start = (bf16[1,256,2752]{1,2,0:T(8,128)(2,1)S(1)}, bf16[1,256,2752]{1,2,0:T(8,128)(2,1)}, u32[]{:S(2)}) copy-start(bf16[1,256,2752]{1,2,0:T(8,128)(2,1)} %param.8) | copy-start | bytes 4227076
  3.3 2.4 %collective-permute-start = (bf16[256,256]{1,0:T(8,128)(2,1)}, bf16[256,256]{1,0:T(8,128)(2,1)S(1)}, u32[]{:S(2)}, u32[]{:S(2)}) collective-permute-start(bf16[256,256]{1,0:T(8,128)(2,1)} %get-tuple-element.17), channel_id=1, source_target_pairs={{0,4},{1,5},{2,6},{3,7},{4,0},{5,1},{6,2},{7,3},{8,12},{9,13},{10,... | collective-permute-start | bytes 393224 | tf_op jit(solution)/shard_map/ppermute | solution.py:28
  3.9 5.7 %collective-permute-start.4 = (bf16[256,256]{1,0:T(8,128)(2,1)}, bf16[256,256]{1,0:T(8,128)(2,1)S(1)}, u32[]{:S(2)}, u32[]{:S(2)}) collective-permute-start(bf16[256,256]{1,0:T(8,128)(2,1)} %get-tuple-element.23), channel_id=1, source_target_pairs={{0,1},{1,0},{2,3},{3,2},{4,5},{5,4},{6,7},{7,6},{8,9},{9,8},{10,11... | collective-permute-start | bytes 393224 | tf_op jit(solution)/shard_map/ppermute | solution.py:28
  5.7 7.9 %collective-permute-start.1 = (bf16[256,256]{1,0:T(8,128)(2,1)S(1)}, bf16[256,256]{1,0:T(8,128)(2,1)S(1)}, u32[]{:S(2)}, u32[]{:S(2)}) collective-permute-start(bf16[256,256]{1,0:T(8,128)(2,1)S(1)} %collective-permute-done), channel_id=1, source_target_pairs={{0,3},{1,2},{2,1},{3,0},{4,7},{5,6},{6,5},{7,4},{8,11},{9,10},{10,... | collective-permute-start | bytes 393224 | tf_op jit(solution)/shard_map/ppermute | solution.py:28
  10.6 6.3 %collective-permute-start.5 = (bf16[256,256]{1,0:T(8,128)(2,1)S(1)}, bf16[256,256]{1,0:T(8,128)(2,1)S(1)}, u32[]{:S(2)}, u32[]{:S(2)}) collective-permute-start(bf16[256,256]{1,0:T(8,128)(2,1)S(1)} %convert_element_type.92), channel_id=1, source_target_pairs={{0,3},{1,2},{2,1},{3,0},{4,7},{5,6},{6,5},{7,4},{8,11},{9,10},{10,... | collective-permute-start | bytes 393224 | tf_op jit(solution)/shard_map/ppermute | solution.py:28
  13.7 5.1 %collective-permute-start.2 = (bf16[256,256]{1,0:T(8,128)(2,1)S(1)}, bf16[256,256]{1,0:T(8,128)(2,1)S(1)}, u32[]{:S(2)}, u32[]{:S(2)}) collective-permute-start(bf16[256,256]{1,0:T(8,128)(2,1)S(1)} %fusion.1), channel_id=1, source_target_pairs={{0,1},{1,0},{2,3},{3,2},{4,5},{5,4},{6,7},{7,6},{8,9},{9,8},{10,11... | collective-permute-start | bytes 393224 | tf_op jit(solution)/shard_map/ppermute | solution.py:28
  19.2 12.1 %collective-permute-start.6 = (bf16[704,256]{1,0:T(8,128)(2,1)S(1)}, bf16[704,256]{1,0:T(8,128)(2,1)S(1)}, u32[]{:S(2)}, u32[]{:S(2)}) collective-permute-start(bf16[704,256]{1,0:T(8,128)(2,1)S(1)} %convolution_convert_fusion.2), channel_id=1, source_target_pairs={{0,192},{1,193},{2,194},{3,195},{4,196},{5,197},{6,198},{7,199},{8... | collective-permute-start | bytes 1081352 | tf_op jit(solution)/shard_map/ppermute | solution.py:28
  22.4 8.3 %collective-permute-start.8 = (bf16[704,256]{1,0:T(8,128)(2,1)S(1)}, bf16[704,256]{1,0:T(8,128)(2,1)S(1)}, u32[]{:S(2)}, u32[]{:S(2)}) collective-permute-start(bf16[704,256]{1,0:T(8,128)(2,1)S(1)} %convolution_convert_fusion.1), channel_id=1, source_target_pairs={{0,64},{1,65},{2,66},{3,67},{4,68},{5,69},{6,70},{7,71},{8,72},{9,... | collective-permute-start | bytes 1081352 | tf_op jit(solution)/shard_map/ppermute | solution.py:28
  30.8 6.8 %collective-permute-start.9 = (bf16[352,256]{1,0:T(8,128)(2,1)S(1)}, bf16[352,256]{1,0:T(8,128)(2,1)S(1)}, u32[]{:S(2)}, u32[]{:S(2)}) collective-permute-start(bf16[352,256]{1,0:T(8,128)(2,1)S(1)} %slice.153), channel_id=1, source_target_pairs={{0,192},{1,193},{2,194},{3,195},{4,196},{5,197},{6,198},{7,199},{8... | collective-permute-start | bytes 540680 | tf_op jit(solution)/shard_map/ppermute | solution.py:28
  31.4 10.1 %collective-permute-start.7 = (bf16[352,256]{1,0:T(8,128)(2,1)S(1)}, bf16[352,256]{1,0:T(8,128)(2,1)S(1)}, u32[]{:S(2)}, u32[]{:S(2)}) collective-permute-start(bf16[352,256]{1,0:T(8,128)(2,1)S(1)} %slice.154), channel_id=1, source_target_pairs={{0,64},{1,65},{2,66},{3,67},{4,68},{5,69},{6,70},{7,71},{8,72},{9,... | collective-permute-start | bytes 540680 | tf_op jit(solution)/shard_map/ppermute | solution.py:28
  37.6 8.6 %collective-permute-start.10 = (bf16[176,256]{1,0:T(8,128)(2,1)S(1)}, bf16[176,256]{1,0:T(8,128)(2,1)S(1)}, u32[]{:S(2)}, u32[]{:S(2)}) collective-permute-start(bf16[176,256]{1,0:T(8,128)(2,1)S(1)} %get-tuple-element.45), channel_id=1, source_target_pairs={{0,8},{1,9},{2,10},{3,11},{4,12},{5,13},{6,14},{7,15},{8,0},{9,1},... | collective-permute-start | bytes 270344 | tf_op jit(solution)/shard_map/ppermute | solution.py:28
  37.8 18.7 %copy-start.2 = (f32[1,43,512]{2,0,1:T(1,128)S(1)}, f32[1,43,512]{2,0,1:T(1,128)}, u32[]{:S(2)}) copy-start(f32[1,43,512]{2,0,1:T(1,128)} %param.11) | copy-start | bytes 264196
  37.8 18.7 %copy-start.3 = (f32[1,43,512]{2,0,1:T(1,128)S(1)}, f32[1,43,512]{2,0,1:T(1,128)}, u32[]{:S(2)}) copy-start(f32[1,43,512]{2,0,1:T(1,128)} %param.10) | copy-start | bytes 264196
  37.8 8.4 %collective-permute-start.11 = (bf16[176,256]{1,0:T(8,128)(2,1)S(1)}, bf16[176,256]{1,0:T(8,128)(2,1)S(1)}, u32[]{:S(2)}, u32[]{:S(2)}) collective-permute-start(bf16[176,256]{1,0:T(8,128)(2,1)S(1)} %get-tuple-element.46), channel_id=1, source_target_pairs={{0,56},{1,57},{2,58},{3,59},{4,60},{5,61},{6,62},{7,63},{8,16},{9,... | collective-permute-start | bytes 270344 | tf_op jit(solution)/shard_map/ppermute | solution.py:28
  41.6 9.5 %collective-permute-start.14 = (bf16[88,256]{1,0:T(8,128)(2,1)S(1)}, bf16[88,256]{1,0:T(8,128)(2,1)S(1)}, u32[]{:S(2)}, u32[]{:S(2)}) collective-permute-start(bf16[88,256]{1,0:T(8,128)(2,1)S(1)} %slice.155), channel_id=1, source_target_pairs={{0,32},{1,33},{2,34},{3,35},{4,36},{5,37},{6,38},{7,39},{8,40},{9,... | collective-permute-start | bytes 135176 | tf_op jit(solution)/shard_map/ppermute | solution.py:28
  46.3 5.1 %collective-permute-start.12 = (bf16[88,256]{1,0:T(8,128)(2,1)S(1)}, bf16[88,256]{1,0:T(8,128)(2,1)S(1)}, u32[]{:S(2)}, u32[]{:S(2)}) collective-permute-start(bf16[88,256]{1,0:T(8,128)(2,1)S(1)} %get-tuple-element.40), channel_id=1, source_target_pairs={{0,16},{1,17},{2,18},{3,19},{4,20},{5,21},{6,22},{7,23},{8,24},{9,... | collective-permute-start | bytes 135176 | tf_op jit(solution)/shard_map/ppermute | solution.py:28
  48.5 6.6 %collective-permute-start.13 = (bf16[88,256]{1,0:T(8,128)(2,1)S(1)}, bf16[88,256]{1,0:T(8,128)(2,1)S(1)}, u32[]{:S(2)}, u32[]{:S(2)}) collective-permute-start(bf16[88,256]{1,0:T(8,128)(2,1)S(1)} %get-tuple-element.41), channel_id=1, source_target_pairs={{0,48},{1,49},{2,50},{3,51},{4,52},{5,53},{6,54},{7,55},{8,56},{9,... | collective-permute-start | bytes 135176 | tf_op jit(solution)/shard_map/ppermute | solution.py:28
  55.2 1.3 %collective-permute-start.15 = (f32[43,256]{1,0:T(8,128)S(1)}, f32[43,256]{1,0:T(8,128)S(1)}, u32[]{:S(2)}, u32[]{:S(2)}) collective-permute-start(f32[43,256]{1,0:T(8,128)S(1)} %slice_select_fusion), channel_id=1, source_target_pairs={{0,4},{1,5},{2,6},{3,7},{4,0},{5,1},{6,2},{7,3},{8,12},{9,13},{10,... | collective-permute-start | bytes 132104 | tf_op jit(solution)/shard_map/ppermute | solution.py:28
  56.6 8.5 %copy-start.1 = (bf16[1,1024,512]{2,1,0:T(8,128)(2,1)S(1)}, bf16[1,1024,512]{2,1,0:T(8,128)(2,1)}, u32[]{:S(2)}) copy-start(bf16[1,1024,512]{2,1,0:T(8,128)(2,1)} %param.9) | copy-start | bytes 3145732
  56.7 8.1 %collective-permute-start.18 = (bf16[64,512]{1,0:T(8,128)(2,1)S(1)}, bf16[64,512]{1,0:T(8,128)(2,1)S(1)}, u32[]{:S(2)}, u32[]{:S(2)}) collective-permute-start(bf16[64,512]{1,0:T(8,128)(2,1)S(1)} %pad.9), channel_id=1, source_target_pairs={{0,3},{1,2},{2,1},{3,0},{4,7},{5,6},{6,5},{7,4},{8,11},{9,10},{10,... | collective-permute-start | bytes 196616 | tf_op jit(solution)/shard_map/ppermute | solution.py:28
  59.2 5.6 %collective-permute-start.17 = (bf16[48,512]{1,0:T(8,128)(2,1)S(1)}, bf16[48,512]{1,0:T(8,128)(2,1)S(1)}, u32[]{:S(2)}, u32[]{:S(2)}) collective-permute-start(bf16[48,512]{1,0:T(8,128)(2,1)S(1)} %pad.8), channel_id=1, source_target_pairs={{0,2},{1,3},{2,0},{3,1},{4,6},{5,7},{6,4},{7,5},{8,10},{9,11},{10,... | collective-permute-start | bytes 147464 | tf_op jit(solution)/shard_map/ppermute | solution.py:28
  59.2 4.2 %collective-permute-start.16 = (bf16[43,512]{1,0:T(8,128)(2,1)S(1)}, bf16[43,512]{1,0:T(8,128)(2,1)S(1)}, u32[]{:S(2)}, u32[]{:S(2)}) collective-permute-start(bf16[43,512]{1,0:T(8,128)(2,1)S(1)} %get-tuple-element.37), channel_id=1, source_target_pairs={{0,1},{1,0},{2,3},{3,2},{4,5},{5,4},{6,7},{7,6},{8,9},{9,8},{10,11... | collective-permute-start | bytes 132104 | tf_op jit(solution)/shard_map/ppermute | solution.py:28
  (1 other events, 4.8 us)

commit v17 on v14

--- a/solution.py
+++ b/solution.py
@@ -141,10 +141,14 @@
     chunks = [p + c.astype(F32) for p, c in zip(chunks, came)]
     projected = jnp.concatenate([p.astype(BF) for p in chunks], axis=0)
 
-    sent = [dot(part, projected).astype(BF) for part in parts[::2]]
+    sent = [dot(parts[0], projected).astype(BF)]
+    after, sent[0] = lax.optimization_barrier((projected, sent[0]))
+    kept = [dot(parts[1], after)]
+    after, kept[0] = lax.optimization_barrier((after, kept[0]))
+    sent.append(dot(parts[2], after).astype(BF))
     came = [swap_x(value, m[0]) for value, m in zip(sent, PAIRS)]
-    projected, sent[1] = lax.optimization_barrier((projected, sent[1]))
-    kept = lax.optimization_barrier([dot(part, projected) for part in parts[1::2]])
+    after, sent[1] = lax.optimization_barrier((after, sent[1]))
+    kept.append(lax.optimization_barrier(dot(parts[3], after)))
     kept = [k + c.astype(F32) for k, c in zip(kept, came)]
     came = [swap_x(k[:HALF].astype(BF), m[1]) for k, m in zip(kept, PAIRS)]
     leave, keep = [k[HALF:] + c.astype(F32) for k, c in zip(kept, came)]

time: 66.6 us -> 64.5 us (0.968)
  waiting for transfers between devices: 25.9 us -> 19.7 us
  starting transfers between devices: 29.5 us -> 32.8 us
    ppermute x19, waiting for transfers between devices: 25.9 us -> 19.7 us  [send(): return lax.ppermute(value, ('dp', 'tensor'), pairs)]
    ppermute x19, starting transfers between devices: 29.5 us -> 32.8 us  [send(): return lax.ppermute(value, ('dp', 'tensor'), pairs)]
  transfers between devices with their start and end apart: 19 -> 19, of which waited for: 10 -> 11; matrix products, arithmetic and copies ran while one was open for 6% -> 6% of each run, Pallas kernels for 3% -> 3%
where the time goes in v17:
time: 64.5 us; the launch traced here: 63.7 us
  starting transfers between devices  32.8 us (51%)
  waiting for transfers between devices  19.7 us (31%)
  local copies, waits for them, and re-layouts  5.07 us (8%)
  matrix products  1.88 us (3%)
  Pallas kernels  1.75 us (3%)
  other arithmetic  1.48 us (2%)
  between operations  0.95 us (1%)
    ppermute x19, starting transfers between devices, send(): return lax.ppermute(value, ('dp', 'tensor'), pairs)  32.8 us
    ppermute x19, waiting for transfers between devices, send(): return lax.ppermute(value, ('dp', 'tensor'), pairs)  19.7 us
    unnamed x18, local copies, waits for them, and re-layouts  3.75 us
    dot_general x5, matrix products, dot(): lax.dot_general(a, b, (((1,), (0,)), ((), ())), preferred_element_type=F32)  1.88 us
    pallas_call x1, Pallas kernels, arrange(): pl.pallas_call(arrange_kernel, out_shape=[shape] * 4, in_specs=[smem, vme...  1.3 us
  transfers between devices with their start and end apart: 19, of which 11 were waited for; matrix products, arithmetic and copies ran while one was open for 6% of the time, Pallas kernels for 3%

profile of v17, /device:TPU:32, one launch (start us, length us, event | category | flops | bytes accessed | tf_op | source)
XLA Modules:
  0.0 63.7 jit_solution(2150876357166937993)
XLA Ops:
  0.8 1.2 %copy-done = bf16[1,1024,512]{2,1,0:T(8,128)(2,1)S(1)} copy-done((bf16[1,1024,512]{2,1,0:T(8,128)(2,1)S(1)}, bf16[1,1024,512]{2,1,0:T(8,128)(2,1)}, u32[]{:S(2)}) %copy-start) | copy-done | bytes 1048600
  4.7 1.6 %collective-permute-start.4 = (bf16[256,256]{1,0:T(8,128)(2,1)}, bf16[256,256]{1,0:T(8,128)(2,1)S(1)}, u32[]{:S(2)}, u32[]{:S(2)}) collective-permute-start(bf16[256,256]{1,0:T(8,128)(2,1)} %convert_element_type.90), channel_id=1, source_target_pairs={{0,1},{1,0},{2,3},{3,2},{4,5},{5,4},{6,7},{7,6},{8,9},{9,8},{10,11... | collective-permute-start | bytes 393224 | tf_op jit(solution)/shard_map/ppermute | solution.py:27
  6.6 2.3 %collective-permute-start.1 = (bf16[256,256]{1,0:T(8,128)(2,1)S(1)}, bf16[256,256]{1,0:T(8,128)(2,1)S(1)}, u32[]{:S(2)}, u32[]{:S(2)}) collective-permute-start(bf16[256,256]{1,0:T(8,128)(2,1)S(1)} %collective-permute-done), channel_id=1, source_target_pairs={{0,3},{1,2},{2,1},{3,0},{4,7},{5,6},{6,5},{7,4},{8,11},{9,10},{10,... | collective-permute-start | bytes 393224 | tf_op jit(solution)/shard_map/ppermute | solution.py:27
  8.9 1.5 %collective-permute-done.4 = bf16[256,256]{1,0:T(8,128)(2,1)S(1)} collective-permute-done((bf16[256,256]{1,0:T(8,128)(2,1)}, bf16[256,256]{1,0:T(8,128)(2,1)S(1)}, u32[]{:S(2)}, u32[]{:S(2)}) %collective-permute-start.4) | collective-permute-done | bytes 131104 | tf_op jit(solution)/shard_map/ppermute | solution.py:27
  10.4 3.1 %collective-permute-start.5 = (bf16[256,256]{1,0:T(8,128)(2,1)S(1)}, bf16[256,256]{1,0:T(8,128)(2,1)S(1)}, u32[]{:S(2)}, u32[]{:S(2)}) collective-permute-start(bf16[256,256]{1,0:T(8,128)(2,1)S(1)} %fusion.2), channel_id=1, source_target_pairs={{0,3},{1,2},{2,1},{3,0},{4,7},{5,6},{6,5},{7,4},{8,11},{9,10},{10,... | collective-permute-start | bytes 393224 | tf_op jit(solution)/shard_map/ppermute | solution.py:27
  13.8 2.9 %collective-permute-done.5 = bf16[256,256]{1,0:T(8,128)(2,1)S(1)} collective-permute-done((bf16[256,256]{1,0:T(8,128)(2,1)S(1)}, bf16[256,256]{1,0:T(8,128)(2,1)S(1)}, u32[]{:S(2)}, u32[]{:S(2)}) %collective-permute-start.5) | collective-permute-done | bytes 131104 | tf_op jit(solution)/shard_map/ppermute | solution.py:27
  16.8 1.3 %shard_map.95 = (bf16[704,512]{1,0:T(8,128)(2,1)S(1)}, bf16[704,512]{1,0:T(8,128)(2,1)S(1)}, bf16[704,512]{1,0:T(8,128)(2,1)S(1)}, bf16[704,512]{1,0:T(8,128)(2,1)S(1)}) custom-call(s32[32]{0:T(128)S(1)} %add.93.order_ref, bf16[2752,256]{1,0:T(8,128)(2,1)S(1)} %bitcast.35, bf16[2752,256]{1,0:T(8,128)(2,1)S(1)} %collective-permute-done.3.came), custom_call_target="tpu_custom_call" | custom-call | bytes 8388608 | tf_op jit(solution)/shard_map/pallas_call | solution.py:77
  19.4 1.6 %collective-permute-start.8 = (bf16[704,256]{1,0:T(8,128)(2,1)S(1)}, bf16[704,256]{1,0:T(8,128)(2,1)S(1)}, u32[]{:S(2)}, u32[]{:S(2)}) collective-permute-start(bf16[704,256]{1,0:T(8,128)(2,1)S(1)} %convolution_convert_fusion.2), channel_id=1, source_target_pairs={{0,64},{1,65},{2,66},{3,67},{4,68},{5,69},{6,70},{7,71},{8,72},{9,... | collective-permute-start | bytes 1081352 | tf_op jit(solution)/shard_map/ppermute | solution.py:27
  21.3 2.2 %collective-permute-start.6 = (bf16[704,256]{1,0:T(8,128)(2,1)S(1)}, bf16[704,256]{1,0:T(8,128)(2,1)S(1)}, u32[]{:S(2)}, u32[]{:S(2)}) collective-permute-start(bf16[704,256]{1,0:T(8,128)(2,1)S(1)} %convolution_convert_fusion.1), channel_id=1, source_target_pairs={{0,192},{1,193},{2,194},{3,195},{4,196},{5,197},{6,198},{7,199},{8... | collective-permute-start | bytes 1081352 | tf_op jit(solution)/shard_map/ppermute | solution.py:27
  23.9 4.0 %collective-permute-done.8 = bf16[704,256]{1,0:T(8,128)(2,1)S(1)} collective-permute-done((bf16[704,256]{1,0:T(8,128)(2,1)S(1)}, bf16[704,256]{1,0:T(8,128)(2,1)S(1)}, u32[]{:S(2)}, u32[]{:S(2)}) %collective-permute-start.8) | collective-permute-done | bytes 360480 | tf_op jit(solution)/shard_map/ppermute | solution.py:27
  28.0 2.8 %collective-permute-start.9 = (bf16[352,256]{1,0:T(8,128)(2,1)S(1)}, bf16[352,256]{1,0:T(8,128)(2,1)S(1)}, u32[]{:S(2)}, u32[]{:S(2)}) collective-permute-start(bf16[352,256]{1,0:T(8,128)(2,1)S(1)} %slice.153), channel_id=1, source_target_pairs={{0,192},{1,193},{2,194},{3,195},{4,196},{5,197},{6,198},{7,199},{8... | collective-permute-start | bytes 540680 | tf_op jit(solution)/shard_map/ppermute | solution.py:27
  30.8 1.6 %collective-permute-done.6 = bf16[704,256]{1,0:T(8,128)(2,1)S(1)} collective-permute-done((bf16[704,256]{1,0:T(8,128)(2,1)S(1)}, bf16[704,256]{1,0:T(8,128)(2,1)S(1)}, u32[]{:S(2)}, u32[]{:S(2)}) %collective-permute-start.6) | collective-permute-done | bytes 360480 | tf_op jit(solution)/shard_map/ppermute | solution.py:27
  32.6 2.2 %collective-permute-done.9 = bf16[352,256]{1,0:T(8,128)(2,1)S(1)} collective-permute-done((bf16[352,256]{1,0:T(8,128)(2,1)S(1)}, bf16[352,256]{1,0:T(8,128)(2,1)S(1)}, u32[]{:S(2)}, u32[]{:S(2)}) %collective-permute-start.9) | collective-permute-done | bytes 180256 | tf_op jit(solution)/shard_map/ppermute | solution.py:27
  34.8 1.4 %collective-permute-start.10 = (bf16[176,256]{1,0:T(8,128)(2,1)S(1)}, bf16[176,256]{1,0:T(8,128)(2,1)S(1)}, u32[]{:S(2)}, u32[]{:S(2)}) collective-permute-start(bf16[176,256]{1,0:T(8,128)(2,1)S(1)} %get-tuple-element.49), channel_id=1, source_target_pairs={{0,8},{1,9},{2,10},{3,11},{4,12},{5,13},{6,14},{7,15},{8,0},{9,1},... | collective-permute-start | bytes 270344 | tf_op jit(solution)/shard_map/ppermute | solution.py:27
  36.2 2.5 %collective-permute-start.11 = (bf16[176,256]{1,0:T(8,128)(2,1)S(1)}, bf16[176,256]{1,0:T(8,128)(2,1)S(1)}, u32[]{:S(2)}, u32[]{:S(2)}) collective-permute-start(bf16[176,256]{1,0:T(8,128)(2,1)S(1)} %get-tuple-element.50), channel_id=1, source_target_pairs={{0,56},{1,57},{2,58},{3,59},{4,60},{5,61},{6,62},{7,63},{8,16},{9,... | collective-permute-start | bytes 270344 | tf_op jit(solution)/shard_map/ppermute | solution.py:27
  38.8 5.7 %collective-permute-start.14 = (bf16[88,256]{1,0:T(8,128)(2,1)S(1)}, bf16[88,256]{1,0:T(8,128)(2,1)S(1)}, u32[]{:S(2)}, u32[]{:S(2)}) collective-permute-start(bf16[88,256]{1,0:T(8,128)(2,1)S(1)} %slice.155), channel_id=1, source_target_pairs={{0,32},{1,33},{2,34},{3,35},{4,36},{5,37},{6,38},{7,39},{8,40},{9,... | collective-permute-start | bytes 135176 | tf_op jit(solution)/shard_map/ppermute | solution.py:27
  44.6 1.6 %collective-permute-start.12 = (bf16[88,256]{1,0:T(8,128)(2,1)S(1)}, bf16[88,256]{1,0:T(8,128)(2,1)S(1)}, u32[]{:S(2)}, u32[]{:S(2)}) collective-permute-start(bf16[88,256]{1,0:T(8,128)(2,1)S(1)} %get-tuple-element.44), channel_id=1, source_target_pairs={{0,16},{1,17},{2,18},{3,19},{4,20},{5,21},{6,22},{7,23},{8,24},{9,... | collective-permute-start | bytes 135176 | tf_op jit(solution)/shard_map/ppermute | solution.py:27
  46.2 2.9 %collective-permute-start.13 = (bf16[88,256]{1,0:T(8,128)(2,1)S(1)}, bf16[88,256]{1,0:T(8,128)(2,1)S(1)}, u32[]{:S(2)}, u32[]{:S(2)}) collective-permute-start(bf16[88,256]{1,0:T(8,128)(2,1)S(1)} %get-tuple-element.45), channel_id=1, source_target_pairs={{0,48},{1,49},{2,50},{3,51},{4,52},{5,53},{6,54},{7,55},{8,56},{9,... | collective-permute-start | bytes 135176 | tf_op jit(solution)/shard_map/ppermute | solution.py:27
  49.7 2.6 %collective-permute-done.13 = bf16[88,256]{1,0:T(8,128)(2,1)S(1)} collective-permute-done((bf16[88,256]{1,0:T(8,128)(2,1)S(1)}, bf16[88,256]{1,0:T(8,128)(2,1)S(1)}, u32[]{:S(2)}, u32[]{:S(2)}) %collective-permute-start.13) | collective-permute-done | bytes 45088 | tf_op jit(solution)/shard_map/ppermute | solution.py:27
  52.5 1.2 %collective-permute-done.15 = f32[43,256]{1,0:T(8,128)S(1)} collective-permute-done((f32[43,256]{1,0:T(8,128)S(1)}, f32[43,256]{1,0:T(8,128)S(1)}, u32[]{:S(2)}, u32[]{:S(2)}) %collective-permute-start.15) | collective-permute-done | bytes 44064 | tf_op jit(solution)/shard_map/ppermute | solution.py:27
  53.8 2.6 %collective-permute-start.18 = (bf16[64,512]{1,0:T(8,128)(2,1)S(1)}, bf16[64,512]{1,0:T(8,128)(2,1)S(1)}, u32[]{:S(2)}, u32[]{:S(2)}) collective-permute-start(bf16[64,512]{1,0:T(8,128)(2,1)S(1)} %pad.9), channel_id=1, source_target_pairs={{0,3},{1,2},{2,1},{3,0},{4,7},{5,6},{6,5},{7,4},{8,11},{9,10},{10,... | collective-permute-start | bytes 196616 | tf_op jit(solution)/shard_map/ppermute | solution.py:27
  56.4 1.6 %collective-permute-start.16 = (bf16[43,512]{1,0:T(8,128)(2,1)S(1)}, bf16[43,512]{1,0:T(8,128)(2,1)S(1)}, u32[]{:S(2)}, u32[]{:S(2)}) collective-permute-start(bf16[43,512]{1,0:T(8,128)(2,1)S(1)} %get-tuple-element.41), channel_id=1, source_target_pairs={{0,1},{1,0},{2,3},{3,2},{4,5},{5,4},{6,7},{7,6},{8,9},{9,8},{10,11... | collective-permute-start | bytes 132104 | tf_op jit(solution)/shard_map/ppermute | solution.py:27
  59.5 1.1 %collective-permute-done.16 = bf16[43,512]{1,0:T(8,128)(2,1)S(1)} collective-permute-done((bf16[43,512]{1,0:T(8,128)(2,1)S(1)}, bf16[43,512]{1,0:T(8,128)(2,1)S(1)}, u32[]{:S(2)}, u32[]{:S(2)}) %collective-permute-start.16) | collective-permute-done | bytes 44064 | tf_op jit(solution)/shard_map/ppermute | solution.py:27
  60.6 1.4 %collective-permute-done.17 = bf16[48,512]{1,0:T(8,128)(2,1)S(1)} collective-permute-done((bf16[48,512]{1,0:T(8,128)(2,1)S(1)}, bf16[48,512]{1,0:T(8,128)(2,1)S(1)}, u32[]{:S(2)}, u32[]{:S(2)}) %collective-permute-start.17) | collective-permute-done | bytes 49184 | tf_op jit(solution)/shard_map/ppermute | solution.py:27
  (73 shorter events, 10.0 us)
Async XLA Ops:
  0.6 5.8 %copy-start.6 = (s32[2,4]{1,0:T(2,128)S(1)}, s32[2,4]{1,0:T(2,128)}, u32[]{:S(2)}) copy-start(s32[2,4]{1,0:T(2,128)} %constant.51.clone) | copy-start | bytes 100
  0.7 16.1 %collective-permute-start.3 = (bf16[2752,256]{1,0:T(8,128)(2,1)}, bf16[2752,256]{1,0:T(8,128)(2,1)S(1)}, u32[]{:S(2)}, u32[]{:S(2)}) collective-permute-start(bf16[2752,256]{1,0:T(8,128)(2,1)} %bitcast.34), channel_id=1, source_target_pairs={{0,4},{1,5},{2,6},{3,7},{4,0},{5,1},{6,2},{7,3},{8,12},{9,13},{10,... | collective-permute-start | bytes 4227080 | tf_op jit(solution)/shard_map/ppermute | solution.py:27
  3.0 13.7 %copy-start.2 = (bf16[1,256,2752]{1,2,0:T(8,128)(2,1)S(1)}, bf16[1,256,2752]{1,2,0:T(8,128)(2,1)}, u32[]{:S(2)}) copy-start(bf16[1,256,2752]{1,2,0:T(8,128)(2,1)} %param.8) | copy-start | bytes 4227076
  3.5 3.1 %collective-permute-start = (bf16[256,256]{1,0:T(8,128)(2,1)S(1)}, bf16[256,256]{1,0:T(8,128)(2,1)S(1)}, u32[]{:S(2)}, u32[]{:S(2)}) collective-permute-start(bf16[256,256]{1,0:T(8,128)(2,1)S(1)} %get-tuple-element.19), channel_id=1, source_target_pairs={{0,4},{1,5},{2,6},{3,7},{4,0},{5,1},{6,2},{7,3},{8,12},{9,13},{10,... | collective-permute-start | bytes 393224 | tf_op jit(solution)/shard_map/ppermute | solution.py:27
  4.7 5.6 %collective-permute-start.4 = (bf16[256,256]{1,0:T(8,128)(2,1)}, bf16[256,256]{1,0:T(8,128)(2,1)S(1)}, u32[]{:S(2)}, u32[]{:S(2)}) collective-permute-start(bf16[256,256]{1,0:T(8,128)(2,1)} %convert_element_type.90), channel_id=1, source_target_pairs={{0,1},{1,0},{2,3},{3,2},{4,5},{5,4},{6,7},{7,6},{8,9},{9,8},{10,11... | collective-permute-start | bytes 393224 | tf_op jit(solution)/shard_map/ppermute | solution.py:27
  6.6 6.9 %collective-permute-start.1 = (bf16[256,256]{1,0:T(8,128)(2,1)S(1)}, bf16[256,256]{1,0:T(8,128)(2,1)S(1)}, u32[]{:S(2)}, u32[]{:S(2)}) collective-permute-start(bf16[256,256]{1,0:T(8,128)(2,1)S(1)} %collective-permute-done), channel_id=1, source_target_pairs={{0,3},{1,2},{2,1},{3,0},{4,7},{5,6},{6,5},{7,4},{8,11},{9,10},{10,... | collective-permute-start | bytes 393224 | tf_op jit(solution)/shard_map/ppermute | solution.py:27
  10.4 6.3 %collective-permute-start.5 = (bf16[256,256]{1,0:T(8,128)(2,1)S(1)}, bf16[256,256]{1,0:T(8,128)(2,1)S(1)}, u32[]{:S(2)}, u32[]{:S(2)}) collective-permute-start(bf16[256,256]{1,0:T(8,128)(2,1)S(1)} %fusion.2), channel_id=1, source_target_pairs={{0,3},{1,2},{2,1},{3,0},{4,7},{5,6},{6,5},{7,4},{8,11},{9,10},{10,... | collective-permute-start | bytes 393224 | tf_op jit(solution)/shard_map/ppermute | solution.py:27
  13.6 5.1 %collective-permute-start.2 = (bf16[256,256]{1,0:T(8,128)(2,1)S(1)}, bf16[256,256]{1,0:T(8,128)(2,1)S(1)}, u32[]{:S(2)}, u32[]{:S(2)}) collective-permute-start(bf16[256,256]{1,0:T(8,128)(2,1)S(1)} %fusion.1), channel_id=1, source_target_pairs={{0,1},{1,0},{2,3},{3,2},{4,5},{5,4},{6,7},{7,6},{8,9},{9,8},{10,11... | collective-permute-start | bytes 393224 | tf_op jit(solution)/shard_map/ppermute | solution.py:27
  19.4 8.4 %collective-permute-start.8 = (bf16[704,256]{1,0:T(8,128)(2,1)S(1)}, bf16[704,256]{1,0:T(8,128)(2,1)S(1)}, u32[]{:S(2)}, u32[]{:S(2)}) collective-permute-start(bf16[704,256]{1,0:T(8,128)(2,1)S(1)} %convolution_convert_fusion.2), channel_id=1, source_target_pairs={{0,64},{1,65},{2,66},{3,67},{4,68},{5,69},{6,70},{7,71},{8,72},{9,... | collective-permute-start | bytes 1081352 | tf_op jit(solution)/shard_map/ppermute | solution.py:27
  21.3 11.0 %collective-permute-start.6 = (bf16[704,256]{1,0:T(8,128)(2,1)S(1)}, bf16[704,256]{1,0:T(8,128)(2,1)S(1)}, u32[]{:S(2)}, u32[]{:S(2)}) collective-permute-start(bf16[704,256]{1,0:T(8,128)(2,1)S(1)} %convolution_convert_fusion.1), channel_id=1, source_target_pairs={{0,192},{1,193},{2,194},{3,195},{4,196},{5,197},{6,198},{7,199},{8... | collective-permute-start | bytes 1081352 | tf_op jit(solution)/shard_map/ppermute | solution.py:27
  28.0 6.8 %collective-permute-start.9 = (bf16[352,256]{1,0:T(8,128)(2,1)S(1)}, bf16[352,256]{1,0:T(8,128)(2,1)S(1)}, u32[]{:S(2)}, u32[]{:S(2)}) collective-permute-start(bf16[352,256]{1,0:T(8,128)(2,1)S(1)} %slice.153), channel_id=1, source_target_pairs={{0,192},{1,193},{2,194},{3,195},{4,196},{5,197},{6,198},{7,199},{8... | collective-permute-start | bytes 540680 | tf_op jit(solution)/shard_map/ppermute | solution.py:27
  32.5 6.3 %collective-permute-start.7 = (bf16[352,256]{1,0:T(8,128)(2,1)S(1)}, bf16[352,256]{1,0:T(8,128)(2,1)S(1)}, u32[]{:S(2)}, u32[]{:S(2)}) collective-permute-start(bf16[352,256]{1,0:T(8,128)(2,1)S(1)} %slice.154), channel_id=1, source_target_pairs={{0,64},{1,65},{2,66},{3,67},{4,68},{5,69},{6,70},{7,71},{8,72},{9,... | collective-permute-start | bytes 540680 | tf_op jit(solution)/shard_map/ppermute | solution.py:27
  34.8 9.7 %collective-permute-start.10 = (bf16[176,256]{1,0:T(8,128)(2,1)S(1)}, bf16[176,256]{1,0:T(8,128)(2,1)S(1)}, u32[]{:S(2)}, u32[]{:S(2)}) collective-permute-start(bf16[176,256]{1,0:T(8,128)(2,1)S(1)} %get-tuple-element.49), channel_id=1, source_target_pairs={{0,8},{1,9},{2,10},{3,11},{4,12},{5,13},{6,14},{7,15},{8,0},{9,1},... | collective-permute-start | bytes 270344 | tf_op jit(solution)/shard_map/ppermute | solution.py:27
  36.2 17.5 %copy-start.4 = (f32[1,43,512]{2,0,1:T(1,128)S(1)}, f32[1,43,512]{2,0,1:T(1,128)}, u32[]{:S(2)}) copy-start(f32[1,43,512]{2,0,1:T(1,128)} %param.11) | copy-start | bytes 264196
  36.2 17.5 %copy-start.5 = (f32[1,43,512]{2,0,1:T(1,128)S(1)}, f32[1,43,512]{2,0,1:T(1,128)}, u32[]{:S(2)}) copy-start(f32[1,43,512]{2,0,1:T(1,128)} %param.10) | copy-start | bytes 264196
  36.2 8.3 %collective-permute-start.11 = (bf16[176,256]{1,0:T(8,128)(2,1)S(1)}, bf16[176,256]{1,0:T(8,128)(2,1)S(1)}, u32[]{:S(2)}, u32[]{:S(2)}) collective-permute-start(bf16[176,256]{1,0:T(8,128)(2,1)S(1)} %get-tuple-element.50), channel_id=1, source_target_pairs={{0,56},{1,57},{2,58},{3,59},{4,60},{5,61},{6,62},{7,63},{8,16},{9,... | collective-permute-start | bytes 270344 | tf_op jit(solution)/shard_map/ppermute | solution.py:27
  38.8 10.2 %collective-permute-start.14 = (bf16[88,256]{1,0:T(8,128)(2,1)S(1)}, bf16[88,256]{1,0:T(8,128)(2,1)S(1)}, u32[]{:S(2)}, u32[]{:S(2)}) collective-permute-start(bf16[88,256]{1,0:T(8,128)(2,1)S(1)} %slice.155), channel_id=1, source_target_pairs={{0,32},{1,33},{2,34},{3,35},{4,36},{5,37},{6,38},{7,39},{8,40},{9,... | collective-permute-start | bytes 135176 | tf_op jit(solution)/shard_map/ppermute | solution.py:27
  44.6 5.1 %collective-permute-start.12 = (bf16[88,256]{1,0:T(8,128)(2,1)S(1)}, bf16[88,256]{1,0:T(8,128)(2,1)S(1)}, u32[]{:S(2)}, u32[]{:S(2)}) collective-permute-start(bf16[88,256]{1,0:T(8,128)(2,1)S(1)} %get-tuple-element.44), channel_id=1, source_target_pairs={{0,16},{1,17},{2,18},{3,19},{4,20},{5,21},{6,22},{7,23},{8,24},{9,... | collective-permute-start | bytes 135176 | tf_op jit(solution)/shard_map/ppermute | solution.py:27
  46.2 6.2 %collective-permute-start.13 = (bf16[88,256]{1,0:T(8,128)(2,1)S(1)}, bf16[88,256]{1,0:T(8,128)(2,1)S(1)}, u32[]{:S(2)}, u32[]{:S(2)}) collective-permute-start(bf16[88,256]{1,0:T(8,128)(2,1)S(1)} %get-tuple-element.45), channel_id=1, source_target_pairs={{0,48},{1,49},{2,50},{3,51},{4,52},{5,53},{6,54},{7,55},{8,56},{9,... | collective-permute-start | bytes 135176 | tf_op jit(solution)/shard_map/ppermute | solution.py:27
  52.4 1.3 %collective-permute-start.15 = (f32[43,256]{1,0:T(8,128)S(1)}, f32[43,256]{1,0:T(8,128)S(1)}, u32[]{:S(2)}, u32[]{:S(2)}) collective-permute-start(f32[43,256]{1,0:T(8,128)S(1)} %slice_select_fusion), channel_id=1, source_target_pairs={{0,4},{1,5},{2,6},{3,7},{4,0},{5,1},{6,2},{7,3},{8,12},{9,13},{10,... | collective-permute-start | bytes 132104 | tf_op jit(solution)/shard_map/ppermute | solution.py:27
  53.7 8.6 %copy-start.1 = (bf16[1,1024,512]{2,1,0:T(8,128)(2,1)S(1)}, bf16[1,1024,512]{2,1,0:T(8,128)(2,1)}, u32[]{:S(2)}) copy-start(bf16[1,1024,512]{2,1,0:T(8,128)(2,1)} %param.9) | copy-start | bytes 3145732
  53.8 8.2 %collective-permute-start.18 = (bf16[64,512]{1,0:T(8,128)(2,1)S(1)}, bf16[64,512]{1,0:T(8,128)(2,1)S(1)}, u32[]{:S(2)}, u32[]{:S(2)}) collective-permute-start(bf16[64,512]{1,0:T(8,128)(2,1)S(1)} %pad.9), channel_id=1, source_target_pairs={{0,3},{1,2},{2,1},{3,0},{4,7},{5,6},{6,5},{7,4},{8,11},{9,10},{10,... | collective-permute-start | bytes 196616 | tf_op jit(solution)/shard_map/ppermute | solution.py:27
  56.4 5.6 %collective-permute-start.17 = (bf16[48,512]{1,0:T(8,128)(2,1)S(1)}, bf16[48,512]{1,0:T(8,128)(2,1)S(1)}, u32[]{:S(2)}, u32[]{:S(2)}) collective-permute-start(bf16[48,512]{1,0:T(8,128)(2,1)S(1)} %pad.8), channel_id=1, source_target_pairs={{0,2},{1,3},{2,0},{3,1},{4,6},{5,7},{6,4},{7,5},{8,10},{9,11},{10,... | collective-permute-start | bytes 147464 | tf_op jit(solution)/shard_map/ppermute | solution.py:27
  56.4 4.2 %collective-permute-start.16 = (bf16[43,512]{1,0:T(8,128)(2,1)S(1)}, bf16[43,512]{1,0:T(8,128)(2,1)S(1)}, u32[]{:S(2)}, u32[]{:S(2)}) collective-permute-start(bf16[43,512]{1,0:T(8,128)(2,1)S(1)} %get-tuple-element.41), channel_id=1, source_target_pairs={{0,1},{1,0},{2,3},{3,2},{4,5},{5,4},{6,7},{7,6},{8,9},{9,8},{10,11... | collective-permute-start | bytes 132104 | tf_op jit(solution)/shard_map/ppermute | solution.py:27
  (3 other events, 8.0 us)

commit v18 on v17

--- a/solution.py
+++ b/solution.py
@@ -110,6 +110,28 @@
             flops=2 * features.size * basis.shape[1], bytes_accessed=2 * 1024 * 1024, transcendentals=0
         ),
     )(core, features, basis)
+
+
+def back_project_kernel(rows, basis, out):
+    wide = lax.dot_general(
+        rows[...], basis[...], (((1,), (1,)), ((), ())), preferred_element_type=F32
+    )
+    for b in range(OWNED):
+        out[b] = wide[b * NY : (b + 1) * NY].astype(BF)
+
+
+def back_project(rows, basis):
+    vmem = pl.BlockSpec(memory_space=pltpu.VMEM)
+    return pl.pallas_call(
+        back_project_kernel,
+        out_shape=jax.ShapeDtypeStruct((OWNED, NY, basis.shape[0]), BF),
+        in_specs=[vmem] * 2,
+        out_specs=vmem,
+        compiler_params=pltpu.CompilerParams(vmem_limit_bytes=8 * 1024 * 1024),
+        cost_estimate=pl.CostEstimate(
+            flops=2 * rows.size * basis.shape[0], bytes_accessed=2 * 1024 * 1024, transcendentals=0
+        ),
+    )(rows, basis)
 
 
 def dot(a, b):
@@ -181,8 +203,8 @@
         around.append(swap_y(jnp.pad(update, ((0, more), (0, 0))), m)[:OWNED])
     ordered = jnp.stack([lax.select_n(y ^ a, *around) for a in range(NY)], axis=1)
     rows = lax.optimization_barrier(ordered.reshape(-1, ordered.shape[2]))
-    change = dot(rows, basis[0].T).reshape(OWNED, NY, -1)
-    return (new_first, new_second, change.astype(BF).transpose(2, 1, 0)[None])
+    change = back_project(rows, basis[0])
+    return (new_first, new_second, change.transpose(2, 1, 0)[None])
 
 
 def solution(mesh):

time: 64.5 us -> 64.4 us (level)
  Pallas kernels: 1.75 us -> 2.98 us
  local copies, waits for them, and re-layouts: 5.07 us -> 4.18 us
    pallas_call x0 -> x1, Pallas kernels: none -> 1.23 us  [back_project(): pl.pallas_call(back_project_kernel, out_shape=jax.ShapeDtypeStruct((OWNED...]
    convert_element_type x1 -> x0, local copies, waits for them, and re-layouts: 0.89 us -> none  [local(): return (new_first, new_second, change.astype(BF).transpose(2, 1, 0)[None])]
    dot_general x5 -> x4, matrix products: 1.88 us -> 1.39 us  [dot(): lax.dot_general(a, b, (((1,), (0,)), ((), ())), preferred_element_type=F32)]
where the time goes in v18:
time: 64.4 us; the launch traced here: 63.5 us
  starting transfers between devices  32.8 us (51%)
  waiting for transfers between devices  19.7 us (31%)
  local copies, waits for them, and re-layouts  4.18 us (6%)
  Pallas kernels  2.98 us (5%)
  other arithmetic  1.48 us (2%)
  matrix products  1.39 us (2%)
  between operations  0.95 us (1%)
    ppermute x19, starting transfers between devices, send(): return lax.ppermute(value, ('dp', 'tensor'), pairs)  32.8 us
    ppermute x19, waiting for transfers between devices, send(): return lax.ppermute(value, ('dp', 'tensor'), pairs)  19.7 us
    unnamed x18, local copies, waits for them, and re-layouts  3.75 us
    dot_general x4, matrix products, dot(): lax.dot_general(a, b, (((1,), (0,)), ((), ())), preferred_element_type=F32)  1.39 us
    pallas_call x1, Pallas kernels, arrange(): pl.pallas_call(arrange_kernel, out_shape=[shape] * 4, in_specs=[smem, vme...  1.3 us
  transfers between devices with their start and end apart: 19, of which 11 were waited for; matrix products, arithmetic and copies ran while one was open for 6% of the time, Pallas kernels for 3%

profile of v18, /device:TPU:32, one launch (start us, length us, event | category | flops | bytes accessed | tf_op | source)
XLA Modules:
  0.0 63.5 jit_solution(13547153919987849655)
XLA Ops:
  0.8 1.2 %copy-done = bf16[1,1024,512]{2,1,0:T(8,128)(2,1)S(1)} copy-done((bf16[1,1024,512]{2,1,0:T(8,128)(2,1)S(1)}, bf16[1,1024,512]{2,1,0:T(8,128)(2,1)}, u32[]{:S(2)}) %copy-start) | copy-done | bytes 1048600
  4.7 1.6 %collective-permute-start.4 = (bf16[256,256]{1,0:T(8,128)(2,1)}, bf16[256,256]{1,0:T(8,128)(2,1)S(1)}, u32[]{:S(2)}, u32[]{:S(2)}) collective-permute-start(bf16[256,256]{1,0:T(8,128)(2,1)} %convert_element_type.84), channel_id=1, source_target_pairs={{0,1},{1,0},{2,3},{3,2},{4,5},{5,4},{6,7},{7,6},{8,9},{9,8},{10,11... | collective-permute-start | bytes 393224 | tf_op jit(solution)/shard_map/ppermute | solution.py:27
  6.6 2.3 %collective-permute-start.1 = (bf16[256,256]{1,0:T(8,128)(2,1)S(1)}, bf16[256,256]{1,0:T(8,128)(2,1)S(1)}, u32[]{:S(2)}, u32[]{:S(2)}) collective-permute-start(bf16[256,256]{1,0:T(8,128)(2,1)S(1)} %collective-permute-done), channel_id=1, source_target_pairs={{0,3},{1,2},{2,1},{3,0},{4,7},{5,6},{6,5},{7,4},{8,11},{9,10},{10,... | collective-permute-start | bytes 393224 | tf_op jit(solution)/shard_map/ppermute | solution.py:27
  8.9 1.5 %collective-permute-done.4 = bf16[256,256]{1,0:T(8,128)(2,1)S(1)} collective-permute-done((bf16[256,256]{1,0:T(8,128)(2,1)}, bf16[256,256]{1,0:T(8,128)(2,1)S(1)}, u32[]{:S(2)}, u32[]{:S(2)}) %collective-permute-start.4) | collective-permute-done | bytes 131104 | tf_op jit(solution)/shard_map/ppermute | solution.py:27
  10.4 3.1 %collective-permute-start.5 = (bf16[256,256]{1,0:T(8,128)(2,1)S(1)}, bf16[256,256]{1,0:T(8,128)(2,1)S(1)}, u32[]{:S(2)}, u32[]{:S(2)}) collective-permute-start(bf16[256,256]{1,0:T(8,128)(2,1)S(1)} %fusion.2), channel_id=1, source_target_pairs={{0,3},{1,2},{2,1},{3,0},{4,7},{5,6},{6,5},{7,4},{8,11},{9,10},{10,... | collective-permute-start | bytes 393224 | tf_op jit(solution)/shard_map/ppermute | solution.py:27
  13.8 2.9 %collective-permute-done.5 = bf16[256,256]{1,0:T(8,128)(2,1)S(1)} collective-permute-done((bf16[256,256]{1,0:T(8,128)(2,1)S(1)}, bf16[256,256]{1,0:T(8,128)(2,1)S(1)}, u32[]{:S(2)}, u32[]{:S(2)}) %collective-permute-start.5) | collective-permute-done | bytes 131104 | tf_op jit(solution)/shard_map/ppermute | solution.py:27
  16.8 1.3 %shard_map.95 = (bf16[704,512]{1,0:T(8,128)(2,1)S(1)}, bf16[704,512]{1,0:T(8,128)(2,1)S(1)}, bf16[704,512]{1,0:T(8,128)(2,1)S(1)}, bf16[704,512]{1,0:T(8,128)(2,1)S(1)}) custom-call(s32[32]{0:T(128)S(1)} %add.93.order_ref, bf16[2752,256]{1,0:T(8,128)(2,1)S(1)} %bitcast.33, bf16[2752,256]{1,0:T(8,128)(2,1)S(1)} %collective-permute-done.3.came), custom_call_target="tpu_custom_call" | custom-call | bytes 8388608 | tf_op jit(solution)/shard_map/pallas_call | solution.py:77
  19.4 1.6 %collective-permute-start.8 = (bf16[704,256]{1,0:T(8,128)(2,1)S(1)}, bf16[704,256]{1,0:T(8,128)(2,1)S(1)}, u32[]{:S(2)}, u32[]{:S(2)}) collective-permute-start(bf16[704,256]{1,0:T(8,128)(2,1)S(1)} %convolution_convert_fusion.1), channel_id=1, source_target_pairs={{0,64},{1,65},{2,66},{3,67},{4,68},{5,69},{6,70},{7,71},{8,72},{9,... | collective-permute-start | bytes 1081352 | tf_op jit(solution)/shard_map/ppermute | solution.py:27
  21.3 2.2 %collective-permute-start.6 = (bf16[704,256]{1,0:T(8,128)(2,1)S(1)}, bf16[704,256]{1,0:T(8,128)(2,1)S(1)}, u32[]{:S(2)}, u32[]{:S(2)}) collective-permute-start(bf16[704,256]{1,0:T(8,128)(2,1)S(1)} %convolution_convert_fusion), channel_id=1, source_target_pairs={{0,192},{1,193},{2,194},{3,195},{4,196},{5,197},{6,198},{7,199},{8... | collective-permute-start | bytes 1081352 | tf_op jit(solution)/shard_map/ppermute | solution.py:27
  23.9 4.0 %collective-permute-done.8 = bf16[704,256]{1,0:T(8,128)(2,1)S(1)} collective-permute-done((bf16[704,256]{1,0:T(8,128)(2,1)S(1)}, bf16[704,256]{1,0:T(8,128)(2,1)S(1)}, u32[]{:S(2)}, u32[]{:S(2)}) %collective-permute-start.8) | collective-permute-done | bytes 360480 | tf_op jit(solution)/shard_map/ppermute | solution.py:27
  28.0 2.8 %collective-permute-start.9 = (bf16[352,256]{1,0:T(8,128)(2,1)S(1)}, bf16[352,256]{1,0:T(8,128)(2,1)S(1)}, u32[]{:S(2)}, u32[]{:S(2)}) collective-permute-start(bf16[352,256]{1,0:T(8,128)(2,1)S(1)} %slice.153), channel_id=1, source_target_pairs={{0,192},{1,193},{2,194},{3,195},{4,196},{5,197},{6,198},{7,199},{8... | collective-permute-start | bytes 540680 | tf_op jit(solution)/shard_map/ppermute | solution.py:27
  30.8 1.6 %collective-permute-done.6 = bf16[704,256]{1,0:T(8,128)(2,1)S(1)} collective-permute-done((bf16[704,256]{1,0:T(8,128)(2,1)S(1)}, bf16[704,256]{1,0:T(8,128)(2,1)S(1)}, u32[]{:S(2)}, u32[]{:S(2)}) %collective-permute-start.6) | collective-permute-done | bytes 360480 | tf_op jit(solution)/shard_map/ppermute | solution.py:27
  32.6 2.2 %collective-permute-done.9 = bf16[352,256]{1,0:T(8,128)(2,1)S(1)} collective-permute-done((bf16[352,256]{1,0:T(8,128)(2,1)S(1)}, bf16[352,256]{1,0:T(8,128)(2,1)S(1)}, u32[]{:S(2)}, u32[]{:S(2)}) %collective-permute-start.9) | collective-permute-done | bytes 180256 | tf_op jit(solution)/shard_map/ppermute | solution.py:27
  34.8 1.4 %collective-permute-start.10 = (bf16[176,256]{1,0:T(8,128)(2,1)S(1)}, bf16[176,256]{1,0:T(8,128)(2,1)S(1)}, u32[]{:S(2)}, u32[]{:S(2)}) collective-permute-start(bf16[176,256]{1,0:T(8,128)(2,1)S(1)} %get-tuple-element.46), channel_id=1, source_target_pairs={{0,8},{1,9},{2,10},{3,11},{4,12},{5,13},{6,14},{7,15},{8,0},{9,1},... | collective-permute-start | bytes 270344 | tf_op jit(solution)/shard_map/ppermute | solution.py:27
  36.2 2.5 %collective-permute-start.11 = (bf16[176,256]{1,0:T(8,128)(2,1)S(1)}, bf16[176,256]{1,0:T(8,128)(2,1)S(1)}, u32[]{:S(2)}, u32[]{:S(2)}) collective-permute-start(bf16[176,256]{1,0:T(8,128)(2,1)S(1)} %get-tuple-element.47), channel_id=1, source_target_pairs={{0,56},{1,57},{2,58},{3,59},{4,60},{5,61},{6,62},{7,63},{8,16},{9,... | collective-permute-start | bytes 270344 | tf_op jit(solution)/shard_map/ppermute | solution.py:27
  38.8 5.7 %collective-permute-start.14 = (bf16[88,256]{1,0:T(8,128)(2,1)S(1)}, bf16[88,256]{1,0:T(8,128)(2,1)S(1)}, u32[]{:S(2)}, u32[]{:S(2)}) collective-permute-start(bf16[88,256]{1,0:T(8,128)(2,1)S(1)} %slice.155), channel_id=1, source_target_pairs={{0,32},{1,33},{2,34},{3,35},{4,36},{5,37},{6,38},{7,39},{8,40},{9,... | collective-permute-start | bytes 135176 | tf_op jit(solution)/shard_map/ppermute | solution.py:27
  44.6 1.6 %collective-permute-start.12 = (bf16[88,256]{1,0:T(8,128)(2,1)S(1)}, bf16[88,256]{1,0:T(8,128)(2,1)S(1)}, u32[]{:S(2)}, u32[]{:S(2)}) collective-permute-start(bf16[88,256]{1,0:T(8,128)(2,1)S(1)} %get-tuple-element.41), channel_id=1, source_target_pairs={{0,16},{1,17},{2,18},{3,19},{4,20},{5,21},{6,22},{7,23},{8,24},{9,... | collective-permute-start | bytes 135176 | tf_op jit(solution)/shard_map/ppermute | solution.py:27
  46.2 2.9 %collective-permute-start.13 = (bf16[88,256]{1,0:T(8,128)(2,1)S(1)}, bf16[88,256]{1,0:T(8,128)(2,1)S(1)}, u32[]{:S(2)}, u32[]{:S(2)}) collective-permute-start(bf16[88,256]{1,0:T(8,128)(2,1)S(1)} %get-tuple-element.42), channel_id=1, source_target_pairs={{0,48},{1,49},{2,50},{3,51},{4,52},{5,53},{6,54},{7,55},{8,56},{9,... | collective-permute-start | bytes 135176 | tf_op jit(solution)/shard_map/ppermute | solution.py:27
  49.7 2.6 %collective-permute-done.13 = bf16[88,256]{1,0:T(8,128)(2,1)S(1)} collective-permute-done((bf16[88,256]{1,0:T(8,128)(2,1)S(1)}, bf16[88,256]{1,0:T(8,128)(2,1)S(1)}, u32[]{:S(2)}, u32[]{:S(2)}) %collective-permute-start.13) | collective-permute-done | bytes 45088 | tf_op jit(solution)/shard_map/ppermute | solution.py:27
  52.5 1.2 %collective-permute-done.15 = f32[43,256]{1,0:T(8,128)S(1)} collective-permute-done((f32[43,256]{1,0:T(8,128)S(1)}, f32[43,256]{1,0:T(8,128)S(1)}, u32[]{:S(2)}, u32[]{:S(2)}) %collective-permute-start.15) | collective-permute-done | bytes 44064 | tf_op jit(solution)/shard_map/ppermute | solution.py:27
  53.8 2.6 %collective-permute-start.18 = (bf16[64,512]{1,0:T(8,128)(2,1)S(1)}, bf16[64,512]{1,0:T(8,128)(2,1)S(1)}, u32[]{:S(2)}, u32[]{:S(2)}) collective-permute-start(bf16[64,512]{1,0:T(8,128)(2,1)S(1)} %pad.9), channel_id=1, source_target_pairs={{0,3},{1,2},{2,1},{3,0},{4,7},{5,6},{6,5},{7,4},{8,11},{9,10},{10,... | collective-permute-start | bytes 196616 | tf_op jit(solution)/shard_map/ppermute | solution.py:27
  56.4 1.6 %collective-permute-start.16 = (bf16[43,512]{1,0:T(8,128)(2,1)S(1)}, bf16[43,512]{1,0:T(8,128)(2,1)S(1)}, u32[]{:S(2)}, u32[]{:S(2)}) collective-permute-start(bf16[43,512]{1,0:T(8,128)(2,1)S(1)} %get-tuple-element.38), channel_id=1, source_target_pairs={{0,1},{1,0},{2,3},{3,2},{4,5},{5,4},{6,7},{7,6},{8,9},{9,8},{10,11... | collective-permute-start | bytes 132104 | tf_op jit(solution)/shard_map/ppermute | solution.py:27
  60.6 1.4 %collective-permute-done.17 = bf16[48,512]{1,0:T(8,128)(2,1)S(1)} collective-permute-done((bf16[48,512]{1,0:T(8,128)(2,1)S(1)}, bf16[48,512]{1,0:T(8,128)(2,1)S(1)}, u32[]{:S(2)}, u32[]{:S(2)}) %collective-permute-start.17) | collective-permute-done | bytes 49184 | tf_op jit(solution)/shard_map/ppermute | solution.py:27
  62.3 1.2 %shard_map.96 = bf16[43,4,1024]{2,1,0:T(4,128)(2,1)} custom-call(bf16[172,512]{1,0:T(8,128)(2,1)S(1)} %reshape.111.rows, bf16[1024,512]{1,0:T(8,128)(2,1)S(1)} %bitcast.31), custom_call_target="tpu_custom_call" | custom-call | flops 180355072 | bytes 2097152 | tf_op jit(solution)/shard_map/pallas_call | solution.py:125
  (72 shorter events, 9.7 us)
Async XLA Ops:
  0.6 5.8 %copy-start.6 = (s32[2,4]{1,0:T(2,128)S(1)}, s32[2,4]{1,0:T(2,128)}, u32[]{:S(2)}) copy-start(s32[2,4]{1,0:T(2,128)} %constant.51.clone) | copy-start | bytes 100
  0.7 16.1 %collective-permute-start.3 = (bf16[2752,256]{1,0:T(8,128)(2,1)}, bf16[2752,256]{1,0:T(8,128)(2,1)S(1)}, u32[]{:S(2)}, u32[]{:S(2)}) collective-permute-start(bf16[2752,256]{1,0:T(8,128)(2,1)} %bitcast.32), channel_id=1, source_target_pairs={{0,4},{1,5},{2,6},{3,7},{4,0},{5,1},{6,2},{7,3},{8,12},{9,13},{10,... | collective-permute-start | bytes 4227080 | tf_op jit(solution)/shard_map/ppermute | solution.py:27
  3.0 13.7 %copy-start.2 = (bf16[1,256,2752]{1,2,0:T(8,128)(2,1)S(1)}, bf16[1,256,2752]{1,2,0:T(8,128)(2,1)}, u32[]{:S(2)}) copy-start(bf16[1,256,2752]{1,2,0:T(8,128)(2,1)} %param.8) | copy-start | bytes 4227076
  3.5 3.1 %collective-permute-start = (bf16[256,256]{1,0:T(8,128)(2,1)S(1)}, bf16[256,256]{1,0:T(8,128)(2,1)S(1)}, u32[]{:S(2)}, u32[]{:S(2)}) collective-permute-start(bf16[256,256]{1,0:T(8,128)(2,1)S(1)} %get-tuple-element.19), channel_id=1, source_target_pairs={{0,4},{1,5},{2,6},{3,7},{4,0},{5,1},{6,2},{7,3},{8,12},{9,13},{10,... | collective-permute-start | bytes 393224 | tf_op jit(solution)/shard_map/ppermute | solution.py:27
  4.7 5.6 %collective-permute-start.4 = (bf16[256,256]{1,0:T(8,128)(2,1)}, bf16[256,256]{1,0:T(8,128)(2,1)S(1)}, u32[]{:S(2)}, u32[]{:S(2)}) collective-permute-start(bf16[256,256]{1,0:T(8,128)(2,1)} %convert_element_type.84), channel_id=1, source_target_pairs={{0,1},{1,0},{2,3},{3,2},{4,5},{5,4},{6,7},{7,6},{8,9},{9,8},{10,11... | collective-permute-start | bytes 393224 | tf_op jit(solution)/shard_map/ppermute | solution.py:27
  6.6 6.9 %collective-permute-start.1 = (bf16[256,256]{1,0:T(8,128)(2,1)S(1)}, bf16[256,256]{1,0:T(8,128)(2,1)S(1)}, u32[]{:S(2)}, u32[]{:S(2)}) collective-permute-start(bf16[256,256]{1,0:T(8,128)(2,1)S(1)} %collective-permute-done), channel_id=1, source_target_pairs={{0,3},{1,2},{2,1},{3,0},{4,7},{5,6},{6,5},{7,4},{8,11},{9,10},{10,... | collective-permute-start | bytes 393224 | tf_op jit(solution)/shard_map/ppermute | solution.py:27
  10.4 6.3 %collective-permute-start.5 = (bf16[256,256]{1,0:T(8,128)(2,1)S(1)}, bf16[256,256]{1,0:T(8,128)(2,1)S(1)}, u32[]{:S(2)}, u32[]{:S(2)}) collective-permute-start(bf16[256,256]{1,0:T(8,128)(2,1)S(1)} %fusion.2), channel_id=1, source_target_pairs={{0,3},{1,2},{2,1},{3,0},{4,7},{5,6},{6,5},{7,4},{8,11},{9,10},{10,... | collective-permute-start | bytes 393224 | tf_op jit(solution)/shard_map/ppermute | solution.py:27
  13.6 5.1 %collective-permute-start.2 = (bf16[256,256]{1,0:T(8,128)(2,1)S(1)}, bf16[256,256]{1,0:T(8,128)(2,1)S(1)}, u32[]{:S(2)}, u32[]{:S(2)}) collective-permute-start(bf16[256,256]{1,0:T(8,128)(2,1)S(1)} %fusion.1), channel_id=1, source_target_pairs={{0,1},{1,0},{2,3},{3,2},{4,5},{5,4},{6,7},{7,6},{8,9},{9,8},{10,11... | collective-permute-start | bytes 393224 | tf_op jit(solution)/shard_map/ppermute | solution.py:27
  19.4 8.4 %collective-permute-start.8 = (bf16[704,256]{1,0:T(8,128)(2,1)S(1)}, bf16[704,256]{1,0:T(8,128)(2,1)S(1)}, u32[]{:S(2)}, u32[]{:S(2)}) collective-permute-start(bf16[704,256]{1,0:T(8,128)(2,1)S(1)} %convolution_convert_fusion.1), channel_id=1, source_target_pairs={{0,64},{1,65},{2,66},{3,67},{4,68},{5,69},{6,70},{7,71},{8,72},{9,... | collective-permute-start | bytes 1081352 | tf_op jit(solution)/shard_map/ppermute | solution.py:27
  21.3 11.0 %collective-permute-start.6 = (bf16[704,256]{1,0:T(8,128)(2,1)S(1)}, bf16[704,256]{1,0:T(8,128)(2,1)S(1)}, u32[]{:S(2)}, u32[]{:S(2)}) collective-permute-start(bf16[704,256]{1,0:T(8,128)(2,1)S(1)} %convolution_convert_fusion), channel_id=1, source_target_pairs={{0,192},{1,193},{2,194},{3,195},{4,196},{5,197},{6,198},{7,199},{8... | collective-permute-start | bytes 1081352 | tf_op jit(solution)/shard_map/ppermute | solution.py:27
  28.0 6.8 %collective-permute-start.9 = (bf16[352,256]{1,0:T(8,128)(2,1)S(1)}, bf16[352,256]{1,0:T(8,128)(2,1)S(1)}, u32[]{:S(2)}, u32[]{:S(2)}) collective-permute-start(bf16[352,256]{1,0:T(8,128)(2,1)S(1)} %slice.153), channel_id=1, source_target_pairs={{0,192},{1,193},{2,194},{3,195},{4,196},{5,197},{6,198},{7,199},{8... | collective-permute-start | bytes 540680 | tf_op jit(solution)/shard_map/ppermute | solution.py:27
  32.5 6.3 %collective-permute-start.7 = (bf16[352,256]{1,0:T(8,128)(2,1)S(1)}, bf16[352,256]{1,0:T(8,128)(2,1)S(1)}, u32[]{:S(2)}, u32[]{:S(2)}) collective-permute-start(bf16[352,256]{1,0:T(8,128)(2,1)S(1)} %slice.154), channel_id=1, source_target_pairs={{0,64},{1,65},{2,66},{3,67},{4,68},{5,69},{6,70},{7,71},{8,72},{9,... | collective-permute-start | bytes 540680 | tf_op jit(solution)/shard_map/ppermute | solution.py:27
  34.8 9.7 %collective-permute-start.10 = (bf16[176,256]{1,0:T(8,128)(2,1)S(1)}, bf16[176,256]{1,0:T(8,128)(2,1)S(1)}, u32[]{:S(2)}, u32[]{:S(2)}) collective-permute-start(bf16[176,256]{1,0:T(8,128)(2,1)S(1)} %get-tuple-element.46), channel_id=1, source_target_pairs={{0,8},{1,9},{2,10},{3,11},{4,12},{5,13},{6,14},{7,15},{8,0},{9,1},... | collective-permute-start | bytes 270344 | tf_op jit(solution)/shard_map/ppermute | solution.py:27
  36.2 17.5 %copy-start.4 = (f32[1,43,512]{2,0,1:T(1,128)S(1)}, f32[1,43,512]{2,0,1:T(1,128)}, u32[]{:S(2)}) copy-start(f32[1,43,512]{2,0,1:T(1,128)} %param.11) | copy-start | bytes 264196
  36.2 17.5 %copy-start.5 = (f32[1,43,512]{2,0,1:T(1,128)S(1)}, f32[1,43,512]{2,0,1:T(1,128)}, u32[]{:S(2)}) copy-start(f32[1,43,512]{2,0,1:T(1,128)} %param.10) | copy-start | bytes 264196
  36.2 8.3 %collective-permute-start.11 = (bf16[176,256]{1,0:T(8,128)(2,1)S(1)}, bf16[176,256]{1,0:T(8,128)(2,1)S(1)}, u32[]{:S(2)}, u32[]{:S(2)}) collective-permute-start(bf16[176,256]{1,0:T(8,128)(2,1)S(1)} %get-tuple-element.47), channel_id=1, source_target_pairs={{0,56},{1,57},{2,58},{3,59},{4,60},{5,61},{6,62},{7,63},{8,16},{9,... | collective-permute-start | bytes 270344 | tf_op jit(solution)/shard_map/ppermute | solution.py:27
  38.8 10.2 %collective-permute-start.14 = (bf16[88,256]{1,0:T(8,128)(2,1)S(1)}, bf16[88,256]{1,0:T(8,128)(2,1)S(1)}, u32[]{:S(2)}, u32[]{:S(2)}) collective-permute-start(bf16[88,256]{1,0:T(8,128)(2,1)S(1)} %slice.155), channel_id=1, source_target_pairs={{0,32},{1,33},{2,34},{3,35},{4,36},{5,37},{6,38},{7,39},{8,40},{9,... | collective-permute-start | bytes 135176 | tf_op jit(solution)/shard_map/ppermute | solution.py:27
  44.6 5.1 %collective-permute-start.12 = (bf16[88,256]{1,0:T(8,128)(2,1)S(1)}, bf16[88,256]{1,0:T(8,128)(2,1)S(1)}, u32[]{:S(2)}, u32[]{:S(2)}) collective-permute-start(bf16[88,256]{1,0:T(8,128)(2,1)S(1)} %get-tuple-element.41), channel_id=1, source_target_pairs={{0,16},{1,17},{2,18},{3,19},{4,20},{5,21},{6,22},{7,23},{8,24},{9,... | collective-permute-start | bytes 135176 | tf_op jit(solution)/shard_map/ppermute | solution.py:27
  46.2 6.2 %collective-permute-start.13 = (bf16[88,256]{1,0:T(8,128)(2,1)S(1)}, bf16[88,256]{1,0:T(8,128)(2,1)S(1)}, u32[]{:S(2)}, u32[]{:S(2)}) collective-permute-start(bf16[88,256]{1,0:T(8,128)(2,1)S(1)} %get-tuple-element.42), channel_id=1, source_target_pairs={{0,48},{1,49},{2,50},{3,51},{4,52},{5,53},{6,54},{7,55},{8,56},{9,... | collective-permute-start | bytes 135176 | tf_op jit(solution)/shard_map/ppermute | solution.py:27
  52.4 1.3 %collective-permute-start.15 = (f32[43,256]{1,0:T(8,128)S(1)}, f32[43,256]{1,0:T(8,128)S(1)}, u32[]{:S(2)}, u32[]{:S(2)}) collective-permute-start(f32[43,256]{1,0:T(8,128)S(1)} %slice_select_fusion), channel_id=1, source_target_pairs={{0,4},{1,5},{2,6},{3,7},{4,0},{5,1},{6,2},{7,3},{8,12},{9,13},{10,... | collective-permute-start | bytes 132104 | tf_op jit(solution)/shard_map/ppermute | solution.py:27
  53.7 8.6 %copy-start.1 = (bf16[1,1024,512]{2,1,0:T(8,128)(2,1)S(1)}, bf16[1,1024,512]{2,1,0:T(8,128)(2,1)}, u32[]{:S(2)}) copy-start(bf16[1,1024,512]{2,1,0:T(8,128)(2,1)} %param.9) | copy-start | bytes 3145732
  53.8 8.2 %collective-permute-start.18 = (bf16[64,512]{1,0:T(8,128)(2,1)S(1)}, bf16[64,512]{1,0:T(8,128)(2,1)S(1)}, u32[]{:S(2)}, u32[]{:S(2)}) collective-permute-start(bf16[64,512]{1,0:T(8,128)(2,1)S(1)} %pad.9), channel_id=1, source_target_pairs={{0,3},{1,2},{2,1},{3,0},{4,7},{5,6},{6,5},{7,4},{8,11},{9,10},{10,... | collective-permute-start | bytes 196616 | tf_op jit(solution)/shard_map/ppermute | solution.py:27
  56.4 5.6 %collective-permute-start.17 = (bf16[48,512]{1,0:T(8,128)(2,1)S(1)}, bf16[48,512]{1,0:T(8,128)(2,1)S(1)}, u32[]{:S(2)}, u32[]{:S(2)}) collective-permute-start(bf16[48,512]{1,0:T(8,128)(2,1)S(1)} %pad.8), channel_id=1, source_target_pairs={{0,2},{1,3},{2,0},{3,1},{4,6},{5,7},{6,4},{7,5},{8,10},{9,11},{10,... | collective-permute-start | bytes 147464 | tf_op jit(solution)/shard_map/ppermute | solution.py:27
  56.4 4.2 %collective-permute-start.16 = (bf16[43,512]{1,0:T(8,128)(2,1)S(1)}, bf16[43,512]{1,0:T(8,128)(2,1)S(1)}, u32[]{:S(2)}, u32[]{:S(2)}) collective-permute-start(bf16[43,512]{1,0:T(8,128)(2,1)S(1)} %get-tuple-element.38), channel_id=1, source_target_pairs={{0,1},{1,0},{2,3},{3,2},{4,5},{5,4},{6,7},{7,6},{8,9},{9,8},{10,11... | collective-permute-start | bytes 132104 | tf_op jit(solution)/shard_map/ppermute | solution.py:27
  (3 other events, 8.0 us)
